TPU v7x, 256 devices: a whole 4x4x8 slice. The times are simulated.
256 devices in a mesh: lon: 64 (over x, z, y_hi), lat: 4 (over y_lo, core).
Axes of the slice: x: 4, y: 4 (y_hi: 2, y_lo: 2; y = y_hi * 2 + y_lo), z: 8, core: 2. Of those that a mesh axis runs over, the one named last changes fastest.
Arguments:
- features: bfloat16 [32, 8192, 256], P('lat', 'lon'), may hold values from -8 to 8
- conv_weight: bfloat16 [3, 3, 256, 256], replicated, may hold values from -0.125 to 0.125
- down_weight: bfloat16 [3, 3, 256, 256], replicated, may hold values from -0.125 to 0.125
- norm_gain: float32 [256], replicated, may hold values from 0.1 to 1.9
- norm_bias: float32 [256], replicated, may hold values from -3 to 3
- cotangent: bfloat16 [16, 4096, 256], P('lat', 'lon'), may hold values from -8 to 8
Outputs:
- output: bfloat16 [16, 4096, 256], P('lat', 'lon')
- input_grad: bfloat16 [32, 8192, 256], P('lat', 'lon')
- conv_grad: float32 [3, 3, 256, 256], replicated
- down_grad: float32 [3, 3, 256, 256], replicated
- gain_grad: float32 [256], replicated
- bias_grad: float32 [256], replicated
All inputs are finite; a program needn't handle non-finite values.
Results may differ from a plain program's by a relative error of at most 0.015.
Values may be sent and summed in bfloat16 or wider, within the bound.
No kernel may reach another device: no remote copies, remote signals or barrier semaphores. Data moves between devices by JAX's collectives and lax.ppermute only.
A program may use at most 64 MiB of HBM per device.

v0:
```python
import math

import jax
import jax.numpy as jnp
from jax import lax
from jax.sharding import PartitionSpec as P

GROUPS = 32


EPS = 1e-05


def extended(value, sides, width, wrap):
    for axis, dim in sides:
        size, length = (lax.axis_size(axis), value.shape[dim])
        up = [(i, (i + 1) % size) for i in range(size if wrap else size - 1)]
        down = [(j, i) for i, j in up]
        last = lax.slice_in_dim(value, length - width, length, axis=dim)
        first = lax.slice_in_dim(value, 0, width, axis=dim)
        before = lax.ppermute(last, axis, up)
        after = lax.ppermute(first, axis, down)
        value = jnp.concatenate([before, value, after], axis=dim)
    return value


def passed_along(value, axis, steps):
    count = lax.axis_size(axis)
    pairs = [(source, (source + steps) % count) for source in range(count)]
    return lax.ppermute(value, axis, pairs)


def shifted_2(block, axis, distance):
    devices = range(lax.axis_size(axis))
    route = [(i - distance, i) for i in devices if i - distance in devices]
    return lax.ppermute(block, axis, route)


def conv_taps(padded, weight, rows, cols, step):
    chans = padded.shape[2]
    total = jnp.zeros((rows * cols, weight.shape[3]), jnp.float32)
    for tap_a in range(3):
        for tap_b in range(3):
            piece = padded[tap_a : tap_a + step * rows : step, tap_b : tap_b + step * cols : step]
            piece = piece.reshape(rows * cols, chans)
            total = total + jnp.dot(piece, weight[tap_a, tap_b], preferred_element_type=jnp.float32)
    return total.reshape(rows, cols, -1)


def tap_grads(padded, grad, rows, cols, step):
    chans = padded.shape[2]
    flat_grad = grad.reshape(rows * cols, grad.shape[2])
    results = []
    for tap_a in range(3):
        for tap_b in range(3):
            piece = padded[tap_a : tap_a + step * rows : step, tap_b : tap_b + step * cols : step]
            piece = piece.reshape(rows * cols, chans)
            results.append(
                lax.dot_general(
                    piece, flat_grad, (((0,), (0,)), ((), ())), preferred_element_type=jnp.float32
                )
            )
    return jnp.stack(results).reshape(3, 3, chans, grad.shape[2])


def conv_data_grad(padded_grad, weight, rows, cols):
    chans = padded_grad.shape[2]
    total = jnp.zeros((rows * cols, weight.shape[2]), jnp.float32)
    for tap_a in range(3):
        for tap_b in range(3):
            piece = padded_grad[2 - tap_a : 2 - tap_a + rows, 2 - tap_b : 2 - tap_b + cols].reshape(
                rows * cols, chans
            )
            total = total + lax.dot_general(
                piece,
                weight[tap_a, tap_b],
                (((1,), (1,)), ((), ())),
                preferred_element_type=jnp.float32,
            )
    return total.reshape(rows, cols, -1)


def down_back(grad, weight, rows, cols):
    flat_grad = grad.reshape(rows * cols, grad.shape[2])
    total = jnp.zeros((2 * rows + 1, 2 * cols + 1, weight.shape[2]), jnp.float32)
    for tap_a in range(3):
        for tap_b in range(3):
            term = lax.dot_general(
                flat_grad,
                weight[tap_a, tap_b],
                (((1,), (1,)), ((), ())),
                preferred_element_type=jnp.float32,
            )
            term = term.reshape(rows, cols, -1)
            total = total + lax.pad(
                term,
                jnp.zeros((), term.dtype),
                ((tap_a, 2 - tap_a, 1), (tap_b, 2 - tap_b, 1), (0, 0, 0)),
            )
    return total


def group_total(vector):
    return vector.reshape(GROUPS, -1).sum(axis=1)


def extend(field):
    widened = extended(field, (("lon", 1),), 1, True)
    return extended(widened, (("lat", 0),), 1, False)


def local(features, conv_weight, down_weight, norm_gain, norm_bias, cotangent):
    rows, cols, chans = features.shape
    out_rows, out_cols = (cotangent.shape[0], cotangent.shape[1])
    width = chans // GROUPS
    cells = rows * lax.axis_size("lat") * cols * lax.axis_size("lon")
    count = cells * width
    framed = extend(features)
    hidden = conv_taps(framed, conv_weight, rows, cols, 1).astype(jnp.bfloat16)
    wide = hidden.astype(jnp.float32)
    local_sum = jnp.sum(wide, axis=(0, 1))
    mean = jnp.repeat(group_total(lax.psum(local_sum, ("lon", "lat"))) / count, width)
    centered = wide - mean
    var_g = group_total(lax.psum(jnp.sum(centered * centered, axis=(0, 1)), ("lon", "lat"))) / count
    inverse = jnp.repeat(lax.rsqrt(var_g + EPS), width)
    normed = centered * inverse
    shifted = norm_gain * normed + norm_bias
    sigma = jax.nn.sigmoid(shifted)
    active = (shifted * sigma).astype(jnp.bfloat16)
    edge_col = passed_along(active[:, -1:], "lon", 1)
    with_col = jnp.concatenate([edge_col, active], axis=1)
    top_row = shifted_2(with_col[-1:], "lat", 1)
    padded_act = jnp.concatenate([top_row, with_col], axis=0)
    output = conv_taps(padded_act, down_weight, out_rows, out_cols, 2).astype(jnp.bfloat16)
    down_part = tap_grads(padded_act, cotangent, out_rows, out_cols, 2)
    frame = down_back(cotangent, down_weight, out_rows, out_cols)
    below = shifted_2(frame[0:1], "lat", -1)
    frame = frame.at[rows : rows + 1].add(below)
    beside = passed_along(frame[1:, 0:1], "lon", -1)
    act_grad = frame[1:, 1:].at[:, cols - 1 : cols].add(beside).astype(jnp.bfloat16)
    pre = act_grad.astype(jnp.float32) * sigma * (1.0 + shifted * (1.0 - sigma))
    bias_sum, gain_sum = lax.psum(
        (jnp.sum(pre, axis=(0, 1)), jnp.sum(pre * normed, axis=(0, 1))), ("lon", "lat")
    )
    first = jnp.repeat(group_total(norm_gain * bias_sum) / count, width)
    second = jnp.repeat(group_total(norm_gain * gain_sum) / count, width)
    hidden_grad = (inverse * (norm_gain * pre - first - normed * second)).astype(jnp.bfloat16)
    grad_framed = extend(hidden_grad)
    input_grad = conv_data_grad(grad_framed, conv_weight, rows, cols).astype(jnp.bfloat16)
    conv_part = tap_grads(framed, hidden_grad, rows, cols, 1)
    conv_total, down_total = lax.psum((conv_part, down_part), ("lon", "lat"))
    factor = 1.0 / math.sqrt(cells)
    return (
        output,
        input_grad,
        conv_total * factor,
        down_total * factor,
        gain_sum * factor,
        bias_sum * factor,
    )


def solution(mesh):
    return jax.shard_map(
        local,
        mesh=mesh,
        in_specs=(P("lat", "lon", None), P(), P(), P(), P(), P("lat", "lon", None)),
        out_specs=(P("lat", "lon", None), P("lat", "lon", None), P(), P(), P(), P()),
        check_vma=False,
    )
```

profile of v0, /device:TPU:1, one launch (start us, length us, event | category | flops | bytes accessed | tf_op | source)
XLA Modules:
  0.0 681.4 jit_solution(1002593147436676068)
XLA Ops:
  9.2 11.2 %collective-permute-start.1 = (bf16[8,1,256]{1,2,0:T(8,128)(2,1)}, bf16[8,1,256]{1,2,0:T(8,128)(2,1)}, u32[]{:S(2)}, u32[]{:S(2)}) collective-permute-start(bf16[8,1,256]{1,2,0:T(8,128)(2,1)} %copy.20), channel_id=1, source_target_pairs={{4,0},{8,4},{12,8},{16,12},{20,16},{24,20},{28,24},{32,28},{36,32}... | collective-permute-start | bytes 12296 | tf_op jit(solution)/shard_map/ppermute | solution.py:22
  28.1 1.8 pad.38
  30.0 4.1 pad.37
  34.0 4.1 pad.36
  38.1 4.1 pad.35
  42.2 4.1 pad.34
  46.3 2.5 pad.33
  48.8 2.5 pad.32
  51.3 2.5 pad.31
  53.8 4.5 add_add_fusion
  59.3 2.9 collective-permute-start.6
  63.6 1.9 collective-permute-start.3
  65.6 3.6 collective-permute-start.2
  69.2 1.8 pad_maximum_fusion.5
  73.2 2.7 pad_maximum_fusion
  75.9 2.1 fusion.119
  77.9 2.1 copy.31
  80.0 2.1 copy.30
  84.1 2.1 copy.23
  86.2 2.1 copy.24
  88.3 1.4 fusion.73
  97.6 75.8 %psum.42 = f32[32,8]{1,0:T(8,128)S(1)} all-reduce(f32[32,8]{1,0:T(8,128)S(1)} %reshape.241), channel_id=1, replica_groups=mesh['lon'=64,'lat'=4] {'lon','lat'}, use_global_device_ids=true, to_apply=%region_1.0 | all-reduce | flops 256 | bytes 2048 | tf_op jit(solution)/shard_map/psum | solution.py:122
  174.0 73.6 %psum.43 = f32[32,8]{1,0:T(8,128)S(1)} all-reduce(f32[32,8]{1,0:T(8,128)S(1)} %reshape.242), channel_id=1, replica_groups=mesh['lon'=64,'lat'=4] {'lon','lat'}, use_global_device_ids=true, to_apply=%region_4.0 | all-reduce | flops 256 | bytes 2048 | tf_op jit(solution)/shard_map/psum | solution.py:124
  247.7 1.6 fusion.24
  250.1 4.1 collective-permute-start.7
  254.4 1.4 slice.337
  256.7 2.3 fusion.118
  259.6 1.4 slice.305
  261.0 1.4 slice.301
  262.4 1.4 slice.299
  263.8 76.7 %all-reduce.9 = (f32[256]{0:T(256)S(1)}, f32[256]{0:T(256)S(1)}) all-reduce(f32[256]{0:T(256)S(1)} %get-tuple-element.31, f32[256]{0:T(256)S(1)} %get-tuple-element.30), channel_id=1, replica_groups=mesh['lon'=64,'lat'=4] {'lon','lat'}, use_global_device_ids=true, to_apply=%region_10.0 | all-reduce | flops 512 | bytes 4096 | tf_op jit(solution)/shard_map/psum | solution.py:142
  341.8 1.6 multiply_convert_fusion
  346.2 1.4 collective-permute-start.4
  357.3 1.4 slice.307
  358.7 5.8 collective-permute-start.9
  365.8 4.0 collective-permute-start.5
  370.5 1.9 collective-permute-start.10
  372.5 3.9 collective-permute-start.11
  377.6 1.6 pad_maximum_fusion.1
  379.2 3.2 slice.297
  382.4 3.0 slice.303
  385.4 1.9 maximum_maximum_fusion.1
  387.3 2.0 slice.295
  389.3 2.0 slice.293
  391.3 2.0 slice.291
  411.1 258.4 %all-reduce.13.cloned.1.call-done = (f32[3,3,256,256]{3,2,1,0:T(8,128)}, f32[3,3,256,256]{3,2,1,0:T(8,128)}) async-done(((f32[3,3,256,256]{3,2,1,0:T(8,128)}, f32[3,3,256,256]{3,2,1,0:T(8,128)}), (f32[3,3,256,256]{3,2,1,0:T(8,128)}, f32[3,3,256,256]{3,2,1,0:T(8,128)})) %all-reduce.13.cloned.1.call-update) | async-done | bytes 4718608 | tf_op jit(solution)/shard_map/psum | solution.py:151
  669.6 3.4 broadcast_multiply_fusion.1
  673.0 1.6 broadcast_multiply_fusion
  (177 shorter events, 62.0 us)
Async XLA Ops:
  7.2 14.3 %copy-start = (bf16[4,64,256]{2,1,0:T(8,128)(2,1)S(1)}, bf16[4,64,256]{2,1,0:T(8,128)(2,1)}, u32[]{:S(2)}) copy-start(bf16[4,64,256]{2,1,0:T(8,128)(2,1)} %param.15) | copy-start | bytes 393220
  7.2 15.4 %copy-start.9 = (bf16[3,3,256,256]{3,2,1,0:T(8,128)(2,1)S(1)}, bf16[3,3,256,256]{3,2,1,0:T(8,128)(2,1)}, u32[]{:S(2)}) copy-start(bf16[3,3,256,256]{3,2,1,0:T(8,128)(2,1)} %param.12) | copy-start | bytes 3538948
  7.2 662.4 %all-reduce.13.cloned.1.call-start = ((), (), s32[]{:S(2)}) async-start(), calls=%async_computation | async-start | bytes 9437184 | tf_op jit(solution)/shard_map/psum | solution.py:151
  9.2 53.3 %collective-permute-start.1 = (bf16[8,1,256]{1,2,0:T(8,128)(2,1)}, bf16[8,1,256]{1,2,0:T(8,128)(2,1)}, u32[]{:S(2)}, u32[]{:S(2)}) collective-permute-start(bf16[8,1,256]{1,2,0:T(8,128)(2,1)} %copy.20), channel_id=1, source_target_pairs={{4,0},{8,4},{12,8},{16,12},{20,16},{24,20},{28,24},{32,28},{36,32}... | collective-permute-start | bytes 12296 | tf_op jit(solution)/shard_map/ppermute | solution.py:22
  21.5 41.0 %collective-permute-start = (bf16[8,1,256]{1,2,0:T(8,128)(2,1)}, bf16[8,1,256]{1,2,0:T(8,128)(2,1)}, u32[]{:S(2)}, u32[]{:S(2)}) collective-permute-start(bf16[8,1,256]{1,2,0:T(8,128)(2,1)} %copy.19), channel_id=1, source_target_pairs={{0,4},{4,8},{8,12},{12,16},{16,20},{20,24},{24,28},{28,32},{32,36}... | collective-permute-start | bytes 12296 | tf_op jit(solution)/shard_map/ppermute | solution.py:21
  53.8 8.4 %copy-start.3 = (bf16[8,128,256]{2,1,0:T(8,128)(2,1)S(1)}, bf16[8,128,256]{2,1,0:T(8,128)(2,1)}, u32[]{:S(2)}) copy-start(bf16[8,128,256]{2,1,0:T(8,128)(2,1)} %param.10) | copy-start | bytes 1572868
  58.3 1.1 copy-start.14
  59.3 188.3 %collective-permute-start.6 = (f32[1,129,256]{2,1,0:T(8,128)}, f32[1,129,256]{2,1,0:T(8,128)S(1)}, u32[]{:S(2)}, u32[]{:S(2)}) collective-permute-start(f32[1,129,256]{2,1,0:T(8,128)} %slice.336), channel_id=1, source_target_pairs={{1,0},{2,1},{3,2},{5,4},{6,5},{7,6},{9,8},{10,9},{11,10},{13,12},{... | collective-permute-start | bytes 396296 | tf_op jit(solution)/shard_map/ppermute | solution.py:36
  63.6 9.6 %collective-permute-start.3 = (bf16[1,130,256]{1,2,0:T(8,128)(2,1)S(1)}, bf16[1,130,256]{1,2,0:T(8,128)(2,1)S(1)}, u32[]{:S(2)}, u32[]{:S(2)}) collective-permute-start(bf16[1,130,256]{1,2,0:T(8,128)(2,1)S(1)} %get-tuple-element.39), channel_id=1, source_target_pairs={{1,0},{2,1},{3,2},{5,4},{6,5},{7,6},{9,8},{10,9},{11,10},{13,12},{... | collective-permute-start | bytes 199688 | tf_op jit(solution)/shard_map/ppermute | solution.py:22
  65.6 7.6 %collective-permute-start.2 = (bf16[1,130,256]{1,2,0:T(8,128)(2,1)S(1)}, bf16[1,130,256]{1,2,0:T(8,128)(2,1)}, u32[]{:S(2)}, u32[]{:S(2)}) collective-permute-start(bf16[1,130,256]{1,2,0:T(8,128)(2,1)S(1)} %get-tuple-element.40), channel_id=1, source_target_pairs={{0,1},{1,2},{2,3},{4,5},{5,6},{6,7},{8,9},{9,10},{10,11},{12,13},{... | collective-permute-start | bytes 199688 | tf_op jit(solution)/shard_map/ppermute | solution.py:21
  71.0 2.2 copy-start.7
  71.0 4.8 copy-start.5
  75.9 2.1 copy-start.1
  84.1 4.2 copy-start.11
  88.3 1.4 copy-start.21
  89.7 1.0 copy-start.22
  90.7 1.0 copy-start.18
  92.1 1.0 copy-start.17
  93.1 1.0 copy-start.20
  94.2 1.0 copy-start.19
  95.2 1.0 copy-start.16
  173.7 83.0 %copy-start.31 = (f32[256]{0:T(256)S(1)}, f32[256]{0:T(256)}, u32[]{:S(2)}) copy-start(f32[256]{0:T(256)} %param.13) | copy-start | bytes 3076
  250.1 5.6 collective-permute-start.7
  341.8 2.2 copy-start.2
  343.4 4.1 copy-start.12
  345.1 24.8 %collective-permute-start.8 = (bf16[8,1,256]{2,1,0:T(2,128)(2,1)}, bf16[8,1,256]{2,1,0:T(2,128)(2,1)S(1)}, u32[]{:S(2)}, u32[]{:S(2)}) collective-permute-start(bf16[8,1,256]{2,1,0:T(2,128)(2,1)} %get-tuple-element.60), channel_id=1, source_target_pairs={{0,4},{4,8},{8,12},{12,16},{16,20},{20,24},{24,28},{28,32},{32,36}... | collective-permute-start | bytes 12296 | tf_op jit(solution)/shard_map/ppermute | solution.py:21
  346.2 18.3 %collective-permute-start.4 = (bf16[8,1,256]{2,1,0:T(2,128)(2,1)}, bf16[8,1,256]{2,1,0:T(2,128)(2,1)}, u32[]{:S(2)}, u32[]{:S(2)}) collective-permute-start(bf16[8,1,256]{2,1,0:T(2,128)(2,1)} %slice.332), channel_id=1, source_target_pairs={{0,4},{4,8},{8,12},{12,16},{16,20},{20,24},{24,28},{28,32},{32,36}... | collective-permute-start | bytes 12296 | tf_op jit(solution)/shard_map/ppermute | solution.py:30
  348.9 2.1 copy-start.8
  350.0 2.1 copy-start.4
  351.1 2.1 copy-start.6
  358.7 11.1 %collective-permute-start.9 = (bf16[8,1,256]{2,1,0:T(2,128)(2,1)}, bf16[8,1,256]{2,1,0:T(2,128)(2,1)S(1)}, u32[]{:S(2)}, u32[]{:S(2)}) collective-permute-start(bf16[8,1,256]{2,1,0:T(2,128)(2,1)} %get-tuple-element.61), channel_id=1, source_target_pairs={{4,0},{8,4},{12,8},{16,12},{20,16},{24,20},{28,24},{32,28},{36,32}... | collective-permute-start | bytes 12296 | tf_op jit(solution)/shard_map/ppermute | solution.py:22
  365.8 19.6 %collective-permute-start.5 = (bf16[1,129,256]{2,1,0:T(8,128)(2,1)}, bf16[1,129,256]{2,1,0:T(8,128)(2,1)}, u32[]{:S(2)}, u32[]{:S(2)}) collective-permute-start(bf16[1,129,256]{2,1,0:T(8,128)(2,1)} %fusion.111), channel_id=1, source_target_pairs={{0,1},{1,2},{2,3},{4,5},{5,6},{6,7},{8,9},{9,10},{10,11},{12,13},{... | collective-permute-start | bytes 198152 | tf_op jit(solution)/shard_map/ppermute | solution.py:36
  370.5 33.7 %collective-permute-start.10 = (bf16[1,130,256]{2,1,0:T(8,128)(2,1)}, bf16[1,130,256]{2,1,0:T(8,128)(2,1)}, u32[]{:S(2)}, u32[]{:S(2)}) collective-permute-start(bf16[1,130,256]{2,1,0:T(8,128)(2,1)} %get-tuple-element.56), channel_id=1, source_target_pairs={{1,0},{2,1},{3,2},{5,4},{6,5},{7,6},{9,8},{10,9},{11,10},{13,12},{... | collective-permute-start | bytes 199688 | tf_op jit(solution)/shard_map/ppermute | solution.py:22
  372.5 31.8 %collective-permute-start.11 = (bf16[1,130,256]{2,1,0:T(8,128)(2,1)}, bf16[1,130,256]{2,1,0:T(8,128)(2,1)}, u32[]{:S(2)}, u32[]{:S(2)}) collective-permute-start(bf16[1,130,256]{2,1,0:T(8,128)(2,1)} %get-tuple-element.57), channel_id=1, source_target_pairs={{0,1},{1,2},{2,3},{4,5},{5,6},{6,7},{8,9},{9,10},{10,11},{12,13},{... | collective-permute-start | bytes 199688 | tf_op jit(solution)/shard_map/ppermute | solution.py:21
  379.2 14.1 %copy-start.10 = (bf16[3,3,256,256]{3,2,1,0:T(8,128)(2,1)S(1)}, bf16[3,3,256,256]{3,2,1,0:T(8,128)(2,1)}, u32[]{:S(2)}) copy-start(bf16[3,3,256,256]{3,2,1,0:T(8,128)(2,1)} %param.12) | copy-start | bytes 3538948
  394.4 2.3 copy-start.30
  395.6 2.3 copy-start.28
  396.7 2.3 copy-start.27
  397.8 2.3 copy-start.29
  399.0 2.3 copy-start.26
  400.1 2.3 copy-start.25
  406.9 1.2 copy-start.13
  407.0 1.3 copy-start.24
  408.3 1.0 copy-start.23
  669.6 3.4 copy-start.15
Sparse Core Ops, SparseCore 0:
  404.3 265.1 all-reduce.12
where the time goes:
time: 685 us; the launch traced here: 681 us
  waiting for transfers between devices  258 us (38%)
  blocking collectives  226 us (33%)
  local copies, waits for them, and re-layouts  73.8 us (11%)
  starting transfers between devices  41.9 us (6%)
  matrix products  35.9 us (5%)
  other arithmetic  30.5 us (4%)
  between operations  14.7 us (2%)
    psum x1, waiting for transfers between devices, local(): conv_total, down_total = lax.psum((conv_part, down_part), ('lon', 'lat'))  258 us
    psum x1, blocking collectives, local(): lax.psum((jnp.sum(pre, axis=(0, 1)), jnp.sum(pre * normed, axis=(0, 1))),...  76.7 us
    psum x1, blocking collectives, local(): lax.psum(local_sum, ('lon', 'lat'))  75.8 us
    psum x1, blocking collectives, local(): lax.psum(jnp.sum(centered * centered, axis=(0, 1)), ('lon', 'lat'))  73.6 us
    slice x18, local copies, waits for them, and re-layouts, conv_taps(): padded[tap_a:tap_a + step * rows:step, tap_b:tap_b + step * cols:step]  32.4 us
    pad x9, local copies, waits for them, and re-layouts, down_back(): lax.pad(term, jnp.zeros((), term.dtype), ((tap_a, 2 - tap_a, 1), (tap_b,...  25.8 us
    ppermute x4, starting transfers between devices, extended(): after = lax.ppermute(first, axis, down)  20.9 us
    dot_general x18, matrix products, tap_grads(): lax.dot_general(piece, flat_grad, (((0,), (0,)), ((), ())), preferred_ele...  17.7 us
  transfers between devices with their start and end apart: 13, of which 1 were waited for; matrix products, arithmetic and copies ran while one was open for 16% of the time, Pallas kernels for 0%

commit v1 on v0

v1 whole, which is shorter than its diff:
```python
import functools
import math

import jax
import jax.numpy as jnp
from jax import lax
from jax.experimental import pallas as pl
from jax.experimental.pallas import tpu as pltpu
from jax.sharding import Mesh
from jax.sharding import PartitionSpec as P

EPS = 1e-05
WIDTH = 8
J = 80
LON = ("x", "z", "y_hi")
LAT = ("y_lo", "core")
PLANE = ("x", "y_hi", "y_lo")
ALL = LON + LAT
BF = jnp.bfloat16
F32 = jnp.float32


def call(body, outs, scratch=(), flops=0, smem=(), n_in=0):
    specs = [
        pl.BlockSpec(memory_space=pltpu.SMEM) if i in smem else pl.BlockSpec(memory_space=pltpu.VMEM)
        for i in range(n_in)
    ]
    return pl.pallas_call(
        body,
        out_shape=[jax.ShapeDtypeStruct(s, d) for s, d in outs],
        in_specs=specs,
        out_specs=[pl.BlockSpec(memory_space=pltpu.VMEM)] * len(outs),
        scratch_shapes=[pltpu.VMEM(s, d) for s, d in scratch],
        compiler_params=pltpu.CompilerParams(vmem_limit_bytes=40 * 1024 * 1024),
        cost_estimate=pl.CostEstimate(flops=flops, bytes_accessed=1 << 20, transcendentals=0),
    )


def dot(a, b):
    return jnp.dot(a, b, preferred_element_type=F32)


def dot_t(a, b):
    return lax.dot_general(a, b, (((1,), (1,)), ((), ())), preferred_element_type=F32)


def t_dot(a, b):
    return lax.dot_general(a, b, (((0,), (0,)), ((), ())), preferred_element_type=F32)


def exact(a, b):
    a8 = jnp.broadcast_to(a, (8, a.shape[1]))
    return jnp.dot(a8, b, preferred_element_type=F32, precision=lax.Precision.HIGHEST)[0:1]


def to_lanes(chans, shift):
    c = lax.broadcasted_iota(jnp.int32, (chans, 128), 0) // WIDTH
    l = lax.broadcasted_iota(jnp.int32, (chans, 128), 1)
    return (c + shift == l).astype(F32)


def from_lanes(chans, shift):
    c = lax.broadcasted_iota(jnp.int32, (128, chans), 1) // WIDTH
    l = lax.broadcasted_iota(jnp.int32, (128, chans), 0)
    return (c + shift == l).astype(F32)


def masks():
    j = lax.broadcasted_iota(jnp.int32, (J, 1), 0)
    odd = jnp.where((j >= 1) & (j <= 64), 1.0, 0.0)
    even = jnp.where(j <= 63, 1.0, 0.0)
    return odd, even


def pack_lon(feat, cot, east, west):
    rows, cols, _ = feat.shape
    half = cot.shape[0]
    east[0:rows] = feat[:, cols - 16 : cols]
    east[rows : rows + half] = cot[:, cot.shape[1] - 16 :]
    west[0:rows] = feat[:, 0:16]
    west[rows : rows + half] = cot[:, 0:16]


def pack_lat(feat, cot, west, east, south, north):
    rows, cols, _ = feat.shape
    half, pairs, _ = cot.shape
    for dest, top, mid in ((south, rows - 2, half - 1), (north, 0, 0)):
        for k in range(2):
            o = k * (cols + 32)
            dest[o : o + 16] = west[top + k]
            dest[o + 16 : o + 16 + cols] = feat[top + k]
            dest[o + 16 + cols : o + 32 + cols] = east[top + k]
        o = 2 * (cols + 32)
        dest[o : o + 16] = west[rows + mid]
        dest[o + 16 : o + 16 + pairs] = cot[mid]
        dest[o + 16 + pairs : o + 32 + pairs] = east[rows + mid]


def conv_kernel(devices, feat, west, east, north, south, w, x_out, hq_out, he_out, stat_out, f32s):
    rows, cols, chans = feat.shape
    wide = cols + 32
    f32s[:, :, wide : wide + 16] = jnp.zeros((rows + 4, 2, 16, 128), F32)
    for v in range(2):
        part = slice(v * 128, v * 128 + 128)
        for k in range(2):
            f32s[k, v, 0:wide] = north[k * wide : (k + 1) * wide, part].astype(F32)
            f32s[rows + 2 + k, v, 0:wide] = south[k * wide : (k + 1) * wide, part].astype(F32)
        f32s[2 : rows + 2, v, 0:16] = west[0:rows, :, part].astype(F32)
        f32s[2 : rows + 2, v, 16 : 16 + cols] = feat[:, :, part].astype(F32)
        f32s[2 : rows + 2, v, 16 + cols : wide] = east[0:rows, :, part].astype(F32)
        for r in range(rows + 4):
            for k in range(4):
                lane = k * chans + v * 128
                x_out[r, :, lane : lane + 128] = f32s[r, v, pl.ds(14 + k, J, stride=2), :].astype(BF)
    odd, even = masks()
    sums = jnp.zeros((1, chans), F32)
    for out, lo in ((hq_out, 0), (he_out, chans)):
        acc = None
        for a in range(3):
            lhs = x_out[a : a + rows + 2, :, lo : lo + 3 * chans].reshape((rows + 2) * J, 3 * chans)
            term = dot(lhs, w[a])
            acc = term if acc is None else acc + term
        out[...] = acc.astype(BF).reshape(rows + 2, J, chans)
    for out, mask in ((hq_out, odd), (he_out, even)):
        part = jnp.zeros((J, chans), F32)
        for r in range(1, rows + 1):
            part = part + out[r].astype(F32)
        sums = sums + jnp.sum(part * mask, axis=0, keepdims=True)
    lanes = to_lanes(chans, 0)
    means = exact(sums, lanes) / (rows * cols * WIDTH)
    mean = exact(means, from_lanes(chans, 0))
    squares = jnp.zeros((1, chans), F32)
    for out, mask in ((hq_out, odd), (he_out, even)):
        part = jnp.zeros((J, chans), F32)
        for r in range(1, rows + 1):
            d = out[r].astype(F32) - mean
            part = part + d * d
        squares = squares + jnp.sum(part * mask, axis=0, keepdims=True)
    stat = means + exact(squares, to_lanes(chans, 32))
    stat_out[...] = jnp.broadcast_to(stat[None], stat_out.shape)


def back_kernel(cot, west, east, north, south, dw, c_out, aq_out, ae_out, f32s):
    half, pairs, chans = cot.shape
    rows = west.shape[0] - half
    wide = pairs + 32
    base = north.shape[0] - wide
    f32s[0, 0:wide] = north[base : base + wide].astype(F32)
    f32s[half + 1, 0:wide] = south[base : base + wide].astype(F32)
    f32s[1 : half + 1, 0:16] = west[rows:].astype(F32)
    f32s[1 : half + 1, 16 : 16 + pairs] = cot[...].astype(F32)
    f32s[1 : half + 1, 16 + pairs : wide] = east[rows:].astype(F32)
    for s in range(half + 2):
        c_out[s, :, 0:chans] = f32s[s, 15 : 15 + J].astype(BF)
        c_out[s, :, chans : 2 * chans] = f32s[s, 16 : 16 + J].astype(BF)
    n = half + 1
    lo_l = c_out[0:n, :, 0:chans].reshape(n * J, chans)
    lo_r = c_out[0:n, :, chans:].reshape(n * J, chans)
    hi_l = c_out[1 : n + 1, :, 0:chans].reshape(n * J, chans)
    hi_r = c_out[1 : n + 1, :, chans:].reshape(n * J, chans)

    def put(out, k, value):
        value = value.astype(BF).reshape(n, J, chans)
        for i in range(n):
            out[2 * i + k] = value[i]

    put(ae_out, 1, dot_t(hi_r, dw[1, 1]))
    put(aq_out, 1, dot_t(hi_r, dw[1, 0]) + dot_t(hi_l, dw[1, 2]))
    put(ae_out, 0, dot_t(hi_r, dw[0, 1]) + dot_t(lo_r, dw[2, 1]))
    put(
        aq_out,
        0,
        dot_t(hi_r, dw[0, 0]) + dot_t(hi_l, dw[0, 2]) + dot_t(lo_r, dw[2, 0]) + dot_t(lo_l, dw[2, 2]),
    )


def act_kernel(cells, flags, stats, hq, he, aq, ae, gain, bias, t_out, pq_out, pe_out, coef_out, sum_out, f32s):
    devices = stats.shape[0]
    rows = hq.shape[0] - 2
    chans = hq.shape[2]
    local_n = float(cells // devices * WIDTH)
    count = float(cells * WIDTH)
    rec = stats[...]
    total = jnp.sum(rec, axis=0)
    centre = total / devices
    dev = rec - centre[None]
    spread = jnp.sum(dev * dev, axis=0)
    mean = exact(centre, from_lanes(chans, 0))
    var = (exact(total, from_lanes(chans, 32)) + local_n * exact(spread, from_lanes(chans, 0))) / count
    inverse = lax.rsqrt(var + EPS)
    coef_out[0:1] = mean
    coef_out[1:2] = inverse
    g = gain[...]
    b = bias[...]
    odd, even = masks()
    top = jnp.where(flags[0] == 1, 0.0, 1.0)
    bias_sum = jnp.zeros((1, chans), F32)
    gain_sum = jnp.zeros((1, chans), F32)
    for h, a, p_out, mask, is_q in ((hq, aq, pq_out, odd, True), (he, ae, pe_out, even, False)):
        acc_b = jnp.zeros((J, chans), F32)
        acc_g = jnp.zeros((J, chans), F32)
        for r in range(rows + 2):
            normed = (h[r].astype(F32) - mean) * inverse
            shifted = g * normed + b
            sigma = jax.nn.sigmoid(shifted)
            pre = a[r].astype(F32) * sigma * (1.0 + shifted * (1.0 - sigma))
            p_out[r] = pre
            if 1 <= r <= rows:
                acc_b = acc_b + pre
                acc_g = acc_g + pre * normed
            if r <= rows:
                active = shifted * sigma
                if r == 0:
                    active = active * top
                if is_q:
                    f32s[...] = active.astype(BF).astype(F32)
                    t_out[r, :, 0:chans] = active[0:64].astype(BF)
                    t_out[r, :, 2 * chans :] = f32s[1:65].astype(BF)
                else:
                    t_out[r, :, chans : 2 * chans] = active[0:64].astype(BF)
        bias_sum = bias_sum + jnp.sum(acc_b * mask, axis=0, keepdims=True)
        gain_sum = gain_sum + jnp.sum(acc_g * mask, axis=0, keepdims=True)
    payload = jnp.concatenate(
        [bias_sum[:, 0:128], bias_sum[:, 128:256], gain_sum[:, 0:128], gain_sum[:, 128:256]], axis=0
    )
    sum_out[...] = jnp.broadcast_to(payload[None], sum_out.shape)


def down_kernel(t, c, dw, out, grad):
    half = out.shape[0]
    pairs, chans = out.shape[1:]
    cot = c[1 : half + 1, 0:pairs, chans:].reshape(half * pairs, chans)
    acc = None
    for a in range(3):
        lhs = jnp.concatenate([t[2 * i + a] for i in range(half)], axis=0)
        term = dot(lhs, dw[a])
        acc = term if acc is None else acc + term
        grad[a] = t_dot(lhs, cot)
    out[...] = acc.astype(BF).reshape(out.shape)


def grad_kernel(cells, flags, sums, coef, hq, he, pq, pe, gain, x, h4_out, conv_out, vec_out, f32s, rq, re):
    rows = hq.shape[0] - 2
    chans = hq.shape[2]
    count = float(cells * WIDTH)
    total = jnp.sum(sums[...], axis=0)
    bias_sum = jnp.concatenate([total[0:1], total[1:2]], axis=1)
    gain_sum = jnp.concatenate([total[2:3], total[3:4]], axis=1)
    factor = 1.0 / math.sqrt(cells)
    vec_out[0:1] = gain_sum * factor
    vec_out[1:2] = bias_sum * factor
    g = gain[...]
    lanes, back = to_lanes(chans, 0), from_lanes(chans, 0)
    first = exact(exact(g * bias_sum, lanes), back) / count
    second = exact(exact(g * gain_sum, lanes), back) / count
    mean = coef[0:1]
    inverse = coef[1:2]
    top = jnp.where(flags[0] == 1, 0.0, 1.0)
    bottom = jnp.where(flags[1] == 1, 0.0, 1.0)
    odd, even = masks()
    zero = jnp.zeros((J, chans), BF)
    for h, p, r_out, mask, is_q in ((hq, pq, rq, odd, True), (he, pe, re, even, False)):
        for f in (0, 1):
            for a in (1, 2):
                if f - a + 1 <= 0:
                    r_out[f, :, a * chans : (a + 1) * chans] = zero
                    r_out[rows + 1 - f, :, (2 - a) * chans : (3 - a) * chans] = zero
        for r in range(rows + 2):
            normed = (h[r].astype(F32) - mean) * inverse
            value = inverse * (g * p[r] - first - normed * second)
            if r == 0:
                value = value * top
            if r == rows + 1:
                value = value * bottom
            rounded = value.astype(BF)
            if 1 <= r <= rows:
                inner = (value * mask).astype(BF)
                for a in range(3):
                    r_out[r + a - 1, :, a * chans : (a + 1) * chans] = inner
            f32s[...] = rounded.astype(F32)
            moved = f32s[1:65].astype(BF)
            lo = 3 if is_q else 2
            h4_out[r, :, lo * chans : (lo + 1) * chans] = rounded[0:64]
            lo = 1 if is_q else 0
            h4_out[r, :, lo * chans : (lo + 1) * chans] = moved
    m = (rows + 2) * J
    lhs = x[1 : rows + 3].reshape(m, 4 * chans)
    part = t_dot(lhs[:, 0 : 3 * chans], rq[...].reshape(m, 3 * chans))
    part = part + t_dot(lhs[:, chans : 4 * chans], re[...].reshape(m, 3 * chans))
    for a in range(3):
        conv_out[a] = part[:, a * chans : (a + 1) * chans]


def input_kernel(h4, w, out, f32s):
    rows, cols, chans = out.shape
    for k, lo in ((0, 1), (1, 0)):
        acc = None
        for a in range(3):
            for b in range(3):
                lane = (lo + b) * chans
                lhs = h4[2 - a : 2 - a + rows, :, lane : lane + chans].reshape(rows * (cols // 2), chans)
                term = dot_t(lhs, w[a, b])
                acc = term if acc is None else acc + term
        acc = acc.reshape(rows, cols // 2, chans)
        for r in range(rows):
            for v in range(2):
                f32s[r, v, pl.ds(k, cols // 2, stride=2), :] = acc[r, :, v * 128 : v * 128 + 128]
    for v in range(2):
        out[:, :, v * 128 : v * 128 + 128] = f32s[:, v].astype(BF)


def passed(value, axes, step, wrap):
    n = lax.axis_size(axes)
    pairs = [(i, (i + step) % n) for i in range(n) if wrap or 0 <= i + step < n]
    return lax.ppermute(value, axes, pairs)


def local(features, conv_weight, down_weight, norm_gain, norm_bias, cotangent):
    rows, cols, chans = features.shape
    half, pairs, _ = cotangent.shape
    devices = lax.axis_size(ALL)
    lats = lax.axis_size(LAT)
    cells = rows * cols * devices
    lat = lax.axis_index(LAT)
    flags = jnp.stack([lat == 0, lat == lats - 1]).astype(jnp.int32)
    gain = norm_gain.reshape(1, chans)
    bias = norm_bias.reshape(1, chans)
    w3 = conv_weight.reshape(3, 3 * chans, chans)
    dw3 = down_weight.reshape(3, 3 * chans, chans)

    with jax.named_scope("halo"):
        slab = (rows + half, 16, chans)
        to_east, to_west = call(pack_lon, [(slab, BF)] * 2, n_in=2)(features, cotangent)
        west = passed(to_east, LON, 1, True)
        east = passed(to_west, LON, -1, True)
        strip = (2 * (cols + 32) + pairs + 32, chans)
        to_south, to_north = call(pack_lat, [(strip, BF)] * 2, n_in=4)(features, cotangent, west, east)
        north = passed(to_south, LAT, 1, False)
        south = passed(to_north, LAT, -1, False)

    plane = (rows + 2, J, chans)
    with jax.named_scope("conv"):
        x, hq, he, stat = call(
            functools.partial(conv_kernel, devices),
            [((rows + 4, J, 4 * chans), BF), (plane, BF), (plane, BF), ((devices, 1, 128), F32)],
            [((rows + 4, 2, cols + 48, 128), F32)],
            flops=2 * 1600 * 2304 * 256,
            n_in=6,
        )(features, west, east, north, south, w3)
        stats = lax.all_to_all(stat, ALL, 0, 0, tiled=True)
    with jax.named_scope("back"):
        c2, aq, ae = call(
            back_kernel,
            [((half + 2, J, 2 * chans), BF), (plane, BF), (plane, BF)],
            [((half + 2, pairs + 32, chans), F32)],
            flops=2 * 400 * 2304 * 256,
            n_in=6,
        )(cotangent, west, east, north, south, down_weight)
    with jax.named_scope("act"):
        t, pq, pe, coef, sums = call(
            functools.partial(act_kernel, cells),
            [
                ((rows + 1, pairs, 3 * chans), BF),
                (plane, F32),
                (plane, F32),
                ((2, chans), F32),
                ((devices, 4, 128), F32),
            ],
            [((J, chans), F32)],
            flops=1600 * 256 * 20,
            smem=(0,),
            n_in=8,
        )(flags, stats, hq, he, aq, ae, gain, bias)
        sums = lax.all_to_all(sums, ALL, 0, 0, tiled=True)
    with jax.named_scope("down"):
        output, down_part = call(
            down_kernel,
            [((half, pairs, chans), BF), ((3, 3 * chans, chans), F32)],
            flops=4 * 256 * 2304 * 256,
            n_in=3,
        )(t, c2, dw3)
    with jax.named_scope("grad"):
        h4, conv_part, vec = call(
            functools.partial(grad_kernel, cells),
            [((rows + 2, pairs, 4 * chans), BF), ((3, 3 * chans, chans), F32), ((2, chans), F32)],
            [((J, chans), F32), ((rows + 2, J, 3 * chans), BF), ((rows + 2, J, 3 * chans), BF)],
            flops=2 * 1600 * 2304 * 256,
            smem=(0,),
            n_in=9,
        )(flags, sums, coef, hq, he, pq, pe, gain, x)
    with jax.named_scope("total"):
        total_rows = 9 * chans
        core = lax.axis_index("core")
        conv_flat = conv_part.reshape(total_rows, chans)
        down_flat = down_part.reshape(total_rows, chans)
        mine = jnp.where(core == 0, conv_flat, down_flat)
        theirs = jnp.where(core == 0, down_flat, conv_flat)
        pair = [(0, 1), (1, 0)]
        other = lax.ppermute(theirs.astype(BF), "core", pair)
        mine = (mine + other.astype(F32)).astype(BF)
        chips = lax.axis_size(PLANE)
        depth = lax.axis_size("z")
        share = total_rows // chips
        got = lax.all_to_all(mine.reshape(chips, share, chans), PLANE, 0, 0, tiled=True)
        piece = jnp.sum(got.astype(F32), axis=0).astype(BF)
        got = lax.all_to_all(jnp.broadcast_to(piece[None], (depth, share, chans)), "z", 0, 0, tiled=True)
        piece = (jnp.sum(got.astype(F32), axis=0) * (1.0 / math.sqrt(cells))).astype(BF)
        whole = lax.all_to_all(jnp.broadcast_to(piece[None], (chips, share, chans)), PLANE, 0, 0, tiled=True)
        other = lax.ppermute(whole, "core", pair)
        whole = whole.reshape(3, 3, chans, chans)
        other = other.reshape(3, 3, chans, chans)
        conv_grad = jnp.where(core == 0, whole, other).astype(F32)
        down_grad = jnp.where(core == 0, other, whole).astype(F32)
    with jax.named_scope("input"):
        (input_grad,) = call(
            input_kernel,
            [((rows, cols, chans), BF)],
            [((rows, 2, cols, 128), F32)],
            flops=2 * 1024 * 2304 * 256,
            n_in=2,
        )(h4, conv_weight)
    return output, input_grad, conv_grad, down_grad, vec[0], vec[1]


SIZES = {64: (4, 8, 2), 2: (1, 2, 1), 4: (2, 2, 1)}


def solution(mesh):
    lon, lat = mesh.devices.shape
    fine = Mesh(mesh.devices.reshape(SIZES[lon] + (lat // 2, 2)), ALL)
    band = P(LAT, LON, None)
    return jax.shard_map(
        local,
        mesh=fine,
        in_specs=(band, P(), P(), P(), P(), band),
        out_specs=(band, band, P(), P(), P(), P()),
        check_vma=False,
    )
```

time: 685 us -> 175 us (0.26)
  waiting for transfers between devices: 258 us -> 36.6 us
  blocking collectives: 226 us -> 59.5 us
  local copies, waits for them, and re-layouts: 73.8 us -> 17 us
  matrix products: 35.9 us -> 0 us
  other arithmetic: 30.5 us -> 4.76 us
  Pallas kernels: 0 us -> 16.2 us
  between operations: 14.7 us -> 0.83 us
    psum x1 -> x0, waiting for transfers between devices: 258 us -> none  [local(): conv_total, down_total = lax.psum((conv_part, down_part), ('lon', 'lat'))]
    psum x3 -> x0, blocking collectives: 226 us -> none  [the longest x1 76.7 us: local(): lax.psum((jnp.sum(pre, axis=(0, 1)), jnp.sum(pre * normed, axis=(0, 1))),...]
    all_to_all x0 -> x3, blocking collectives: none -> 59.5 us  [the longest x1 21.5 us: local(): lax.all_to_all(mine.reshape(chips, share, chans), PLANE, 0, 0, tiled=True)]
    slice x28 -> x1, local copies, waits for them, and re-layouts: 40.1 us -> 0.57 us  [local(): return (output, input_grad, conv_grad, down_grad, vec[0], vec[1])]
    dot_general x54 -> x0, matrix products: 35.9 us -> none  [the longest x18 17.7 us: tap_grads(): lax.dot_general(piece, flat_grad, (((0,), (0,)), ((), ())), preferred_ele...]
    all_to_all x0 -> x2, waiting for transfers between devices: none -> 26.4 us  [the longest x1 16.1 us: local(): sums = lax.all_to_all(sums, ALL, 0, 0, tiled=True)]
    pad x9 -> x0, local copies, waits for them, and re-layouts: 25.8 us -> none  [down_back(): lax.pad(term, jnp.zeros((), term.dtype), ((tap_a, 2 - tap_a, 1), (tap_b,...]
    ppermute x12 -> x6, starting transfers between devices: 41.8 us -> 20.9 us  [the longest x4 16.7 us: passed(): return lax.ppermute(value, axes, pairs)]
  transfers between devices with their start and end apart: 13 -> 8, of which waited for: 1 -> 6; matrix products, arithmetic and copies ran while one was open for 16% -> 1% of each run, Pallas kernels for 0% -> 3%
where the time goes in v1:
time: 175 us; the launch traced here: 174 us
  blocking collectives  59.5 us (34%)
  starting transfers between devices  38.9 us (22%)
  waiting for transfers between devices  36.6 us (21%)
  local copies, waits for them, and re-layouts  17 us (10%)
  Pallas kernels  16.2 us (9%)
  other arithmetic  4.76 us (3%)
    all_to_all x1, blocking collectives, local(): lax.all_to_all(mine.reshape(chips, share, chans), PLANE, 0, 0, tiled=True)  21.5 us
    all_to_all x1, blocking collectives, local(): lax.all_to_all(jnp.broadcast_to(piece[None], (depth, share, chans)), 'z',...  19.3 us
    all_to_all x1, blocking collectives, local(): lax.all_to_all(jnp.broadcast_to(piece[None], (chips, share, chans)), PLAN...  18.7 us
    ppermute x4, starting transfers between devices, passed(): return lax.ppermute(value, axes, pairs)  16.7 us
    unnamed x52, local copies, waits for them, and re-layouts  16.3 us
    all_to_all x1, waiting for transfers between devices, local(): sums = lax.all_to_all(sums, ALL, 0, 0, tiled=True)  16.1 us
    all_to_all x1, starting transfers between devices, local(): stats = lax.all_to_all(stat, ALL, 0, 0, tiled=True)  10.9 us
    all_to_all x1, waiting for transfers between devices, local(): stats = lax.all_to_all(stat, ALL, 0, 0, tiled=True)  10.3 us
  transfers between devices with their start and end apart: 8, of which 6 were waited for; matrix products, arithmetic and copies ran while one was open for 1% of the time, Pallas kernels for 3%

profile of v1, /device:TPU:1, one launch (start us, length us, event | category | flops | bytes accessed | tf_op | source)
XLA Modules:
  0.0 173.9 jit_solution(15492989137153745162)
XLA Ops:
  0.6 1.0 copy-done.1
  1.7 0.9 copy-done.2
  2.6 3.8 %collective-permute-start = (bf16[12,16,256]{2,1,0:T(8,128)(2,1)S(1)}, bf16[12,16,256]{2,1,0:T(8,128)(2,1)S(1)}, u32[]{:S(2)}, u32[]{:S(2)}) collective-permute-start(bf16[12,16,256]{2,1,0:T(8,128)(2,1)S(1)} %get-tuple-element.27), channel_id=1, source_target_pairs={{0,4},{4,8},{8,12},{12,16},{16,20},{20,24},{24,28},{28,32},{32,36}... | collective-permute-start | bytes 294920 | tf_op jit(solution)/shard_map/halo/ppermute | solution.py:315
  6.4 7.6 %collective-permute-start.1 = (bf16[12,16,256]{2,1,0:T(8,128)(2,1)S(1)}, bf16[12,16,256]{2,1,0:T(8,128)(2,1)S(1)}, u32[]{:S(2)}, u32[]{:S(2)}) collective-permute-start(bf16[12,16,256]{2,1,0:T(8,128)(2,1)S(1)} %get-tuple-element.28), channel_id=1, source_target_pairs={{0,252},{4,0},{8,4},{12,8},{16,12},{20,16},{24,20},{28,24},{32,28}... | collective-permute-start | bytes 294920 | tf_op jit(solution)/shard_map/halo/ppermute | solution.py:315
  14.0 2.4 %collective-permute-done.west = bf16[12,16,256]{2,1,0:T(8,128)(2,1)S(1)} collective-permute-done((bf16[12,16,256]{2,1,0:T(8,128)(2,1)S(1)}, bf16[12,16,256]{2,1,0:T(8,128)(2,1)S(1)}, u32[]{:S(2)}, u32[]{:S(2)}) %collective-permute-start) | collective-permute-done | bytes 98336 | tf_op jit(solution)/shard_map/halo/ppermute | solution.py:315
  16.5 3.4 %collective-permute-start.2 = (bf16[416,256]{1,0:T(8,128)(2,1)S(1)}, bf16[416,256]{1,0:T(8,128)(2,1)S(1)}, u32[]{:S(2)}, u32[]{:S(2)}) collective-permute-start(bf16[416,256]{1,0:T(8,128)(2,1)S(1)} %get-tuple-element.29), channel_id=1, source_target_pairs={{0,1},{1,2},{2,3},{4,5},{5,6},{6,7},{8,9},{9,10},{10,11},{12,13},{... | collective-permute-start | bytes 638984 | tf_op jit(solution)/shard_map/halo/ppermute | solution.py:315
  19.9 1.9 %collective-permute-start.3 = (bf16[416,256]{1,0:T(8,128)(2,1)S(1)}, bf16[416,256]{1,0:T(8,128)(2,1)S(1)}, u32[]{:S(2)}, u32[]{:S(2)}) collective-permute-start(bf16[416,256]{1,0:T(8,128)(2,1)S(1)} %get-tuple-element.30), channel_id=1, source_target_pairs={{1,0},{2,1},{3,2},{5,4},{6,5},{7,6},{9,8},{10,9},{11,10},{13,12},{... | collective-permute-start | bytes 638984 | tf_op jit(solution)/shard_map/halo/ppermute | solution.py:315
  21.8 0.8 collective-permute-done.2.north
  22.7 4.4 %collective-permute-done.3.south = bf16[416,256]{1,0:T(8,128)(2,1)S(1)} collective-permute-done((bf16[416,256]{1,0:T(8,128)(2,1)S(1)}, bf16[416,256]{1,0:T(8,128)(2,1)S(1)}, u32[]{:S(2)}, u32[]{:S(2)}) %collective-permute-start.3) | collective-permute-done | bytes 213024 | tf_op jit(solution)/shard_map/halo/ppermute | solution.py:315
  27.1 3.8 %conv.1 = (bf16[12,80,1024]{2,1,0:T(8,128)(2,1)S(1)}, bf16[10,80,256]{2,1,0:T(8,128)(2,1)S(1)}, bf16[10,80,256]{2,1,0:T(8,128)(2,1)S(1)}, f32[256,1,128]{2,1,0:T(1,128)}) custom-call(bf16[8,128,256]{2,1,0:T(8,128)(2,1)S(1)} %copy-done.1, bf16[12,16,256]{2,1,0:T(8,128)(2,1)S(1)} %collective-permute-done.west, ...), custom_call_target="tpu_custom_call" | custom-call | flops 1887436800 | bytes 1048576 | tf_op jit(solution)/shard_map/conv/pallas_call | solution.py:343
  30.8 1.3 copy-done.24
  32.1 10.9 %all-to-all-start = ((f32[256,1,128]{2,1,0:T(1,128)}), f32[256,1,128]{2,1,0:T(1,128)S(1)}, u32[]{:S(2)}, u32[]{:S(2)}) async-start(f32[256,1,128]{2,1,0:T(1,128)} %get-tuple-element.31), calls=%async_computation | async-start | bytes 262144 | tf_op jit(solution)/shard_map/conv/all_to_all | solution.py:350
  43.1 0.9 copy-done.13
  44.0 0.7 back.1
  44.7 0.8 copy-done.6
  45.5 10.3 %all-to-all-done.stats = f32[256,1,128]{2,1,0:T(1,128)S(1)} async-done(((f32[256,1,128]{2,1,0:T(1,128)}), f32[256,1,128]{2,1,0:T(1,128)S(1)}, u32[]{:S(2)}, u32[]{:S(2)}) %all-to-all-start) | async-done | bytes 131104 | tf_op jit(solution)/shard_map/conv/all_to_all | solution.py:350
  55.8 3.5 %act.1 = (bf16[9,64,768]{2,1,0:T(8,128)(2,1)S(1)}, f32[10,80,256]{2,1,0:T(8,128)S(1)}, f32[10,80,256]{2,1,0:T(8,128)S(1)}, f32[2,256]{1,0:T(2,128)S(1)}, f32[256,4,128]{2,1,0:T(4,128)}) custom-call(s32[2]{0:T(128)S(1)} %add_convert_fusion.flags, f32[256,1,128]{2,1,0:T(1,128)S(1)} %all-to-all-done.stats, bf16[10,80,256]{2,1,0:T(8,128)(2,1)S(1)} %get-tuple-element.32.hq, ...), custom_call_target="tpu_custom_call" | custom-call | flops 8192000 | bytes 1048576 | tf_op jit(solution)/shard_map/act/pallas_call | solution.py:360
  59.3 0.9 copy-done.4
  60.2 0.9 copy-done.18
  61.1 0.9 copy-done.20
  62.0 7.1 %all-to-all-start.1 = ((f32[256,4,128]{2,1,0:T(4,128)}), f32[256,4,128]{2,1,0:T(4,128)}, u32[]{:S(2)}, u32[]{:S(2)}) async-start(f32[256,4,128]{2,1,0:T(4,128)} %get-tuple-element.39), calls=%async_computation.1 | async-start | bytes 1048576 | tf_op jit(solution)/shard_map/act/all_to_all | solution.py:374
  69.1 1.2 copy-done.5
  70.2 1.0 copy-done.7
  71.3 1.4 down.1
  72.7 16.1 %all-to-all-done.1.sums = f32[256,4,128]{2,1,0:T(4,128)} async-done(((f32[256,4,128]{2,1,0:T(4,128)}), f32[256,4,128]{2,1,0:T(4,128)}, u32[]{:S(2)}, u32[]{:S(2)}) %all-to-all-start.1) | async-done | bytes 524320 | tf_op jit(solution)/shard_map/act/all_to_all | solution.py:374
  88.8 1.0 copy-done.9
  89.8 1.0 copy-done.11
  90.8 1.1 copy-done.19
  92.0 1.1 copy-done.21
  93.1 1.5 copy-done.25
  94.7 4.6 %grad.1 = (bf16[10,64,1024]{2,1,0:T(8,128)(2,1)S(1)}, f32[3,768,256]{2,1,0:T(8,128)S(1)}, f32[2,256]{1,0:T(2,128)S(1)}) custom-call(s32[2]{0:T(128)S(1)} %add_convert_fusion.flags, f32[256,4,128]{2,1,0:T(4,128)} %all-to-all-done.1.sums, f32[2,256]{1,0:T(2,128)S(1)} %get-tuple-element.40.coef, bf16[10,80,256]{2,1,0:T(8,128)(2,1)S(1)} %copy-done.9, ...), custom_call_target="tpu_custom_call" | custom-call | flops 1887436800 | bytes 1048576 | tf_op jit(solution)/shard_map/grad/pallas_call | solution.py:383
  99.2 0.4 select_convert_fusion
  99.7 0.6 copy-done.22
  100.3 0.3 broadcast_select_fusion
  100.6 2.5 %collective-permute-done.4 = bf16[2304,256]{1,0:T(8,128)(2,1)S(1)} collective-permute-done((bf16[2304,256]{1,0:T(8,128)(2,1)S(1)}, bf16[2304,256]{1,0:T(8,128)(2,1)S(1)}, u32[]{:S(2)}, u32[]{:S(2)}) %collective-permute-start.4) | collective-permute-done | bytes 1179680 | tf_op jit(solution)/shard_map/total/ppermute | solution.py:399
  103.1 0.3 fusion
  103.5 21.5 %all_to_all.25 = bf16[16,144,256]{2,1,0:T(8,128)(2,1)S(1)} all-to-all(bf16[16,144,256]{2,1,0:T(8,128)(2,1)S(1)} %bitcast.25), channel_id=1, replica_groups=mesh['x'=4,'z'=8,'y_hi'=2,'y_lo'=2,'core'=2] {'x','y_hi','y_lo'}, dimensions={0} | all-to-all | bytes 2359296 | tf_op jit(solution)/shard_map/total/all_to_all | solution.py:404
  125.0 0.2 reduce_sum.21
  125.2 19.3 %all_to_all.26 = bf16[8,144,256]{2,1,0:T(8,128)(2,1)S(1)} all-to-all(bf16[8,144,256]{2,1,0:T(8,128)(2,1)S(1)} %broadcast_in_dim.4), channel_id=1, replica_groups=mesh['x'=4,'z'=8,'y_hi'=2,'y_lo'=2,'core'=2] {'z'}, dimensions={0} | all-to-all | bytes 1179648 | tf_op jit(solution)/shard_map/total/all_to_all | solution.py:406
  144.5 0.1 convert_reduce_fusion
  144.6 0.1 broadcast_in_dim.5
  144.7 18.7 %all_to_all.27 = bf16[16,144,256]{2,1,0:T(8,128)(2,1)S(1)} all-to-all(bf16[16,144,256]{2,1,0:T(8,128)(2,1)S(1)} %broadcast_in_dim.5), channel_id=1, replica_groups=mesh['x'=4,'z'=8,'y_hi'=2,'y_lo'=2,'core'=2] {'x','y_hi','y_lo'}, dimensions={0} | all-to-all | bytes 2359296 | tf_op jit(solution)/shard_map/total/all_to_all | solution.py:408
  163.4 4.2 %collective-permute-start.5 = (bf16[16,144,256]{2,1,0:T(8,128)(2,1)S(1)}, bf16[16,144,256]{2,1,0:T(8,128)(2,1)S(1)}, u32[]{:S(2)}, u32[]{:S(2)}) collective-permute-start(bf16[16,144,256]{2,1,0:T(8,128)(2,1)S(1)} %all_to_all.27), channel_id=1, source_target_pairs={{0,1},{1,0},{2,3},{3,2},{4,5},{5,4},{6,7},{7,6},{8,9},{9,8},{10,11... | collective-permute-start | bytes 3538952 | tf_op jit(solution)/shard_map/total/ppermute | solution.py:409
  167.6 2.3 %input.1 = bf16[8,128,256]{2,1,0:T(8,128)(2,1)} custom-call(bf16[10,64,1024]{2,1,0:T(8,128)(2,1)S(1)} %copy-done.23, bf16[3,3,256,256]{3,2,1,0:T(8,128)(2,1)S(1)} %copy-done.17), custom_call_target="tpu_custom_call" | custom-call | flops 1207959552 | bytes 1048576 | tf_op jit(solution)/shard_map/input/pallas_call | solution.py:415
  169.9 0.6 fusion.1
  170.5 0.2 broadcast_select_fusion.1
  170.6 1.6 convert.3
  172.3 1.6 convert.4
  (44 shorter events, 0.3 us)
Async XLA Ops:
  0.6 1.0 copy-start.1
  1.7 0.9 copy-start.2
  2.6 24.5 %copy-start.16 = (bf16[3,3,256,256]{3,2,1,0:T(8,128)(2,1)S(1)}, bf16[3,3,256,256]{3,2,1,0:T(8,128)(2,1)}, u32[]{:S(2)}) copy-start(bf16[3,3,256,256]{3,2,1,0:T(8,128)(2,1)} %w.1) | copy-start | bytes 3538948
  2.6 13.8 %collective-permute-start = (bf16[12,16,256]{2,1,0:T(8,128)(2,1)S(1)}, bf16[12,16,256]{2,1,0:T(8,128)(2,1)S(1)}, u32[]{:S(2)}, u32[]{:S(2)}) collective-permute-start(bf16[12,16,256]{2,1,0:T(8,128)(2,1)S(1)} %get-tuple-element.27), channel_id=1, source_target_pairs={{0,4},{4,8},{8,12},{12,16},{16,20},{20,24},{24,28},{28,32},{32,36}... | collective-permute-start | bytes 294920 | tf_op jit(solution)/shard_map/halo/ppermute | solution.py:315
  6.4 10.0 %collective-permute-start.1 = (bf16[12,16,256]{2,1,0:T(8,128)(2,1)S(1)}, bf16[12,16,256]{2,1,0:T(8,128)(2,1)S(1)}, u32[]{:S(2)}, u32[]{:S(2)}) collective-permute-start(bf16[12,16,256]{2,1,0:T(8,128)(2,1)S(1)} %get-tuple-element.28), channel_id=1, source_target_pairs={{0,252},{4,0},{8,4},{12,8},{16,12},{20,16},{24,20},{28,24},{32,28}... | collective-permute-start | bytes 294920 | tf_op jit(solution)/shard_map/halo/ppermute | solution.py:315
  16.5 6.2 %collective-permute-start.2 = (bf16[416,256]{1,0:T(8,128)(2,1)S(1)}, bf16[416,256]{1,0:T(8,128)(2,1)S(1)}, u32[]{:S(2)}, u32[]{:S(2)}) collective-permute-start(bf16[416,256]{1,0:T(8,128)(2,1)S(1)} %get-tuple-element.29), channel_id=1, source_target_pairs={{0,1},{1,2},{2,3},{4,5},{5,6},{6,7},{8,9},{9,10},{10,11},{12,13},{... | collective-permute-start | bytes 638984 | tf_op jit(solution)/shard_map/halo/ppermute | solution.py:315
  19.9 7.2 %collective-permute-start.3 = (bf16[416,256]{1,0:T(8,128)(2,1)S(1)}, bf16[416,256]{1,0:T(8,128)(2,1)S(1)}, u32[]{:S(2)}, u32[]{:S(2)}) collective-permute-start(bf16[416,256]{1,0:T(8,128)(2,1)S(1)} %get-tuple-element.30), channel_id=1, source_target_pairs={{1,0},{2,1},{3,2},{5,4},{6,5},{7,6},{9,8},{10,9},{11,10},{13,12},{... | collective-permute-start | bytes 638984 | tf_op jit(solution)/shard_map/halo/ppermute | solution.py:315
  27.1 3.8 %copy-start.12 = (bf16[416,256]{1,0:T(8,128)(2,1)}, bf16[416,256]{1,0:T(8,128)(2,1)S(1)}, u32[]{:S(2)}) copy-start(bf16[416,256]{1,0:T(8,128)(2,1)S(1)} %collective-permute-done.3.south) | copy-start | bytes 638980
  27.1 16.0 %copy-start = (bf16[3,3,256,256]{3,2,1,0:T(8,128)(2,1)S(1)}, bf16[3,3,256,256]{3,2,1,0:T(8,128)(2,1)}, u32[]{:S(2)}) copy-start(bf16[3,3,256,256]{3,2,1,0:T(8,128)(2,1)} %dw.1) | copy-start | bytes 3538948
  27.1 16.0 %copy-start.3 = (bf16[4,64,256]{2,1,0:T(8,128)(2,1)S(1)}, bf16[4,64,256]{2,1,0:T(8,128)(2,1)}, u32[]{:S(2)}) copy-start(bf16[4,64,256]{2,1,0:T(8,128)(2,1)} %cot.5) | copy-start | bytes 393220
  30.8 1.3 copy-start.24
  32.1 27.1 %copy-start.8 = (bf16[10,80,256]{2,1,0:T(8,128)(2,1)}, bf16[10,80,256]{2,1,0:T(8,128)(2,1)S(1)}, u32[]{:S(2)}) copy-start(bf16[10,80,256]{2,1,0:T(8,128)(2,1)S(1)} %get-tuple-element.32.hq) | copy-start | bytes 1228804
  32.1 27.1 %copy-start.10 = (bf16[10,80,256]{2,1,0:T(8,128)(2,1)}, bf16[10,80,256]{2,1,0:T(8,128)(2,1)S(1)}, u32[]{:S(2)}) copy-start(bf16[10,80,256]{2,1,0:T(8,128)(2,1)S(1)} %get-tuple-element.33.he) | copy-start | bytes 1228804
  32.1 23.7 %copy-start.14 = (f32[256]{0:T(256)S(1)}, f32[256]{0:T(256)}, u32[]{:S(2)}) copy-start(f32[256]{0:T(256)} %param.10) | copy-start | bytes 3076
  32.1 23.7 %copy-start.15 = (f32[256]{0:T(256)S(1)}, f32[256]{0:T(256)}, u32[]{:S(2)}) copy-start(f32[256]{0:T(256)} %param.9) | copy-start | bytes 3076
  32.1 23.7 %all-to-all-start = ((f32[256,1,128]{2,1,0:T(1,128)}), f32[256,1,128]{2,1,0:T(1,128)S(1)}, u32[]{:S(2)}, u32[]{:S(2)}) async-start(f32[256,1,128]{2,1,0:T(1,128)} %get-tuple-element.31), calls=%async_computation | async-start | bytes 262144 | tf_op jit(solution)/shard_map/conv/all_to_all | solution.py:350
  43.1 0.9 copy-start.13
  44.7 0.8 copy-start.6
  59.3 0.9 copy-start.4
  60.2 0.9 copy-start.18
  61.1 0.9 copy-start.20
  62.0 26.9 %all-to-all-start.1 = ((f32[256,4,128]{2,1,0:T(4,128)}), f32[256,4,128]{2,1,0:T(4,128)}, u32[]{:S(2)}, u32[]{:S(2)}) async-start(f32[256,4,128]{2,1,0:T(4,128)} %get-tuple-element.39), calls=%async_computation.1 | async-start | bytes 1048576 | tf_op jit(solution)/shard_map/act/all_to_all | solution.py:374
  69.1 1.2 copy-start.5
  70.2 1.0 copy-start.7
  88.8 1.0 copy-start.9
  89.8 1.0 copy-start.11
  90.8 1.1 copy-start.19
  92.0 1.1 copy-start.21
  93.1 1.5 copy-start.25
  99.2 1.1 copy-start.22
  100.3 2.8 %collective-permute-start.4 = (bf16[2304,256]{1,0:T(8,128)(2,1)S(1)}, bf16[2304,256]{1,0:T(8,128)(2,1)S(1)}, u32[]{:S(2)}, u32[]{:S(2)}) collective-permute-start(bf16[2304,256]{1,0:T(8,128)(2,1)S(1)} %bitcast.26), channel_id=1, source_target_pairs={{0,1},{1,0},{2,3},{3,2},{4,5},{5,4},{6,7},{7,6},{8,9},{9,8},{10,11... | collective-permute-start | bytes 3538952 | tf_op jit(solution)/shard_map/total/ppermute | solution.py:399
  144.6 23.0 %copy-start.23 = (bf16[10,64,1024]{2,1,0:T(8,128)(2,1)S(1)}, bf16[10,64,1024]{2,1,0:T(8,128)(2,1)}, u32[]{:S(2)}) copy-start(bf16[10,64,1024]{2,1,0:T(8,128)(2,1)} %copy-done.22) | copy-start | bytes 3932164
  144.7 22.9 %copy-start.17 = (bf16[3,3,256,256]{3,2,1,0:T(8,128)(2,1)S(1)}, bf16[3,3,256,256]{3,2,1,0:T(8,128)(2,1)}, u32[]{:S(2)}) copy-start(bf16[3,3,256,256]{3,2,1,0:T(8,128)(2,1)} %w.1) | copy-start | bytes 3538948
  163.4 7.1 %collective-permute-start.5 = (bf16[16,144,256]{2,1,0:T(8,128)(2,1)S(1)}, bf16[16,144,256]{2,1,0:T(8,128)(2,1)S(1)}, u32[]{:S(2)}, u32[]{:S(2)}) collective-permute-start(bf16[16,144,256]{2,1,0:T(8,128)(2,1)S(1)} %all_to_all.27), channel_id=1, source_target_pairs={{0,1},{1,0},{2,3},{3,2},{4,5},{5,4},{6,7},{7,6},{8,9},{9,8},{10,11... | collective-permute-start | bytes 3538952 | tf_op jit(solution)/shard_map/total/ppermute | solution.py:409

commit v2 on v1

v2 whole, which is shorter than its diff:
```python
import functools
import math

import jax
import jax.numpy as jnp
from jax import lax
from jax.experimental import pallas as pl
from jax.experimental.pallas import tpu as pltpu
from jax.sharding import Mesh
from jax.sharding import PartitionSpec as P

EPS = 1e-05
WIDTH = 8
J = 80
LON = ("x", "z", "y_hi")
LAT = ("y_lo", "core")
PLANE = ("x", "y_hi", "y_lo")
ALL = LON + LAT
CHIPS = ("x", "z", "y_hi", "y_lo")
BF = jnp.bfloat16
F32 = jnp.float32


def call(body, outs, scratch=(), flops=0, smem=(), hbm=(), n_in=0, sems=0):
    spaces = [pltpu.SMEM if i in smem else pltpu.HBM if i in hbm else pltpu.VMEM for i in range(n_in)]
    out_spaces = [pltpu.HBM if len(o) > 2 else pltpu.VMEM for o in outs]
    return pl.pallas_call(
        body,
        out_shape=[pltpu.HBM(o[0], o[1]) if len(o) > 2 else jax.ShapeDtypeStruct(o[0], o[1]) for o in outs],
        in_specs=[pl.BlockSpec(memory_space=m) for m in spaces],
        out_specs=[pl.BlockSpec(memory_space=m) for m in out_spaces],
        scratch_shapes=[pltpu.VMEM(s, d) for s, d in scratch]
        + ([pltpu.SemaphoreType.DMA((sems,))] if sems else []),
        compiler_params=pltpu.CompilerParams(vmem_limit_bytes=24 * 1024 * 1024),
        cost_estimate=pl.CostEstimate(flops=flops, bytes_accessed=1 << 20, transcendentals=0),
    )


def pinned(value):
    return pltpu.with_memory_space_constraint(value, pltpu.HBM)


def dot(a, b):
    return jnp.dot(a, b, preferred_element_type=F32)


def dot_t(a, b):
    return lax.dot_general(a, b, (((1,), (1,)), ((), ())), preferred_element_type=F32)


def t_dot(a, b):
    return lax.dot_general(a, b, (((0,), (0,)), ((), ())), preferred_element_type=F32)


def exact(a, b):
    a8 = jnp.broadcast_to(a, (8, a.shape[1]))
    return jnp.dot(a8, b, preferred_element_type=F32, precision=lax.Precision.HIGHEST)[0:1]


def to_lanes(chans):
    c = lax.broadcasted_iota(jnp.int32, (chans, 128), 0) // WIDTH
    l = lax.broadcasted_iota(jnp.int32, (chans, 128), 1)
    return (c == l).astype(F32)


def from_lanes(chans):
    c = lax.broadcasted_iota(jnp.int32, (128, chans), 1) // WIDTH
    l = lax.broadcasted_iota(jnp.int32, (128, chans), 0)
    return (c == l).astype(F32)


def masks():
    j = lax.broadcasted_iota(jnp.int32, (J, 1), 0)
    odd = jnp.where((j >= 1) & (j <= 64), 1.0, 0.0)
    even = jnp.where(j <= 63, 1.0, 0.0)
    return odd, even


def pack_lon(feat, cot, east, west, sems):
    rows, cols, _ = feat.shape
    half, pairs, _ = cot.shape
    copies = [
        pltpu.make_async_copy(feat.at[:, cols - 16 : cols], east.at[0:rows], sems.at[0]),
        pltpu.make_async_copy(cot.at[:, pairs - 16 : pairs], east.at[rows : rows + half], sems.at[1]),
        pltpu.make_async_copy(feat.at[:, 0:16], west.at[0:rows], sems.at[2]),
        pltpu.make_async_copy(cot.at[:, 0:16], west.at[rows : rows + half], sems.at[3]),
    ]
    for copy in copies:
        copy.start()
    for copy in copies:
        copy.wait()


def pack_lat(feat, cot, west, east, south, north, sems):
    rows, cols, _ = feat.shape
    half, pairs, _ = cot.shape
    copies = []
    ends = ((south, rows - 2, half - 1), (north, 0, 0))
    for dest, top, mid in ends:
        parts = [(feat.at[top + k], k * (cols + 32) + 16, cols) for k in range(2)]
        parts.append((cot.at[mid], 2 * (cols + 32) + 16, pairs))
        for src, o, n in parts:
            copies.append(pltpu.make_async_copy(src, dest.at[o : o + n], sems.at[len(copies)]))
            copies[-1].start()
    for dest, top, mid in ends:
        for row, o, n in (
            (top, 0, cols),
            (top + 1, cols + 32, cols),
            (rows + mid, 2 * (cols + 32), pairs),
        ):
            dest[o : o + 16] = west[row]
            dest[o + 16 + n : o + 32 + n] = east[row]
    for copy in copies:
        copy.wait()


def conv_kernel(
    feat_hbm, west, east, north, south, w_hbm, x_hbm, h_hbm, hq_out, he_out, stat_out, f32s, x_out, feat, w, sems
):
    rows, cols, chans = feat.shape
    load_f = pltpu.make_async_copy(feat_hbm, feat, sems.at[1])
    load_f.start()
    load_w = pltpu.make_async_copy(w_hbm, w, sems.at[2])
    load_w.start()
    wide = cols + 32
    f32s[:, :, wide : wide + 16] = jnp.zeros((rows + 4, 2, 16, 128), F32)
    load_f.wait()
    for v in range(2):
        part = slice(v * 128, v * 128 + 128)
        for k in range(2):
            f32s[k, v, 0:wide] = north[k * wide : (k + 1) * wide, part].astype(F32)
            f32s[rows + 2 + k, v, 0:wide] = south[k * wide : (k + 1) * wide, part].astype(F32)
        f32s[2 : rows + 2, v, 0:16] = west[0:rows, :, part].astype(F32)
        f32s[2 : rows + 2, v, 16 : 16 + cols] = feat[:, :, part].astype(F32)
        f32s[2 : rows + 2, v, 16 + cols : wide] = east[0:rows, :, part].astype(F32)
        for r in range(rows + 4):
            for k in range(4):
                lane = k * chans + v * 128
                x_out[r, :, lane : lane + 128] = f32s[r, v, pl.ds(14 + k, J, stride=2), :].astype(BF)
    keep = pltpu.make_async_copy(x_out, x_hbm, sems.at[0])
    keep.start()
    load_w.wait()
    copies = [keep]
    odd, even = masks()
    sums = jnp.zeros((1, chans), F32)
    for out, lo in ((hq_out, 0), (he_out, chans)):
        acc = None
        for a in range(3):
            lhs = x_out[a : a + rows + 2, :, lo : lo + 3 * chans].reshape((rows + 2) * J, 3 * chans)
            term = dot(lhs, w[a])
            acc = term if acc is None else acc + term
        out[...] = acc.astype(BF).reshape(rows + 2, J, chans)
        k = lo // chans
        copies.append(pltpu.make_async_copy(out, h_hbm.at[k], sems.at[3 + k]))
        copies[-1].start()
    for out, mask in ((hq_out, odd), (he_out, even)):
        part = jnp.zeros((J, chans), F32)
        for r in range(1, rows + 1):
            part = part + out[r].astype(F32)
        sums = sums + jnp.sum(part * mask, axis=0, keepdims=True)
    lanes = to_lanes(chans)
    means = exact(sums, lanes) / (rows * cols * WIDTH)
    mean = exact(means, from_lanes(chans))
    squares = jnp.zeros((1, chans), F32)
    for out, mask in ((hq_out, odd), (he_out, even)):
        part = jnp.zeros((J, chans), F32)
        for r in range(1, rows + 1):
            d = out[r].astype(F32) - mean
            part = part + d * d
        squares = squares + jnp.sum(part * mask, axis=0, keepdims=True)
    stat_out[...] = jnp.concatenate([means, exact(squares, lanes)], axis=0)
    for copy in copies:
        copy.wait()


def pair_stats(local_n, stat, other, out):
    mine, theirs = stat[...], other[...]
    gap = mine[0:1] - theirs[0:1]
    mean = 0.5 * (mine[0:1] + theirs[0:1])
    squares = mine[1:2] + theirs[1:2] + (0.5 * local_n) * gap * gap
    both = jnp.concatenate([mean, squares], axis=0)
    out[...] = jnp.broadcast_to(both[None], out.shape)


def pair_sums(mine, other, out):
    both = mine[...] + other[...]
    out[...] = jnp.broadcast_to(both[None], out.shape)


def back_kernel(cot, west, east, north, south, dw, c_out, aq_out, ae_out, f32s):
    half, pairs, chans = cot.shape
    rows = west.shape[0] - half
    wide = pairs + 32
    base = north.shape[0] - wide
    f32s[0, 0:wide] = north[base : base + wide].astype(F32)
    f32s[half + 1, 0:wide] = south[base : base + wide].astype(F32)
    f32s[1 : half + 1, 0:16] = west[rows:].astype(F32)
    f32s[1 : half + 1, 16 : 16 + pairs] = cot[...].astype(F32)
    f32s[1 : half + 1, 16 + pairs : wide] = east[rows:].astype(F32)
    for s in range(half + 2):
        c_out[s, :, 0:chans] = f32s[s, 15 : 15 + J].astype(BF)
        c_out[s, :, chans : 2 * chans] = f32s[s, 16 : 16 + J].astype(BF)
    n = half + 1
    lo_l = c_out[0:n, :, 0:chans].reshape(n * J, chans)
    lo_r = c_out[0:n, :, chans:].reshape(n * J, chans)
    hi_l = c_out[1 : n + 1, :, 0:chans].reshape(n * J, chans)
    hi_r = c_out[1 : n + 1, :, chans:].reshape(n * J, chans)

    def put(out, k, value):
        value = value.astype(BF).reshape(n, J, chans)
        for i in range(n):
            out[2 * i + k] = value[i]

    put(ae_out, 1, dot_t(hi_r, dw[1, 1]))
    put(aq_out, 1, dot_t(hi_r, dw[1, 0]) + dot_t(hi_l, dw[1, 2]))
    put(ae_out, 0, dot_t(hi_r, dw[0, 1]) + dot_t(lo_r, dw[2, 1]))
    put(
        aq_out,
        0,
        dot_t(hi_r, dw[0, 0]) + dot_t(hi_l, dw[0, 2]) + dot_t(lo_r, dw[2, 0]) + dot_t(lo_l, dw[2, 2]),
    )


def act_kernel(cells, flags, stats, hq, he, aq, ae, gain, bias, t_hbm, p_hbm, coef_out, sum_out, f32s, t_out, p_out, sems):
    chips = stats.shape[0]
    rows = hq.shape[0] - 2
    chans = hq.shape[2]
    chip_n = float(cells // chips * WIDTH)
    count = float(cells * WIDTH)
    rec = stats[...]
    total = jnp.sum(rec, axis=0)
    centre = total[0:1] / chips
    dev = rec[:, 0, :] - centre
    spread = jnp.sum(dev * dev, axis=0, keepdims=True)
    back = from_lanes(chans)
    mean = exact(centre, back)
    var = exact((total[1:2] + chip_n * spread) / count, back)
    inverse = lax.rsqrt(var + EPS)
    coef_out[0:1] = mean
    coef_out[1:2] = inverse
    g = gain[...]
    b = bias[...]
    odd, even = masks()
    top = jnp.where(flags[0] == 1, 0.0, 1.0)
    bias_sum = jnp.zeros((1, chans), F32)
    gain_sum = jnp.zeros((1, chans), F32)
    copies = []
    for k, (h, a, mask) in enumerate(((hq, aq, odd), (he, ae, even))):
        is_q = k == 0
        acc_b = jnp.zeros((J, chans), F32)
        acc_g = jnp.zeros((J, chans), F32)
        for r in range(rows + 2):
            normed = (h[r].astype(F32) - mean) * inverse
            shifted = g * normed + b
            sigma = jax.nn.sigmoid(shifted)
            pre = a[r].astype(F32) * sigma * (1.0 + shifted * (1.0 - sigma))
            p_out[k, r] = pre
            copies.append(pltpu.make_async_copy(p_out.at[k, r], p_hbm.at[k, r], sems.at[len(copies)]))
            copies[-1].start()
            if 1 <= r <= rows:
                acc_b = acc_b + pre
                acc_g = acc_g + pre * normed
            if r <= rows:
                active = shifted * sigma
                if r == 0:
                    active = active * top
                if is_q:
                    f32s[...] = active.astype(BF).astype(F32)
                    t_out[r, :, 0:chans] = active[0:64].astype(BF)
                    t_out[r, :, 2 * chans :] = f32s[1:65].astype(BF)
                else:
                    t_out[r, :, chans : 2 * chans] = active[0:64].astype(BF)
                    copies.append(pltpu.make_async_copy(t_out.at[r], t_hbm.at[r], sems.at[len(copies)]))
                    copies[-1].start()
        bias_sum = bias_sum + jnp.sum(acc_b * mask, axis=0, keepdims=True)
        gain_sum = gain_sum + jnp.sum(acc_g * mask, axis=0, keepdims=True)
    sum_out[...] = jnp.concatenate(
        [bias_sum[:, 0:128], bias_sum[:, 128:256], gain_sum[:, 0:128], gain_sum[:, 128:256]], axis=0
    )
    for copy in copies:
        copy.wait()


def down_kernel(t, c, dw, out, grad):
    half = out.shape[0]
    pairs, chans = out.shape[1:]
    cot = c[1 : half + 1, 0:pairs, chans:].reshape(half * pairs, chans)
    acc = None
    for a in range(3):
        lhs = jnp.concatenate([t[2 * i + a] for i in range(half)], axis=0)
        term = dot(lhs, dw[a])
        acc = term if acc is None else acc + term
        grad[a * 3 * chans : (a + 1) * 3 * chans] = t_dot(lhs, cot)
    out[...] = acc.astype(BF).reshape(out.shape)


def grad_kernel(
    cells, flags, sums, coef, gain, h_hbm, p_hbm, x_hbm, h4_hbm, conv_out, vec_out, f32s, rq, re, h_in, p_in, x, h4_out, sems
):
    rows = p_in.shape[1] - 2
    chans = p_in.shape[3]
    loads = []
    for k in range(2):
        loads.append(pltpu.make_async_copy(h_hbm.at[k], h_in.at[k], sems.at[len(loads)]))
        loads[-1].start()
        for r in range(rows + 2):
            loads.append(pltpu.make_async_copy(p_hbm.at[k, r], p_in.at[k, r], sems.at[len(loads)]))
            loads[-1].start()
    load_x = pltpu.make_async_copy(x_hbm, x, sems.at[len(loads)])
    load_x.start()
    first_out = len(loads) + 1
    copies = []
    count = float(cells * WIDTH)
    total = jnp.sum(sums[...], axis=0)
    bias_sum = jnp.concatenate([total[0:1], total[1:2]], axis=1)
    gain_sum = jnp.concatenate([total[2:3], total[3:4]], axis=1)
    factor = 1.0 / math.sqrt(cells)
    vec_out[0:1] = gain_sum * factor
    vec_out[1:2] = bias_sum * factor
    g = gain[...]
    lanes, back = to_lanes(chans), from_lanes(chans)
    first = exact(exact(g * bias_sum, lanes), back) / count
    second = exact(exact(g * gain_sum, lanes), back) / count
    mean = coef[0:1]
    inverse = coef[1:2]
    top = jnp.where(flags[0] == 1, 0.0, 1.0)
    bottom = jnp.where(flags[1] == 1, 0.0, 1.0)
    odd, even = masks()
    zero = jnp.zeros((J, chans), BF)
    for k, (r_out, mask) in enumerate(((rq, odd), (re, even))):
        is_q = k == 0
        loads[k * (rows + 3)].wait()
        for f in (0, 1):
            for a in (1, 2):
                if f - a + 1 <= 0:
                    r_out[f, :, a * chans : (a + 1) * chans] = zero
                    r_out[rows + 1 - f, :, (2 - a) * chans : (3 - a) * chans] = zero
        for r in range(rows + 2):
            loads[k * (rows + 3) + 1 + r].wait()
            normed = (h_in[k, r].astype(F32) - mean) * inverse
            value = inverse * (g * p_in[k, r] - first - normed * second)
            if r == 0:
                value = value * top
            if r == rows + 1:
                value = value * bottom
            rounded = value.astype(BF)
            if 1 <= r <= rows:
                inner = (value * mask).astype(BF)
                for a in range(3):
                    r_out[r + a - 1, :, a * chans : (a + 1) * chans] = inner
            f32s[...] = rounded.astype(F32)
            moved = f32s[1:65].astype(BF)
            lo = 3 if is_q else 2
            h4_out[r, :, lo * chans : (lo + 1) * chans] = rounded[0:64]
            lo = 1 if is_q else 0
            h4_out[r, :, lo * chans : (lo + 1) * chans] = moved
            if not is_q:
                copies.append(pltpu.make_async_copy(h4_out.at[r], h4_hbm.at[r], sems.at[first_out + r]))
                copies[-1].start()
    m = (rows + 2) * J
    load_x.wait()
    lhs = x[1 : rows + 3].reshape(m, 4 * chans)
    part = t_dot(lhs[:, 0 : 3 * chans], rq[...].reshape(m, 3 * chans))
    part = part + t_dot(lhs[:, chans : 4 * chans], re[...].reshape(m, 3 * chans))
    for a in range(3):
        conv_out[a * 3 * chans : (a + 1) * 3 * chans] = part[:, a * chans : (a + 1) * chans]
    for copy in copies:
        copy.wait()


def input_kernel(h4, w, out, f32s):
    rows, cols, chans = out.shape
    for k, lo in ((0, 1), (1, 0)):
        acc = None
        for a in range(3):
            for b in range(3):
                lane = (lo + b) * chans
                lhs = h4[2 - a : 2 - a + rows, :, lane : lane + chans].reshape(rows * (cols // 2), chans)
                term = dot_t(lhs, w[a, b])
                acc = term if acc is None else acc + term
        acc = acc.reshape(rows, cols // 2, chans)
        for r in range(rows):
            for v in range(2):
                f32s[r, v, pl.ds(k, cols // 2, stride=2), :] = acc[r, :, v * 128 : v * 128 + 128]
    for v in range(2):
        out[:, :, v * 128 : v * 128 + 128] = f32s[:, v].astype(BF)


def passed(value, axes, step, wrap):
    n = lax.axis_size(axes)
    pairs = [(i, (i + step) % n) for i in range(n) if wrap or 0 <= i + step < n]
    return lax.ppermute(value, axes, pairs)


def unpack_kernel(flags, whole, other, conv, down, f32s, sems):
    n = whole.shape[0]
    step = n // 4
    for core, one, two in ((0, whole, other), (1, other, whole)):

        @pl.when(flags[2] == core)
        def _():
            copies = []
            for k, (src, dst) in enumerate(((one, conv), (two, down))):
                for q in range(4):
                    part = slice(q * step, (q + 1) * step)
                    f32s[k, part] = src[part].astype(F32)
                    copies.append(pltpu.make_async_copy(f32s.at[k, part], dst.at[part], sems.at[k * 4 + q]))
                    copies[-1].start()
            for copy in copies:
                copy.wait()


def core_swap(value):
    return lax.ppermute(value, "core", [(0, 1), (1, 0)])


def local(features, conv_weight, down_weight, norm_gain, norm_bias, cotangent):
    rows, cols, chans = features.shape
    half, pairs, _ = cotangent.shape
    devices = lax.axis_size(ALL)
    lats = lax.axis_size(LAT)
    cells = rows * cols * devices
    factor = 1.0 / math.sqrt(cells)
    lat = lax.axis_index(LAT)
    flags = jnp.stack([lat == 0, lat == lats - 1, lax.axis_index("core") == 1]).astype(jnp.int32)
    gain = norm_gain.reshape(1, chans)
    bias = norm_bias.reshape(1, chans)
    w3 = conv_weight.reshape(3, 3 * chans, chans)
    dw3 = down_weight.reshape(3, 3 * chans, chans)
    all_rows = 9 * chans

    with jax.named_scope("halo"):
        slab = (rows + half, 16, chans)
        to_east, to_west = call(pack_lon, [(slab, BF)] * 2, n_in=2, hbm=(0, 1), sems=4)(
            pinned(features), pinned(cotangent)
        )
        west = passed(to_east, LON, 1, True)
        east = passed(to_west, LON, -1, True)
        strip = (2 * (cols + 32) + pairs + 32, chans)
        to_south, to_north = call(pack_lat, [(strip, BF)] * 2, n_in=4, hbm=(0, 1), sems=6)(
            pinned(features), pinned(cotangent), west, east
        )
        north = passed(to_south, LAT, 1, False)
        south = passed(to_north, LAT, -1, False)

    plane = (rows + 2, J, chans)
    x_shape = (rows + 4, J, 4 * chans)
    with jax.named_scope("conv"):
        x, h, hq, he, stat = call(
            conv_kernel,
            [(x_shape, BF, True), ((2,) + plane, BF, True), (plane, BF), (plane, BF), ((2, 128), F32)],
            [((rows + 4, 2, cols + 48, 128), F32), (x_shape, BF), ((rows, cols, chans), BF), (w3.shape, BF)],
            flops=2 * 1600 * 2304 * 256,
            n_in=6,
            hbm=(0, 5),
            sems=5,
        )(pinned(features), west, east, north, south, pinned(w3))
        chips = lax.axis_size(CHIPS)
        local_n = float(rows * cols * WIDTH)
        (wide,) = call(functools.partial(pair_stats, local_n), [((chips, 2, 128), F32)], n_in=2)(stat, core_swap(stat))
        stats = lax.all_to_all(wide, CHIPS, 0, 0, tiled=True)
    with jax.named_scope("back"):
        c2, aq, ae = call(
            back_kernel,
            [((half + 2, J, 2 * chans), BF), (plane, BF), (plane, BF)],
            [((half + 2, pairs + 32, chans), F32)],
            flops=2 * 400 * 2304 * 256,
            n_in=6,
        )(cotangent, west, east, north, south, down_weight)
    t_shape = (rows + 1, pairs, 3 * chans)
    with jax.named_scope("act"):
        t, p, coef, sums = call(
            functools.partial(act_kernel, cells),
            [(t_shape, BF, True), ((2,) + plane, F32, True), ((2, chans), F32), ((4, 128), F32)],
            [((J, chans), F32), (t_shape, BF), ((2,) + plane, F32)],
            flops=1600 * 256 * 20,
            smem=(0,),
            n_in=8,
            sems=3 * rows + 5,
        )(flags, stats, hq, he, aq, ae, gain, bias)
        (wide,) = call(pair_sums, [((chips, 4, 128), F32)], n_in=2)(sums, core_swap(sums))
        sums = lax.all_to_all(wide, CHIPS, 0, 0, tiled=True)
    with jax.named_scope("down"):
        output, down_part = call(
            down_kernel,
            [((half, pairs, chans), BF), ((all_rows, chans), F32)],
            flops=4 * 256 * 2304 * 256,
            n_in=3,
        )(t, c2, dw3)
    h4_shape = (rows + 2, pairs, 4 * chans)
    with jax.named_scope("grad"):
        h4, conv_part, vec = call(
            functools.partial(grad_kernel, cells),
            [(h4_shape, BF, True), ((all_rows, chans), F32), ((2, chans), F32)],
            [
                ((J, chans), F32),
                ((rows + 2, J, 3 * chans), BF),
                ((rows + 2, J, 3 * chans), BF),
                ((2,) + plane, BF),
                ((2,) + plane, F32),
                (x_shape, BF),
                (h4_shape, BF),
            ],
            flops=2 * 1600 * 2304 * 256,
            smem=(0,),
            hbm=(4, 5, 6),
            n_in=7,
            sems=3 * (rows + 2) + 3,
        )(flags, sums, coef, gain, pinned(h), pinned(p), pinned(x))
    with jax.named_scope("input"):
        (input_grad,) = call(
            input_kernel,
            [((rows, cols, chans), BF)],
            [((rows, 2, cols, 128), F32)],
            flops=2 * 1024 * 2304 * 256,
            n_in=2,
        )(h4, conv_weight)
    with jax.named_scope("total"):
        first = lax.axis_index("core") == 0
        other = core_swap(jnp.where(first, down_part, conv_part).astype(BF))
        mine = (jnp.where(first, conv_part, down_part) + other.astype(F32)).astype(BF)
        chips = lax.axis_size(PLANE)
        depth = lax.axis_size("z")
        share = all_rows // chips
        got = lax.all_to_all(mine.reshape(chips, share, chans), PLANE, 0, 0, tiled=True)
        got, input_grad = lax.optimization_barrier((got, input_grad))
        piece = jnp.sum(got.astype(F32), axis=0).astype(BF)
        got = lax.all_to_all(jnp.broadcast_to(piece[None], (depth, share, chans)), "z", 0, 0, tiled=True)
        piece = (jnp.sum(got.astype(F32), axis=0) * factor).astype(BF)
        whole = lax.all_to_all(jnp.broadcast_to(piece[None], (chips, share, chans)), PLANE, 0, 0, tiled=True)
        whole = whole.reshape(all_rows, chans)
        flat = ((all_rows, chans), F32, True)
        conv_grad, down_grad = call(
            unpack_kernel, [flat, flat], [((2, all_rows, chans), F32)], smem=(0,), n_in=3, sems=8
        )(flags, whole, core_swap(whole))
    shape = (3, 3, chans, chans)
    return output, input_grad, conv_grad.reshape(shape), down_grad.reshape(shape), vec[0], vec[1]


SIZES = {64: (4, 8, 2), 2: (1, 2, 1), 4: (2, 2, 1)}


def solution(mesh):
    lon, lat = mesh.devices.shape
    fine = Mesh(mesh.devices.reshape(SIZES[lon] + (lat // 2, 2)), ALL)
    band = P(LAT, LON, None)
    return jax.shard_map(
        local,
        mesh=fine,
        in_specs=(band, P(), P(), P(), P(), band),
        out_specs=(band, band, P(), P(), P(), P()),
        check_vma=False,
    )
```

time: 175 us -> 168 us (0.960)
  blocking collectives: 59.5 us -> 37.6 us
  local copies, waits for them, and re-layouts: 17 us -> 5.92 us
  starting transfers between devices: 38.9 us -> 49.3 us
  waiting for transfers between devices: 36.6 us -> 46.2 us
  Pallas kernels: 16.2 us -> 25.6 us
  other arithmetic: 4.76 us -> 2.11 us
    all_to_all x1 -> x0, blocking collectives: 21.5 us -> none  [local(): lax.all_to_all(mine.reshape(chips, share, chans), PLANE, 0, 0, tiled=True)]
    unnamed x52 -> x22, local copies, waits for them, and re-layouts: 16.3 us -> 5.23 us
    pallas_call x6 -> x9, Pallas kernels: 13.3 us -> 22.7 us  [the longest x1 6.47 us: local(): call(functools.partial(grad_kernel, cells), [(h4_shape, BF, True), ((all_...]
    all_to_all x2 -> x3, waiting for transfers between devices: 26.4 us -> 32.2 us  [the longest x1 14.8 us: local(): lax.all_to_all(mine.reshape(chips, share, chans), PLANE, 0, 0, tiled=True)]
    all_to_all x2 -> x3, starting transfers between devices: 17.9 us -> 23.4 us  [the longest x1 12.1 us: local(): stats = lax.all_to_all(wide, CHIPS, 0, 0, tiled=True)]
    ppermute x2 -> x4, starting transfers between devices: 4.21 us -> 9.12 us  [core_swap(): return lax.ppermute(value, 'core', [(0, 1), (1, 0)])]
    ppermute x2 -> x4, waiting for transfers between devices: 2.54 us -> 6.32 us  [core_swap(): return lax.ppermute(value, 'core', [(0, 1), (1, 0)])]
    convert_element_type x6 -> x4, other arithmetic: 4.06 us -> 1.87 us  [the longest x1 1.43 us: local(): (jnp.where(first, conv_part, down_part) + other.astype(F32)).astype(BF)]
  transfers between devices with their start and end apart: 8 -> 11, of which waited for: 6 -> 10; matrix products, arithmetic and copies ran while one was open for 1% -> 0% of each run, Pallas kernels for 3% -> 3%
where the time goes in v2:
time: 168 us
  starting transfers between devices  49.3 us (29%)
  waiting for transfers between devices  46.2 us (28%)
  blocking collectives  37.6 us (22%)
  Pallas kernels  25.6 us (15%)
  local copies, waits for them, and re-layouts  5.92 us (4%)
  other arithmetic  2.11 us (1%)
    all_to_all x1, blocking collectives, local(): lax.all_to_all(jnp.broadcast_to(piece[None], (chips, share, chans)), PLAN...  19.3 us
    all_to_all x1, blocking collectives, local(): lax.all_to_all(jnp.broadcast_to(piece[None], (depth, share, chans)), 'z',...  18.3 us
    ppermute x4, starting transfers between devices, passed(): return lax.ppermute(value, axes, pairs)  16.7 us
    all_to_all x1, waiting for transfers between devices, local(): lax.all_to_all(mine.reshape(chips, share, chans), PLANE, 0, 0, tiled=True)  14.8 us
    all_to_all x1, starting transfers between devices, local(): stats = lax.all_to_all(wide, CHIPS, 0, 0, tiled=True)  12.1 us
    ppermute x4, starting transfers between devices, core_swap(): return lax.ppermute(value, 'core', [(0, 1), (1, 0)])  9.12 us
    all_to_all x1, waiting for transfers between devices, local(): sums = lax.all_to_all(wide, CHIPS, 0, 0, tiled=True)  9.08 us
    all_to_all x1, waiting for transfers between devices, local(): stats = lax.all_to_all(wide, CHIPS, 0, 0, tiled=True)  8.3 us
  transfers between devices with their start and end apart: 11, of which 10 were waited for; matrix products, arithmetic and copies ran while one was open for 0% of the time, Pallas kernels for 3%

profile of v2, /device:TPU:1, one launch (start us, length us, event | category | flops | bytes accessed | tf_op | source)
XLA Modules:
  0.0 167.7 jit_solution(13959221613704351887)
XLA Ops:
  0.6 0.9 halo.2
  1.6 3.8 %collective-permute-start = (bf16[12,16,256]{2,1,0:T(8,128)(2,1)S(1)}, bf16[12,16,256]{2,1,0:T(8,128)(2,1)S(1)}, u32[]{:S(2)}, u32[]{:S(2)}) collective-permute-start(bf16[12,16,256]{2,1,0:T(8,128)(2,1)S(1)} %get-tuple-element.31), channel_id=1, source_target_pairs={{0,4},{4,8},{8,12},{12,16},{16,20},{20,24},{24,28},{28,32},{32,36}... | collective-permute-start | bytes 294920 | tf_op jit(solution)/shard_map/halo/ppermute | solution.py:392
  5.4 7.6 %collective-permute-start.1 = (bf16[12,16,256]{2,1,0:T(8,128)(2,1)S(1)}, bf16[12,16,256]{2,1,0:T(8,128)(2,1)S(1)}, u32[]{:S(2)}, u32[]{:S(2)}) collective-permute-start(bf16[12,16,256]{2,1,0:T(8,128)(2,1)S(1)} %get-tuple-element.32), channel_id=1, source_target_pairs={{0,252},{4,0},{8,4},{12,8},{16,12},{20,16},{24,20},{28,24},{32,28}... | collective-permute-start | bytes 294920 | tf_op jit(solution)/shard_map/halo/ppermute | solution.py:392
  13.0 2.4 %collective-permute-done.west = bf16[12,16,256]{2,1,0:T(8,128)(2,1)S(1)} collective-permute-done((bf16[12,16,256]{2,1,0:T(8,128)(2,1)S(1)}, bf16[12,16,256]{2,1,0:T(8,128)(2,1)S(1)}, u32[]{:S(2)}, u32[]{:S(2)}) %collective-permute-start) | collective-permute-done | bytes 98336 | tf_op jit(solution)/shard_map/halo/ppermute | solution.py:392
  15.4 1.0 halo.3
  16.4 3.4 %collective-permute-start.2 = (bf16[416,256]{1,0:T(8,128)(2,1)S(1)}, bf16[416,256]{1,0:T(8,128)(2,1)S(1)}, u32[]{:S(2)}, u32[]{:S(2)}) collective-permute-start(bf16[416,256]{1,0:T(8,128)(2,1)S(1)} %get-tuple-element.33), channel_id=1, source_target_pairs={{0,1},{1,2},{2,3},{4,5},{5,6},{6,7},{8,9},{9,10},{10,11},{12,13},{... | collective-permute-start | bytes 638984 | tf_op jit(solution)/shard_map/halo/ppermute | solution.py:392
  19.8 1.9 %collective-permute-start.3 = (bf16[416,256]{1,0:T(8,128)(2,1)S(1)}, bf16[416,256]{1,0:T(8,128)(2,1)S(1)}, u32[]{:S(2)}, u32[]{:S(2)}) collective-permute-start(bf16[416,256]{1,0:T(8,128)(2,1)S(1)} %get-tuple-element.34), channel_id=1, source_target_pairs={{1,0},{2,1},{3,2},{5,4},{6,5},{7,6},{9,8},{10,9},{11,10},{13,12},{... | collective-permute-start | bytes 638984 | tf_op jit(solution)/shard_map/halo/ppermute | solution.py:392
  21.8 0.8 collective-permute-done.2.north
  22.6 4.4 %collective-permute-done.3.south = bf16[416,256]{1,0:T(8,128)(2,1)S(1)} collective-permute-done((bf16[416,256]{1,0:T(8,128)(2,1)S(1)}, bf16[416,256]{1,0:T(8,128)(2,1)S(1)}, u32[]{:S(2)}, u32[]{:S(2)}) %collective-permute-start.3) | collective-permute-done | bytes 213024 | tf_op jit(solution)/shard_map/halo/ppermute | solution.py:392
  27.0 4.7 %conv.2 = (bf16[12,80,1024]{2,1,0:T(8,128)(2,1)}, bf16[2,10,80,256]{3,2,1,0:T(8,128)(2,1)}, bf16[10,80,256]{2,1,0:T(8,128)(2,1)S(1)}, bf16[10,80,256]{2,1,0:T(8,128)(2,1)S(1)}, f32[2,128]{1,0:T(2,128)S(1)}) custom-call(bf16[8,128,256]{2,1,0:T(8,128)(2,1)} %feat_hbm.1, bf16[12,16,256]{2,1,0:T(8,128)(2,1)S(1)} %collective-permute-done.west, ...), custom_call_target="tpu_custom_call" | custom-call | flops 1887436800 | bytes 1048576 | tf_op jit(solution)/shard_map/conv/pallas_call | solution.py:449
  31.7 0.0 copy-start.7
  31.7 0.1 collective-permute-start.4
  31.8 1.1 collective-permute-done.4.other
  33.0 0.7 conv.3
  33.7 12.1 %all-to-all-start = ((f32[128,2,128]{2,1,0:T(2,128)}), f32[128,2,128]{2,1,0:T(2,128)S(1)}, u32[]{:S(2)}, u32[]{:S(2)}) async-start(f32[128,2,128]{2,1,0:T(2,128)} %conv.3), calls=%async_computation | async-start | bytes 262144 | tf_op jit(solution)/shard_map/conv/all_to_all | solution.py:461
  45.8 0.1 add_convert_fusion.1.flags
  45.9 0.9 copy-done.6
  46.8 0.7 back.1
  47.5 0.0 copy-start.3
  47.5 0.8 copy-done.3
  48.3 8.3 %all-to-all-done.stats = f32[128,2,128]{2,1,0:T(2,128)S(1)} async-done(((f32[128,2,128]{2,1,0:T(2,128)}), f32[128,2,128]{2,1,0:T(2,128)S(1)}, u32[]{:S(2)}, u32[]{:S(2)}) %all-to-all-start) | async-done | bytes 131104 | tf_op jit(solution)/shard_map/conv/all_to_all | solution.py:461
  56.6 3.9 %act.2 = (bf16[9,64,768]{2,1,0:T(8,128)(2,1)}, f32[2,10,80,256]{3,2,1,0:T(8,128)}, f32[2,256]{1,0:T(2,128)S(1)}, f32[4,128]{1,0:T(4,128)S(1)}) custom-call(s32[3]{0:T(128)S(1)} %add_convert_fusion.1.flags, f32[128,2,128]{2,1,0:T(2,128)S(1)} %all-to-all-done.stats, bf16[10,80,256]{2,1,0:T(8,128)(2,1)S(1)} %get-tuple-element.36.hq, ...), custom_call_target="tpu_custom_call" | custom-call | flops 8192000 | bytes 1048576 | tf_op jit(solution)/shard_map/act/pallas_call | solution.py:472
  60.4 2.3 %collective-permute-start.5 = (f32[4,128]{1,0:T(4,128)S(1)}, f32[4,128]{1,0:T(4,128)S(1)}, u32[]{:S(2)}, u32[]{:S(2)}) collective-permute-start(f32[4,128]{1,0:T(4,128)S(1)} %get-tuple-element.43.mine), channel_id=1, source_target_pairs={{0,1},{1,0},{2,3},{3,2},{4,5},{5,4},{6,7},{7,6},{8,9},{9,8},{10,11... | collective-permute-start | bytes 6152 | tf_op jit(solution)/shard_map/act/ppermute | solution.py:414
  62.8 0.8 collective-permute-done.5.other
  63.6 0.7 act.3
  64.3 7.5 %all-to-all-start.1 = ((f32[128,4,128]{2,1,0:T(4,128)}), f32[128,4,128]{2,1,0:T(4,128)}, u32[]{:S(2)}, u32[]{:S(2)}) async-start(f32[128,4,128]{2,1,0:T(4,128)} %act.3), calls=%async_computation.1 | async-start | bytes 524288 | tf_op jit(solution)/shard_map/act/all_to_all | solution.py:482
  71.8 1.2 copy-done.2
  73.0 1.0 copy-done.4
  74.0 1.4 down.1
  75.5 9.1 %all-to-all-done.1.sums = f32[128,4,128]{2,1,0:T(4,128)} async-done(((f32[128,4,128]{2,1,0:T(4,128)}), f32[128,4,128]{2,1,0:T(4,128)}, u32[]{:S(2)}, u32[]{:S(2)}) %all-to-all-start.1) | async-done | bytes 262176 | tf_op jit(solution)/shard_map/act/all_to_all | solution.py:482
  84.5 6.5 %grad.1 = (bf16[10,64,1024]{2,1,0:T(8,128)(2,1)}, f32[2304,256]{1,0:T(8,128)S(1)}, f32[2,256]{1,0:T(2,128)S(1)}) custom-call(s32[3]{0:T(128)S(1)} %add_convert_fusion.1.flags, f32[128,4,128]{2,1,0:T(4,128)} %all-to-all-done.1.sums, f32[2,256]{1,0:T(2,128)S(1)} %get-tuple-element.44.coef, f32[1,256]{1,0:T(1,128)S(1)} %bitcast.18, ...), custom_call_target="tpu_custom_call" | custom-call | flops 1887436800 | bytes 1048576 | tf_op jit(solution)/shard_map/grad/pallas_call | solution.py:492
  91.0 0.4 select_convert_fusion
  91.4 2.3 %collective-permute-start.6 = (bf16[2304,256]{1,0:T(8,128)(2,1)S(1)}, bf16[2304,256]{1,0:T(8,128)(2,1)S(1)}, u32[]{:S(2)}, u32[]{:S(2)}) collective-permute-start(bf16[2304,256]{1,0:T(8,128)(2,1)S(1)} %select_convert_fusion), channel_id=1, source_target_pairs={{0,1},{1,0},{2,3},{3,2},{4,5},{5,4},{6,7},{7,6},{8,9},{9,8},{10,11... | collective-permute-start | bytes 3538952 | tf_op jit(solution)/shard_map/total/ppermute | solution.py:414
  93.7 2.5 %collective-permute-done.6 = bf16[2304,256]{1,0:T(8,128)(2,1)S(1)} collective-permute-done((bf16[2304,256]{1,0:T(8,128)(2,1)S(1)}, bf16[2304,256]{1,0:T(8,128)(2,1)S(1)}, u32[]{:S(2)}, u32[]{:S(2)}) %collective-permute-start.6) | collective-permute-done | bytes 1179680 | tf_op jit(solution)/shard_map/total/ppermute | solution.py:414
  96.2 1.4 add_convert_fusion
  97.6 3.8 %all-to-all-start.2 = ((bf16[16,144,256]{2,1,0:T(8,128)(2,1)}), bf16[16,144,256]{2,1,0:T(8,128)(2,1)S(1)}, u32[]{:S(2)}, u32[]{:S(2)}) async-start(bf16[16,144,256]{2,1,0:T(8,128)(2,1)} %bitcast.20), calls=%async_computation.2 | async-start | bytes 2359296 | tf_op jit(solution)/shard_map/total/all_to_all | solution.py:525
  101.4 1.3 copy-done.10
  102.8 2.3 %input.1 = bf16[8,128,256]{2,1,0:T(8,128)(2,1)} custom-call(bf16[10,64,1024]{2,1,0:T(8,128)(2,1)S(1)} %copy-done.10, bf16[3,3,256,256]{3,2,1,0:T(8,128)(2,1)S(1)} %copy-done.9), custom_call_target="tpu_custom_call" | custom-call | flops 1207959552 | bytes 1048576 | tf_op jit(solution)/shard_map/input/pallas_call | solution.py:511
  105.0 14.8 %all-to-all-done.2 = bf16[16,144,256]{2,1,0:T(8,128)(2,1)S(1)} async-done(((bf16[16,144,256]{2,1,0:T(8,128)(2,1)}), bf16[16,144,256]{2,1,0:T(8,128)(2,1)S(1)}, u32[]{:S(2)}, u32[]{:S(2)}) %all-to-all-start.2) | async-done | bytes 1179680 | tf_op jit(solution)/shard_map/total/all_to_all | solution.py:525
  119.8 0.2 reduce_sum.21
  120.0 18.3 %all_to_all.25 = bf16[8,144,256]{2,1,0:T(8,128)(2,1)S(1)} all-to-all(bf16[8,144,256]{2,1,0:T(8,128)(2,1)S(1)} %broadcast_in_dim.4), channel_id=1, replica_groups=mesh['x'=4,'z'=8,'y_hi'=2,'y_lo'=2,'core'=2] {'z'}, dimensions={0} | all-to-all | bytes 1179648 | tf_op jit(solution)/shard_map/total/all_to_all | solution.py:528
  138.3 0.1 convert_reduce_fusion
  138.4 0.1 broadcast_in_dim.5
  138.5 19.3 %all_to_all.26 = bf16[16,144,256]{2,1,0:T(8,128)(2,1)S(1)} all-to-all(bf16[16,144,256]{2,1,0:T(8,128)(2,1)S(1)} %broadcast_in_dim.5), channel_id=1, replica_groups=mesh['x'=4,'z'=8,'y_hi'=2,'y_lo'=2,'core'=2] {'x','y_hi','y_lo'}, dimensions={0} | all-to-all | bytes 2359296 | tf_op jit(solution)/shard_map/total/all_to_all | solution.py:530
  157.8 4.4 %collective-permute-start.7 = (bf16[2304,256]{1,0:T(8,128)(2,1)S(1)}, bf16[2304,256]{1,0:T(8,128)(2,1)S(1)}, u32[]{:S(2)}, u32[]{:S(2)}) collective-permute-start(bf16[2304,256]{1,0:T(8,128)(2,1)S(1)} %bitcast.13), channel_id=1, source_target_pairs={{0,1},{1,0},{2,3},{3,2},{4,5},{5,4},{6,7},{7,6},{8,9},{9,8},{10,11... | collective-permute-start | bytes 3538952 | tf_op jit(solution)/shard_map/total/ppermute | solution.py:414
  162.2 0.6 fusion
  162.8 1.9 %collective-permute-done.7.other = bf16[2304,256]{1,0:T(8,128)(2,1)S(1)} collective-permute-done((bf16[2304,256]{1,0:T(8,128)(2,1)S(1)}, bf16[2304,256]{1,0:T(8,128)(2,1)S(1)}, u32[]{:S(2)}, u32[]{:S(2)}) %collective-permute-start.7) | collective-permute-done | bytes 1179680 | tf_op jit(solution)/shard_map/total/ppermute | solution.py:414
  164.7 2.8 %total.1 = (f32[2304,256]{1,0:T(8,128)}, f32[2304,256]{1,0:T(8,128)}) custom-call(s32[3]{0:T(128)S(1)} %add_convert_fusion.1.flags, bf16[2304,256]{1,0:T(8,128)(2,1)S(1)} %bitcast.14, bf16[2304,256]{1,0:T(8,128)(2,1)S(1)} %collective-permute-done.7.other), custom_call_target="tpu_custom_call" | custom-call | bytes 1048576 | tf_op jit(solution)/shard_map/total/pallas_call | solution.py:533
  (18 shorter events, 0.1 us)
Async XLA Ops:
  1.6 13.8 %collective-permute-start = (bf16[12,16,256]{2,1,0:T(8,128)(2,1)S(1)}, bf16[12,16,256]{2,1,0:T(8,128)(2,1)S(1)}, u32[]{:S(2)}, u32[]{:S(2)}) collective-permute-start(bf16[12,16,256]{2,1,0:T(8,128)(2,1)S(1)} %get-tuple-element.31), channel_id=1, source_target_pairs={{0,4},{4,8},{8,12},{12,16},{16,20},{20,24},{24,28},{28,32},{32,36}... | collective-permute-start | bytes 294920 | tf_op jit(solution)/shard_map/halo/ppermute | solution.py:392
  5.4 10.0 %collective-permute-start.1 = (bf16[12,16,256]{2,1,0:T(8,128)(2,1)S(1)}, bf16[12,16,256]{2,1,0:T(8,128)(2,1)S(1)}, u32[]{:S(2)}, u32[]{:S(2)}) collective-permute-start(bf16[12,16,256]{2,1,0:T(8,128)(2,1)S(1)} %get-tuple-element.32), channel_id=1, source_target_pairs={{0,252},{4,0},{8,4},{12,8},{16,12},{20,16},{24,20},{28,24},{32,28}... | collective-permute-start | bytes 294920 | tf_op jit(solution)/shard_map/halo/ppermute | solution.py:392
  16.4 6.2 %collective-permute-start.2 = (bf16[416,256]{1,0:T(8,128)(2,1)S(1)}, bf16[416,256]{1,0:T(8,128)(2,1)S(1)}, u32[]{:S(2)}, u32[]{:S(2)}) collective-permute-start(bf16[416,256]{1,0:T(8,128)(2,1)S(1)} %get-tuple-element.33), channel_id=1, source_target_pairs={{0,1},{1,2},{2,3},{4,5},{5,6},{6,7},{8,9},{9,10},{10,11},{12,13},{... | collective-permute-start | bytes 638984 | tf_op jit(solution)/shard_map/halo/ppermute | solution.py:392
  19.8 7.2 %collective-permute-start.3 = (bf16[416,256]{1,0:T(8,128)(2,1)S(1)}, bf16[416,256]{1,0:T(8,128)(2,1)S(1)}, u32[]{:S(2)}, u32[]{:S(2)}) collective-permute-start(bf16[416,256]{1,0:T(8,128)(2,1)S(1)} %get-tuple-element.34), channel_id=1, source_target_pairs={{1,0},{2,1},{3,2},{5,4},{6,5},{7,6},{9,8},{10,9},{11,10},{13,12},{... | collective-permute-start | bytes 638984 | tf_op jit(solution)/shard_map/halo/ppermute | solution.py:392
  27.0 4.7 %copy-start.5 = (bf16[416,256]{1,0:T(8,128)(2,1)}, bf16[416,256]{1,0:T(8,128)(2,1)S(1)}, u32[]{:S(2)}) copy-start(bf16[416,256]{1,0:T(8,128)(2,1)S(1)} %collective-permute-done.3.south) | copy-start | bytes 638980
  27.0 18.8 %copy-start = (bf16[3,3,256,256]{3,2,1,0:T(8,128)(2,1)S(1)}, bf16[3,3,256,256]{3,2,1,0:T(8,128)(2,1)}, u32[]{:S(2)}) copy-start(bf16[3,3,256,256]{3,2,1,0:T(8,128)(2,1)} %dw.1) | copy-start | bytes 3538948
  27.0 18.8 %copy-start.1 = (bf16[4,64,256]{2,1,0:T(8,128)(2,1)S(1)}, bf16[4,64,256]{2,1,0:T(8,128)(2,1)}, u32[]{:S(2)}) copy-start(bf16[4,64,256]{2,1,0:T(8,128)(2,1)} %cot.5) | copy-start | bytes 393220
  31.7 24.9 %copy-start.7 = (f32[256]{0:T(256)S(1)}, f32[256]{0:T(256)}, u32[]{:S(2)}) copy-start(f32[256]{0:T(256)} %param.10) | copy-start | bytes 3076
  31.7 24.8 %copy-start.8 = (f32[256]{0:T(256)S(1)}, f32[256]{0:T(256)}, u32[]{:S(2)}) copy-start(f32[256]{0:T(256)} %param.9) | copy-start | bytes 3076
  31.7 1.2 collective-permute-start.4
  33.7 22.9 %all-to-all-start = ((f32[128,2,128]{2,1,0:T(2,128)}), f32[128,2,128]{2,1,0:T(2,128)S(1)}, u32[]{:S(2)}, u32[]{:S(2)}) async-start(f32[128,2,128]{2,1,0:T(2,128)} %conv.3), calls=%async_computation | async-start | bytes 262144 | tf_op jit(solution)/shard_map/conv/all_to_all | solution.py:461
  45.9 0.9 copy-start.6
  47.5 0.8 copy-start.3
  60.4 3.1 %collective-permute-start.5 = (f32[4,128]{1,0:T(4,128)S(1)}, f32[4,128]{1,0:T(4,128)S(1)}, u32[]{:S(2)}, u32[]{:S(2)}) collective-permute-start(f32[4,128]{1,0:T(4,128)S(1)} %get-tuple-element.43.mine), channel_id=1, source_target_pairs={{0,1},{1,0},{2,3},{3,2},{4,5},{5,4},{6,7},{7,6},{8,9},{9,8},{10,11... | collective-permute-start | bytes 6152 | tf_op jit(solution)/shard_map/act/ppermute | solution.py:414
  64.3 20.2 %all-to-all-start.1 = ((f32[128,4,128]{2,1,0:T(4,128)}), f32[128,4,128]{2,1,0:T(4,128)}, u32[]{:S(2)}, u32[]{:S(2)}) async-start(f32[128,4,128]{2,1,0:T(4,128)} %act.3), calls=%async_computation.1 | async-start | bytes 524288 | tf_op jit(solution)/shard_map/act/all_to_all | solution.py:482
  71.8 1.2 copy-start.2
  73.0 1.0 copy-start.4
  91.4 4.8 %collective-permute-start.6 = (bf16[2304,256]{1,0:T(8,128)(2,1)S(1)}, bf16[2304,256]{1,0:T(8,128)(2,1)S(1)}, u32[]{:S(2)}, u32[]{:S(2)}) collective-permute-start(bf16[2304,256]{1,0:T(8,128)(2,1)S(1)} %select_convert_fusion), channel_id=1, source_target_pairs={{0,1},{1,0},{2,3},{3,2},{4,5},{5,4},{6,7},{7,6},{8,9},{9,8},{10,11... | collective-permute-start | bytes 3538952 | tf_op jit(solution)/shard_map/total/ppermute | solution.py:414
  97.6 3.8 %copy-start.9 = (bf16[3,3,256,256]{3,2,1,0:T(8,128)(2,1)S(1)}, bf16[3,3,256,256]{3,2,1,0:T(8,128)(2,1)}, u32[]{:S(2)}) copy-start(bf16[3,3,256,256]{3,2,1,0:T(8,128)(2,1)} %w.1) | copy-start | bytes 3538948
  97.6 22.2 %all-to-all-start.2 = ((bf16[16,144,256]{2,1,0:T(8,128)(2,1)}), bf16[16,144,256]{2,1,0:T(8,128)(2,1)S(1)}, u32[]{:S(2)}, u32[]{:S(2)}) async-start(bf16[16,144,256]{2,1,0:T(8,128)(2,1)} %bitcast.20), calls=%async_computation.2 | async-start | bytes 2359296 | tf_op jit(solution)/shard_map/total/all_to_all | solution.py:525
  101.4 1.3 copy-start.10
  157.8 6.9 %collective-permute-start.7 = (bf16[2304,256]{1,0:T(8,128)(2,1)S(1)}, bf16[2304,256]{1,0:T(8,128)(2,1)S(1)}, u32[]{:S(2)}, u32[]{:S(2)}) collective-permute-start(bf16[2304,256]{1,0:T(8,128)(2,1)S(1)} %bitcast.13), channel_id=1, source_target_pairs={{0,1},{1,0},{2,3},{3,2},{4,5},{5,4},{6,7},{7,6},{8,9},{9,8},{10,11... | collective-permute-start | bytes 3538952 | tf_op jit(solution)/shard_map/total/ppermute | solution.py:414

commit v3 on v2

--- a/solution.py
+++ b/solution.py
@@ -12,11 +12,12 @@
 EPS = 1e-05
 WIDTH = 8
 J = 80
-LON = ("x", "z", "y_hi")
+LON = ("x", "z_hi", "z_lo", "y_hi")
 LAT = ("y_lo", "core")
-PLANE = ("x", "y_hi", "y_lo")
+NEAR = ("x", "z_lo", "y_hi", "y_lo")
+FEW = ("x", "core")
+REST = ("z_hi", "z_lo", "y_hi", "y_lo")
 ALL = LON + LAT
-CHIPS = ("x", "z", "y_hi", "y_lo")
 BF = jnp.bfloat16
 F32 = jnp.float32
 
@@ -76,63 +77,79 @@
     return odd, even
 
 
-def pack_lon(feat, cot, east, west, sems):
-    rows, cols, _ = feat.shape
-    half, pairs, _ = cot.shape
-    copies = [
-        pltpu.make_async_copy(feat.at[:, cols - 16 : cols], east.at[0:rows], sems.at[0]),
-        pltpu.make_async_copy(cot.at[:, pairs - 16 : pairs], east.at[rows : rows + half], sems.at[1]),
-        pltpu.make_async_copy(feat.at[:, 0:16], west.at[0:rows], sems.at[2]),
-        pltpu.make_async_copy(cot.at[:, 0:16], west.at[rows : rows + half], sems.at[3]),
-    ]
+def pack_lon(feat_hbm, cot_hbm, east, west, feat, cot, f32s, sems):
+    rows, cols, chans = feat_hbm.shape
+    half, pairs, _ = cot_hbm.shape
+    copies = []
+    for k, (lo_f, lo_c) in enumerate(((cols - 16, pairs - 16), (0, 0))):
+        copies.append(pltpu.make_async_copy(feat_hbm.at[:, lo_f : lo_f + 16], feat.at[k], sems.at[2 * k]))
+        copies.append(pltpu.make_async_copy(cot_hbm.at[:, lo_c : lo_c + 16], cot.at[k], sems.at[2 * k + 1]))
     for copy in copies:
         copy.start()
+    f32s[...] = jnp.zeros(f32s.shape, F32)
     for copy in copies:
         copy.wait()
-
-
-def pack_lat(feat, cot, west, east, south, north, sems):
+    for k, (out, at_f, at_c) in enumerate(((east, 14, 15), (west, 0, 0))):
+        for r in range(rows):
+            f32s[2 * r : 2 * r + 2] = feat[k, r].astype(F32)[at_f : at_f + 2]
+        for i in range(half):
+            f32s[2 * rows + i : 2 * rows + i + 1] = cot[k, i].astype(F32)[at_c : at_c + 1]
+        out[...] = f32s[...].astype(BF)
+
+
+def pack_lat(feat, cot, west, east, south, north, w32, e32, corner, sems):
     rows, cols, _ = feat.shape
     half, pairs, _ = cot.shape
     copies = []
     ends = ((south, rows - 2, half - 1), (north, 0, 0))
     for dest, top, mid in ends:
-        parts = [(feat.at[top + k], k * (cols + 32) + 16, cols) for k in range(2)]
-        parts.append((cot.at[mid], 2 * (cols + 32) + 16, pairs))
+        parts = [(feat.at[top + k], k * cols, cols) for k in range(2)]
+        parts.append((cot.at[mid], 2 * cols, pairs))
         for src, o, n in parts:
             copies.append(pltpu.make_async_copy(src, dest.at[o : o + n], sems.at[len(copies)]))
             copies[-1].start()
+    w32[...] = west[...].astype(F32)
+    e32[...] = east[...].astype(F32)
+    corner[...] = jnp.zeros(corner.shape, F32)
+    o = 2 * cols + pairs
     for dest, top, mid in ends:
-        for row, o, n in (
-            (top, 0, cols),
-            (top + 1, cols + 32, cols),
-            (rows + mid, 2 * (cols + 32), pairs),
-        ):
-            dest[o : o + 16] = west[row]
-            dest[o + 16 + n : o + 32 + n] = east[row]
+        corner[0:4] = w32[2 * top : 2 * top + 4]
+        corner[4:8] = e32[2 * top : 2 * top + 4]
+        corner[8:9] = w32[2 * rows + mid : 2 * rows + mid + 1]
+        corner[9:10] = e32[2 * rows + mid : 2 * rows + mid + 1]
+        dest[o : o + 16] = corner[...].astype(BF)
     for copy in copies:
         copy.wait()
 
 
 def conv_kernel(
-    feat_hbm, west, east, north, south, w_hbm, x_hbm, h_hbm, hq_out, he_out, stat_out, f32s, x_out, feat, w, sems
+    feat_hbm, west, east, north, south, w_hbm, x_hbm, h_hbm, hq_out, he_out, stat_out, f32s, edge, x_out, feat, w, sems
 ):
     rows, cols, chans = feat.shape
     load_f = pltpu.make_async_copy(feat_hbm, feat, sems.at[1])
     load_f.start()
     load_w = pltpu.make_async_copy(w_hbm, w, sems.at[2])
     load_w.start()
-    wide = cols + 32
-    f32s[:, :, wide : wide + 16] = jnp.zeros((rows + 4, 2, 16, 128), F32)
+    f32s[:, :, 16 + cols : 56 + cols] = jnp.zeros((rows + 4, 2, 40, 128), F32)
+    pairs = cols // 2
+    for v in range(2):
+        part = slice(v * 128, v * 128 + 128)
+        for k, side in enumerate((west, east)):
+            edge[k, v] = side[:, part].astype(F32)
+        for k, side in enumerate((north, south)):
+            edge[2 + k, v, 0:16] = side[2 * cols + pairs : 2 * cols + pairs + 16, part].astype(F32)
+            for q in range(2):
+                row = q + k * (rows + 2)
+                f32s[row, v, 16 : 16 + cols] = side[q * cols : (q + 1) * cols, part].astype(F32)
+                f32s[row, v, 14:16] = edge[2 + k, v, 2 * q : 2 * q + 2]
+                f32s[row, v, 16 + cols : 18 + cols] = edge[2 + k, v, 4 + 2 * q : 6 + 2 * q]
+        for r in range(rows):
+            f32s[2 + r, v, 14:16] = edge[0, v, 2 * r : 2 * r + 2]
+            f32s[2 + r, v, 16 + cols : 18 + cols] = edge[1, v, 2 * r : 2 * r + 2]
     load_f.wait()
     for v in range(2):
         part = slice(v * 128, v * 128 + 128)
-        for k in range(2):
-            f32s[k, v, 0:wide] = north[k * wide : (k + 1) * wide, part].astype(F32)
-            f32s[rows + 2 + k, v, 0:wide] = south[k * wide : (k + 1) * wide, part].astype(F32)
-        f32s[2 : rows + 2, v, 0:16] = west[0:rows, :, part].astype(F32)
         f32s[2 : rows + 2, v, 16 : 16 + cols] = feat[:, :, part].astype(F32)
-        f32s[2 : rows + 2, v, 16 + cols : wide] = east[0:rows, :, part].astype(F32)
         for r in range(rows + 4):
             for k in range(4):
                 lane = k * chans + v * 128
@@ -168,35 +185,42 @@
             d = out[r].astype(F32) - mean
             part = part + d * d
         squares = squares + jnp.sum(part * mask, axis=0, keepdims=True)
-    stat_out[...] = jnp.concatenate([means, exact(squares, lanes)], axis=0)
+    stat = jnp.concatenate([means, exact(squares, lanes)], axis=0)
+    stat_out[...] = jnp.broadcast_to(stat[None], stat_out.shape)
     for copy in copies:
         copy.wait()
 
 
-def pair_stats(local_n, stat, other, out):
-    mine, theirs = stat[...], other[...]
-    gap = mine[0:1] - theirs[0:1]
-    mean = 0.5 * (mine[0:1] + theirs[0:1])
-    squares = mine[1:2] + theirs[1:2] + (0.5 * local_n) * gap * gap
+def merged_stats(local_n, rec, out):
+    means = rec[:, 0, :]
+    mean = jnp.sum(means, axis=0, keepdims=True) / rec.shape[0]
+    gap = means - mean
+    squares = jnp.sum(rec[:, 1, :] + local_n * gap * gap, axis=0, keepdims=True)
     both = jnp.concatenate([mean, squares], axis=0)
     out[...] = jnp.broadcast_to(both[None], out.shape)
 
 
-def pair_sums(mine, other, out):
-    both = mine[...] + other[...]
-    out[...] = jnp.broadcast_to(both[None], out.shape)
-
-
-def back_kernel(cot, west, east, north, south, dw, c_out, aq_out, ae_out, f32s):
+def merged_sums(rec, out):
+    out[...] = jnp.broadcast_to(jnp.sum(rec[...], axis=0)[None], out.shape)
+
+
+def back_kernel(cot, west, east, north, south, dw, c_out, aq_out, ae_out, f32s, edge):
     half, pairs, chans = cot.shape
-    rows = west.shape[0] - half
-    wide = pairs + 32
-    base = north.shape[0] - wide
-    f32s[0, 0:wide] = north[base : base + wide].astype(F32)
-    f32s[half + 1, 0:wide] = south[base : base + wide].astype(F32)
-    f32s[1 : half + 1, 0:16] = west[rows:].astype(F32)
+    rows = 2 * half
+    cols = 2 * pairs
+    f32s[:, 16 + pairs :] = jnp.zeros((half + 2, 16, chans), F32)
+    for k, side in enumerate((west, east)):
+        edge[k] = side[...].astype(F32)
+    for k, side in enumerate((north, south)):
+        row = k * (half + 1)
+        f32s[row, 16 : 16 + pairs] = side[2 * cols : 2 * cols + pairs].astype(F32)
+        edge[2 + k, 0:16] = side[2 * cols + pairs : 2 * cols + pairs + 16].astype(F32)
+        f32s[row, 15:16] = edge[2 + k, 8:9]
+        f32s[row, 16 + pairs : 17 + pairs] = edge[2 + k, 9:10]
     f32s[1 : half + 1, 16 : 16 + pairs] = cot[...].astype(F32)
-    f32s[1 : half + 1, 16 + pairs : wide] = east[rows:].astype(F32)
+    for i in range(half):
+        f32s[1 + i, 15:16] = edge[0, 2 * rows + i : 2 * rows + i + 1]
+        f32s[1 + i, 16 + pairs : 17 + pairs] = edge[1, 2 * rows + i : 2 * rows + i + 1]
     for s in range(half + 2):
         c_out[s, :, 0:chans] = f32s[s, 15 : 15 + J].astype(BF)
         c_out[s, :, chans : 2 * chans] = f32s[s, 16 : 16 + J].astype(BF)
@@ -222,19 +246,19 @@
 
 
 def act_kernel(cells, flags, stats, hq, he, aq, ae, gain, bias, t_hbm, p_hbm, coef_out, sum_out, f32s, t_out, p_out, sems):
-    chips = stats.shape[0]
+    parts = stats.shape[0]
     rows = hq.shape[0] - 2
     chans = hq.shape[2]
-    chip_n = float(cells // chips * WIDTH)
+    part_n = float(cells // parts * WIDTH)
     count = float(cells * WIDTH)
     rec = stats[...]
     total = jnp.sum(rec, axis=0)
-    centre = total[0:1] / chips
+    centre = total[0:1] / parts
     dev = rec[:, 0, :] - centre
     spread = jnp.sum(dev * dev, axis=0, keepdims=True)
     back = from_lanes(chans)
     mean = exact(centre, back)
-    var = exact((total[1:2] + chip_n * spread) / count, back)
+    var = exact((total[1:2] + part_n * spread) / count, back)
     inverse = lax.rsqrt(var + EPS)
     coef_out[0:1] = mean
     coef_out[1:2] = inverse
@@ -274,9 +298,10 @@
                     copies[-1].start()
         bias_sum = bias_sum + jnp.sum(acc_b * mask, axis=0, keepdims=True)
         gain_sum = gain_sum + jnp.sum(acc_g * mask, axis=0, keepdims=True)
-    sum_out[...] = jnp.concatenate(
+    payload = jnp.concatenate(
         [bias_sum[:, 0:128], bias_sum[:, 128:256], gain_sum[:, 0:128], gain_sum[:, 128:256]], axis=0
     )
+    sum_out[...] = jnp.broadcast_to(payload[None], sum_out.shape)
     for copy in copies:
         copy.wait()
 
@@ -383,7 +408,7 @@
             for v in range(2):
                 f32s[r, v, pl.ds(k, cols // 2, stride=2), :] = acc[r, :, v * 128 : v * 128 + 128]
     for v in range(2):
-        out[:, :, v * 128 : v * 128 + 128] = f32s[:, v].astype(BF)
+        out[:, :, v * 128 : v * 128 + 128] = f32s[:, v, 0:cols].astype(BF)
 
 
 def passed(value, axes, step, wrap):
@@ -428,18 +453,30 @@
     w3 = conv_weight.reshape(3, 3 * chans, chans)
     dw3 = down_weight.reshape(3, 3 * chans, chans)
     all_rows = 9 * chans
+    few = lax.axis_size(FEW)
+    rest = lax.axis_size(REST)
 
     with jax.named_scope("halo"):
-        slab = (rows + half, 16, chans)
-        to_east, to_west = call(pack_lon, [(slab, BF)] * 2, n_in=2, hbm=(0, 1), sems=4)(
-            pinned(features), pinned(cotangent)
-        )
+        slab = (2 * rows + 16, chans)
+        to_east, to_west = call(
+            pack_lon,
+            [(slab, BF)] * 2,
+            [((2, rows, 16, chans), BF), ((2, half, 16, chans), BF), (slab, F32)],
+            n_in=2,
+            hbm=(0, 1),
+            sems=4,
+        )(pinned(features), pinned(cotangent))
         west = passed(to_east, LON, 1, True)
         east = passed(to_west, LON, -1, True)
-        strip = (2 * (cols + 32) + pairs + 32, chans)
-        to_south, to_north = call(pack_lat, [(strip, BF)] * 2, n_in=4, hbm=(0, 1), sems=6)(
-            pinned(features), pinned(cotangent), west, east
-        )
+        strip = (2 * cols + pairs + 16, chans)
+        to_south, to_north = call(
+            pack_lat,
+            [(strip, BF)] * 2,
+            [(slab, F32), (slab, F32), ((16, chans), F32)],
+            n_in=4,
+            hbm=(0, 1),
+            sems=6,
+        )(pinned(features), pinned(cotangent), west, east)
         north = passed(to_south, LAT, 1, False)
         south = passed(to_north, LAT, -1, False)
 
@@ -448,22 +485,22 @@
     with jax.named_scope("conv"):
         x, h, hq, he, stat = call(
             conv_kernel,
-            [(x_shape, BF, True), ((2,) + plane, BF, True), (plane, BF), (plane, BF), ((2, 128), F32)],
-            [((rows + 4, 2, cols + 48, 128), F32), (x_shape, BF), ((rows, cols, chans), BF), (w3.shape, BF)],
+            [(x_shape, BF, True), ((2,) + plane, BF, True), (plane, BF), (plane, BF), ((few, 2, 128), F32)],
+            [((rows + 4, 2, cols + 56, 128), F32), ((4, 2) + (slab[0], 128), F32), (x_shape, BF), ((rows, cols, chans), BF), (w3.shape, BF)],
             flops=2 * 1600 * 2304 * 256,
             n_in=6,
             hbm=(0, 5),
             sems=5,
         )(pinned(features), west, east, north, south, pinned(w3))
-        chips = lax.axis_size(CHIPS)
         local_n = float(rows * cols * WIDTH)
-        (wide,) = call(functools.partial(pair_stats, local_n), [((chips, 2, 128), F32)], n_in=2)(stat, core_swap(stat))
-        stats = lax.all_to_all(wide, CHIPS, 0, 0, tiled=True)
+        stat = lax.all_to_all(stat, FEW, 0, 0, tiled=True)
+        (stat,) = call(functools.partial(merged_stats, local_n), [((rest, 2, 128), F32)], n_in=1)(stat)
+        stats = lax.all_to_all(stat, REST, 0, 0, tiled=True)
     with jax.named_scope("back"):
         c2, aq, ae = call(
             back_kernel,
             [((half + 2, J, 2 * chans), BF), (plane, BF), (plane, BF)],
-            [((half + 2, pairs + 32, chans), F32)],
+            [((half + 2, pairs + 32, chans), F32), ((4,) + slab, F32)],
             flops=2 * 400 * 2304 * 256,
             n_in=6,
         )(cotangent, west, east, north, south, down_weight)
@@ -471,15 +508,16 @@
     with jax.named_scope("act"):
         t, p, coef, sums = call(
             functools.partial(act_kernel, cells),
-            [(t_shape, BF, True), ((2,) + plane, F32, True), ((2, chans), F32), ((4, 128), F32)],
+            [(t_shape, BF, True), ((2,) + plane, F32, True), ((2, chans), F32), ((few, 4, 128), F32)],
             [((J, chans), F32), (t_shape, BF), ((2,) + plane, F32)],
             flops=1600 * 256 * 20,
             smem=(0,),
             n_in=8,
             sems=3 * rows + 5,
         )(flags, stats, hq, he, aq, ae, gain, bias)
-        (wide,) = call(pair_sums, [((chips, 4, 128), F32)], n_in=2)(sums, core_swap(sums))
-        sums = lax.all_to_all(wide, CHIPS, 0, 0, tiled=True)
+        sums = lax.all_to_all(sums, FEW, 0, 0, tiled=True)
+        (sums,) = call(merged_sums, [((rest, 4, 128), F32)], n_in=1)(sums)
+        sums = lax.all_to_all(sums, REST, 0, 0, tiled=True)
     with jax.named_scope("down"):
         output, down_part = call(
             down_kernel,
@@ -511,7 +549,7 @@
         (input_grad,) = call(
             input_kernel,
             [((rows, cols, chans), BF)],
-            [((rows, 2, cols, 128), F32)],
+            [((rows, 2, cols + 8, 128), F32)],
             flops=2 * 1024 * 2304 * 256,
             n_in=2,
         )(h4, conv_weight)
@@ -519,15 +557,15 @@
         first = lax.axis_index("core") == 0
         other = core_swap(jnp.where(first, down_part, conv_part).astype(BF))
         mine = (jnp.where(first, conv_part, down_part) + other.astype(F32)).astype(BF)
-        chips = lax.axis_size(PLANE)
-        depth = lax.axis_size("z")
+        chips = lax.axis_size(NEAR)
+        depth = lax.axis_size("z_hi")
         share = all_rows // chips
-        got = lax.all_to_all(mine.reshape(chips, share, chans), PLANE, 0, 0, tiled=True)
+        got = lax.all_to_all(mine.reshape(chips, share, chans), NEAR, 0, 0, tiled=True)
         got, input_grad = lax.optimization_barrier((got, input_grad))
         piece = jnp.sum(got.astype(F32), axis=0).astype(BF)
-        got = lax.all_to_all(jnp.broadcast_to(piece[None], (depth, share, chans)), "z", 0, 0, tiled=True)
+        got = lax.all_to_all(jnp.broadcast_to(piece[None], (depth, share, chans)), "z_hi", 0, 0, tiled=True)
         piece = (jnp.sum(got.astype(F32), axis=0) * factor).astype(BF)
-        whole = lax.all_to_all(jnp.broadcast_to(piece[None], (chips, share, chans)), PLANE, 0, 0, tiled=True)
+        whole = lax.all_to_all(jnp.broadcast_to(piece[None], (chips, share, chans)), NEAR, 0, 0, tiled=True)
         whole = whole.reshape(all_rows, chans)
         flat = ((all_rows, chans), F32, True)
         conv_grad, down_grad = call(
@@ -537,7 +575,7 @@
     return output, input_grad, conv_grad.reshape(shape), down_grad.reshape(shape), vec[0], vec[1]
 
 
-SIZES = {64: (4, 8, 2), 2: (1, 2, 1), 4: (2, 2, 1)}
+SIZES = {64: (4, 4, 2, 2), 2: (1, 1, 2, 1), 4: (2, 1, 2, 1), 8: (1, 2, 2, 2)}
 
 
 def solution(mesh):

time: 168 us -> 159 us (0.946)
  waiting for transfers between devices: 46.2 us -> 39.5 us
  starting transfers between devices: 49.3 us -> 45.9 us
    all_to_all x3 -> x4, waiting for transfers between devices: 32.2 us -> 29.3 us  [the longest x1 13.6 us: local(): lax.all_to_all(mine.reshape(chips, share, chans), NEAR, 0, 0, tiled=True)]
    ppermute x4 -> x2, starting transfers between devices: 9.12 us -> 6.58 us  [core_swap(): return lax.ppermute(value, 'core', [(0, 1), (1, 0)])]
    ppermute x4 -> x2, waiting for transfers between devices: 6.32 us -> 4.38 us  [core_swap(): return lax.ppermute(value, 'core', [(0, 1), (1, 0)])]
    ppermute x4, waiting for transfers between devices: 7.67 us -> 5.84 us  [passed(): return lax.ppermute(value, axes, pairs)]
    all_to_all x2 -> x3, blocking collectives: 37.6 us -> 39.2 us  [the longest x1 20.3 us: local(): lax.all_to_all(jnp.broadcast_to(piece[None], (chips, share, chans)), NEAR...]
    all_to_all x3 -> x4, starting transfers between devices: 23.4 us -> 22.3 us  [the longest x1 10.2 us: local(): stats = lax.all_to_all(stat, REST, 0, 0, tiled=True)]
    unnamed x22 -> x18, local copies, waits for them, and re-layouts: 5.23 us -> 4.3 us
  transfers between devices with their start and end apart: 11 -> 10, of which waited for: 10 -> 9; matrix products, arithmetic and copies ran while one was open for 0% -> 0% of each run, Pallas kernels for 3% -> 3%
where the time goes in v3:
time: 159 us; the launch traced here: 158 us
  starting transfers between devices  45.9 us (29%)
  waiting for transfers between devices  39.5 us (25%)
  blocking collectives  39.2 us (25%)
  Pallas kernels  25.7 us (16%)
  local copies, waits for them, and re-layouts  4.96 us (3%)
  other arithmetic  2.06 us (1%)
    all_to_all x1, blocking collectives, local(): lax.all_to_all(jnp.broadcast_to(piece[None], (chips, share, chans)), NEAR...  20.3 us
    ppermute x4, starting transfers between devices, passed(): return lax.ppermute(value, axes, pairs)  17.1 us
    all_to_all x1, waiting for transfers between devices, local(): lax.all_to_all(mine.reshape(chips, share, chans), NEAR, 0, 0, tiled=True)  13.6 us
    all_to_all x1, starting transfers between devices, local(): stats = lax.all_to_all(stat, REST, 0, 0, tiled=True)  10.2 us
    all_to_all x1, blocking collectives, local(): lax.all_to_all(jnp.broadcast_to(piece[None], (depth, share, chans)), 'z_h...  9.76 us
    all_to_all x1, blocking collectives, local(): sums = lax.all_to_all(sums, FEW, 0, 0, tiled=True)  9.14 us
    all_to_all x1, waiting for transfers between devices, local(): stats = lax.all_to_all(stat, REST, 0, 0, tiled=True)  7.1 us
    ppermute x2, starting transfers between devices, core_swap(): return lax.ppermute(value, 'core', [(0, 1), (1, 0)])  6.58 us
  transfers between devices with their start and end apart: 10, of which 9 were waited for; matrix products, arithmetic and copies ran while one was open for 0% of the time, Pallas kernels for 3%

profile of v3, /device:TPU:1, one launch (start us, length us, event | category | flops | bytes accessed | tf_op | source)
XLA Modules:
  0.0 158.4 jit_solution(3807521578317220602)
XLA Ops:
  0.6 1.0 halo.2
  1.6 3.8 %collective-permute-start = (bf16[32,256]{1,0:T(8,128)(2,1)S(1)}, bf16[32,256]{1,0:T(8,128)(2,1)S(1)}, u32[]{:S(2)}, u32[]{:S(2)}) collective-permute-start(bf16[32,256]{1,0:T(8,128)(2,1)S(1)} %get-tuple-element.31), channel_id=1, source_target_pairs={{0,4},{4,8},{8,12},{12,16},{16,20},{20,24},{24,28},{28,32},{32,36}... | collective-permute-start | bytes 49160 | tf_op jit(solution)/shard_map/halo/ppermute | solution.py:417
  5.4 7.6 %collective-permute-start.1 = (bf16[32,256]{1,0:T(8,128)(2,1)S(1)}, bf16[32,256]{1,0:T(8,128)(2,1)S(1)}, u32[]{:S(2)}, u32[]{:S(2)}) collective-permute-start(bf16[32,256]{1,0:T(8,128)(2,1)S(1)} %get-tuple-element.32), channel_id=1, source_target_pairs={{0,252},{4,0},{8,4},{12,8},{16,12},{20,16},{24,20},{28,24},{32,28}... | collective-permute-start | bytes 49160 | tf_op jit(solution)/shard_map/halo/ppermute | solution.py:417
  13.0 1.0 collective-permute-done.west
  14.0 0.0 collective-permute-done.1.east
  14.0 1.0 halo.3
  15.1 3.7 %collective-permute-start.2 = (bf16[336,256]{1,0:T(8,128)(2,1)S(1)}, bf16[336,256]{1,0:T(8,128)(2,1)S(1)}, u32[]{:S(2)}, u32[]{:S(2)}) collective-permute-start(bf16[336,256]{1,0:T(8,128)(2,1)S(1)} %get-tuple-element.33), channel_id=1, source_target_pairs={{0,1},{1,2},{2,3},{4,5},{5,6},{6,7},{8,9},{9,10},{10,11},{12,13},{... | collective-permute-start | bytes 516104 | tf_op jit(solution)/shard_map/halo/ppermute | solution.py:417
  18.8 1.9 %collective-permute-start.3 = (bf16[336,256]{1,0:T(8,128)(2,1)S(1)}, bf16[336,256]{1,0:T(8,128)(2,1)S(1)}, u32[]{:S(2)}, u32[]{:S(2)}) collective-permute-start(bf16[336,256]{1,0:T(8,128)(2,1)S(1)} %get-tuple-element.34), channel_id=1, source_target_pairs={{1,0},{2,1},{3,2},{5,4},{6,5},{7,6},{9,8},{10,9},{11,10},{13,12},{... | collective-permute-start | bytes 516104 | tf_op jit(solution)/shard_map/halo/ppermute | solution.py:417
  20.7 0.4 collective-permute-done.2.north
  21.1 4.4 %collective-permute-done.3.south = bf16[336,256]{1,0:T(8,128)(2,1)S(1)} collective-permute-done((bf16[336,256]{1,0:T(8,128)(2,1)S(1)}, bf16[336,256]{1,0:T(8,128)(2,1)S(1)}, u32[]{:S(2)}, u32[]{:S(2)}) %collective-permute-start.3) | collective-permute-done | bytes 172064 | tf_op jit(solution)/shard_map/halo/ppermute | solution.py:417
  25.5 5.2 %conv.2 = (bf16[12,80,1024]{2,1,0:T(8,128)(2,1)}, bf16[2,10,80,256]{3,2,1,0:T(8,128)(2,1)}, bf16[10,80,256]{2,1,0:T(8,128)(2,1)S(1)}, bf16[10,80,256]{2,1,0:T(8,128)(2,1)S(1)}, f32[8,2,128]{2,1,0:T(2,128)}) custom-call(bf16[8,128,256]{2,1,0:T(8,128)(2,1)} %feat_hbm.3, bf16[32,256]{1,0:T(8,128)(2,1)S(1)} %collective-permute-done.west, ...), custom_call_target="tpu_custom_call" | custom-call | flops 1887436800 | bytes 1048576 | tf_op jit(solution)/shard_map/conv/pallas_call | solution.py:486
  30.7 0.0 copy-start.5
  30.8 0.0 copy-start.6
  30.8 3.3 %all-to-all-start = ((f32[8,2,128]{2,1,0:T(2,128)}), f32[8,2,128]{2,1,0:T(2,128)S(1)}, u32[]{:S(2)}, u32[]{:S(2)}) async-start(f32[8,2,128]{2,1,0:T(2,128)} %get-tuple-element.35), calls=%async_computation | async-start | bytes 16384 | tf_op jit(solution)/shard_map/conv/all_to_all | solution.py:496
  34.1 3.5 %all-to-all-done.rec = f32[8,2,128]{2,1,0:T(2,128)S(1)} async-done(((f32[8,2,128]{2,1,0:T(2,128)}), f32[8,2,128]{2,1,0:T(2,128)S(1)}, u32[]{:S(2)}, u32[]{:S(2)}) %all-to-all-start) | async-done | bytes 8224 | tf_op jit(solution)/shard_map/conv/all_to_all | solution.py:496
  37.6 0.6 conv.3
  38.3 10.2 %all-to-all-start.1 = ((f32[32,2,128]{2,1,0:T(2,128)}), f32[32,2,128]{2,1,0:T(2,128)S(1)}, u32[]{:S(2)}, u32[]{:S(2)}) async-start(f32[32,2,128]{2,1,0:T(2,128)} %conv.3), calls=%async_computation.1 | async-start | bytes 65536 | tf_op jit(solution)/shard_map/conv/all_to_all | solution.py:498
  48.5 0.1 add_convert_fusion.1.flags
  48.5 0.7 back.1
  49.3 0.0 copy-start.3
  49.3 0.8 copy-done.3
  50.0 7.1 %all-to-all-done.1.stats = f32[32,2,128]{2,1,0:T(2,128)S(1)} async-done(((f32[32,2,128]{2,1,0:T(2,128)}), f32[32,2,128]{2,1,0:T(2,128)S(1)}, u32[]{:S(2)}, u32[]{:S(2)}) %all-to-all-start.1) | async-done | bytes 32800 | tf_op jit(solution)/shard_map/conv/all_to_all | solution.py:498
  57.2 0.0 copy-done.6
  57.2 3.8 %act.2 = (bf16[9,64,768]{2,1,0:T(8,128)(2,1)}, f32[2,10,80,256]{3,2,1,0:T(8,128)}, f32[2,256]{1,0:T(2,128)S(1)}, f32[8,4,128]{2,1,0:T(4,128)S(1)}) custom-call(s32[3]{0:T(128)S(1)} %add_convert_fusion.1.flags, f32[32,2,128]{2,1,0:T(2,128)S(1)} %all-to-all-done.1.stats, bf16[10,80,256]{2,1,0:T(8,128)(2,1)S(1)} %get-tuple-element.36.hq, ...), custom_call_target="tpu_custom_call" | custom-call | flops 8192000 | bytes 1048576 | tf_op jit(solution)/shard_map/act/pallas_call | solution.py:509
  60.9 9.1 %all_to_all.35.rec = f32[8,4,128]{2,1,0:T(4,128)S(1)} all-to-all(f32[8,4,128]{2,1,0:T(4,128)S(1)} %get-tuple-element.43), channel_id=1, replica_groups=mesh['x'=4,'z_hi'=4,'z_lo'=2,'y_hi'=2,'y_lo'=2,'core'=2] {'x','core'}, dimensions={0} | all-to-all | bytes 32768 | tf_op jit(solution)/shard_map/act/all_to_all | solution.py:518
  70.1 0.6 act.3
  70.7 4.7 %all-to-all-start.3 = ((f32[32,4,128]{2,1,0:T(4,128)}), f32[32,4,128]{2,1,0:T(4,128)}, u32[]{:S(2)}, u32[]{:S(2)}) async-start(f32[32,4,128]{2,1,0:T(4,128)} %act.3), calls=%async_computation.3 | async-start | bytes 131072 | tf_op jit(solution)/shard_map/act/all_to_all | solution.py:520
  75.5 1.2 copy-done.1
  76.6 1.0 copy-done.4
  77.6 1.4 down.1
  79.1 5.0 %all-to-all-done.3.sums = f32[32,4,128]{2,1,0:T(4,128)} async-done(((f32[32,4,128]{2,1,0:T(4,128)}), f32[32,4,128]{2,1,0:T(4,128)}, u32[]{:S(2)}, u32[]{:S(2)}) %all-to-all-start.3) | async-done | bytes 65568 | tf_op jit(solution)/shard_map/act/all_to_all | solution.py:520
  84.1 6.3 %grad.1 = (bf16[10,64,1024]{2,1,0:T(8,128)(2,1)}, f32[2304,256]{1,0:T(8,128)S(1)}, f32[2,256]{1,0:T(2,128)S(1)}) custom-call(s32[3]{0:T(128)S(1)} %add_convert_fusion.1.flags, f32[32,4,128]{2,1,0:T(4,128)} %all-to-all-done.3.sums, f32[2,256]{1,0:T(2,128)S(1)} %get-tuple-element.44.coef, f32[1,256]{1,0:T(1,128)S(1)} %bitcast.18, ...), custom_call_target="tpu_custom_call" | custom-call | flops 1887436800 | bytes 1048576 | tf_op jit(solution)/shard_map/grad/pallas_call | solution.py:530
  90.4 0.4 select_convert_fusion
  90.8 1.9 %collective-permute-start.4 = (bf16[2304,256]{1,0:T(8,128)(2,1)S(1)}, bf16[2304,256]{1,0:T(8,128)(2,1)S(1)}, u32[]{:S(2)}, u32[]{:S(2)}) collective-permute-start(bf16[2304,256]{1,0:T(8,128)(2,1)S(1)} %select_convert_fusion), channel_id=1, source_target_pairs={{0,1},{1,0},{2,3},{3,2},{4,5},{5,4},{6,7},{7,6},{8,9},{9,8},{10,11... | collective-permute-start | bytes 3538952 | tf_op jit(solution)/shard_map/total/ppermute | solution.py:439
  92.7 2.5 %collective-permute-done.4 = bf16[2304,256]{1,0:T(8,128)(2,1)S(1)} collective-permute-done((bf16[2304,256]{1,0:T(8,128)(2,1)S(1)}, bf16[2304,256]{1,0:T(8,128)(2,1)S(1)}, u32[]{:S(2)}, u32[]{:S(2)}) %collective-permute-start.4) | collective-permute-done | bytes 1179680 | tf_op jit(solution)/shard_map/total/ppermute | solution.py:439
  95.2 1.4 add_convert_fusion
  96.6 4.1 %all-to-all-start.4 = ((bf16[32,72,256]{2,1,0:T(8,128)(2,1)}), bf16[32,72,256]{2,1,0:T(8,128)(2,1)S(1)}, u32[]{:S(2)}, u32[]{:S(2)}) async-start(bf16[32,72,256]{2,1,0:T(8,128)(2,1)} %bitcast.20), calls=%async_computation.4 | async-start | bytes 2359296 | tf_op jit(solution)/shard_map/total/all_to_all | solution.py:563
  100.7 1.3 copy-done.8
  102.0 2.3 %input.1 = bf16[8,128,256]{2,1,0:T(8,128)(2,1)} custom-call(bf16[10,64,1024]{2,1,0:T(8,128)(2,1)S(1)} %copy-done.8, bf16[3,3,256,256]{3,2,1,0:T(8,128)(2,1)S(1)} %copy-done.7), custom_call_target="tpu_custom_call" | custom-call | flops 1207959552 | bytes 1048576 | tf_op jit(solution)/shard_map/input/pallas_call | solution.py:549
  104.3 13.6 %all-to-all-done.4 = bf16[32,72,256]{2,1,0:T(8,128)(2,1)S(1)} async-done(((bf16[32,72,256]{2,1,0:T(8,128)(2,1)}), bf16[32,72,256]{2,1,0:T(8,128)(2,1)S(1)}, u32[]{:S(2)}, u32[]{:S(2)}) %all-to-all-start.4) | async-done | bytes 1179680 | tf_op jit(solution)/shard_map/total/all_to_all | solution.py:563
  117.9 0.2 reduce_sum.21
  118.1 9.8 %all_to_all.36 = bf16[4,72,256]{2,1,0:T(8,128)(2,1)S(1)} all-to-all(bf16[4,72,256]{2,1,0:T(8,128)(2,1)S(1)} %broadcast_in_dim.4), channel_id=1, replica_groups=mesh['x'=4,'z_hi'=4,'z_lo'=2,'y_hi'=2,'y_lo'=2,'core'=2] {'z_hi'}, dimensions={0} | all-to-all | bytes 294912 | tf_op jit(solution)/shard_map/total/all_to_all | solution.py:566
  127.9 0.1 broadcast_in_dim.5
  127.9 20.3 %all_to_all.37 = bf16[32,72,256]{2,1,0:T(8,128)(2,1)S(1)} all-to-all(bf16[32,72,256]{2,1,0:T(8,128)(2,1)S(1)} %broadcast_in_dim.5), channel_id=1, replica_groups=mesh['x'=4,'z_hi'=4,'z_lo'=2,'y_hi'=2,'y_lo'=2,'core'=2] {'x','z_lo','y_..., dimensions={0} | all-to-all | bytes 2359296 | tf_op jit(solution)/shard_map/total/all_to_all | solution.py:568
  148.3 4.6 %collective-permute-start.5 = (bf16[2304,256]{1,0:T(8,128)(2,1)S(1)}, bf16[2304,256]{1,0:T(8,128)(2,1)S(1)}, u32[]{:S(2)}, u32[]{:S(2)}) collective-permute-start(bf16[2304,256]{1,0:T(8,128)(2,1)S(1)} %bitcast.13), channel_id=1, source_target_pairs={{0,1},{1,0},{2,3},{3,2},{4,5},{5,4},{6,7},{7,6},{8,9},{9,8},{10,11... | collective-permute-start | bytes 3538952 | tf_op jit(solution)/shard_map/total/ppermute | solution.py:439
  152.9 0.6 fusion
  153.5 1.9 %collective-permute-done.5.other = bf16[2304,256]{1,0:T(8,128)(2,1)S(1)} collective-permute-done((bf16[2304,256]{1,0:T(8,128)(2,1)S(1)}, bf16[2304,256]{1,0:T(8,128)(2,1)S(1)}, u32[]{:S(2)}, u32[]{:S(2)}) %collective-permute-start.5) | collective-permute-done | bytes 1179680 | tf_op jit(solution)/shard_map/total/ppermute | solution.py:439
  155.4 2.8 %total.1 = (f32[2304,256]{1,0:T(8,128)}, f32[2304,256]{1,0:T(8,128)}) custom-call(s32[3]{0:T(128)S(1)} %add_convert_fusion.1.flags, bf16[2304,256]{1,0:T(8,128)(2,1)S(1)} %bitcast.14, bf16[2304,256]{1,0:T(8,128)(2,1)S(1)} %collective-permute-done.5.other), custom_call_target="tpu_custom_call" | custom-call | bytes 1048576 | tf_op jit(solution)/shard_map/total/pallas_call | solution.py:571
  (13 shorter events, 0.1 us)
Async XLA Ops:
  1.6 12.4 %collective-permute-start = (bf16[32,256]{1,0:T(8,128)(2,1)S(1)}, bf16[32,256]{1,0:T(8,128)(2,1)S(1)}, u32[]{:S(2)}, u32[]{:S(2)}) collective-permute-start(bf16[32,256]{1,0:T(8,128)(2,1)S(1)} %get-tuple-element.31), channel_id=1, source_target_pairs={{0,4},{4,8},{8,12},{12,16},{16,20},{20,24},{24,28},{28,32},{32,36}... | collective-permute-start | bytes 49160 | tf_op jit(solution)/shard_map/halo/ppermute | solution.py:417
  5.4 8.6 %collective-permute-start.1 = (bf16[32,256]{1,0:T(8,128)(2,1)S(1)}, bf16[32,256]{1,0:T(8,128)(2,1)S(1)}, u32[]{:S(2)}, u32[]{:S(2)}) collective-permute-start(bf16[32,256]{1,0:T(8,128)(2,1)S(1)} %get-tuple-element.32), channel_id=1, source_target_pairs={{0,252},{4,0},{8,4},{12,8},{16,12},{20,16},{24,20},{28,24},{32,28}... | collective-permute-start | bytes 49160 | tf_op jit(solution)/shard_map/halo/ppermute | solution.py:417
  15.1 6.1 %collective-permute-start.2 = (bf16[336,256]{1,0:T(8,128)(2,1)S(1)}, bf16[336,256]{1,0:T(8,128)(2,1)S(1)}, u32[]{:S(2)}, u32[]{:S(2)}) collective-permute-start(bf16[336,256]{1,0:T(8,128)(2,1)S(1)} %get-tuple-element.33), channel_id=1, source_target_pairs={{0,1},{1,2},{2,3},{4,5},{5,6},{6,7},{8,9},{9,10},{10,11},{12,13},{... | collective-permute-start | bytes 516104 | tf_op jit(solution)/shard_map/halo/ppermute | solution.py:417
  18.8 6.7 %collective-permute-start.3 = (bf16[336,256]{1,0:T(8,128)(2,1)S(1)}, bf16[336,256]{1,0:T(8,128)(2,1)S(1)}, u32[]{:S(2)}, u32[]{:S(2)}) collective-permute-start(bf16[336,256]{1,0:T(8,128)(2,1)S(1)} %get-tuple-element.34), channel_id=1, source_target_pairs={{1,0},{2,1},{3,2},{5,4},{6,5},{7,6},{9,8},{10,9},{11,10},{13,12},{... | collective-permute-start | bytes 516104 | tf_op jit(solution)/shard_map/halo/ppermute | solution.py:417
  25.5 23.0 %copy-start = (bf16[3,3,256,256]{3,2,1,0:T(8,128)(2,1)S(1)}, bf16[3,3,256,256]{3,2,1,0:T(8,128)(2,1)}, u32[]{:S(2)}) copy-start(bf16[3,3,256,256]{3,2,1,0:T(8,128)(2,1)} %dw.1) | copy-start | bytes 3538948
  25.5 23.0 %copy-start.2 = (bf16[4,64,256]{2,1,0:T(8,128)(2,1)S(1)}, bf16[4,64,256]{2,1,0:T(8,128)(2,1)}, u32[]{:S(2)}) copy-start(bf16[4,64,256]{2,1,0:T(8,128)(2,1)} %cot.3) | copy-start | bytes 393220
  30.7 26.4 %copy-start.5 = (f32[256]{0:T(256)S(1)}, f32[256]{0:T(256)}, u32[]{:S(2)}) copy-start(f32[256]{0:T(256)} %param.10) | copy-start | bytes 3076
  30.8 26.4 %copy-start.6 = (f32[256]{0:T(256)S(1)}, f32[256]{0:T(256)}, u32[]{:S(2)}) copy-start(f32[256]{0:T(256)} %param.9) | copy-start | bytes 3076
  30.8 6.8 %all-to-all-start = ((f32[8,2,128]{2,1,0:T(2,128)}), f32[8,2,128]{2,1,0:T(2,128)S(1)}, u32[]{:S(2)}, u32[]{:S(2)}) async-start(f32[8,2,128]{2,1,0:T(2,128)} %get-tuple-element.35), calls=%async_computation | async-start | bytes 16384 | tf_op jit(solution)/shard_map/conv/all_to_all | solution.py:496
  38.3 18.9 %all-to-all-start.1 = ((f32[32,2,128]{2,1,0:T(2,128)}), f32[32,2,128]{2,1,0:T(2,128)S(1)}, u32[]{:S(2)}, u32[]{:S(2)}) async-start(f32[32,2,128]{2,1,0:T(2,128)} %conv.3), calls=%async_computation.1 | async-start | bytes 65536 | tf_op jit(solution)/shard_map/conv/all_to_all | solution.py:498
  49.3 0.8 copy-start.3
  70.7 13.4 %all-to-all-start.3 = ((f32[32,4,128]{2,1,0:T(4,128)}), f32[32,4,128]{2,1,0:T(4,128)}, u32[]{:S(2)}, u32[]{:S(2)}) async-start(f32[32,4,128]{2,1,0:T(4,128)} %act.3), calls=%async_computation.3 | async-start | bytes 131072 | tf_op jit(solution)/shard_map/act/all_to_all | solution.py:520
  75.4 1.2 copy-start.1
  76.6 1.0 copy-start.4
  90.8 4.4 %collective-permute-start.4 = (bf16[2304,256]{1,0:T(8,128)(2,1)S(1)}, bf16[2304,256]{1,0:T(8,128)(2,1)S(1)}, u32[]{:S(2)}, u32[]{:S(2)}) collective-permute-start(bf16[2304,256]{1,0:T(8,128)(2,1)S(1)} %select_convert_fusion), channel_id=1, source_target_pairs={{0,1},{1,0},{2,3},{3,2},{4,5},{5,4},{6,7},{7,6},{8,9},{9,8},{10,11... | collective-permute-start | bytes 3538952 | tf_op jit(solution)/shard_map/total/ppermute | solution.py:439
  96.6 4.1 %copy-start.7 = (bf16[3,3,256,256]{3,2,1,0:T(8,128)(2,1)S(1)}, bf16[3,3,256,256]{3,2,1,0:T(8,128)(2,1)}, u32[]{:S(2)}) copy-start(bf16[3,3,256,256]{3,2,1,0:T(8,128)(2,1)} %w.1) | copy-start | bytes 3538948
  96.6 21.3 %all-to-all-start.4 = ((bf16[32,72,256]{2,1,0:T(8,128)(2,1)}), bf16[32,72,256]{2,1,0:T(8,128)(2,1)S(1)}, u32[]{:S(2)}, u32[]{:S(2)}) async-start(bf16[32,72,256]{2,1,0:T(8,128)(2,1)} %bitcast.20), calls=%async_computation.4 | async-start | bytes 2359296 | tf_op jit(solution)/shard_map/total/all_to_all | solution.py:563
  100.7 1.3 copy-start.8
  148.3 7.1 %collective-permute-start.5 = (bf16[2304,256]{1,0:T(8,128)(2,1)S(1)}, bf16[2304,256]{1,0:T(8,128)(2,1)S(1)}, u32[]{:S(2)}, u32[]{:S(2)}) collective-permute-start(bf16[2304,256]{1,0:T(8,128)(2,1)S(1)} %bitcast.13), channel_id=1, source_target_pairs={{0,1},{1,0},{2,3},{3,2},{4,5},{5,4},{6,7},{7,6},{8,9},{9,8},{10,11... | collective-permute-start | bytes 3538952 | tf_op jit(solution)/shard_map/total/ppermute | solution.py:439

commit v4 on v3

--- a/solution.py
+++ b/solution.py
@@ -22,7 +22,7 @@
 F32 = jnp.float32
 
 
-def call(body, outs, scratch=(), flops=0, smem=(), hbm=(), n_in=0, sems=0):
+def call(body, outs, scratch=(), flops=0, smem=(), hbm=(), n_in=0, sems=0, aliases=None):
     spaces = [pltpu.SMEM if i in smem else pltpu.HBM if i in hbm else pltpu.VMEM for i in range(n_in)]
     out_spaces = [pltpu.HBM if len(o) > 2 else pltpu.VMEM for o in outs]
     return pl.pallas_call(
@@ -32,6 +32,7 @@
         out_specs=[pl.BlockSpec(memory_space=m) for m in out_spaces],
         scratch_shapes=[pltpu.VMEM(s, d) for s, d in scratch]
         + ([pltpu.SemaphoreType.DMA((sems,))] if sems else []),
+        input_output_aliases=aliases or {},
         compiler_params=pltpu.CompilerParams(vmem_limit_bytes=24 * 1024 * 1024),
         cost_estimate=pl.CostEstimate(flops=flops, bytes_accessed=1 << 20, transcendentals=0),
     )
@@ -97,12 +98,13 @@
         out[...] = f32s[...].astype(BF)
 
 
-def pack_lat(feat, cot, west, east, south, north, w32, e32, corner, sems):
+def pack_lat(flags, feat, cot, west, east, near, far, w32, e32, corner, sems):
     rows, cols, _ = feat.shape
     half, pairs, _ = cot.shape
+    core = flags[2]
     copies = []
-    ends = ((south, rows - 2, half - 1), (north, 0, 0))
-    for dest, top, mid in ends:
+    for dest, last in ((near, 1 - core), (far, core)):
+        top, mid = last * (rows - 2), last * (half - 1)
         parts = [(feat.at[top + k], k * cols, cols) for k in range(2)]
         parts.append((cot.at[mid], 2 * cols, pairs))
         for src, o, n in parts:
@@ -111,19 +113,32 @@
     w32[...] = west[...].astype(F32)
     e32[...] = east[...].astype(F32)
     corner[...] = jnp.zeros(corner.shape, F32)
+    for k, (top, mid) in enumerate(((rows - 2, half - 1), (0, 0))):
+        corner[k, 0:4] = w32[2 * top : 2 * top + 4]
+        corner[k, 4:8] = e32[2 * top : 2 * top + 4]
+        corner[k, 8:9] = w32[2 * rows + mid : 2 * rows + mid + 1]
+        corner[k, 9:10] = e32[2 * rows + mid : 2 * rows + mid + 1]
     o = 2 * cols + pairs
-    for dest, top, mid in ends:
-        corner[0:4] = w32[2 * top : 2 * top + 4]
-        corner[4:8] = e32[2 * top : 2 * top + 4]
-        corner[8:9] = w32[2 * rows + mid : 2 * rows + mid + 1]
-        corner[9:10] = e32[2 * rows + mid : 2 * rows + mid + 1]
-        dest[o : o + 16] = corner[...].astype(BF)
+    near[o : o + 16] = corner[core].astype(BF)
+    far[o : o + 16] = corner[1 - core].astype(BF)
     for copy in copies:
         copy.wait()
 
 
+def sides(flags, near, far):
+    low = flags[2] == 0
+
+    def north(lo, hi, part):
+        return jnp.where(low, far[lo:hi, part].astype(F32), near[lo:hi, part].astype(F32))
+
+    def south(lo, hi, part):
+        return jnp.where(low, near[lo:hi, part].astype(F32), far[lo:hi, part].astype(F32))
+
+    return north, south
+
+
 def conv_kernel(
-    feat_hbm, west, east, north, south, w_hbm, x_hbm, h_hbm, hq_out, he_out, stat_out, f32s, edge, x_out, feat, w, sems
+    flags, feat_hbm, west, east, near, far, w_hbm, x_hbm, h_hbm, hq_out, he_out, stat_out, f32s, edge, x_out, feat, w, sems
 ):
     rows, cols, chans = feat.shape
     load_f = pltpu.make_async_copy(feat_hbm, feat, sems.at[1])
@@ -136,11 +151,11 @@
         part = slice(v * 128, v * 128 + 128)
         for k, side in enumerate((west, east)):
             edge[k, v] = side[:, part].astype(F32)
-        for k, side in enumerate((north, south)):
-            edge[2 + k, v, 0:16] = side[2 * cols + pairs : 2 * cols + pairs + 16, part].astype(F32)
+        for k, side in enumerate(sides(flags, near, far)):
+            edge[2 + k, v, 0:16] = side(2 * cols + pairs, 2 * cols + pairs + 16, part)
             for q in range(2):
                 row = q + k * (rows + 2)
-                f32s[row, v, 16 : 16 + cols] = side[q * cols : (q + 1) * cols, part].astype(F32)
+                f32s[row, v, 16 : 16 + cols] = side(q * cols, (q + 1) * cols, part)
                 f32s[row, v, 14:16] = edge[2 + k, v, 2 * q : 2 * q + 2]
                 f32s[row, v, 16 + cols : 18 + cols] = edge[2 + k, v, 4 + 2 * q : 6 + 2 * q]
         for r in range(rows):
@@ -151,10 +166,11 @@
         part = slice(v * 128, v * 128 + 128)
         f32s[2 : rows + 2, v, 16 : 16 + cols] = feat[:, :, part].astype(F32)
         for r in range(rows + 4):
-            for k in range(4):
+            for k in range(5):
                 lane = k * chans + v * 128
                 x_out[r, :, lane : lane + 128] = f32s[r, v, pl.ds(14 + k, J, stride=2), :].astype(BF)
-    keep = pltpu.make_async_copy(x_out, x_hbm, sems.at[0])
+    kept = x_out.at[1 : rows + 3, 0:pairs, chans : 5 * chans]
+    keep = pltpu.make_async_copy(kept, x_hbm, sems.at[0])
     keep.start()
     load_w.wait()
     copies = [keep]
@@ -204,17 +220,18 @@
     out[...] = jnp.broadcast_to(jnp.sum(rec[...], axis=0)[None], out.shape)
 
 
-def back_kernel(cot, west, east, north, south, dw, c_out, aq_out, ae_out, f32s, edge):
+def back_kernel(flags, cot, west, east, near, far, dw, c_hbm, aq_out, ae_out, f32s, edge, c_out, sems):
     half, pairs, chans = cot.shape
     rows = 2 * half
     cols = 2 * pairs
     f32s[:, 16 + pairs :] = jnp.zeros((half + 2, 16, chans), F32)
     for k, side in enumerate((west, east)):
         edge[k] = side[...].astype(F32)
-    for k, side in enumerate((north, south)):
+    every = slice(None)
+    for k, side in enumerate(sides(flags, near, far)):
         row = k * (half + 1)
-        f32s[row, 16 : 16 + pairs] = side[2 * cols : 2 * cols + pairs].astype(F32)
-        edge[2 + k, 0:16] = side[2 * cols + pairs : 2 * cols + pairs + 16].astype(F32)
+        f32s[row, 16 : 16 + pairs] = side(2 * cols, 2 * cols + pairs, every)
+        edge[2 + k, 0:16] = side(2 * cols + pairs, 2 * cols + pairs + 16, every)
         f32s[row, 15:16] = edge[2 + k, 8:9]
         f32s[row, 16 + pairs : 17 + pairs] = edge[2 + k, 9:10]
     f32s[1 : half + 1, 16 : 16 + pairs] = cot[...].astype(F32)
@@ -224,6 +241,8 @@
     for s in range(half + 2):
         c_out[s, :, 0:chans] = f32s[s, 15 : 15 + J].astype(BF)
         c_out[s, :, chans : 2 * chans] = f32s[s, 16 : 16 + J].astype(BF)
+    keep = pltpu.make_async_copy(c_out, c_hbm, sems.at[0])
+    keep.start()
     n = half + 1
     lo_l = c_out[0:n, :, 0:chans].reshape(n * J, chans)
     lo_r = c_out[0:n, :, chans:].reshape(n * J, chans)
@@ -243,6 +262,7 @@
         0,
         dot_t(hi_r, dw[0, 0]) + dot_t(hi_l, dw[0, 2]) + dot_t(lo_r, dw[2, 0]) + dot_t(lo_l, dw[2, 2]),
     )
+    keep.wait()
 
 
 def act_kernel(cells, flags, stats, hq, he, aq, ae, gain, bias, t_hbm, p_hbm, coef_out, sum_out, f32s, t_out, p_out, sems):
@@ -276,7 +296,7 @@
         for r in range(rows + 2):
             normed = (h[r].astype(F32) - mean) * inverse
             shifted = g * normed + b
-            sigma = jax.nn.sigmoid(shifted)
+            sigma = 0.5 + 0.5 * jnp.tanh(0.5 * shifted)
             pre = a[r].astype(F32) * sigma * (1.0 + shifted * (1.0 - sigma))
             p_out[k, r] = pre
             copies.append(pltpu.make_async_copy(p_out.at[k, r], p_hbm.at[k, r], sems.at[len(copies)]))
@@ -306,9 +326,21 @@
         copy.wait()
 
 
-def down_kernel(t, c, dw, out, grad):
+def halves(flags, full, keep, send):
+    n = keep.shape[0]
+    core = flags[2]
+    keep[...] = full[pl.ds(pl.multiple_of(core * n, n), n)]
+    send[...] = full[pl.ds(pl.multiple_of((1 - core) * n, n), n)].astype(BF)
+
+
+def down_kernel(flags, t_hbm, c_hbm, dw, out, keep, send, t, c, grad, sems):
     half = out.shape[0]
     pairs, chans = out.shape[1:]
+    loads = [pltpu.make_async_copy(t_hbm, t, sems.at[0]), pltpu.make_async_copy(c_hbm, c, sems.at[1])]
+    for load in loads:
+        load.start()
+    for load in loads:
+        load.wait()
     cot = c[1 : half + 1, 0:pairs, chans:].reshape(half * pairs, chans)
     acc = None
     for a in range(3):
@@ -317,10 +349,11 @@
         acc = term if acc is None else acc + term
         grad[a * 3 * chans : (a + 1) * 3 * chans] = t_dot(lhs, cot)
     out[...] = acc.astype(BF).reshape(out.shape)
+    halves(flags, grad, keep, send)
 
 
 def grad_kernel(
-    cells, flags, sums, coef, gain, h_hbm, p_hbm, x_hbm, h4_hbm, conv_out, vec_out, f32s, rq, re, h_in, p_in, x, h4_out, sems
+    cells, flags, sums, coef, gain, h_hbm, p_hbm, x_hbm, h4_hbm, keep, send, vec_out, f32s, conv_out, h_in, p_in, x, h4_out, sems
 ):
     rows = p_in.shape[1] - 2
     chans = p_in.shape[3]
@@ -350,16 +383,9 @@
     inverse = coef[1:2]
     top = jnp.where(flags[0] == 1, 0.0, 1.0)
     bottom = jnp.where(flags[1] == 1, 0.0, 1.0)
-    odd, even = masks()
-    zero = jnp.zeros((J, chans), BF)
-    for k, (r_out, mask) in enumerate(((rq, odd), (re, even))):
+    for k in range(2):
         is_q = k == 0
         loads[k * (rows + 3)].wait()
-        for f in (0, 1):
-            for a in (1, 2):
-                if f - a + 1 <= 0:
-                    r_out[f, :, a * chans : (a + 1) * chans] = zero
-                    r_out[rows + 1 - f, :, (2 - a) * chans : (3 - a) * chans] = zero
         for r in range(rows + 2):
             loads[k * (rows + 3) + 1 + r].wait()
             normed = (h_in[k, r].astype(F32) - mean) * inverse
@@ -369,10 +395,6 @@
             if r == rows + 1:
                 value = value * bottom
             rounded = value.astype(BF)
-            if 1 <= r <= rows:
-                inner = (value * mask).astype(BF)
-                for a in range(3):
-                    r_out[r + a - 1, :, a * chans : (a + 1) * chans] = inner
             f32s[...] = rounded.astype(F32)
             moved = f32s[1:65].astype(BF)
             lo = 3 if is_q else 2
@@ -382,13 +404,16 @@
             if not is_q:
                 copies.append(pltpu.make_async_copy(h4_out.at[r], h4_hbm.at[r], sems.at[first_out + r]))
                 copies[-1].start()
-    m = (rows + 2) * J
     load_x.wait()
-    lhs = x[1 : rows + 3].reshape(m, 4 * chans)
-    part = t_dot(lhs[:, 0 : 3 * chans], rq[...].reshape(m, 3 * chans))
-    part = part + t_dot(lhs[:, chans : 4 * chans], re[...].reshape(m, 3 * chans))
+    pairs = h4_out.shape[1]
+    cells_here = rows * pairs
+    odd = h4_out[1 : rows + 1, :, chans : 2 * chans].reshape(cells_here, chans)
+    even = h4_out[1 : rows + 1, :, 2 * chans : 3 * chans].reshape(cells_here, chans)
     for a in range(3):
-        conv_out[a * 3 * chans : (a + 1) * 3 * chans] = part[:, a * chans : (a + 1) * chans]
+        lhs = x[a : a + rows].reshape(cells_here, 4 * chans)
+        part = t_dot(lhs[:, 0 : 3 * chans], even) + t_dot(lhs[:, chans : 4 * chans], odd)
+        conv_out[a * 3 * chans : (a + 1) * 3 * chans] = part
+    halves(flags, conv_out, keep, send)
     for copy in copies:
         copy.wait()
 
@@ -417,22 +442,43 @@
     return lax.ppermute(value, axes, pairs)
 
 
-def unpack_kernel(flags, whole, other, conv, down, f32s, sems):
-    n = whole.shape[0]
-    step = n // 4
-    for core, one, two in ((0, whole, other), (1, other, whole)):
-
-        @pl.when(flags[2] == core)
-        def _():
-            copies = []
-            for k, (src, dst) in enumerate(((one, conv), (two, down))):
-                for q in range(4):
-                    part = slice(q * step, (q + 1) * step)
-                    f32s[k, part] = src[part].astype(F32)
-                    copies.append(pltpu.make_async_copy(f32s.at[k, part], dst.at[part], sems.at[k * 4 + q]))
-                    copies[-1].start()
-            for copy in copies:
-                copy.wait()
+def join_kernel(conv_keep, conv_other, down_keep, down_other, out, both, sems):
+    n = conv_keep.shape[0]
+    step = n // 2
+    copies = []
+    for k, (keep, other) in enumerate(((down_keep, down_other), (conv_keep, conv_other))):
+        for q in range(2):
+            part = slice(q * step, (q + 1) * step)
+            o = (1 - k) * n + q * step
+            both[o : o + step] = (keep[part] + other[part].astype(F32)).astype(BF)
+            copies.append(pltpu.make_async_copy(both.at[o : o + step], out.at[o : o + step], sems.at[2 * k + q]))
+            copies[-1].start()
+    for copy in copies:
+        copy.wait()
+
+
+def unpack_rows(core, rows, conv, down, f32s, sems):
+    n = rows.shape[0] // 2
+    step = n // 2
+    base = pl.multiple_of(core * n, n)
+    copies = []
+    for k, dst in enumerate((conv, down)):
+        for q in range(2):
+            o = k * n + q * step
+            f32s[o : o + step] = rows[o : o + step].astype(F32)
+            part = dst.at[pl.ds(base + q * step, step)]
+            copies.append(pltpu.make_async_copy(f32s.at[o : o + step], part, sems.at[k * 2 + q]))
+            copies[-1].start()
+    for copy in copies:
+        copy.wait()
+
+
+def unpack_own(flags, rows, conv, down, f32s, sems):
+    unpack_rows(flags[2], rows, conv, down, f32s, sems)
+
+
+def unpack_other(flags, rows, conv_in, down_in, conv, down, f32s, sems):
+    unpack_rows(1 - flags[2], rows, conv, down, f32s, sems)
 
 
 def core_swap(value):
@@ -469,41 +515,48 @@
         west = passed(to_east, LON, 1, True)
         east = passed(to_west, LON, -1, True)
         strip = (2 * cols + pairs + 16, chans)
-        to_south, to_north = call(
+        to_near, to_far = call(
             pack_lat,
             [(strip, BF)] * 2,
-            [(slab, F32), (slab, F32), ((16, chans), F32)],
-            n_in=4,
-            hbm=(0, 1),
+            [(slab, F32), (slab, F32), ((2, 16, chans), F32)],
+            n_in=5,
+            smem=(0,),
+            hbm=(1, 2),
             sems=6,
-        )(pinned(features), pinned(cotangent), west, east)
-        north = passed(to_south, LAT, 1, False)
-        south = passed(to_north, LAT, -1, False)
+        )(flags, pinned(features), pinned(cotangent), west, east)
+        near = lax.ppermute(to_near, LAT, [(i, i ^ 1) for i in range(lats)])
+        gaps = range(1, lats - 1, 2)
+        far = lax.ppermute(to_far, LAT, [(i, i + 1) for i in gaps] + [(i + 1, i) for i in gaps])
 
     plane = (rows + 2, J, chans)
-    x_shape = (rows + 4, J, 4 * chans)
+    x_shape = (rows + 2, pairs, 4 * chans)
+    x_full = (rows + 4, J, 5 * chans)
     with jax.named_scope("conv"):
         x, h, hq, he, stat = call(
             conv_kernel,
             [(x_shape, BF, True), ((2,) + plane, BF, True), (plane, BF), (plane, BF), ((few, 2, 128), F32)],
-            [((rows + 4, 2, cols + 56, 128), F32), ((4, 2) + (slab[0], 128), F32), (x_shape, BF), ((rows, cols, chans), BF), (w3.shape, BF)],
+            [((rows + 4, 2, cols + 56, 128), F32), ((4, 2) + (slab[0], 128), F32), (x_full, BF), ((rows, cols, chans), BF), (w3.shape, BF)],
             flops=2 * 1600 * 2304 * 256,
-            n_in=6,
-            hbm=(0, 5),
+            n_in=7,
+            smem=(0,),
+            hbm=(1, 6),
             sems=5,
-        )(pinned(features), west, east, north, south, pinned(w3))
+        )(flags, pinned(features), west, east, near, far, pinned(w3))
         local_n = float(rows * cols * WIDTH)
         stat = lax.all_to_all(stat, FEW, 0, 0, tiled=True)
         (stat,) = call(functools.partial(merged_stats, local_n), [((rest, 2, 128), F32)], n_in=1)(stat)
         stats = lax.all_to_all(stat, REST, 0, 0, tiled=True)
+    c_shape = (half + 2, J, 2 * chans)
     with jax.named_scope("back"):
         c2, aq, ae = call(
             back_kernel,
-            [((half + 2, J, 2 * chans), BF), (plane, BF), (plane, BF)],
-            [((half + 2, pairs + 32, chans), F32), ((4,) + slab, F32)],
+            [(c_shape, BF, True), (plane, BF), (plane, BF)],
+            [((half + 2, pairs + 32, chans), F32), ((4,) + slab, F32), (c_shape, BF)],
             flops=2 * 400 * 2304 * 256,
-            n_in=6,
-        )(cotangent, west, east, north, south, down_weight)
+            n_in=7,
+            smem=(0,),
+            sems=1,
+        )(flags, cotangent, west, east, near, far, down_weight)
     t_shape = (rows + 1, pairs, 3 * chans)
     with jax.named_scope("act"):
         t, p, coef, sums = call(
@@ -517,23 +570,29 @@
         )(flags, stats, hq, he, aq, ae, gain, bias)
         sums = lax.all_to_all(sums, FEW, 0, 0, tiled=True)
         (sums,) = call(merged_sums, [((rest, 4, 128), F32)], n_in=1)(sums)
+        sums, c2 = lax.optimization_barrier((sums, c2))
         sums = lax.all_to_all(sums, REST, 0, 0, tiled=True)
+    half_rows = (all_rows // 2, chans)
     with jax.named_scope("down"):
-        output, down_part = call(
+        output, down_keep, down_send = call(
             down_kernel,
-            [((half, pairs, chans), BF), ((all_rows, chans), F32)],
+            [((half, pairs, chans), BF), (half_rows, F32), (half_rows, BF)],
+            [(t_shape, BF), (c_shape, BF), ((all_rows, chans), F32)],
             flops=4 * 256 * 2304 * 256,
-            n_in=3,
-        )(t, c2, dw3)
+            smem=(0,),
+            hbm=(1, 2),
+            n_in=4,
+            sems=2,
+        )(flags, pinned(t), pinned(c2), dw3)
+        down_other = core_swap(down_send)
     h4_shape = (rows + 2, pairs, 4 * chans)
     with jax.named_scope("grad"):
-        h4, conv_part, vec = call(
+        h4, conv_keep, conv_send, vec = call(
             functools.partial(grad_kernel, cells),
-            [(h4_shape, BF, True), ((all_rows, chans), F32), ((2, chans), F32)],
+            [(h4_shape, BF, True), (half_rows, F32), (half_rows, BF), ((2, chans), F32)],
             [
                 ((J, chans), F32),
-                ((rows + 2, J, 3 * chans), BF),
-                ((rows + 2, J, 3 * chans), BF),
+                ((all_rows, chans), F32),
                 ((2,) + plane, BF),
                 ((2,) + plane, F32),
                 (x_shape, BF),
@@ -554,9 +613,10 @@
             n_in=2,
         )(h4, conv_weight)
     with jax.named_scope("total"):
-        first = lax.axis_index("core") == 0
-        other = core_swap(jnp.where(first, down_part, conv_part).astype(BF))
-        mine = (jnp.where(first, conv_part, down_part) + other.astype(F32)).astype(BF)
+        whole_rows = (all_rows, chans)
+        (mine,) = call(
+            join_kernel, [(whole_rows, BF, True)], [(whole_rows, BF)], n_in=4, sems=4
+        )(conv_keep, core_swap(conv_send), down_keep, down_other)
         chips = lax.axis_size(NEAR)
         depth = lax.axis_size("z_hi")
         share = all_rows // chips
@@ -567,10 +627,13 @@
         piece = (jnp.sum(got.astype(F32), axis=0) * factor).astype(BF)
         whole = lax.all_to_all(jnp.broadcast_to(piece[None], (chips, share, chans)), NEAR, 0, 0, tiled=True)
         whole = whole.reshape(all_rows, chans)
-        flat = ((all_rows, chans), F32, True)
+        other = core_swap(whole)
+        flat = (whole_rows, F32, True)
+        room = [(whole_rows, F32)]
+        conv_grad, down_grad = call(unpack_own, [flat, flat], room, smem=(0,), n_in=2, sems=4)(flags, whole)
         conv_grad, down_grad = call(
-            unpack_kernel, [flat, flat], [((2, all_rows, chans), F32)], smem=(0,), n_in=3, sems=8
-        )(flags, whole, core_swap(whole))
+            unpack_other, [flat, flat], room, smem=(0,), hbm=(2, 3), n_in=4, sems=4, aliases={2: 0, 3: 1}
+        )(flags, other, pinned(conv_grad), pinned(down_grad))
     shape = (3, 3, chans, chans)
     return output, input_grad, conv_grad.reshape(shape), down_grad.reshape(shape), vec[0], vec[1]
 

time: 159 us -> 152 us (0.956)
  waiting for transfers between devices: 39.5 us -> 31.8 us
  blocking collectives: 39.2 us -> 45.8 us
  starting transfers between devices: 45.9 us -> 40 us
  Pallas kernels: 25.7 us -> 30.1 us
  local copies, waits for them, and re-layouts: 4.96 us -> 2 us
  other arithmetic: 2.06 us -> 0.28 us
    all_to_all x0 -> x1, blocking collectives: none -> 6.63 us  [local(): stat = lax.all_to_all(stat, FEW, 0, 0, tiled=True)]
    ppermute x4 -> x2, starting transfers between devices: 17.1 us -> 11.4 us  [passed(): return lax.ppermute(value, axes, pairs)]
    ppermute x4 -> x2, waiting for transfers between devices: 5.84 us -> 0.97 us  [passed(): return lax.ppermute(value, axes, pairs)]
    ppermute x0 -> x2, waiting for transfers between devices: none -> 4.49 us  [the longest x1 4.49 us: local(): lax.ppermute(to_far, LAT, [(i, i + 1) for i in gaps] + [(i + 1, i) for i...]
    pallas_call x5 -> x7, Pallas kernels: 12.3 us -> 16.7 us  [the longest x1 4.61 us: local(): call(functools.partial(grad_kernel, cells), [(h4_shape, BF, True), (half_...]
    ppermute x0 -> x2, starting transfers between devices: none -> 3.84 us  [the longest x1 2.2 us: local(): lax.ppermute(to_far, LAT, [(i, i + 1) for i in gaps] + [(i + 1, i) for i...]
    all_to_all x1 -> x0, waiting for transfers between devices: 3.52 us -> none  [local(): stat = lax.all_to_all(stat, FEW, 0, 0, tiled=True)]
    all_to_all x1 -> x0, starting transfers between devices: 3.3 us -> none  [local(): stat = lax.all_to_all(stat, FEW, 0, 0, tiled=True)]
  transfers between devices with their start and end apart: 10 -> 10, of which waited for: 9 -> 6; matrix products, arithmetic and copies ran while one was open for 0% -> 0% of each run, Pallas kernels for 3% -> 9%
where the time goes in v4:
time: 152 us; the launch traced here: 151 us
  blocking collectives  45.8 us (30%)
  starting transfers between devices  40 us (26%)
  waiting for transfers between devices  31.8 us (21%)
  Pallas kernels  30.1 us (20%)
  local copies, waits for them, and re-layouts  2 us (1%)
    all_to_all x1, blocking collectives, local(): lax.all_to_all(jnp.broadcast_to(piece[None], (chips, share, chans)), NEAR...  20.3 us
    all_to_all x1, waiting for transfers between devices, local(): lax.all_to_all(mine.reshape(chips, share, chans), NEAR, 0, 0, tiled=True)  13.6 us
    ppermute x2, starting transfers between devices, passed(): return lax.ppermute(value, axes, pairs)  11.4 us
    all_to_all x1, blocking collectives, local(): lax.all_to_all(jnp.broadcast_to(piece[None], (depth, share, chans)), 'z_h...  9.76 us
    all_to_all x1, starting transfers between devices, local(): stats = lax.all_to_all(stat, REST, 0, 0, tiled=True)  9.31 us
    all_to_all x1, blocking collectives, local(): sums = lax.all_to_all(sums, FEW, 0, 0, tiled=True)  9.14 us
    ppermute x3, starting transfers between devices, core_swap(): return lax.ppermute(value, 'core', [(0, 1), (1, 0)])  7.55 us
    all_to_all x1, waiting for transfers between devices, local(): stats = lax.all_to_all(stat, REST, 0, 0, tiled=True)  6.84 us
  transfers between devices with their start and end apart: 10, of which 6 were waited for; matrix products, arithmetic and copies ran while one was open for 0% of the time, Pallas kernels for 9%

profile of v4, /device:TPU:1, one launch (start us, length us, event | category | flops | bytes accessed | tf_op | source)
XLA Modules:
  0.0 151.0 jit_solution(9234523374545203157)
XLA Ops:
  0.6 1.0 halo.2
  1.6 3.8 %collective-permute-start = (bf16[32,256]{1,0:T(8,128)(2,1)S(1)}, bf16[32,256]{1,0:T(8,128)(2,1)S(1)}, u32[]{:S(2)}, u32[]{:S(2)}) collective-permute-start(bf16[32,256]{1,0:T(8,128)(2,1)S(1)} %get-tuple-element.37), channel_id=1, source_target_pairs={{0,4},{4,8},{8,12},{12,16},{16,20},{20,24},{24,28},{28,32},{32,36}... | collective-permute-start | bytes 49160 | tf_op jit(solution)/shard_map/halo/ppermute | solution.py:442
  5.4 7.6 %collective-permute-start.1 = (bf16[32,256]{1,0:T(8,128)(2,1)S(1)}, bf16[32,256]{1,0:T(8,128)(2,1)S(1)}, u32[]{:S(2)}, u32[]{:S(2)}) collective-permute-start(bf16[32,256]{1,0:T(8,128)(2,1)S(1)} %get-tuple-element.38), channel_id=1, source_target_pairs={{0,252},{4,0},{8,4},{12,8},{16,12},{20,16},{24,20},{28,24},{32,28}... | collective-permute-start | bytes 49160 | tf_op jit(solution)/shard_map/halo/ppermute | solution.py:442
  13.0 0.1 add_convert_fusion.flags
  13.1 1.0 collective-permute-done.west
  14.0 0.0 collective-permute-done.1.east
  14.0 1.6 %halo.3 = (bf16[336,256]{1,0:T(8,128)(2,1)S(1)}, bf16[336,256]{1,0:T(8,128)(2,1)S(1)}) custom-call(s32[3]{0:T(128)S(1)} %add_convert_fusion.flags, bf16[8,128,256]{2,1,0:T(8,128)(2,1)} %feat_hbm.3, bf16[4,64,256]{2,1,0:T(8,128)(2,1)} %cot.3, bf16[32,256]{1,0:T(8,128)(2,1)S(1)} %collective-permute-done.west, bf16[32,256]{1,0:T(8,128)(2,1)S(1)} %collective-permute-done.1.east), custom_call_target="tpu_custom_call" | custom-call | bytes 1048576 | tf_op jit(solution)/shard_map/halo/pallas_call | solution.py:518
  15.6 1.6 %collective-permute-start.2 = (bf16[336,256]{1,0:T(8,128)(2,1)S(1)}, bf16[336,256]{1,0:T(8,128)(2,1)S(1)}, u32[]{:S(2)}, u32[]{:S(2)}) collective-permute-start(bf16[336,256]{1,0:T(8,128)(2,1)S(1)} %get-tuple-element.39), channel_id=1, source_target_pairs={{0,1},{1,0},{2,3},{3,2},{4,5},{5,4},{6,7},{7,6},{8,9},{9,8},{10,11... | collective-permute-start | bytes 516104 | tf_op jit(solution)/shard_map/halo/ppermute | solution.py:527
  17.2 2.2 %collective-permute-start.3 = (bf16[336,256]{1,0:T(8,128)(2,1)S(1)}, bf16[336,256]{1,0:T(8,128)(2,1)S(1)}, u32[]{:S(2)}, u32[]{:S(2)}) collective-permute-start(bf16[336,256]{1,0:T(8,128)(2,1)S(1)} %get-tuple-element.40), channel_id=1, source_target_pairs={{1,2},{2,1},{5,6},{6,5},{9,10},{10,9},{13,14},{14,13},{17,18},{18,... | collective-permute-start | bytes 516104 | tf_op jit(solution)/shard_map/halo/ppermute | solution.py:529
  19.4 0.0 collective-permute-done.2.near
  19.5 4.5 %collective-permute-done.3.far = bf16[336,256]{1,0:T(8,128)(2,1)S(1)} collective-permute-done((bf16[336,256]{1,0:T(8,128)(2,1)S(1)}, bf16[336,256]{1,0:T(8,128)(2,1)S(1)}, u32[]{:S(2)}, u32[]{:S(2)}) %collective-permute-start.3) | collective-permute-done | bytes 172064 | tf_op jit(solution)/shard_map/halo/ppermute | solution.py:529
  24.0 5.0 %conv.2 = (bf16[10,64,1024]{2,1,0:T(8,128)(2,1)}, bf16[2,10,80,256]{3,2,1,0:T(8,128)(2,1)}, bf16[10,80,256]{2,1,0:T(8,128)(2,1)S(1)}, bf16[10,80,256]{2,1,0:T(8,128)(2,1)S(1)}, f32[8,2,128]{2,1,0:T(2,128)S(1)}) custom-call(s32[3]{0:T(128)S(1)} %add_convert_fusion.flags, bf16[8,128,256]{2,1,0:T(8,128)(2,1)} %feat_hbm.3, ...), custom_call_target="tpu_custom_call" | custom-call | flops 1887436800 | bytes 1048576 | tf_op jit(solution)/shard_map/conv/pallas_call | solution.py:535
  29.0 0.0 copy-start.2
  29.0 0.0 copy-start.3
  29.0 6.6 %all_to_all.35.rec = f32[8,2,128]{2,1,0:T(2,128)S(1)} all-to-all(f32[8,2,128]{2,1,0:T(2,128)S(1)} %get-tuple-element.41), channel_id=1, replica_groups=mesh['x'=4,'z_hi'=4,'z_lo'=2,'y_hi'=2,'y_lo'=2,'core'=2] {'x','core'}, dimensions={0} | all-to-all | bytes 16384 | tf_op jit(solution)/shard_map/conv/all_to_all | solution.py:546
  35.7 0.6 conv.3
  36.3 9.3 %all-to-all-start.1 = ((f32[32,2,128]{2,1,0:T(2,128)}), f32[32,2,128]{2,1,0:T(2,128)S(1)}, u32[]{:S(2)}, u32[]{:S(2)}) async-start(f32[32,2,128]{2,1,0:T(2,128)} %conv.3), calls=%async_computation.1 | async-start | bytes 65536 | tf_op jit(solution)/shard_map/conv/all_to_all | solution.py:548
  45.6 0.0 copy-done
  45.6 0.0 copy-done.1
  45.6 1.8 %back.1 = (bf16[6,80,512]{2,1,0:T(8,128)(2,1)}, bf16[10,80,256]{2,1,0:T(8,128)(2,1)S(1)}, bf16[10,80,256]{2,1,0:T(8,128)(2,1)S(1)}) custom-call(s32[3]{0:T(128)S(1)} %add_convert_fusion.flags, bf16[4,64,256]{2,1,0:T(8,128)(2,1)S(1)} %copy-done.1, bf16[32,256]{1,0:T(8,128)(2,1)S(1)} %collective-permute-done.west, ...), custom_call_target="tpu_custom_call" | custom-call | flops 471859200 | bytes 1048576 | tf_op jit(solution)/shard_map/back/pallas_call | solution.py:551
  47.5 6.8 %all-to-all-done.1.stats = f32[32,2,128]{2,1,0:T(2,128)S(1)} async-done(((f32[32,2,128]{2,1,0:T(2,128)}), f32[32,2,128]{2,1,0:T(2,128)S(1)}, u32[]{:S(2)}, u32[]{:S(2)}) %all-to-all-start.1) | async-done | bytes 32800 | tf_op jit(solution)/shard_map/conv/all_to_all | solution.py:548
  54.3 0.0 copy-done.2
  54.3 3.8 %act.2 = (bf16[9,64,768]{2,1,0:T(8,128)(2,1)}, f32[2,10,80,256]{3,2,1,0:T(8,128)}, f32[2,256]{1,0:T(2,128)S(1)}, f32[8,4,128]{2,1,0:T(4,128)S(1)}) custom-call(s32[3]{0:T(128)S(1)} %add_convert_fusion.flags, f32[32,2,128]{2,1,0:T(2,128)S(1)} %all-to-all-done.1.stats, bf16[10,80,256]{2,1,0:T(8,128)(2,1)S(1)} %get-tuple-element.42.hq, ...), custom_call_target="tpu_custom_call" | custom-call | flops 8192000 | bytes 1048576 | tf_op jit(solution)/shard_map/act/pallas_call | solution.py:562
  58.1 9.1 %all_to_all.36.rec = f32[8,4,128]{2,1,0:T(4,128)S(1)} all-to-all(f32[8,4,128]{2,1,0:T(4,128)S(1)} %get-tuple-element.47), channel_id=1, replica_groups=mesh['x'=4,'z_hi'=4,'z_lo'=2,'y_hi'=2,'y_lo'=2,'core'=2] {'x','core'}, dimensions={0} | all-to-all | bytes 32768 | tf_op jit(solution)/shard_map/act/all_to_all | solution.py:571
  67.2 0.6 act.3
  67.9 3.8 %all-to-all-start.3 = ((f32[32,4,128]{2,1,0:T(4,128)}), f32[32,4,128]{2,1,0:T(4,128)S(1)}, u32[]{:S(2)}, u32[]{:S(2)}) async-start(f32[32,4,128]{2,1,0:T(4,128)} %act.3), calls=%async_computation.3 | async-start | bytes 131072 | tf_op jit(solution)/shard_map/act/all_to_all | solution.py:574
  71.7 3.6 %down.1 = (bf16[4,64,256]{2,1,0:T(8,128)(2,1)}, f32[1152,256]{1,0:T(8,128)S(1)}, bf16[1152,256]{1,0:T(8,128)(2,1)}) custom-call(s32[3]{0:T(128)S(1)} %add_convert_fusion.flags, bf16[9,64,768]{2,1,0:T(8,128)(2,1)} %get-tuple-element.46.t_hbm, bf16[6,80,512]{2,1,0:T(8,128)(2,1)} %get-tuple-element.49.c_hbm, bf16[3,768,256]{2,1,0:T(8,128)(2,1)S(1)} %bitcast.15), custom_call_target="tpu_custom_call" | custom-call | flops 603979776 | bytes 1048576 | tf_op jit(solution)/shard_map/down/pallas_call | solution.py:577
  75.3 1.0 collective-permute-start.5
  76.3 4.3 %all-to-all-done.3.sums = f32[32,4,128]{2,1,0:T(4,128)S(1)} async-done(((f32[32,4,128]{2,1,0:T(4,128)}), f32[32,4,128]{2,1,0:T(4,128)S(1)}, u32[]{:S(2)}, u32[]{:S(2)}) %all-to-all-start.3) | async-done | bytes 65568 | tf_op jit(solution)/shard_map/act/all_to_all | solution.py:574
  80.6 4.6 %grad.1 = (bf16[10,64,1024]{2,1,0:T(8,128)(2,1)}, f32[1152,256]{1,0:T(8,128)S(1)}, bf16[1152,256]{1,0:T(8,128)(2,1)S(1)}, f32[2,256]{1,0:T(2,128)S(1)}) custom-call(s32[3]{0:T(128)S(1)} %add_convert_fusion.flags, f32[32,4,128]{2,1,0:T(4,128)S(1)} %all-to-all-done.3.sums, f32[2,256]{1,0:T(2,128)S(1)} %get-tuple-element.52.coef, f32[1,256]{1,0:T(1,128)S(1)} %bitcast.18, ...), custom_call_target="tpu_custom_call" | custom-call | flops 1887436800 | bytes 1048576 | tf_op jit(solution)/shard_map/grad/pallas_call | solution.py:590
  85.2 1.9 %collective-permute-start.4 = (bf16[1152,256]{1,0:T(8,128)(2,1)S(1)}, bf16[1152,256]{1,0:T(8,128)(2,1)S(1)}, u32[]{:S(2)}, u32[]{:S(2)}) collective-permute-start(bf16[1152,256]{1,0:T(8,128)(2,1)S(1)} %get-tuple-element.57), channel_id=1, source_target_pairs={{0,1},{1,0},{2,3},{3,2},{4,5},{5,4},{6,7},{7,6},{8,9},{9,8},{10,11... | collective-permute-start | bytes 1769480 | tf_op jit(solution)/shard_map/total/ppermute | solution.py:485
  87.2 0.0 collective-permute-done.5.down_other
  87.2 1.6 %collective-permute-done.4.conv_other = bf16[1152,256]{1,0:T(8,128)(2,1)S(1)} collective-permute-done((bf16[1152,256]{1,0:T(8,128)(2,1)S(1)}, bf16[1152,256]{1,0:T(8,128)(2,1)S(1)}, u32[]{:S(2)}, u32[]{:S(2)}) %collective-permute-start.4) | collective-permute-done | bytes 589856 | tf_op jit(solution)/shard_map/total/ppermute | solution.py:485
  88.8 1.1 total.3
  89.9 0.0 copy-start.4
  89.9 4.1 %all-to-all-start.4 = ((bf16[32,72,256]{2,1,0:T(8,128)(2,1)}), bf16[32,72,256]{2,1,0:T(8,128)(2,1)S(1)}, u32[]{:S(2)}, u32[]{:S(2)}) async-start(bf16[32,72,256]{2,1,0:T(8,128)(2,1)} %bitcast.20), calls=%async_computation.4 | async-start | bytes 2359296 | tf_op jit(solution)/shard_map/total/all_to_all | solution.py:623
  94.0 1.3 copy-done.5
  95.3 2.3 %input.1 = bf16[8,128,256]{2,1,0:T(8,128)(2,1)} custom-call(bf16[10,64,1024]{2,1,0:T(8,128)(2,1)S(1)} %copy-done.5, bf16[3,3,256,256]{3,2,1,0:T(8,128)(2,1)S(1)} %copy-done.4), custom_call_target="tpu_custom_call" | custom-call | flops 1207959552 | bytes 1048576 | tf_op jit(solution)/shard_map/input/pallas_call | solution.py:608
  97.6 13.6 %all-to-all-done.4 = bf16[32,72,256]{2,1,0:T(8,128)(2,1)S(1)} async-done(((bf16[32,72,256]{2,1,0:T(8,128)(2,1)}), bf16[32,72,256]{2,1,0:T(8,128)(2,1)S(1)}, u32[]{:S(2)}, u32[]{:S(2)}) %all-to-all-start.4) | async-done | bytes 1179680 | tf_op jit(solution)/shard_map/total/all_to_all | solution.py:623
  111.2 0.2 reduce_sum.21
  111.4 9.8 %all_to_all.37 = bf16[4,72,256]{2,1,0:T(8,128)(2,1)S(1)} all-to-all(bf16[4,72,256]{2,1,0:T(8,128)(2,1)S(1)} %broadcast_in_dim.4), channel_id=1, replica_groups=mesh['x'=4,'z_hi'=4,'z_lo'=2,'y_hi'=2,'y_lo'=2,'core'=2] {'z_hi'}, dimensions={0} | all-to-all | bytes 294912 | tf_op jit(solution)/shard_map/total/all_to_all | solution.py:626
  121.2 0.1 broadcast_in_dim.5
  121.3 20.3 %all_to_all.38 = bf16[32,72,256]{2,1,0:T(8,128)(2,1)S(1)} all-to-all(bf16[32,72,256]{2,1,0:T(8,128)(2,1)S(1)} %broadcast_in_dim.5), channel_id=1, replica_groups=mesh['x'=4,'z_hi'=4,'z_lo'=2,'y_hi'=2,'y_lo'=2,'core'=2] {'x','z_lo','y_..., dimensions={0} | all-to-all | bytes 2359296 | tf_op jit(solution)/shard_map/total/all_to_all | solution.py:628
  141.6 4.6 %collective-permute-start.6 = (bf16[2304,256]{1,0:T(8,128)(2,1)S(1)}, bf16[2304,256]{1,0:T(8,128)(2,1)S(1)}, u32[]{:S(2)}, u32[]{:S(2)}) collective-permute-start(bf16[2304,256]{1,0:T(8,128)(2,1)S(1)} %bitcast.13), channel_id=1, source_target_pairs={{0,1},{1,0},{2,3},{3,2},{4,5},{5,4},{6,7},{7,6},{8,9},{9,8},{10,11... | collective-permute-start | bytes 3538952 | tf_op jit(solution)/shard_map/total/ppermute | solution.py:485
  146.2 0.6 fusion
  146.8 2.0 %total.4 = (f32[2304,256]{1,0:T(8,128)}, f32[2304,256]{1,0:T(8,128)}) custom-call(s32[3]{0:T(128)S(1)} %add_convert_fusion.flags, bf16[2304,256]{1,0:T(8,128)(2,1)S(1)} %bitcast.14), custom_call_target="tpu_custom_call" | custom-call | bytes 1048576 | tf_op jit(solution)/shard_map/total/pallas_call | solution.py:633
  148.8 0.0 collective-permute-done.6.rows
  148.8 2.0 %total.5 = (f32[2304,256]{1,0:T(8,128)}, f32[2304,256]{1,0:T(8,128)}) custom-call(s32[3]{0:T(128)S(1)} %add_convert_fusion.flags, bf16[2304,256]{1,0:T(8,128)(2,1)S(1)} %collective-permute-done.6.rows, f32[2304,256]{1,0:T(8,128)} %get-tuple-element.63.conv_in, f32[2304,256]{1,0:T(8,128)} %get-tuple-element.64.down_in), custom_call_target="tpu_custom_call", output_to_operand_aliasing={{0}: (2, {}), {1}: (3, {})} | custom-call | bytes 1048576 | tf_op jit(solution)/shard_map/total/pallas_call | solution.py:634
  (8 shorter events, 0.1 us)
Async XLA Ops:
  1.6 12.4 %collective-permute-start = (bf16[32,256]{1,0:T(8,128)(2,1)S(1)}, bf16[32,256]{1,0:T(8,128)(2,1)S(1)}, u32[]{:S(2)}, u32[]{:S(2)}) collective-permute-start(bf16[32,256]{1,0:T(8,128)(2,1)S(1)} %get-tuple-element.37), channel_id=1, source_target_pairs={{0,4},{4,8},{8,12},{12,16},{16,20},{20,24},{24,28},{28,32},{32,36}... | collective-permute-start | bytes 49160 | tf_op jit(solution)/shard_map/halo/ppermute | solution.py:442
  5.4 8.6 %collective-permute-start.1 = (bf16[32,256]{1,0:T(8,128)(2,1)S(1)}, bf16[32,256]{1,0:T(8,128)(2,1)S(1)}, u32[]{:S(2)}, u32[]{:S(2)}) collective-permute-start(bf16[32,256]{1,0:T(8,128)(2,1)S(1)} %get-tuple-element.38), channel_id=1, source_target_pairs={{0,252},{4,0},{8,4},{12,8},{16,12},{20,16},{24,20},{28,24},{32,28}... | collective-permute-start | bytes 49160 | tf_op jit(solution)/shard_map/halo/ppermute | solution.py:442
  15.6 3.8 %collective-permute-start.2 = (bf16[336,256]{1,0:T(8,128)(2,1)S(1)}, bf16[336,256]{1,0:T(8,128)(2,1)S(1)}, u32[]{:S(2)}, u32[]{:S(2)}) collective-permute-start(bf16[336,256]{1,0:T(8,128)(2,1)S(1)} %get-tuple-element.39), channel_id=1, source_target_pairs={{0,1},{1,0},{2,3},{3,2},{4,5},{5,4},{6,7},{7,6},{8,9},{9,8},{10,11... | collective-permute-start | bytes 516104 | tf_op jit(solution)/shard_map/halo/ppermute | solution.py:527
  17.2 6.7 %collective-permute-start.3 = (bf16[336,256]{1,0:T(8,128)(2,1)S(1)}, bf16[336,256]{1,0:T(8,128)(2,1)S(1)}, u32[]{:S(2)}, u32[]{:S(2)}) collective-permute-start(bf16[336,256]{1,0:T(8,128)(2,1)S(1)} %get-tuple-element.40), channel_id=1, source_target_pairs={{1,2},{2,1},{5,6},{6,5},{9,10},{10,9},{13,14},{14,13},{17,18},{18,... | collective-permute-start | bytes 516104 | tf_op jit(solution)/shard_map/halo/ppermute | solution.py:529
  23.9 21.7 %copy-start = (bf16[3,3,256,256]{3,2,1,0:T(8,128)(2,1)S(1)}, bf16[3,3,256,256]{3,2,1,0:T(8,128)(2,1)}, u32[]{:S(2)}) copy-start(bf16[3,3,256,256]{3,2,1,0:T(8,128)(2,1)} %dw.1) | copy-start | bytes 3538948
  23.9 21.7 %copy-start.1 = (bf16[4,64,256]{2,1,0:T(8,128)(2,1)S(1)}, bf16[4,64,256]{2,1,0:T(8,128)(2,1)}, u32[]{:S(2)}) copy-start(bf16[4,64,256]{2,1,0:T(8,128)(2,1)} %cot.3) | copy-start | bytes 393220
  29.0 25.3 %copy-start.2 = (f32[256]{0:T(256)S(1)}, f32[256]{0:T(256)}, u32[]{:S(2)}) copy-start(f32[256]{0:T(256)} %param.10) | copy-start | bytes 3076
  29.0 25.3 %copy-start.3 = (f32[256]{0:T(256)S(1)}, f32[256]{0:T(256)}, u32[]{:S(2)}) copy-start(f32[256]{0:T(256)} %param.9) | copy-start | bytes 3076
  36.3 18.0 %all-to-all-start.1 = ((f32[32,2,128]{2,1,0:T(2,128)}), f32[32,2,128]{2,1,0:T(2,128)S(1)}, u32[]{:S(2)}, u32[]{:S(2)}) async-start(f32[32,2,128]{2,1,0:T(2,128)} %conv.3), calls=%async_computation.1 | async-start | bytes 65536 | tf_op jit(solution)/shard_map/conv/all_to_all | solution.py:548
  67.9 12.7 %all-to-all-start.3 = ((f32[32,4,128]{2,1,0:T(4,128)}), f32[32,4,128]{2,1,0:T(4,128)S(1)}, u32[]{:S(2)}, u32[]{:S(2)}) async-start(f32[32,4,128]{2,1,0:T(4,128)} %act.3), calls=%async_computation.3 | async-start | bytes 131072 | tf_op jit(solution)/shard_map/act/all_to_all | solution.py:574
  75.3 11.8 %collective-permute-start.5 = (bf16[1152,256]{1,0:T(8,128)(2,1)}, bf16[1152,256]{1,0:T(8,128)(2,1)S(1)}, u32[]{:S(2)}, u32[]{:S(2)}) collective-permute-start(bf16[1152,256]{1,0:T(8,128)(2,1)} %get-tuple-element.59), channel_id=1, source_target_pairs={{0,1},{1,0},{2,3},{3,2},{4,5},{5,4},{6,7},{7,6},{8,9},{9,8},{10,11... | collective-permute-start | bytes 1769480 | tf_op jit(solution)/shard_map/down/ppermute | solution.py:485
  85.2 3.6 %collective-permute-start.4 = (bf16[1152,256]{1,0:T(8,128)(2,1)S(1)}, bf16[1152,256]{1,0:T(8,128)(2,1)S(1)}, u32[]{:S(2)}, u32[]{:S(2)}) collective-permute-start(bf16[1152,256]{1,0:T(8,128)(2,1)S(1)} %get-tuple-element.57), channel_id=1, source_target_pairs={{0,1},{1,0},{2,3},{3,2},{4,5},{5,4},{6,7},{7,6},{8,9},{9,8},{10,11... | collective-permute-start | bytes 1769480 | tf_op jit(solution)/shard_map/total/ppermute | solution.py:485
  89.9 4.1 %copy-start.4 = (bf16[3,3,256,256]{3,2,1,0:T(8,128)(2,1)S(1)}, bf16[3,3,256,256]{3,2,1,0:T(8,128)(2,1)}, u32[]{:S(2)}) copy-start(bf16[3,3,256,256]{3,2,1,0:T(8,128)(2,1)} %w.1) | copy-start | bytes 3538948
  89.9 21.3 %all-to-all-start.4 = ((bf16[32,72,256]{2,1,0:T(8,128)(2,1)}), bf16[32,72,256]{2,1,0:T(8,128)(2,1)S(1)}, u32[]{:S(2)}, u32[]{:S(2)}) async-start(bf16[32,72,256]{2,1,0:T(8,128)(2,1)} %bitcast.20), calls=%async_computation.4 | async-start | bytes 2359296 | tf_op jit(solution)/shard_map/total/all_to_all | solution.py:623
  94.0 1.3 copy-start.5
  141.6 7.2 %collective-permute-start.6 = (bf16[2304,256]{1,0:T(8,128)(2,1)S(1)}, bf16[2304,256]{1,0:T(8,128)(2,1)S(1)}, u32[]{:S(2)}, u32[]{:S(2)}) collective-permute-start(bf16[2304,256]{1,0:T(8,128)(2,1)S(1)} %bitcast.13), channel_id=1, source_target_pairs={{0,1},{1,0},{2,3},{3,2},{4,5},{5,4},{6,7},{7,6},{8,9},{9,8},{10,11... | collective-permute-start | bytes 3538952 | tf_op jit(solution)/shard_map/total/ppermute | solution.py:485

commit v5 on v4

--- a/solution.py
+++ b/solution.py
@@ -54,21 +54,21 @@
     return lax.dot_general(a, b, (((0,), (0,)), ((), ())), preferred_element_type=F32)
 
 
-def exact(a, b):
-    a8 = jnp.broadcast_to(a, (8, a.shape[1]))
-    return jnp.dot(a8, b, preferred_element_type=F32, precision=lax.Precision.HIGHEST)[0:1]
-
-
-def to_lanes(chans):
-    c = lax.broadcasted_iota(jnp.int32, (chans, 128), 0) // WIDTH
-    l = lax.broadcasted_iota(jnp.int32, (chans, 128), 1)
-    return (c == l).astype(F32)
-
-
-def from_lanes(chans):
-    c = lax.broadcasted_iota(jnp.int32, (128, chans), 1) // WIDTH
-    l = lax.broadcasted_iota(jnp.int32, (128, chans), 0)
-    return (c == l).astype(F32)
+def spread_dot(table, *vectors):
+    parts = []
+    for v in vectors:
+        high = v.astype(BF).astype(F32)
+        mid = (v - high).astype(BF).astype(F32)
+        parts += [high, mid, v - high - mid]
+    parts.append(jnp.zeros((8 - len(parts), vectors[0].shape[1]), F32))
+    out = dot(jnp.concatenate(parts, axis=0).astype(BF), table)
+    return [out[3 * i : 3 * i + 1] + out[3 * i + 1 : 3 * i + 2] + out[3 * i + 2 : 3 * i + 3] for i in range(len(vectors))]
+
+
+def table(n, m, row_width, col_width, shift):
+    r = lax.broadcasted_iota(jnp.int32, (n, m), 0) // row_width
+    c = lax.broadcasted_iota(jnp.int32, (n, m), 1) // col_width
+    return jnp.where(r == c + shift, 1.0, 0.0).astype(BF)
 
 
 def masks():
@@ -137,63 +137,102 @@
     return north, south
 
 
-def conv_kernel(
-    flags, feat_hbm, west, east, near, far, w_hbm, x_hbm, h_hbm, hq_out, he_out, stat_out, f32s, edge, x_out, feat, w, sems
-):
+def taps(f32s, x_out, rows, lanes):
+    for r in range(rows):
+        for v in range(2):
+            for k in range(lanes):
+                lane = k * 256 + v * 128
+                x_out[r, :, lane : lane + 128] = f32s[r, v, pl.ds(14 + k, J, stride=2), :].astype(BF)
+
+
+def inner_kernel(feat_hbm, west, east, w_hbm, x_hbm, rim, hq_out, he_out, f32s, edge, x_out, feat, w, sems):
     rows, cols, chans = feat.shape
+    pairs = cols // 2
     load_f = pltpu.make_async_copy(feat_hbm, feat, sems.at[1])
     load_f.start()
     load_w = pltpu.make_async_copy(w_hbm, w, sems.at[2])
     load_w.start()
-    f32s[:, :, 16 + cols : 56 + cols] = jnp.zeros((rows + 4, 2, 40, 128), F32)
-    pairs = cols // 2
+    f32s[:, :, 16 + cols : 56 + cols] = jnp.zeros((rows, 2, 40, 128), F32)
     for v in range(2):
         part = slice(v * 128, v * 128 + 128)
         for k, side in enumerate((west, east)):
             edge[k, v] = side[:, part].astype(F32)
-        for k, side in enumerate(sides(flags, near, far)):
-            edge[2 + k, v, 0:16] = side(2 * cols + pairs, 2 * cols + pairs + 16, part)
-            for q in range(2):
-                row = q + k * (rows + 2)
-                f32s[row, v, 16 : 16 + cols] = side(q * cols, (q + 1) * cols, part)
-                f32s[row, v, 14:16] = edge[2 + k, v, 2 * q : 2 * q + 2]
-                f32s[row, v, 16 + cols : 18 + cols] = edge[2 + k, v, 4 + 2 * q : 6 + 2 * q]
         for r in range(rows):
-            f32s[2 + r, v, 14:16] = edge[0, v, 2 * r : 2 * r + 2]
-            f32s[2 + r, v, 16 + cols : 18 + cols] = edge[1, v, 2 * r : 2 * r + 2]
+            f32s[r, v, 14:16] = edge[0, v, 2 * r : 2 * r + 2]
+            f32s[r, v, 16 + cols : 18 + cols] = edge[1, v, 2 * r : 2 * r + 2]
     load_f.wait()
     for v in range(2):
-        part = slice(v * 128, v * 128 + 128)
-        f32s[2 : rows + 2, v, 16 : 16 + cols] = feat[:, :, part].astype(F32)
-        for r in range(rows + 4):
-            for k in range(5):
-                lane = k * chans + v * 128
-                x_out[r, :, lane : lane + 128] = f32s[r, v, pl.ds(14 + k, J, stride=2), :].astype(BF)
-    kept = x_out.at[1 : rows + 3, 0:pairs, chans : 5 * chans]
-    keep = pltpu.make_async_copy(kept, x_hbm, sems.at[0])
+        f32s[:, v, 16 : 16 + cols] = feat[:, :, v * 128 : v * 128 + 128].astype(F32)
+    taps(f32s, x_out, rows, 5)
+    keep = pltpu.make_async_copy(x_out.at[:, 0:pairs, chans : 5 * chans], x_hbm, sems.at[0])
     keep.start()
+    for i, r in enumerate((0, 1, rows - 2, rows - 1)):
+        rim[i] = x_out[r, :, 0 : 4 * chans]
     load_w.wait()
-    copies = [keep]
-    odd, even = masks()
-    sums = jnp.zeros((1, chans), F32)
+    n = rows - 2
     for out, lo in ((hq_out, 0), (he_out, chans)):
         acc = None
         for a in range(3):
-            lhs = x_out[a : a + rows + 2, :, lo : lo + 3 * chans].reshape((rows + 2) * J, 3 * chans)
+            lhs = x_out[a : a + n, :, lo : lo + 3 * chans].reshape(n * J, 3 * chans)
             term = dot(lhs, w[a])
             acc = term if acc is None else acc + term
-        out[...] = acc.astype(BF).reshape(rows + 2, J, chans)
-        k = lo // chans
+        out[...] = acc.astype(BF).reshape(n, J, chans)
+    keep.wait()
+
+
+def outer_kernel(
+    cols, flags, near, far, rim, hq_in, he_in, w_hbm, x_hbm, h_hbm, hq_out, he_out, stat_out, f32s, edge, x_out, w, sems
+):
+    rows = hq_in.shape[0] + 2
+    chans = hq_in.shape[2]
+    pairs = cols // 2
+    load_w = pltpu.make_async_copy(w_hbm, w, sems.at[0])
+    load_w.start()
+    f32s[:, :, 16 + cols : 56 + cols] = jnp.zeros((4, 2, 40, 128), F32)
+    for v in range(2):
+        part = slice(v * 128, v * 128 + 128)
+        for k, side in enumerate(sides(flags, near, far)):
+            edge[k, v] = side(2 * cols + pairs, 2 * cols + pairs + 16, part)
+            for q in range(2):
+                row = q + 2 * k
+                f32s[row, v, 16 : 16 + cols] = side(q * cols, (q + 1) * cols, part)
+                f32s[row, v, 14:16] = edge[k, v, 2 * q : 2 * q + 2]
+                f32s[row, v, 16 + cols : 18 + cols] = edge[k, v, 4 + 2 * q : 6 + 2 * q]
+    taps(f32s, x_out, 4, 5)
+    copies = []
+    for i, r in enumerate((1, 2)):
+        copies.append(pltpu.make_async_copy(x_out.at[r, 0:pairs, chans : 5 * chans], x_hbm.at[i], sems.at[1 + i]))
+        copies[-1].start()
+    hq_out[2:rows] = hq_in[...]
+    he_out[2:rows] = he_in[...]
+    load_w.wait()
+    wanted = (
+        ((x_out, 0), (x_out, 1), (rim, 2), (rim, 3)),
+        ((x_out, 1), (rim, 0), (rim, 3), (x_out, 2)),
+        ((rim, 0), (rim, 1), (x_out, 2), (x_out, 3)),
+    )
+    for k, out in enumerate((hq_out, he_out)):
+        lo = k * chans
+        acc = None
+        for a in range(3):
+            lhs = jnp.concatenate([ref[r, :, lo : lo + 3 * chans] for ref, r in wanted[a]], axis=0)
+            term = dot(lhs, w[a])
+            acc = term if acc is None else acc + term
+        value = acc.astype(BF).reshape(4, J, chans)
+        out[0:2] = value[0:2]
+        out[rows : rows + 2] = value[2:4]
         copies.append(pltpu.make_async_copy(out, h_hbm.at[k], sems.at[3 + k]))
         copies[-1].start()
+    odd, even = masks()
+    sums = jnp.zeros((1, chans), F32)
     for out, mask in ((hq_out, odd), (he_out, even)):
         part = jnp.zeros((J, chans), F32)
         for r in range(1, rows + 1):
             part = part + out[r].astype(F32)
         sums = sums + jnp.sum(part * mask, axis=0, keepdims=True)
-    lanes = to_lanes(chans)
-    means = exact(sums, lanes) / (rows * cols * WIDTH)
-    mean = exact(means, from_lanes(chans))
+    n = rows * cols * WIDTH
+    (total,) = spread_dot(table(chans, chans, WIDTH, WIDTH, 0), sums)
+    mean = total / n
     squares = jnp.zeros((1, chans), F32)
     for out, mask in ((hq_out, odd), (he_out, even)):
         part = jnp.zeros((J, chans), F32)
@@ -201,19 +240,12 @@
             d = out[r].astype(F32) - mean
             part = part + d * d
         squares = squares + jnp.sum(part * mask, axis=0, keepdims=True)
-    stat = jnp.concatenate([means, exact(squares, lanes)], axis=0)
+    (means,) = spread_dot(table(chans, 128, WIDTH, 1, 0), sums)
+    (spreads,) = spread_dot(table(chans, 128, WIDTH, 1, -32), squares)
+    stat = means / n + spreads
     stat_out[...] = jnp.broadcast_to(stat[None], stat_out.shape)
     for copy in copies:
         copy.wait()
-
-
-def merged_stats(local_n, rec, out):
-    means = rec[:, 0, :]
-    mean = jnp.sum(means, axis=0, keepdims=True) / rec.shape[0]
-    gap = means - mean
-    squares = jnp.sum(rec[:, 1, :] + local_n * gap * gap, axis=0, keepdims=True)
-    both = jnp.concatenate([mean, squares], axis=0)
-    out[...] = jnp.broadcast_to(both[None], out.shape)
 
 
 def merged_sums(rec, out):
@@ -266,19 +298,19 @@
 
 
 def act_kernel(cells, flags, stats, hq, he, aq, ae, gain, bias, t_hbm, p_hbm, coef_out, sum_out, f32s, t_out, p_out, sems):
-    parts = stats.shape[0]
+    devices = stats.shape[0]
     rows = hq.shape[0] - 2
     chans = hq.shape[2]
-    part_n = float(cells // parts * WIDTH)
     count = float(cells * WIDTH)
+    local_n = count / devices
     rec = stats[...]
     total = jnp.sum(rec, axis=0)
-    centre = total[0:1] / parts
-    dev = rec[:, 0, :] - centre
-    spread = jnp.sum(dev * dev, axis=0, keepdims=True)
-    back = from_lanes(chans)
-    mean = exact(centre, back)
-    var = exact((total[1:2] + part_n * spread) / count, back)
+    centre = total / devices
+    dev = rec - centre[None]
+    between = jnp.sum(dev * dev, axis=0)
+    mean, gaps = spread_dot(table(128, chans, 1, WIDTH, 0), centre, between)
+    (within,) = spread_dot(table(128, chans, 1, WIDTH, 32), total)
+    var = (within + local_n * gaps) / count
     inverse = lax.rsqrt(var + EPS)
     coef_out[0:1] = mean
     coef_out[1:2] = inverse
@@ -353,7 +385,7 @@
 
 
 def grad_kernel(
-    cells, flags, sums, coef, gain, h_hbm, p_hbm, x_hbm, h4_hbm, keep, send, vec_out, f32s, conv_out, h_in, p_in, x, h4_out, sems
+    cells, flags, sums, coef, gain, h_hbm, p_hbm, x_hbm, rim_hbm, h4_hbm, keep, send, vec_out, f32s, conv_out, h_in, p_in, x, h4_out, sems
 ):
     rows = p_in.shape[1] - 2
     chans = p_in.shape[3]
@@ -364,9 +396,11 @@
         for r in range(rows + 2):
             loads.append(pltpu.make_async_copy(p_hbm.at[k, r], p_in.at[k, r], sems.at[len(loads)]))
             loads[-1].start()
-    load_x = pltpu.make_async_copy(x_hbm, x, sems.at[len(loads)])
-    load_x.start()
-    first_out = len(loads) + 1
+    load_x = []
+    for src, dst in ((x_hbm, x.at[1 : rows + 1]), (rim_hbm.at[0], x.at[0]), (rim_hbm.at[1], x.at[rows + 1])):
+        load_x.append(pltpu.make_async_copy(src, dst, sems.at[len(loads) + len(load_x)]))
+        load_x[-1].start()
+    first_out = len(loads) + len(load_x)
     copies = []
     count = float(cells * WIDTH)
     total = jnp.sum(sums[...], axis=0)
@@ -376,9 +410,9 @@
     vec_out[0:1] = gain_sum * factor
     vec_out[1:2] = bias_sum * factor
     g = gain[...]
-    lanes, back = to_lanes(chans), from_lanes(chans)
-    first = exact(exact(g * bias_sum, lanes), back) / count
-    second = exact(exact(g * gain_sum, lanes), back) / count
+    first, second = spread_dot(table(chans, chans, WIDTH, WIDTH, 0), g * bias_sum, g * gain_sum)
+    first = first / count
+    second = second / count
     mean = coef[0:1]
     inverse = coef[1:2]
     top = jnp.where(flags[0] == 1, 0.0, 1.0)
@@ -404,7 +438,8 @@
             if not is_q:
                 copies.append(pltpu.make_async_copy(h4_out.at[r], h4_hbm.at[r], sems.at[first_out + r]))
                 copies[-1].start()
-    load_x.wait()
+    for load in load_x:
+        load.wait()
     pairs = h4_out.shape[1]
     cells_here = rows * pairs
     odd = h4_out[1 : rows + 1, :, chans : 2 * chans].reshape(cells_here, chans)
@@ -529,23 +564,41 @@
         far = lax.ppermute(to_far, LAT, [(i, i + 1) for i in gaps] + [(i + 1, i) for i in gaps])
 
     plane = (rows + 2, J, chans)
-    x_shape = (rows + 2, pairs, 4 * chans)
-    x_full = (rows + 4, J, 5 * chans)
+    x_shape = (rows, pairs, 4 * chans)
+    rim_shape = (2, pairs, 4 * chans)
+    inner_plane = (rows - 2, J, chans)
     with jax.named_scope("conv"):
-        x, h, hq, he, stat = call(
-            conv_kernel,
-            [(x_shape, BF, True), ((2,) + plane, BF, True), (plane, BF), (plane, BF), ((few, 2, 128), F32)],
-            [((rows + 4, 2, cols + 56, 128), F32), ((4, 2) + (slab[0], 128), F32), (x_full, BF), ((rows, cols, chans), BF), (w3.shape, BF)],
-            flops=2 * 1600 * 2304 * 256,
+        x, rim, hq_in, he_in = call(
+            inner_kernel,
+            [(x_shape, BF, True), ((4, J, 4 * chans), BF), (inner_plane, BF), (inner_plane, BF)],
+            [
+                ((rows, 2, cols + 56, 128), F32),
+                ((2, 2, slab[0], 128), F32),
+                ((rows, J, 5 * chans), BF),
+                ((rows, cols, chans), BF),
+                (w3.shape, BF),
+            ],
+            flops=2 * 960 * 2304 * 256,
+            n_in=4,
+            hbm=(0, 3),
+            sems=3,
+        )(pinned(features), west, east, pinned(w3))
+        x_rim, h, hq, he, stat = call(
+            functools.partial(outer_kernel, cols),
+            [(rim_shape, BF, True), ((2,) + plane, BF, True), (plane, BF), (plane, BF), ((devices, 1, 128), F32)],
+            [
+                ((4, 2, cols + 56, 128), F32),
+                ((2, 2, 16, 128), F32),
+                ((4, J, 5 * chans), BF),
+                (w3.shape, BF),
+            ],
+            flops=2 * 640 * 2304 * 256,
             n_in=7,
             smem=(0,),
-            hbm=(1, 6),
+            hbm=(6,),
             sems=5,
-        )(flags, pinned(features), west, east, near, far, pinned(w3))
-        local_n = float(rows * cols * WIDTH)
-        stat = lax.all_to_all(stat, FEW, 0, 0, tiled=True)
-        (stat,) = call(functools.partial(merged_stats, local_n), [((rest, 2, 128), F32)], n_in=1)(stat)
-        stats = lax.all_to_all(stat, REST, 0, 0, tiled=True)
+        )(flags, near, far, rim, hq_in, he_in, pinned(w3))
+        stats = lax.all_to_all(stat, ALL, 0, 0, tiled=True)
     c_shape = (half + 2, J, 2 * chans)
     with jax.named_scope("back"):
         c2, aq, ae = call(
@@ -595,15 +648,15 @@
                 ((all_rows, chans), F32),
                 ((2,) + plane, BF),
                 ((2,) + plane, F32),
-                (x_shape, BF),
+                ((rows + 2, pairs, 4 * chans), BF),
                 (h4_shape, BF),
             ],
             flops=2 * 1600 * 2304 * 256,
             smem=(0,),
-            hbm=(4, 5, 6),
-            n_in=7,
-            sems=3 * (rows + 2) + 3,
-        )(flags, sums, coef, gain, pinned(h), pinned(p), pinned(x))
+            hbm=(4, 5, 6, 7),
+            n_in=8,
+            sems=3 * (rows + 2) + 5,
+        )(flags, sums, coef, gain, pinned(h), pinned(p), pinned(x), pinned(x_rim))
     with jax.named_scope("input"):
         (input_grad,) = call(
             input_kernel,

time: 152 us -> 147 us (0.967)
  blocking collectives: 45.8 us -> 37.5 us
    all_to_all x1 -> x0, blocking collectives: 6.63 us -> none  [local(): stat = lax.all_to_all(stat, FEW, 0, 0, tiled=True)]
    all_to_all x1, waiting for transfers between devices: 6.84 us -> 10.9 us  [local(): stats = lax.all_to_all(stat, ALL, 0, 0, tiled=True)]
    ppermute x1, waiting for transfers between devices: 4.49 us -> 1.71 us  [local(): lax.ppermute(to_far, LAT, [(i, i + 1) for i in gaps] + [(i + 1, i) for i...]
    all_to_all x1, blocking collectives: 9.14 us -> 7.45 us  [local(): sums = lax.all_to_all(sums, FEW, 0, 0, tiled=True)]
    pallas_call x2, Pallas kernels: 5.69 us -> 7.23 us  [the longest x1 4.46 us: local(): call(functools.partial(outer_kernel, cols), [(rim_shape, BF, True), ((2,)...]
  transfers between devices with their start and end apart: 10 -> 10, of which waited for: 6 -> 6; matrix products, arithmetic and copies ran while one was open for 0% -> 0% of each run, Pallas kernels for 9% -> 11%
where the time goes in v5:
time: 147 us; the launch traced here: 146 us
  starting transfers between devices  41.1 us (28%)
  blocking collectives  37.5 us (26%)
  waiting for transfers between devices  33.3 us (23%)
  Pallas kernels  30.8 us (21%)
  local copies, waits for them, and re-layouts  2 us (1%)
    all_to_all x1, blocking collectives, local(): lax.all_to_all(jnp.broadcast_to(piece[None], (chips, share, chans)), NEAR...  20.3 us
    all_to_all x1, waiting for transfers between devices, local(): lax.all_to_all(mine.reshape(chips, share, chans), NEAR, 0, 0, tiled=True)  13.6 us
    ppermute x2, starting transfers between devices, passed(): return lax.ppermute(value, axes, pairs)  11.4 us
    all_to_all x1, waiting for transfers between devices, local(): stats = lax.all_to_all(stat, ALL, 0, 0, tiled=True)  10.9 us
    all_to_all x1, starting transfers between devices, local(): stats = lax.all_to_all(stat, ALL, 0, 0, tiled=True)  10.2 us
    all_to_all x1, blocking collectives, local(): lax.all_to_all(jnp.broadcast_to(piece[None], (depth, share, chans)), 'z_h...  9.76 us
    ppermute x3, starting transfers between devices, core_swap(): return lax.ppermute(value, 'core', [(0, 1), (1, 0)])  7.74 us
    all_to_all x1, blocking collectives, local(): sums = lax.all_to_all(sums, FEW, 0, 0, tiled=True)  7.45 us
  transfers between devices with their start and end apart: 10, of which 6 were waited for; matrix products, arithmetic and copies ran while one was open for 0% of the time, Pallas kernels for 11%

profile of v5, /device:TPU:1, one launch (start us, length us, event | category | flops | bytes accessed | tf_op | source)
XLA Modules:
  0.0 146.0 jit_solution(8944040007126557768)
XLA Ops:
  0.6 1.0 halo.2
  1.6 3.8 %collective-permute-start = (bf16[32,256]{1,0:T(8,128)(2,1)S(1)}, bf16[32,256]{1,0:T(8,128)(2,1)S(1)}, u32[]{:S(2)}, u32[]{:S(2)}) collective-permute-start(bf16[32,256]{1,0:T(8,128)(2,1)S(1)} %get-tuple-element.41), channel_id=1, source_target_pairs={{0,4},{4,8},{8,12},{12,16},{16,20},{20,24},{24,28},{28,32},{32,36}... | collective-permute-start | bytes 49160 | tf_op jit(solution)/shard_map/halo/ppermute | solution.py:477
  5.4 7.6 %collective-permute-start.1 = (bf16[32,256]{1,0:T(8,128)(2,1)S(1)}, bf16[32,256]{1,0:T(8,128)(2,1)S(1)}, u32[]{:S(2)}, u32[]{:S(2)}) collective-permute-start(bf16[32,256]{1,0:T(8,128)(2,1)S(1)} %get-tuple-element.42), channel_id=1, source_target_pairs={{0,252},{4,0},{8,4},{12,8},{16,12},{20,16},{24,20},{28,24},{32,28}... | collective-permute-start | bytes 49160 | tf_op jit(solution)/shard_map/halo/ppermute | solution.py:477
  13.0 0.1 add_convert_fusion.flags
  13.1 1.0 collective-permute-done.west
  14.0 0.0 collective-permute-done.1.east
  14.0 1.6 %halo.3 = (bf16[336,256]{1,0:T(8,128)(2,1)S(1)}, bf16[336,256]{1,0:T(8,128)(2,1)S(1)}) custom-call(s32[3]{0:T(128)S(1)} %add_convert_fusion.flags, bf16[8,128,256]{2,1,0:T(8,128)(2,1)} %feat_hbm.3, bf16[4,64,256]{2,1,0:T(8,128)(2,1)} %cot.3, bf16[32,256]{1,0:T(8,128)(2,1)S(1)} %collective-permute-done.west, bf16[32,256]{1,0:T(8,128)(2,1)S(1)} %collective-permute-done.1.east), custom_call_target="tpu_custom_call" | custom-call | bytes 1048576 | tf_op jit(solution)/shard_map/halo/pallas_call | solution.py:553
  15.6 1.6 %collective-permute-start.2 = (bf16[336,256]{1,0:T(8,128)(2,1)S(1)}, bf16[336,256]{1,0:T(8,128)(2,1)S(1)}, u32[]{:S(2)}, u32[]{:S(2)}) collective-permute-start(bf16[336,256]{1,0:T(8,128)(2,1)S(1)} %get-tuple-element.43), channel_id=1, source_target_pairs={{0,1},{1,0},{2,3},{3,2},{4,5},{5,4},{6,7},{7,6},{8,9},{9,8},{10,11... | collective-permute-start | bytes 516104 | tf_op jit(solution)/shard_map/halo/ppermute | solution.py:562
  17.2 2.2 %collective-permute-start.3 = (bf16[336,256]{1,0:T(8,128)(2,1)S(1)}, bf16[336,256]{1,0:T(8,128)(2,1)S(1)}, u32[]{:S(2)}, u32[]{:S(2)}) collective-permute-start(bf16[336,256]{1,0:T(8,128)(2,1)S(1)} %get-tuple-element.44), channel_id=1, source_target_pairs={{1,2},{2,1},{5,6},{6,5},{9,10},{10,9},{13,14},{14,13},{17,18},{18,... | collective-permute-start | bytes 516104 | tf_op jit(solution)/shard_map/halo/ppermute | solution.py:564
  19.4 2.8 %conv.2 = (bf16[8,64,1024]{2,1,0:T(8,128)(2,1)}, bf16[4,80,1024]{2,1,0:T(8,128)(2,1)S(1)}, bf16[6,80,256]{2,1,0:T(8,128)(2,1)S(1)}, bf16[6,80,256]{2,1,0:T(8,128)(2,1)S(1)}) custom-call(bf16[8,128,256]{2,1,0:T(8,128)(2,1)} %feat_hbm.3, bf16[32,256]{1,0:T(8,128)(2,1)S(1)} %collective-permute-done.west, bf16[32,256]{1,0:T(8,128)(2,1)S(1)} %collective-permute-done.1.east, ...), custom_call_target="tpu_custom_call" | custom-call | flops 1132462080 | bytes 1048576 | tf_op jit(solution)/shard_map/conv/pallas_call | solution.py:571
  22.2 0.0 collective-permute-done.2.near
  22.2 1.7 %collective-permute-done.3.far = bf16[336,256]{1,0:T(8,128)(2,1)S(1)} collective-permute-done((bf16[336,256]{1,0:T(8,128)(2,1)S(1)}, bf16[336,256]{1,0:T(8,128)(2,1)S(1)}, u32[]{:S(2)}, u32[]{:S(2)}) %collective-permute-start.3) | collective-permute-done | bytes 172064 | tf_op jit(solution)/shard_map/halo/ppermute | solution.py:564
  24.0 4.5 %conv.3 = (bf16[2,64,1024]{2,1,0:T(8,128)(2,1)}, bf16[2,10,80,256]{3,2,1,0:T(8,128)(2,1)}, bf16[10,80,256]{2,1,0:T(8,128)(2,1)S(1)}, bf16[10,80,256]{2,1,0:T(8,128)(2,1)S(1)}, f32[256,1,128]{2,1,0:T(1,128)}) custom-call(s32[3]{0:T(128)S(1)} %add_convert_fusion.flags, bf16[336,256]{1,0:T(8,128)(2,1)S(1)} %collective-permute-done.2.near, ...), custom_call_target="tpu_custom_call" | custom-call | flops 754974720 | bytes 1048576 | tf_op jit(solution)/shard_map/conv/pallas_call | solution.py:586
  28.4 0.0 copy-start.2
  28.4 0.0 copy-start.3
  28.4 10.2 %all-to-all-start = ((f32[256,1,128]{2,1,0:T(1,128)}), f32[256,1,128]{2,1,0:T(1,128)S(1)}, u32[]{:S(2)}, u32[]{:S(2)}) async-start(f32[256,1,128]{2,1,0:T(1,128)} %get-tuple-element.48), calls=%async_computation | async-start | bytes 262144 | tf_op jit(solution)/shard_map/conv/all_to_all | solution.py:601
  38.6 0.0 copy-done
  38.7 0.0 copy-done.1
  38.7 1.8 %back.1 = (bf16[6,80,512]{2,1,0:T(8,128)(2,1)}, bf16[10,80,256]{2,1,0:T(8,128)(2,1)S(1)}, bf16[10,80,256]{2,1,0:T(8,128)(2,1)S(1)}) custom-call(s32[3]{0:T(128)S(1)} %add_convert_fusion.flags, bf16[4,64,256]{2,1,0:T(8,128)(2,1)S(1)} %copy-done.1, bf16[32,256]{1,0:T(8,128)(2,1)S(1)} %collective-permute-done.west, ...), custom_call_target="tpu_custom_call" | custom-call | flops 471859200 | bytes 1048576 | tf_op jit(solution)/shard_map/back/pallas_call | solution.py:604
  40.5 10.9 %all-to-all-done.stats = f32[256,1,128]{2,1,0:T(1,128)S(1)} async-done(((f32[256,1,128]{2,1,0:T(1,128)}), f32[256,1,128]{2,1,0:T(1,128)S(1)}, u32[]{:S(2)}, u32[]{:S(2)}) %all-to-all-start) | async-done | bytes 131104 | tf_op jit(solution)/shard_map/conv/all_to_all | solution.py:601
  51.4 0.0 copy-done.2
  51.4 3.4 %act.2 = (bf16[9,64,768]{2,1,0:T(8,128)(2,1)}, f32[2,10,80,256]{3,2,1,0:T(8,128)}, f32[2,256]{1,0:T(2,128)S(1)}, f32[8,4,128]{2,1,0:T(4,128)S(1)}) custom-call(s32[3]{0:T(128)S(1)} %add_convert_fusion.flags, f32[256,1,128]{2,1,0:T(1,128)S(1)} %all-to-all-done.stats, bf16[10,80,256]{2,1,0:T(8,128)(2,1)S(1)} %get-tuple-element.49.hq, ...), custom_call_target="tpu_custom_call" | custom-call | flops 8192000 | bytes 1048576 | tf_op jit(solution)/shard_map/act/pallas_call | solution.py:615
  54.9 7.5 %all_to_all.30.rec = f32[8,4,128]{2,1,0:T(4,128)S(1)} all-to-all(f32[8,4,128]{2,1,0:T(4,128)S(1)} %get-tuple-element.54), channel_id=1, replica_groups=mesh['x'=4,'z_hi'=4,'z_lo'=2,'y_hi'=2,'y_lo'=2,'core'=2] {'x','core'}, dimensions={0} | all-to-all | bytes 32768 | tf_op jit(solution)/shard_map/act/all_to_all | solution.py:624
  62.3 0.7 act.3
  63.0 3.8 %all-to-all-start.2 = ((f32[32,4,128]{2,1,0:T(4,128)}), f32[32,4,128]{2,1,0:T(4,128)S(1)}, u32[]{:S(2)}, u32[]{:S(2)}) async-start(f32[32,4,128]{2,1,0:T(4,128)} %act.3), calls=%async_computation.2 | async-start | bytes 131072 | tf_op jit(solution)/shard_map/act/all_to_all | solution.py:627
  66.8 3.3 %down.1 = (bf16[4,64,256]{2,1,0:T(8,128)(2,1)}, f32[1152,256]{1,0:T(8,128)S(1)}, bf16[1152,256]{1,0:T(8,128)(2,1)S(1)}) custom-call(s32[3]{0:T(128)S(1)} %add_convert_fusion.flags, bf16[9,64,768]{2,1,0:T(8,128)(2,1)} %get-tuple-element.53.t_hbm, bf16[6,80,512]{2,1,0:T(8,128)(2,1)} %get-tuple-element.56.c_hbm, bf16[3,768,256]{2,1,0:T(8,128)(2,1)S(1)} %bitcast.15), custom_call_target="tpu_custom_call" | custom-call | flops 603979776 | bytes 1048576 | tf_op jit(solution)/shard_map/down/pallas_call | solution.py:630
  70.1 1.1 collective-permute-start.5
  71.2 4.5 %all-to-all-done.2.sums = f32[32,4,128]{2,1,0:T(4,128)S(1)} async-done(((f32[32,4,128]{2,1,0:T(4,128)}), f32[32,4,128]{2,1,0:T(4,128)S(1)}, u32[]{:S(2)}, u32[]{:S(2)}) %all-to-all-start.2) | async-done | bytes 65568 | tf_op jit(solution)/shard_map/act/all_to_all | solution.py:627
  75.7 4.5 %grad.1 = (bf16[10,64,1024]{2,1,0:T(8,128)(2,1)}, f32[1152,256]{1,0:T(8,128)S(1)}, bf16[1152,256]{1,0:T(8,128)(2,1)S(1)}, f32[2,256]{1,0:T(2,128)S(1)}) custom-call(s32[3]{0:T(128)S(1)} %add_convert_fusion.flags, f32[32,4,128]{2,1,0:T(4,128)S(1)} %all-to-all-done.2.sums, f32[2,256]{1,0:T(2,128)S(1)} %get-tuple-element.59.coef, f32[1,256]{1,0:T(1,128)S(1)} %bitcast.18, ...), custom_call_target="tpu_custom_call" | custom-call | flops 1887436800 | bytes 1048576 | tf_op jit(solution)/shard_map/grad/pallas_call | solution.py:643
  80.2 2.0 %collective-permute-start.4 = (bf16[1152,256]{1,0:T(8,128)(2,1)S(1)}, bf16[1152,256]{1,0:T(8,128)(2,1)S(1)}, u32[]{:S(2)}, u32[]{:S(2)}) collective-permute-start(bf16[1152,256]{1,0:T(8,128)(2,1)S(1)} %get-tuple-element.65), channel_id=1, source_target_pairs={{0,1},{1,0},{2,3},{3,2},{4,5},{5,4},{6,7},{7,6},{8,9},{9,8},{10,11... | collective-permute-start | bytes 1769480 | tf_op jit(solution)/shard_map/total/ppermute | solution.py:520
  82.2 0.0 collective-permute-done.5.down_other
  82.2 1.6 %collective-permute-done.4.conv_other = bf16[1152,256]{1,0:T(8,128)(2,1)S(1)} collective-permute-done((bf16[1152,256]{1,0:T(8,128)(2,1)S(1)}, bf16[1152,256]{1,0:T(8,128)(2,1)S(1)}, u32[]{:S(2)}, u32[]{:S(2)}) %collective-permute-start.4) | collective-permute-done | bytes 589856 | tf_op jit(solution)/shard_map/total/ppermute | solution.py:520
  83.8 1.1 total.3
  84.9 0.0 copy-start.4
  84.9 4.1 %all-to-all-start.3 = ((bf16[32,72,256]{2,1,0:T(8,128)(2,1)}), bf16[32,72,256]{2,1,0:T(8,128)(2,1)S(1)}, u32[]{:S(2)}, u32[]{:S(2)}) async-start(bf16[32,72,256]{2,1,0:T(8,128)(2,1)} %bitcast.21), calls=%async_computation.3 | async-start | bytes 2359296 | tf_op jit(solution)/shard_map/total/all_to_all | solution.py:676
  89.0 0.0 copy-start.5
  89.0 1.3 copy-done.5
  90.3 2.3 %input.1 = bf16[8,128,256]{2,1,0:T(8,128)(2,1)} custom-call(bf16[10,64,1024]{2,1,0:T(8,128)(2,1)S(1)} %copy-done.5, bf16[3,3,256,256]{3,2,1,0:T(8,128)(2,1)S(1)} %copy-done.4), custom_call_target="tpu_custom_call" | custom-call | flops 1207959552 | bytes 1048576 | tf_op jit(solution)/shard_map/input/pallas_call | solution.py:661
  92.6 13.6 %all-to-all-done.3 = bf16[32,72,256]{2,1,0:T(8,128)(2,1)S(1)} async-done(((bf16[32,72,256]{2,1,0:T(8,128)(2,1)}), bf16[32,72,256]{2,1,0:T(8,128)(2,1)S(1)}, u32[]{:S(2)}, u32[]{:S(2)}) %all-to-all-start.3) | async-done | bytes 1179680 | tf_op jit(solution)/shard_map/total/all_to_all | solution.py:676
  106.2 0.2 reduce_sum.21
  106.4 9.8 %all_to_all.31 = bf16[4,72,256]{2,1,0:T(8,128)(2,1)S(1)} all-to-all(bf16[4,72,256]{2,1,0:T(8,128)(2,1)S(1)} %broadcast_in_dim.4), channel_id=1, replica_groups=mesh['x'=4,'z_hi'=4,'z_lo'=2,'y_hi'=2,'y_lo'=2,'core'=2] {'z_hi'}, dimensions={0} | all-to-all | bytes 294912 | tf_op jit(solution)/shard_map/total/all_to_all | solution.py:679
  116.2 0.1 broadcast_in_dim.5
  116.3 20.3 %all_to_all.32 = bf16[32,72,256]{2,1,0:T(8,128)(2,1)S(1)} all-to-all(bf16[32,72,256]{2,1,0:T(8,128)(2,1)S(1)} %broadcast_in_dim.5), channel_id=1, replica_groups=mesh['x'=4,'z_hi'=4,'z_lo'=2,'y_hi'=2,'y_lo'=2,'core'=2] {'x','z_lo','y_..., dimensions={0} | all-to-all | bytes 2359296 | tf_op jit(solution)/shard_map/total/all_to_all | solution.py:681
  136.6 4.6 %collective-permute-start.6 = (bf16[2304,256]{1,0:T(8,128)(2,1)S(1)}, bf16[2304,256]{1,0:T(8,128)(2,1)S(1)}, u32[]{:S(2)}, u32[]{:S(2)}) collective-permute-start(bf16[2304,256]{1,0:T(8,128)(2,1)S(1)} %bitcast.13), channel_id=1, source_target_pairs={{0,1},{1,0},{2,3},{3,2},{4,5},{5,4},{6,7},{7,6},{8,9},{9,8},{10,11... | collective-permute-start | bytes 3538952 | tf_op jit(solution)/shard_map/total/ppermute | solution.py:520
  141.2 0.6 fusion
  141.8 2.0 %total.4 = (f32[2304,256]{1,0:T(8,128)}, f32[2304,256]{1,0:T(8,128)}) custom-call(s32[3]{0:T(128)S(1)} %add_convert_fusion.flags, bf16[2304,256]{1,0:T(8,128)(2,1)S(1)} %bitcast.14), custom_call_target="tpu_custom_call" | custom-call | bytes 1048576 | tf_op jit(solution)/shard_map/total/pallas_call | solution.py:686
  143.8 0.0 collective-permute-done.6.rows
  143.8 2.0 %total.5 = (f32[2304,256]{1,0:T(8,128)}, f32[2304,256]{1,0:T(8,128)}) custom-call(s32[3]{0:T(128)S(1)} %add_convert_fusion.flags, bf16[2304,256]{1,0:T(8,128)(2,1)S(1)} %collective-permute-done.6.rows, f32[2304,256]{1,0:T(8,128)} %get-tuple-element.71.conv_in, f32[2304,256]{1,0:T(8,128)} %get-tuple-element.72.down_in), custom_call_target="tpu_custom_call", output_to_operand_aliasing={{0}: (2, {}), {1}: (3, {})} | custom-call | bytes 1048576 | tf_op jit(solution)/shard_map/total/pallas_call | solution.py:687
  (7 shorter events, 0.0 us)
Async XLA Ops:
  1.6 12.4 %collective-permute-start = (bf16[32,256]{1,0:T(8,128)(2,1)S(1)}, bf16[32,256]{1,0:T(8,128)(2,1)S(1)}, u32[]{:S(2)}, u32[]{:S(2)}) collective-permute-start(bf16[32,256]{1,0:T(8,128)(2,1)S(1)} %get-tuple-element.41), channel_id=1, source_target_pairs={{0,4},{4,8},{8,12},{12,16},{16,20},{20,24},{24,28},{28,32},{32,36}... | collective-permute-start | bytes 49160 | tf_op jit(solution)/shard_map/halo/ppermute | solution.py:477
  5.4 8.6 %collective-permute-start.1 = (bf16[32,256]{1,0:T(8,128)(2,1)S(1)}, bf16[32,256]{1,0:T(8,128)(2,1)S(1)}, u32[]{:S(2)}, u32[]{:S(2)}) collective-permute-start(bf16[32,256]{1,0:T(8,128)(2,1)S(1)} %get-tuple-element.42), channel_id=1, source_target_pairs={{0,252},{4,0},{8,4},{12,8},{16,12},{20,16},{24,20},{28,24},{32,28}... | collective-permute-start | bytes 49160 | tf_op jit(solution)/shard_map/halo/ppermute | solution.py:477
  15.6 6.6 %collective-permute-start.2 = (bf16[336,256]{1,0:T(8,128)(2,1)S(1)}, bf16[336,256]{1,0:T(8,128)(2,1)S(1)}, u32[]{:S(2)}, u32[]{:S(2)}) collective-permute-start(bf16[336,256]{1,0:T(8,128)(2,1)S(1)} %get-tuple-element.43), channel_id=1, source_target_pairs={{0,1},{1,0},{2,3},{3,2},{4,5},{5,4},{6,7},{7,6},{8,9},{9,8},{10,11... | collective-permute-start | bytes 516104 | tf_op jit(solution)/shard_map/halo/ppermute | solution.py:562
  17.2 6.7 %collective-permute-start.3 = (bf16[336,256]{1,0:T(8,128)(2,1)S(1)}, bf16[336,256]{1,0:T(8,128)(2,1)S(1)}, u32[]{:S(2)}, u32[]{:S(2)}) collective-permute-start(bf16[336,256]{1,0:T(8,128)(2,1)S(1)} %get-tuple-element.44), channel_id=1, source_target_pairs={{1,2},{2,1},{5,6},{6,5},{9,10},{10,9},{13,14},{14,13},{17,18},{18,... | collective-permute-start | bytes 516104 | tf_op jit(solution)/shard_map/halo/ppermute | solution.py:564
  23.9 14.7 %copy-start = (bf16[3,3,256,256]{3,2,1,0:T(8,128)(2,1)S(1)}, bf16[3,3,256,256]{3,2,1,0:T(8,128)(2,1)}, u32[]{:S(2)}) copy-start(bf16[3,3,256,256]{3,2,1,0:T(8,128)(2,1)} %dw.1) | copy-start | bytes 3538948
  23.9 14.7 %copy-start.1 = (bf16[4,64,256]{2,1,0:T(8,128)(2,1)S(1)}, bf16[4,64,256]{2,1,0:T(8,128)(2,1)}, u32[]{:S(2)}) copy-start(bf16[4,64,256]{2,1,0:T(8,128)(2,1)} %cot.3) | copy-start | bytes 393220
  28.4 23.0 %copy-start.2 = (f32[256]{0:T(256)S(1)}, f32[256]{0:T(256)}, u32[]{:S(2)}) copy-start(f32[256]{0:T(256)} %param.10) | copy-start | bytes 3076
  28.4 23.0 %copy-start.3 = (f32[256]{0:T(256)S(1)}, f32[256]{0:T(256)}, u32[]{:S(2)}) copy-start(f32[256]{0:T(256)} %param.9) | copy-start | bytes 3076
  28.4 23.0 %all-to-all-start = ((f32[256,1,128]{2,1,0:T(1,128)}), f32[256,1,128]{2,1,0:T(1,128)S(1)}, u32[]{:S(2)}, u32[]{:S(2)}) async-start(f32[256,1,128]{2,1,0:T(1,128)} %get-tuple-element.48), calls=%async_computation | async-start | bytes 262144 | tf_op jit(solution)/shard_map/conv/all_to_all | solution.py:601
  63.0 12.7 %all-to-all-start.2 = ((f32[32,4,128]{2,1,0:T(4,128)}), f32[32,4,128]{2,1,0:T(4,128)S(1)}, u32[]{:S(2)}, u32[]{:S(2)}) async-start(f32[32,4,128]{2,1,0:T(4,128)} %act.3), calls=%async_computation.2 | async-start | bytes 131072 | tf_op jit(solution)/shard_map/act/all_to_all | solution.py:627
  70.1 12.1 %collective-permute-start.5 = (bf16[1152,256]{1,0:T(8,128)(2,1)S(1)}, bf16[1152,256]{1,0:T(8,128)(2,1)S(1)}, u32[]{:S(2)}, u32[]{:S(2)}) collective-permute-start(bf16[1152,256]{1,0:T(8,128)(2,1)S(1)} %get-tuple-element.67), channel_id=1, source_target_pairs={{0,1},{1,0},{2,3},{3,2},{4,5},{5,4},{6,7},{7,6},{8,9},{9,8},{10,11... | collective-permute-start | bytes 1769480 | tf_op jit(solution)/shard_map/down/ppermute | solution.py:520
  80.2 3.6 %collective-permute-start.4 = (bf16[1152,256]{1,0:T(8,128)(2,1)S(1)}, bf16[1152,256]{1,0:T(8,128)(2,1)S(1)}, u32[]{:S(2)}, u32[]{:S(2)}) collective-permute-start(bf16[1152,256]{1,0:T(8,128)(2,1)S(1)} %get-tuple-element.65), channel_id=1, source_target_pairs={{0,1},{1,0},{2,3},{3,2},{4,5},{5,4},{6,7},{7,6},{8,9},{9,8},{10,11... | collective-permute-start | bytes 1769480 | tf_op jit(solution)/shard_map/total/ppermute | solution.py:520
  84.9 4.1 %copy-start.4 = (bf16[3,3,256,256]{3,2,1,0:T(8,128)(2,1)S(1)}, bf16[3,3,256,256]{3,2,1,0:T(8,128)(2,1)}, u32[]{:S(2)}) copy-start(bf16[3,3,256,256]{3,2,1,0:T(8,128)(2,1)} %w.1) | copy-start | bytes 3538948
  84.9 21.3 %all-to-all-start.3 = ((bf16[32,72,256]{2,1,0:T(8,128)(2,1)}), bf16[32,72,256]{2,1,0:T(8,128)(2,1)S(1)}, u32[]{:S(2)}, u32[]{:S(2)}) async-start(bf16[32,72,256]{2,1,0:T(8,128)(2,1)} %bitcast.21), calls=%async_computation.3 | async-start | bytes 2359296 | tf_op jit(solution)/shard_map/total/all_to_all | solution.py:676
  89.0 1.3 copy-start.5
  136.6 7.2 %collective-permute-start.6 = (bf16[2304,256]{1,0:T(8,128)(2,1)S(1)}, bf16[2304,256]{1,0:T(8,128)(2,1)S(1)}, u32[]{:S(2)}, u32[]{:S(2)}) collective-permute-start(bf16[2304,256]{1,0:T(8,128)(2,1)S(1)} %bitcast.13), channel_id=1, source_target_pairs={{0,1},{1,0},{2,3},{3,2},{4,5},{5,4},{6,7},{7,6},{8,9},{9,8},{10,11... | collective-permute-start | bytes 3538952 | tf_op jit(solution)/shard_map/total/ppermute | solution.py:520

commit v6 on v5

--- a/solution.py
+++ b/solution.py
@@ -78,7 +78,7 @@
     return odd, even
 
 
-def pack_lon(feat_hbm, cot_hbm, east, west, feat, cot, f32s, sems):
+def pack_lon(feat_hbm, cot_hbm, out, feat, cot, f32s, sems):
     rows, cols, chans = feat_hbm.shape
     half, pairs, _ = cot_hbm.shape
     copies = []
@@ -90,15 +90,22 @@
     f32s[...] = jnp.zeros(f32s.shape, F32)
     for copy in copies:
         copy.wait()
-    for k, (out, at_f, at_c) in enumerate(((east, 14, 15), (west, 0, 0))):
+    for k, (at_f, at_c) in enumerate(((14, 15), (0, 0))):
         for r in range(rows):
             f32s[2 * r : 2 * r + 2] = feat[k, r].astype(F32)[at_f : at_f + 2]
         for i in range(half):
             f32s[2 * rows + i : 2 * rows + i + 1] = cot[k, i].astype(F32)[at_c : at_c + 1]
-        out[...] = f32s[...].astype(BF)
-
-
-def pack_lat(flags, feat, cot, west, east, near, far, w32, e32, corner, sems):
+        out[k] = f32s[...].astype(BF)
+
+
+def columns(flags, pair, next_pair, part=slice(None)):
+    low = flags[3] == 0
+    west = jnp.where(low, next_pair[0, :, part].astype(F32), pair[0, :, part].astype(F32))
+    east = jnp.where(low, pair[1, :, part].astype(F32), next_pair[1, :, part].astype(F32))
+    return west, east
+
+
+def pack_lat(flags, feat, cot, pair, next_pair, near, far, w32, e32, corner, sems):
     rows, cols, _ = feat.shape
     half, pairs, _ = cot.shape
     core = flags[2]
@@ -110,8 +117,7 @@
         for src, o, n in parts:
             copies.append(pltpu.make_async_copy(src, dest.at[o : o + n], sems.at[len(copies)]))
             copies[-1].start()
-    w32[...] = west[...].astype(F32)
-    e32[...] = east[...].astype(F32)
+    w32[...], e32[...] = columns(flags, pair, next_pair)
     corner[...] = jnp.zeros(corner.shape, F32)
     for k, (top, mid) in enumerate(((rows - 2, half - 1), (0, 0))):
         corner[k, 0:4] = w32[2 * top : 2 * top + 4]
@@ -145,7 +151,29 @@
                 x_out[r, :, lane : lane + 128] = f32s[r, v, pl.ds(14 + k, J, stride=2), :].astype(BF)
 
 
-def inner_kernel(feat_hbm, west, east, w_hbm, x_hbm, rim, hq_out, he_out, f32s, edge, x_out, feat, w, sems):
+def moments(planes, cols):
+    chans = planes[0][0].shape[2]
+    sums = jnp.zeros((1, chans), F32)
+    for (ref, rows), mask in zip(planes, masks()):
+        part = jnp.zeros((J, chans), F32)
+        for r in rows:
+            part = part + ref[r].astype(F32)
+        sums = sums + jnp.sum(part * mask, axis=0, keepdims=True)
+    (total,) = spread_dot(table(chans, chans, WIDTH, WIDTH, 0), sums)
+    mean = total / (len(planes[0][1]) * cols * WIDTH)
+    squares = jnp.zeros((1, chans), F32)
+    for (ref, rows), mask in zip(planes, masks()):
+        part = jnp.zeros((J, chans), F32)
+        for r in rows:
+            d = ref[r].astype(F32) - mean
+            part = part + d * d
+        squares = squares + jnp.sum(part * mask, axis=0, keepdims=True)
+    return sums, squares
+
+
+def inner_kernel(
+    flags, feat_hbm, pair, next_pair, w_hbm, x_hbm, rim, hq_out, he_out, vec_out, f32s, edge, x_out, feat, w, sems
+):
     rows, cols, chans = feat.shape
     pairs = cols // 2
     load_f = pltpu.make_async_copy(feat_hbm, feat, sems.at[1])
@@ -155,8 +183,7 @@
     f32s[:, :, 16 + cols : 56 + cols] = jnp.zeros((rows, 2, 40, 128), F32)
     for v in range(2):
         part = slice(v * 128, v * 128 + 128)
-        for k, side in enumerate((west, east)):
-            edge[k, v] = side[:, part].astype(F32)
+        edge[0, v], edge[1, v] = columns(flags, pair, next_pair, part)
         for r in range(rows):
             f32s[r, v, 14:16] = edge[0, v, 2 * r : 2 * r + 2]
             f32s[r, v, 16 + cols : 18 + cols] = edge[1, v, 2 * r : 2 * r + 2]
@@ -177,11 +204,14 @@
             term = dot(lhs, w[a])
             acc = term if acc is None else acc + term
         out[...] = acc.astype(BF).reshape(n, J, chans)
+    sums, squares = moments(((hq_out, range(n)), (he_out, range(n))), cols)
+    vec_out[0:1] = sums
+    vec_out[1:2] = squares
     keep.wait()
 
 
 def outer_kernel(
-    cols, flags, near, far, rim, hq_in, he_in, w_hbm, x_hbm, h_hbm, hq_out, he_out, stat_out, f32s, edge, x_out, w, sems
+    cols, flags, near, far, rim, hq_in, he_in, vec, w_hbm, x_hbm, h_hbm, hq_out, he_out, stat_out, f32s, edge, x_out, w, sems
 ):
     rows = hq_in.shape[0] + 2
     chans = hq_in.shape[2]
@@ -223,26 +253,15 @@
         out[rows : rows + 2] = value[2:4]
         copies.append(pltpu.make_async_copy(out, h_hbm.at[k], sems.at[3 + k]))
         copies[-1].start()
-    odd, even = masks()
-    sums = jnp.zeros((1, chans), F32)
-    for out, mask in ((hq_out, odd), (he_out, even)):
-        part = jnp.zeros((J, chans), F32)
-        for r in range(1, rows + 1):
-            part = part + out[r].astype(F32)
-        sums = sums + jnp.sum(part * mask, axis=0, keepdims=True)
-    n = rows * cols * WIDTH
-    (total,) = spread_dot(table(chans, chans, WIDTH, WIDTH, 0), sums)
-    mean = total / n
-    squares = jnp.zeros((1, chans), F32)
-    for out, mask in ((hq_out, odd), (he_out, even)):
-        part = jnp.zeros((J, chans), F32)
-        for r in range(1, rows + 1):
-            d = out[r].astype(F32) - mean
-            part = part + d * d
-        squares = squares + jnp.sum(part * mask, axis=0, keepdims=True)
-    (means,) = spread_dot(table(chans, 128, WIDTH, 1, 0), sums)
-    (spreads,) = spread_dot(table(chans, 128, WIDTH, 1, -32), squares)
-    stat = means / n + spreads
+    edges = (1, rows)
+    sums, squares = moments(((hq_out, edges), (he_out, edges)), cols)
+    n_in = (rows - 2) * cols * WIDTH
+    n_out = 2 * cols * WIDTH
+    n = n_in + n_out
+    gap = vec[0:1] / n_in - sums / n_out
+    (means,) = spread_dot(table(chans, 128, WIDTH, 1, 0), vec[0:1] + sums)
+    within, gaps = spread_dot(table(chans, 128, WIDTH, 1, -32), vec[1:2] + squares, gap)
+    stat = means / n + within + (n_in * n_out / n) * gaps * gaps
     stat_out[...] = jnp.broadcast_to(stat[None], stat_out.shape)
     for copy in copies:
         copy.wait()
@@ -252,13 +271,12 @@
     out[...] = jnp.broadcast_to(jnp.sum(rec[...], axis=0)[None], out.shape)
 
 
-def back_kernel(flags, cot, west, east, near, far, dw, c_hbm, aq_out, ae_out, f32s, edge, c_out, sems):
+def back_kernel(flags, cot, pair, next_pair, near, far, dw, c_hbm, aq_out, ae_out, f32s, edge, c_out, sems):
     half, pairs, chans = cot.shape
     rows = 2 * half
     cols = 2 * pairs
     f32s[:, 16 + pairs :] = jnp.zeros((half + 2, 16, chans), F32)
-    for k, side in enumerate((west, east)):
-        edge[k] = side[...].astype(F32)
+    edge[0], edge[1] = columns(flags, pair, next_pair)
     every = slice(None)
     for k, side in enumerate(sides(flags, near, far)):
         row = k * (half + 1)
@@ -471,10 +489,13 @@
         out[:, :, v * 128 : v * 128 + 128] = f32s[:, v, 0:cols].astype(BF)
 
 
-def passed(value, axes, step, wrap):
-    n = lax.axis_size(axes)
-    pairs = [(i, (i + step) % n) for i in range(n) if wrap or 0 <= i + step < n]
-    return lax.ppermute(value, axes, pairs)
+def ring_total(value, axis):
+    n = lax.axis_size(axis)
+    total = value.astype(F32)
+    if n == 1:
+        return total
+    after, across, before = (lax.ppermute(value, axis, [(i, (i + k) % n) for i in range(n)]).astype(F32) for k in (1, 2, 3))
+    return (total + across) + (after + before)
 
 
 def join_kernel(conv_keep, conv_other, down_keep, down_other, out, both, sems):
@@ -494,15 +515,15 @@
 
 def unpack_rows(core, rows, conv, down, f32s, sems):
     n = rows.shape[0] // 2
-    step = n // 2
+    step = n // 6
     base = pl.multiple_of(core * n, n)
     copies = []
     for k, dst in enumerate((conv, down)):
-        for q in range(2):
+        for q in range(6):
             o = k * n + q * step
             f32s[o : o + step] = rows[o : o + step].astype(F32)
             part = dst.at[pl.ds(base + q * step, step)]
-            copies.append(pltpu.make_async_copy(f32s.at[o : o + step], part, sems.at[k * 2 + q]))
+            copies.append(pltpu.make_async_copy(f32s.at[o : o + step], part, sems.at[k * 6 + q]))
             copies[-1].start()
     for copy in copies:
         copy.wait()
@@ -528,7 +549,8 @@
     cells = rows * cols * devices
     factor = 1.0 / math.sqrt(cells)
     lat = lax.axis_index(LAT)
-    flags = jnp.stack([lat == 0, lat == lats - 1, lax.axis_index("core") == 1]).astype(jnp.int32)
+    odd = lax.axis_index(LON) % 2 == 1
+    flags = jnp.stack([lat == 0, lat == lats - 1, lax.axis_index("core") == 1, odd]).astype(jnp.int32)
     gain = norm_gain.reshape(1, chans)
     bias = norm_bias.reshape(1, chans)
     w3 = conv_weight.reshape(3, 3 * chans, chans)
@@ -539,16 +561,17 @@
 
     with jax.named_scope("halo"):
         slab = (2 * rows + 16, chans)
-        to_east, to_west = call(
+        (edges,) = call(
             pack_lon,
-            [(slab, BF)] * 2,
+            [((2,) + slab, BF)],
             [((2, rows, 16, chans), BF), ((2, half, 16, chans), BF), (slab, F32)],
             n_in=2,
             hbm=(0, 1),
             sems=4,
         )(pinned(features), pinned(cotangent))
-        west = passed(to_east, LON, 1, True)
-        east = passed(to_west, LON, -1, True)
+        lons = lax.axis_size(LON)
+        pair = lax.ppermute(edges, LON, [(i, i ^ 1) for i in range(lons)])
+        next_pair = lax.ppermute(edges, LON, [(i, (i + 2 * (i % 2) - 1) % lons) for i in range(lons)])
         strip = (2 * cols + pairs + 16, chans)
         to_near, to_far = call(
             pack_lat,
@@ -558,7 +581,7 @@
             smem=(0,),
             hbm=(1, 2),
             sems=6,
-        )(flags, pinned(features), pinned(cotangent), west, east)
+        )(flags, pinned(features), pinned(cotangent), pair, next_pair)
         near = lax.ppermute(to_near, LAT, [(i, i ^ 1) for i in range(lats)])
         gaps = range(1, lats - 1, 2)
         far = lax.ppermute(to_far, LAT, [(i, i + 1) for i in gaps] + [(i + 1, i) for i in gaps])
@@ -568,9 +591,9 @@
     rim_shape = (2, pairs, 4 * chans)
     inner_plane = (rows - 2, J, chans)
     with jax.named_scope("conv"):
-        x, rim, hq_in, he_in = call(
+        x, rim, hq_in, he_in, vec = call(
             inner_kernel,
-            [(x_shape, BF, True), ((4, J, 4 * chans), BF), (inner_plane, BF), (inner_plane, BF)],
+            [(x_shape, BF, True), ((4, J, 4 * chans), BF), (inner_plane, BF), (inner_plane, BF), ((2, chans), F32)],
             [
                 ((rows, 2, cols + 56, 128), F32),
                 ((2, 2, slab[0], 128), F32),
@@ -579,10 +602,11 @@
                 (w3.shape, BF),
             ],
             flops=2 * 960 * 2304 * 256,
-            n_in=4,
-            hbm=(0, 3),
+            n_in=5,
+            smem=(0,),
+            hbm=(1, 4),
             sems=3,
-        )(pinned(features), west, east, pinned(w3))
+        )(flags, pinned(features), pair, next_pair, pinned(w3))
         x_rim, h, hq, he, stat = call(
             functools.partial(outer_kernel, cols),
             [(rim_shape, BF, True), ((2,) + plane, BF, True), (plane, BF), (plane, BF), ((devices, 1, 128), F32)],
@@ -593,11 +617,11 @@
                 (w3.shape, BF),
             ],
             flops=2 * 640 * 2304 * 256,
-            n_in=7,
+            n_in=8,
             smem=(0,),
-            hbm=(6,),
+            hbm=(7,),
             sems=5,
-        )(flags, near, far, rim, hq_in, he_in, pinned(w3))
+        )(flags, near, far, rim, hq_in, he_in, vec, pinned(w3))
         stats = lax.all_to_all(stat, ALL, 0, 0, tiled=True)
     c_shape = (half + 2, J, 2 * chans)
     with jax.named_scope("back"):
@@ -609,7 +633,7 @@
             n_in=7,
             smem=(0,),
             sems=1,
-        )(flags, cotangent, west, east, near, far, down_weight)
+        )(flags, cotangent, pair, next_pair, near, far, down_weight)
     t_shape = (rows + 1, pairs, 3 * chans)
     with jax.named_scope("act"):
         t, p, coef, sums = call(
@@ -671,21 +695,19 @@
             join_kernel, [(whole_rows, BF, True)], [(whole_rows, BF)], n_in=4, sems=4
         )(conv_keep, core_swap(conv_send), down_keep, down_other)
         chips = lax.axis_size(NEAR)
-        depth = lax.axis_size("z_hi")
         share = all_rows // chips
         got = lax.all_to_all(mine.reshape(chips, share, chans), NEAR, 0, 0, tiled=True)
         got, input_grad = lax.optimization_barrier((got, input_grad))
         piece = jnp.sum(got.astype(F32), axis=0).astype(BF)
-        got = lax.all_to_all(jnp.broadcast_to(piece[None], (depth, share, chans)), "z_hi", 0, 0, tiled=True)
-        piece = (jnp.sum(got.astype(F32), axis=0) * factor).astype(BF)
+        piece = (ring_total(piece, "z_hi") * factor).astype(BF)
         whole = lax.all_to_all(jnp.broadcast_to(piece[None], (chips, share, chans)), NEAR, 0, 0, tiled=True)
         whole = whole.reshape(all_rows, chans)
         other = core_swap(whole)
         flat = (whole_rows, F32, True)
         room = [(whole_rows, F32)]
-        conv_grad, down_grad = call(unpack_own, [flat, flat], room, smem=(0,), n_in=2, sems=4)(flags, whole)
+        conv_grad, down_grad = call(unpack_own, [flat, flat], room, smem=(0,), n_in=2, sems=12)(flags, whole)
         conv_grad, down_grad = call(
-            unpack_other, [flat, flat], room, smem=(0,), hbm=(2, 3), n_in=4, sems=4, aliases={2: 0, 3: 1}
+            unpack_other, [flat, flat], room, smem=(0,), hbm=(2, 3), n_in=4, sems=12, aliases={2: 0, 3: 1}
         )(flags, other, pinned(conv_grad), pinned(down_grad))
     shape = (3, 3, chans, chans)
     return output, input_grad, conv_grad.reshape(shape), down_grad.reshape(shape), vec[0], vec[1]

time: 147 us -> 146 us (level)
  blocking collectives: 37.5 us -> 27.7 us
  waiting for transfers between devices: 33.3 us -> 40.9 us
    all_to_all x1 -> x0, blocking collectives: 9.76 us -> none  [local(): lax.all_to_all(jnp.broadcast_to(piece[None], (depth, share, chans)), 'z_h...]
    ppermute x2 -> x5, waiting for transfers between devices: 0.97 us -> 9.36 us  [the longest x3 5.17 us: ring_total(): lax.ppermute(value, axis, [(i, (i + k) % n) for i in range(n)]).astype(F32)]
    ppermute x2 -> x5, starting transfers between devices: 11.4 us -> 15.4 us  [the longest x1 11.3 us: local(): lax.ppermute(edges, LON, [(i, (i + 2 * (i % 2) - 1) % lons) for i in rang...]
    all_to_all x1, starting transfers between devices: 10.2 us -> 6.22 us  [local(): stats = lax.all_to_all(stat, ALL, 0, 0, tiled=True)]
  transfers between devices with their start and end apart: 10 -> 13, of which waited for: 6 -> 9; matrix products, arithmetic and copies ran while one was open for 0% -> 0% of each run, Pallas kernels for 11% -> 12%
where the time goes in v6:
time: 146 us; the launch traced here: 145 us
  starting transfers between devices  41.5 us (28%)
  waiting for transfers between devices  40.9 us (28%)
  Pallas kernels  31.7 us (22%)
  blocking collectives  27.7 us (19%)
  local copies, waits for them, and re-layouts  1.99 us (1%)
    all_to_all x1, blocking collectives, local(): lax.all_to_all(jnp.broadcast_to(piece[None], (chips, share, chans)), NEAR...  20.3 us
    all_to_all x1, waiting for transfers between devices, local(): lax.all_to_all(mine.reshape(chips, share, chans), NEAR, 0, 0, tiled=True)  13.6 us
    ppermute x1, starting transfers between devices, local(): lax.ppermute(edges, LON, [(i, (i + 2 * (i % 2) - 1) % lons) for i in rang...  11.3 us
    all_to_all x1, waiting for transfers between devices, local(): stats = lax.all_to_all(stat, ALL, 0, 0, tiled=True)  10.9 us
    ppermute x3, starting transfers between devices, core_swap(): return lax.ppermute(value, 'core', [(0, 1), (1, 0)])  7.59 us
    all_to_all x1, blocking collectives, local(): sums = lax.all_to_all(sums, FEW, 0, 0, tiled=True)  7.45 us
    all_to_all x1, starting transfers between devices, local(): stats = lax.all_to_all(stat, ALL, 0, 0, tiled=True)  6.22 us
    ppermute x3, waiting for transfers between devices, ring_total(): lax.ppermute(value, axis, [(i, (i + k) % n) for i in range(n)]).astype(F32)  5.17 us
  transfers between devices with their start and end apart: 13, of which 9 were waited for; matrix products, arithmetic and copies ran while one was open for 0% of the time, Pallas kernels for 12%

profile of v6, /device:TPU:1, one launch (start us, length us, event | category | flops | bytes accessed | tf_op | source)
XLA Modules:
  0.0 145.1 jit_solution(17397245640865709999)
XLA Ops:
  0.6 1.0 halo.2
  1.6 11.3 %collective-permute-start.1 = (bf16[2,32,256]{2,1,0:T(8,128)(2,1)S(1)}, bf16[2,32,256]{2,1,0:T(8,128)(2,1)S(1)}, u32[]{:S(2)}, u32[]{:S(2)}) collective-permute-start(bf16[2,32,256]{2,1,0:T(8,128)(2,1)S(1)} %halo.2), channel_id=1, source_target_pairs={{0,252},{4,8},{8,4},{12,16},{16,12},{20,24},{24,20},{28,32},{32,28... | collective-permute-start | bytes 98312 | tf_op jit(solution)/shard_map/halo/ppermute | solution.py:574
  12.9 0.0 collective-permute-start
  12.9 0.1 add_convert_fusion.flags
  13.0 1.2 collective-permute-done.1.next_pair
  14.2 3.0 %collective-permute-done.pair = bf16[2,32,256]{2,1,0:T(8,128)(2,1)S(1)} collective-permute-done((bf16[2,32,256]{2,1,0:T(8,128)(2,1)S(1)}, bf16[2,32,256]{2,1,0:T(8,128)(2,1)S(1)}, u32[]{:S(2)}, u32[]{:S(2)}) %collective-permute-start) | collective-permute-done | bytes 32800 | tf_op jit(solution)/shard_map/halo/ppermute | solution.py:573
  17.2 1.6 %halo.3 = (bf16[336,256]{1,0:T(8,128)(2,1)S(1)}, bf16[336,256]{1,0:T(8,128)(2,1)S(1)}) custom-call(s32[4]{0:T(128)S(1)} %add_convert_fusion.flags, bf16[8,128,256]{2,1,0:T(8,128)(2,1)} %feat_hbm.3, bf16[4,64,256]{2,1,0:T(8,128)(2,1)} %cot.3, bf16[2,32,256]{2,1,0:T(8,128)(2,1)S(1)} %collective-permute-done.pair, ...), custom_call_target="tpu_custom_call" | custom-call | bytes 1048576 | tf_op jit(solution)/shard_map/halo/pallas_call | solution.py:576
  18.7 2.2 %collective-permute-start.2 = (bf16[336,256]{1,0:T(8,128)(2,1)S(1)}, bf16[336,256]{1,0:T(8,128)(2,1)S(1)}, u32[]{:S(2)}, u32[]{:S(2)}) collective-permute-start(bf16[336,256]{1,0:T(8,128)(2,1)S(1)} %get-tuple-element.40), channel_id=1, source_target_pairs={{0,1},{1,0},{2,3},{3,2},{4,5},{5,4},{6,7},{7,6},{8,9},{9,8},{10,11... | collective-permute-start | bytes 516104 | tf_op jit(solution)/shard_map/halo/ppermute | solution.py:585
  20.9 2.2 %collective-permute-start.3 = (bf16[336,256]{1,0:T(8,128)(2,1)S(1)}, bf16[336,256]{1,0:T(8,128)(2,1)S(1)}, u32[]{:S(2)}, u32[]{:S(2)}) collective-permute-start(bf16[336,256]{1,0:T(8,128)(2,1)S(1)} %get-tuple-element.41), channel_id=1, source_target_pairs={{1,2},{2,1},{5,6},{6,5},{9,10},{10,9},{13,14},{14,13},{17,18},{18,... | collective-permute-start | bytes 516104 | tf_op jit(solution)/shard_map/halo/ppermute | solution.py:587
  23.1 3.6 %conv.2 = (bf16[8,64,1024]{2,1,0:T(8,128)(2,1)}, bf16[4,80,1024]{2,1,0:T(8,128)(2,1)S(1)}, bf16[6,80,256]{2,1,0:T(8,128)(2,1)S(1)}, bf16[6,80,256]{2,1,0:T(8,128)(2,1)S(1)}, f32[2,256]{1,0:T(2,128)S(1)}) custom-call(s32[4]{0:T(128)S(1)} %add_convert_fusion.flags, bf16[8,128,256]{2,1,0:T(8,128)(2,1)} %feat_hbm.3, ...), custom_call_target="tpu_custom_call" | custom-call | flops 1132462080 | bytes 1048576 | tf_op jit(solution)/shard_map/conv/pallas_call | solution.py:594
  26.8 0.0 collective-permute-done.2.near
  26.8 0.9 collective-permute-done.3.far
  27.7 4.4 %conv.3 = (bf16[2,64,1024]{2,1,0:T(8,128)(2,1)}, bf16[2,10,80,256]{3,2,1,0:T(8,128)(2,1)}, bf16[10,80,256]{2,1,0:T(8,128)(2,1)S(1)}, bf16[10,80,256]{2,1,0:T(8,128)(2,1)S(1)}, f32[256,1,128]{2,1,0:T(1,128)}) custom-call(s32[4]{0:T(128)S(1)} %add_convert_fusion.flags, bf16[336,256]{1,0:T(8,128)(2,1)S(1)} %collective-permute-done.2.near, ...), custom_call_target="tpu_custom_call" | custom-call | flops 754974720 | bytes 1048576 | tf_op jit(solution)/shard_map/conv/pallas_call | solution.py:610
  32.1 0.0 copy-start.2
  32.1 0.0 copy-start.3
  32.1 6.2 %all-to-all-start = ((f32[256,1,128]{2,1,0:T(1,128)}), f32[256,1,128]{2,1,0:T(1,128)S(1)}, u32[]{:S(2)}, u32[]{:S(2)}) async-start(f32[256,1,128]{2,1,0:T(1,128)} %get-tuple-element.46), calls=%async_computation | async-start | bytes 262144 | tf_op jit(solution)/shard_map/conv/all_to_all | solution.py:625
  38.4 1.8 %back.1 = (bf16[6,80,512]{2,1,0:T(8,128)(2,1)}, bf16[10,80,256]{2,1,0:T(8,128)(2,1)S(1)}, bf16[10,80,256]{2,1,0:T(8,128)(2,1)S(1)}) custom-call(s32[4]{0:T(128)S(1)} %add_convert_fusion.flags, bf16[4,64,256]{2,1,0:T(8,128)(2,1)S(1)} %copy-done.1, bf16[2,32,256]{2,1,0:T(8,128)(2,1)S(1)} %collective-permute-done.pair, ...), custom_call_target="tpu_custom_call" | custom-call | flops 471859200 | bytes 1048576 | tf_op jit(solution)/shard_map/back/pallas_call | solution.py:628
  40.2 10.9 %all-to-all-done.stats = f32[256,1,128]{2,1,0:T(1,128)S(1)} async-done(((f32[256,1,128]{2,1,0:T(1,128)}), f32[256,1,128]{2,1,0:T(1,128)S(1)}, u32[]{:S(2)}, u32[]{:S(2)}) %all-to-all-start) | async-done | bytes 131104 | tf_op jit(solution)/shard_map/conv/all_to_all | solution.py:625
  51.1 3.5 %act.2 = (bf16[9,64,768]{2,1,0:T(8,128)(2,1)}, f32[2,10,80,256]{3,2,1,0:T(8,128)}, f32[2,256]{1,0:T(2,128)S(1)}, f32[8,4,128]{2,1,0:T(4,128)S(1)}) custom-call(s32[4]{0:T(128)S(1)} %add_convert_fusion.flags, f32[256,1,128]{2,1,0:T(1,128)S(1)} %all-to-all-done.stats, bf16[10,80,256]{2,1,0:T(8,128)(2,1)S(1)} %get-tuple-element.47.hq, ...), custom_call_target="tpu_custom_call" | custom-call | flops 8192000 | bytes 1048576 | tf_op jit(solution)/shard_map/act/pallas_call | solution.py:639
  54.6 7.5 %all_to_all.25.rec = f32[8,4,128]{2,1,0:T(4,128)S(1)} all-to-all(f32[8,4,128]{2,1,0:T(4,128)S(1)} %get-tuple-element.52), channel_id=1, replica_groups=mesh['x'=4,'z_hi'=4,'z_lo'=2,'y_hi'=2,'y_lo'=2,'core'=2] {'x','core'}, dimensions={0} | all-to-all | bytes 32768 | tf_op jit(solution)/shard_map/act/all_to_all | solution.py:648
  62.0 0.6 act.3
  62.7 3.8 %all-to-all-start.2 = ((f32[32,4,128]{2,1,0:T(4,128)}), f32[32,4,128]{2,1,0:T(4,128)S(1)}, u32[]{:S(2)}, u32[]{:S(2)}) async-start(f32[32,4,128]{2,1,0:T(4,128)} %act.3), calls=%async_computation.2 | async-start | bytes 131072 | tf_op jit(solution)/shard_map/act/all_to_all | solution.py:651
  66.5 3.3 %down.1 = (bf16[4,64,256]{2,1,0:T(8,128)(2,1)}, f32[1152,256]{1,0:T(8,128)S(1)}, bf16[1152,256]{1,0:T(8,128)(2,1)S(1)}) custom-call(s32[4]{0:T(128)S(1)} %add_convert_fusion.flags, bf16[9,64,768]{2,1,0:T(8,128)(2,1)} %get-tuple-element.51.t_hbm, bf16[6,80,512]{2,1,0:T(8,128)(2,1)} %get-tuple-element.54.c_hbm, bf16[3,768,256]{2,1,0:T(8,128)(2,1)S(1)} %bitcast.16), custom_call_target="tpu_custom_call" | custom-call | flops 603979776 | bytes 1048576 | tf_op jit(solution)/shard_map/down/pallas_call | solution.py:654
  69.8 1.1 collective-permute-start.5
  70.9 4.5 %all-to-all-done.2.sums = f32[32,4,128]{2,1,0:T(4,128)S(1)} async-done(((f32[32,4,128]{2,1,0:T(4,128)}), f32[32,4,128]{2,1,0:T(4,128)S(1)}, u32[]{:S(2)}, u32[]{:S(2)}) %all-to-all-start.2) | async-done | bytes 65568 | tf_op jit(solution)/shard_map/act/all_to_all | solution.py:651
  75.4 4.5 %grad.1 = (bf16[10,64,1024]{2,1,0:T(8,128)(2,1)}, f32[1152,256]{1,0:T(8,128)S(1)}, bf16[1152,256]{1,0:T(8,128)(2,1)S(1)}, f32[2,256]{1,0:T(2,128)S(1)}) custom-call(s32[4]{0:T(128)S(1)} %add_convert_fusion.flags, f32[32,4,128]{2,1,0:T(4,128)S(1)} %all-to-all-done.2.sums, f32[2,256]{1,0:T(2,128)S(1)} %get-tuple-element.57.coef, f32[1,256]{1,0:T(1,128)S(1)} %bitcast.19, ...), custom_call_target="tpu_custom_call" | custom-call | flops 1887436800 | bytes 1048576 | tf_op jit(solution)/shard_map/grad/pallas_call | solution.py:667
  79.9 2.0 %collective-permute-start.4 = (bf16[1152,256]{1,0:T(8,128)(2,1)S(1)}, bf16[1152,256]{1,0:T(8,128)(2,1)S(1)}, u32[]{:S(2)}, u32[]{:S(2)}) collective-permute-start(bf16[1152,256]{1,0:T(8,128)(2,1)S(1)} %get-tuple-element.63), channel_id=1, source_target_pairs={{0,1},{1,0},{2,3},{3,2},{4,5},{5,4},{6,7},{7,6},{8,9},{9,8},{10,11... | collective-permute-start | bytes 1769480 | tf_op jit(solution)/shard_map/total/ppermute | solution.py:541
  81.9 0.0 collective-permute-done.5.down_other
  81.9 1.6 %collective-permute-done.4.conv_other = bf16[1152,256]{1,0:T(8,128)(2,1)S(1)} collective-permute-done((bf16[1152,256]{1,0:T(8,128)(2,1)S(1)}, bf16[1152,256]{1,0:T(8,128)(2,1)S(1)}, u32[]{:S(2)}, u32[]{:S(2)}) %collective-permute-start.4) | collective-permute-done | bytes 589856 | tf_op jit(solution)/shard_map/total/ppermute | solution.py:541
  83.5 1.1 total.3
  84.6 0.0 copy-start.4
  84.6 4.1 %all-to-all-start.3 = ((bf16[32,72,256]{2,1,0:T(8,128)(2,1)}), bf16[32,72,256]{2,1,0:T(8,128)(2,1)S(1)}, u32[]{:S(2)}, u32[]{:S(2)}) async-start(bf16[32,72,256]{2,1,0:T(8,128)(2,1)} %bitcast.22), calls=%async_computation.3 | async-start | bytes 2359296 | tf_op jit(solution)/shard_map/total/all_to_all | solution.py:699
  88.7 0.0 copy-start.5
  88.7 1.3 copy-done.5
  90.0 2.3 %input.1 = bf16[8,128,256]{2,1,0:T(8,128)(2,1)} custom-call(bf16[10,64,1024]{2,1,0:T(8,128)(2,1)S(1)} %copy-done.5, bf16[3,3,256,256]{3,2,1,0:T(8,128)(2,1)S(1)} %copy-done.4), custom_call_target="tpu_custom_call" | custom-call | flops 1207959552 | bytes 1048576 | tf_op jit(solution)/shard_map/input/pallas_call | solution.py:685
  92.3 13.6 %all-to-all-done.3 = bf16[32,72,256]{2,1,0:T(8,128)(2,1)S(1)} async-done(((bf16[32,72,256]{2,1,0:T(8,128)(2,1)}), bf16[32,72,256]{2,1,0:T(8,128)(2,1)S(1)}, u32[]{:S(2)}, u32[]{:S(2)}) %all-to-all-start.3) | async-done | bytes 1179680 | tf_op jit(solution)/shard_map/total/all_to_all | solution.py:699
  105.9 0.2 reduce_sum.12
  106.1 0.4 collective-permute-start.8
  106.5 2.0 %collective-permute-start.7 = (bf16[72,256]{1,0:T(8,128)(2,1)S(1)}, bf16[72,256]{1,0:T(8,128)(2,1)S(1)}, u32[]{:S(2)}, u32[]{:S(2)}) collective-permute-start(bf16[72,256]{1,0:T(8,128)(2,1)S(1)} %reduce_sum.12), channel_id=1, source_target_pairs={{0,16},{16,32},{32,48},{48,0},{1,17},{17,33},{33,49},{49,1},{2,18}... | collective-permute-start | bytes 110600 | tf_op jit(solution)/shard_map/total/ppermute | solution.py:497
  108.5 1.6 %collective-permute-start.6 = (bf16[72,256]{1,0:T(8,128)(2,1)S(1)}, bf16[72,256]{1,0:T(8,128)(2,1)S(1)}, u32[]{:S(2)}, u32[]{:S(2)}) collective-permute-start(bf16[72,256]{1,0:T(8,128)(2,1)S(1)} %reduce_sum.12), channel_id=1, source_target_pairs={{0,32},{16,48},{32,0},{48,16},{1,33},{17,49},{33,1},{49,17},{2,34}... | collective-permute-start | bytes 110600 | tf_op jit(solution)/shard_map/total/ppermute | solution.py:497
  110.2 1.4 collective-permute-done.7
  111.5 3.8 %collective-permute-done.6 = bf16[72,256]{1,0:T(8,128)(2,1)S(1)} collective-permute-done((bf16[72,256]{1,0:T(8,128)(2,1)S(1)}, bf16[72,256]{1,0:T(8,128)(2,1)S(1)}, u32[]{:S(2)}, u32[]{:S(2)}) %collective-permute-start.6) | collective-permute-done | bytes 36896 | tf_op jit(solution)/shard_map/total/ppermute | solution.py:497
  115.4 0.1 broadcast_in_dim.2
  115.4 20.3 %all_to_all.26 = bf16[32,72,256]{2,1,0:T(8,128)(2,1)S(1)} all-to-all(bf16[32,72,256]{2,1,0:T(8,128)(2,1)S(1)} %broadcast_in_dim.2), channel_id=1, replica_groups=mesh['x'=4,'z_hi'=4,'z_lo'=2,'y_hi'=2,'y_lo'=2,'core'=2] {'x','z_lo','y_..., dimensions={0} | all-to-all | bytes 2359296 | tf_op jit(solution)/shard_map/total/all_to_all | solution.py:703
  135.7 4.6 %collective-permute-start.9 = (bf16[2304,256]{1,0:T(8,128)(2,1)S(1)}, bf16[2304,256]{1,0:T(8,128)(2,1)S(1)}, u32[]{:S(2)}, u32[]{:S(2)}) collective-permute-start(bf16[2304,256]{1,0:T(8,128)(2,1)S(1)} %bitcast.14), channel_id=1, source_target_pairs={{0,1},{1,0},{2,3},{3,2},{4,5},{5,4},{6,7},{7,6},{8,9},{9,8},{10,11... | collective-permute-start | bytes 3538952 | tf_op jit(solution)/shard_map/total/ppermute | solution.py:541
  140.3 0.6 fusion
  140.9 2.0 %total.4 = (f32[2304,256]{1,0:T(8,128)}, f32[2304,256]{1,0:T(8,128)}) custom-call(s32[4]{0:T(128)S(1)} %add_convert_fusion.flags, bf16[2304,256]{1,0:T(8,128)(2,1)S(1)} %bitcast.15), custom_call_target="tpu_custom_call" | custom-call | bytes 1048576 | tf_op jit(solution)/shard_map/total/pallas_call | solution.py:708
  142.9 2.0 %total.5 = (f32[2304,256]{1,0:T(8,128)}, f32[2304,256]{1,0:T(8,128)}) custom-call(s32[4]{0:T(128)S(1)} %add_convert_fusion.flags, bf16[2304,256]{1,0:T(8,128)(2,1)S(1)} %collective-permute-done.9.rows, f32[2304,256]{1,0:T(8,128)} %get-tuple-element.69.conv_in, f32[2304,256]{1,0:T(8,128)} %get-tuple-element.70.down_in), custom_call_target="tpu_custom_call", output_to_operand_aliasing={{0}: (2, {}), {1}: (3, {})} | custom-call | bytes 1048576 | tf_op jit(solution)/shard_map/total/pallas_call | solution.py:709
  (10 shorter events, 0.0 us)
Async XLA Ops:
  1.6 12.6 %collective-permute-start.1 = (bf16[2,32,256]{2,1,0:T(8,128)(2,1)S(1)}, bf16[2,32,256]{2,1,0:T(8,128)(2,1)S(1)}, u32[]{:S(2)}, u32[]{:S(2)}) collective-permute-start(bf16[2,32,256]{2,1,0:T(8,128)(2,1)S(1)} %halo.2), channel_id=1, source_target_pairs={{0,252},{4,8},{8,4},{12,16},{16,12},{20,24},{24,20},{28,32},{32,28... | collective-permute-start | bytes 98312 | tf_op jit(solution)/shard_map/halo/ppermute | solution.py:574
  12.9 4.3 %collective-permute-start = (bf16[2,32,256]{2,1,0:T(8,128)(2,1)S(1)}, bf16[2,32,256]{2,1,0:T(8,128)(2,1)S(1)}, u32[]{:S(2)}, u32[]{:S(2)}) collective-permute-start(bf16[2,32,256]{2,1,0:T(8,128)(2,1)S(1)} %halo.2), channel_id=1, source_target_pairs={{0,4},{4,0},{8,12},{12,8},{16,20},{20,16},{24,28},{28,24},{32,36},... | collective-permute-start | bytes 98312 | tf_op jit(solution)/shard_map/halo/ppermute | solution.py:573
  18.7 8.0 %collective-permute-start.2 = (bf16[336,256]{1,0:T(8,128)(2,1)S(1)}, bf16[336,256]{1,0:T(8,128)(2,1)S(1)}, u32[]{:S(2)}, u32[]{:S(2)}) collective-permute-start(bf16[336,256]{1,0:T(8,128)(2,1)S(1)} %get-tuple-element.40), channel_id=1, source_target_pairs={{0,1},{1,0},{2,3},{3,2},{4,5},{5,4},{6,7},{7,6},{8,9},{9,8},{10,11... | collective-permute-start | bytes 516104 | tf_op jit(solution)/shard_map/halo/ppermute | solution.py:585
  20.9 6.7 %collective-permute-start.3 = (bf16[336,256]{1,0:T(8,128)(2,1)S(1)}, bf16[336,256]{1,0:T(8,128)(2,1)S(1)}, u32[]{:S(2)}, u32[]{:S(2)}) collective-permute-start(bf16[336,256]{1,0:T(8,128)(2,1)S(1)} %get-tuple-element.41), channel_id=1, source_target_pairs={{1,2},{2,1},{5,6},{6,5},{9,10},{10,9},{13,14},{14,13},{17,18},{18,... | collective-permute-start | bytes 516104 | tf_op jit(solution)/shard_map/halo/ppermute | solution.py:587
  27.7 10.7 %copy-start = (bf16[3,3,256,256]{3,2,1,0:T(8,128)(2,1)S(1)}, bf16[3,3,256,256]{3,2,1,0:T(8,128)(2,1)}, u32[]{:S(2)}) copy-start(bf16[3,3,256,256]{3,2,1,0:T(8,128)(2,1)} %dw.1) | copy-start | bytes 3538948
  27.7 10.7 %copy-start.1 = (bf16[4,64,256]{2,1,0:T(8,128)(2,1)S(1)}, bf16[4,64,256]{2,1,0:T(8,128)(2,1)}, u32[]{:S(2)}) copy-start(bf16[4,64,256]{2,1,0:T(8,128)(2,1)} %cot.3) | copy-start | bytes 393220
  32.1 19.0 %copy-start.2 = (f32[256]{0:T(256)S(1)}, f32[256]{0:T(256)}, u32[]{:S(2)}) copy-start(f32[256]{0:T(256)} %param.10) | copy-start | bytes 3076
  32.1 19.0 %copy-start.3 = (f32[256]{0:T(256)S(1)}, f32[256]{0:T(256)}, u32[]{:S(2)}) copy-start(f32[256]{0:T(256)} %param.9) | copy-start | bytes 3076
  32.1 19.0 %all-to-all-start = ((f32[256,1,128]{2,1,0:T(1,128)}), f32[256,1,128]{2,1,0:T(1,128)S(1)}, u32[]{:S(2)}, u32[]{:S(2)}) async-start(f32[256,1,128]{2,1,0:T(1,128)} %get-tuple-element.46), calls=%async_computation | async-start | bytes 262144 | tf_op jit(solution)/shard_map/conv/all_to_all | solution.py:625
  62.7 12.7 %all-to-all-start.2 = ((f32[32,4,128]{2,1,0:T(4,128)}), f32[32,4,128]{2,1,0:T(4,128)S(1)}, u32[]{:S(2)}, u32[]{:S(2)}) async-start(f32[32,4,128]{2,1,0:T(4,128)} %act.3), calls=%async_computation.2 | async-start | bytes 131072 | tf_op jit(solution)/shard_map/act/all_to_all | solution.py:651
  69.8 12.1 %collective-permute-start.5 = (bf16[1152,256]{1,0:T(8,128)(2,1)S(1)}, bf16[1152,256]{1,0:T(8,128)(2,1)S(1)}, u32[]{:S(2)}, u32[]{:S(2)}) collective-permute-start(bf16[1152,256]{1,0:T(8,128)(2,1)S(1)} %get-tuple-element.65), channel_id=1, source_target_pairs={{0,1},{1,0},{2,3},{3,2},{4,5},{5,4},{6,7},{7,6},{8,9},{9,8},{10,11... | collective-permute-start | bytes 1769480 | tf_op jit(solution)/shard_map/down/ppermute | solution.py:541
  79.9 3.6 %collective-permute-start.4 = (bf16[1152,256]{1,0:T(8,128)(2,1)S(1)}, bf16[1152,256]{1,0:T(8,128)(2,1)S(1)}, u32[]{:S(2)}, u32[]{:S(2)}) collective-permute-start(bf16[1152,256]{1,0:T(8,128)(2,1)S(1)} %get-tuple-element.63), channel_id=1, source_target_pairs={{0,1},{1,0},{2,3},{3,2},{4,5},{5,4},{6,7},{7,6},{8,9},{9,8},{10,11... | collective-permute-start | bytes 1769480 | tf_op jit(solution)/shard_map/total/ppermute | solution.py:541
  84.6 4.1 %copy-start.4 = (bf16[3,3,256,256]{3,2,1,0:T(8,128)(2,1)S(1)}, bf16[3,3,256,256]{3,2,1,0:T(8,128)(2,1)}, u32[]{:S(2)}) copy-start(bf16[3,3,256,256]{3,2,1,0:T(8,128)(2,1)} %w.1) | copy-start | bytes 3538948
  84.6 21.3 %all-to-all-start.3 = ((bf16[32,72,256]{2,1,0:T(8,128)(2,1)}), bf16[32,72,256]{2,1,0:T(8,128)(2,1)S(1)}, u32[]{:S(2)}, u32[]{:S(2)}) async-start(bf16[32,72,256]{2,1,0:T(8,128)(2,1)} %bitcast.22), calls=%async_computation.3 | async-start | bytes 2359296 | tf_op jit(solution)/shard_map/total/all_to_all | solution.py:699
  88.7 1.3 copy-start.5
  106.1 4.1 %collective-permute-start.8 = (bf16[72,256]{1,0:T(8,128)(2,1)S(1)}, bf16[72,256]{1,0:T(8,128)(2,1)S(1)}, u32[]{:S(2)}, u32[]{:S(2)}) collective-permute-start(bf16[72,256]{1,0:T(8,128)(2,1)S(1)} %reduce_sum.12), channel_id=1, source_target_pairs={{0,48},{16,0},{32,16},{48,32},{1,49},{17,1},{33,17},{49,33},{2,50}... | collective-permute-start | bytes 110600 | tf_op jit(solution)/shard_map/total/ppermute | solution.py:497
  106.5 5.1 %collective-permute-start.7 = (bf16[72,256]{1,0:T(8,128)(2,1)S(1)}, bf16[72,256]{1,0:T(8,128)(2,1)S(1)}, u32[]{:S(2)}, u32[]{:S(2)}) collective-permute-start(bf16[72,256]{1,0:T(8,128)(2,1)S(1)} %reduce_sum.12), channel_id=1, source_target_pairs={{0,16},{16,32},{32,48},{48,0},{1,17},{17,33},{33,49},{49,1},{2,18}... | collective-permute-start | bytes 110600 | tf_op jit(solution)/shard_map/total/ppermute | solution.py:497
  108.5 6.8 %collective-permute-start.6 = (bf16[72,256]{1,0:T(8,128)(2,1)S(1)}, bf16[72,256]{1,0:T(8,128)(2,1)S(1)}, u32[]{:S(2)}, u32[]{:S(2)}) collective-permute-start(bf16[72,256]{1,0:T(8,128)(2,1)S(1)} %reduce_sum.12), channel_id=1, source_target_pairs={{0,32},{16,48},{32,0},{48,16},{1,33},{17,49},{33,1},{49,17},{2,34}... | collective-permute-start | bytes 110600 | tf_op jit(solution)/shard_map/total/ppermute | solution.py:497
  135.7 7.2 %collective-permute-start.9 = (bf16[2304,256]{1,0:T(8,128)(2,1)S(1)}, bf16[2304,256]{1,0:T(8,128)(2,1)S(1)}, u32[]{:S(2)}, u32[]{:S(2)}) collective-permute-start(bf16[2304,256]{1,0:T(8,128)(2,1)S(1)} %bitcast.14), channel_id=1, source_target_pairs={{0,1},{1,0},{2,3},{3,2},{4,5},{5,4},{6,7},{7,6},{8,9},{9,8},{10,11... | collective-permute-start | bytes 3538952 | tf_op jit(solution)/shard_map/total/ppermute | solution.py:541

commit v7 on v6

--- a/solution.py
+++ b/solution.py
@@ -98,6 +98,17 @@
         out[k] = f32s[...].astype(BF)
 
 
+def fetch(feat_hbm, cot_hbm, w_hbm, feat, cot, w, sems):
+    copies = [
+        pltpu.make_async_copy(src, dst, sems.at[i])
+        for i, (src, dst) in enumerate(((feat_hbm, feat), (cot_hbm, cot), (w_hbm, w)))
+    ]
+    for copy in copies:
+        copy.start()
+    for copy in copies:
+        copy.wait()
+
+
 def columns(flags, pair, next_pair, part=slice(None)):
     low = flags[3] == 0
     west = jnp.where(low, next_pair[0, :, part].astype(F32), pair[0, :, part].astype(F32))
@@ -105,18 +116,15 @@
     return west, east
 
 
-def pack_lat(flags, feat, cot, pair, next_pair, near, far, w32, e32, corner, sems):
+def pack_lat(flags, feat, cot, pair, next_pair, near, far, w32, e32, corner):
     rows, cols, _ = feat.shape
     half, pairs, _ = cot.shape
     core = flags[2]
-    copies = []
     for dest, last in ((near, 1 - core), (far, core)):
         top, mid = last * (rows - 2), last * (half - 1)
-        parts = [(feat.at[top + k], k * cols, cols) for k in range(2)]
-        parts.append((cot.at[mid], 2 * cols, pairs))
-        for src, o, n in parts:
-            copies.append(pltpu.make_async_copy(src, dest.at[o : o + n], sems.at[len(copies)]))
-            copies[-1].start()
+        for k in range(2):
+            dest[k * cols : (k + 1) * cols] = feat[top + k]
+        dest[2 * cols : 2 * cols + pairs] = cot[mid]
     w32[...], e32[...] = columns(flags, pair, next_pair)
     corner[...] = jnp.zeros(corner.shape, F32)
     for k, (top, mid) in enumerate(((rows - 2, half - 1), (0, 0))):
@@ -127,8 +135,6 @@
     o = 2 * cols + pairs
     near[o : o + 16] = corner[core].astype(BF)
     far[o : o + 16] = corner[1 - core].astype(BF)
-    for copy in copies:
-        copy.wait()
 
 
 def sides(flags, near, far):
@@ -172,14 +178,10 @@
 
 
 def inner_kernel(
-    flags, feat_hbm, pair, next_pair, w_hbm, x_hbm, rim, hq_out, he_out, vec_out, f32s, edge, x_out, feat, w, sems
+    flags, feat, pair, next_pair, w, x_hbm, rim, hq_out, he_out, vec_out, f32s, edge, x_out, sems
 ):
     rows, cols, chans = feat.shape
     pairs = cols // 2
-    load_f = pltpu.make_async_copy(feat_hbm, feat, sems.at[1])
-    load_f.start()
-    load_w = pltpu.make_async_copy(w_hbm, w, sems.at[2])
-    load_w.start()
     f32s[:, :, 16 + cols : 56 + cols] = jnp.zeros((rows, 2, 40, 128), F32)
     for v in range(2):
         part = slice(v * 128, v * 128 + 128)
@@ -187,7 +189,6 @@
         for r in range(rows):
             f32s[r, v, 14:16] = edge[0, v, 2 * r : 2 * r + 2]
             f32s[r, v, 16 + cols : 18 + cols] = edge[1, v, 2 * r : 2 * r + 2]
-    load_f.wait()
     for v in range(2):
         f32s[:, v, 16 : 16 + cols] = feat[:, :, v * 128 : v * 128 + 128].astype(F32)
     taps(f32s, x_out, rows, 5)
@@ -195,7 +196,6 @@
     keep.start()
     for i, r in enumerate((0, 1, rows - 2, rows - 1)):
         rim[i] = x_out[r, :, 0 : 4 * chans]
-    load_w.wait()
     n = rows - 2
     for out, lo in ((hq_out, 0), (he_out, chans)):
         acc = None
@@ -211,13 +211,11 @@
 
 
 def outer_kernel(
-    cols, flags, near, far, rim, hq_in, he_in, vec, w_hbm, x_hbm, h_hbm, hq_out, he_out, stat_out, f32s, edge, x_out, w, sems
+    cols, flags, near, far, rim, hq_in, he_in, vec, w, x_hbm, hq_out, he_out, stat_out, f32s, edge, x_out, sems
 ):
     rows = hq_in.shape[0] + 2
     chans = hq_in.shape[2]
     pairs = cols // 2
-    load_w = pltpu.make_async_copy(w_hbm, w, sems.at[0])
-    load_w.start()
     f32s[:, :, 16 + cols : 56 + cols] = jnp.zeros((4, 2, 40, 128), F32)
     for v in range(2):
         part = slice(v * 128, v * 128 + 128)
@@ -231,11 +229,10 @@
     taps(f32s, x_out, 4, 5)
     copies = []
     for i, r in enumerate((1, 2)):
-        copies.append(pltpu.make_async_copy(x_out.at[r, 0:pairs, chans : 5 * chans], x_hbm.at[i], sems.at[1 + i]))
+        copies.append(pltpu.make_async_copy(x_out.at[r, 0:pairs, chans : 5 * chans], x_hbm.at[i], sems.at[i]))
         copies[-1].start()
     hq_out[2:rows] = hq_in[...]
     he_out[2:rows] = he_in[...]
-    load_w.wait()
     wanted = (
         ((x_out, 0), (x_out, 1), (rim, 2), (rim, 3)),
         ((x_out, 1), (rim, 0), (rim, 3), (x_out, 2)),
@@ -251,8 +248,6 @@
         value = acc.astype(BF).reshape(4, J, chans)
         out[0:2] = value[0:2]
         out[rows : rows + 2] = value[2:4]
-        copies.append(pltpu.make_async_copy(out, h_hbm.at[k], sems.at[3 + k]))
-        copies[-1].start()
     edges = (1, rows)
     sums, squares = moments(((hq_out, edges), (he_out, edges)), cols)
     n_in = (rows - 2) * cols * WIDTH
@@ -271,7 +266,10 @@
     out[...] = jnp.broadcast_to(jnp.sum(rec[...], axis=0)[None], out.shape)
 
 
-def back_kernel(flags, cot, pair, next_pair, near, far, dw, c_hbm, aq_out, ae_out, f32s, edge, c_out, sems):
+def back_kernel(flags, cot, pair, next_pair, near, far, dw, hq, he, c_hbm, h_hbm, aq_out, ae_out, f32s, edge, c_out, sems):
+    keep_h = [pltpu.make_async_copy(h, h_hbm.at[k], sems.at[1 + k]) for k, h in enumerate((hq, he))]
+    for copy in keep_h:
+        copy.start()
     half, pairs, chans = cot.shape
     rows = 2 * half
     cols = 2 * pairs
@@ -313,9 +311,11 @@
         dot_t(hi_r, dw[0, 0]) + dot_t(hi_l, dw[0, 2]) + dot_t(lo_r, dw[2, 0]) + dot_t(lo_l, dw[2, 2]),
     )
     keep.wait()
-
-
-def act_kernel(cells, flags, stats, hq, he, aq, ae, gain, bias, t_hbm, p_hbm, coef_out, sum_out, f32s, t_out, p_out, sems):
+    for copy in keep_h:
+        copy.wait()
+
+
+def act_kernel(cells, flags, stats, hq, he, aq, ae, gain, bias, t_hbm, pq_hbm, pe_hbm, coef_out, sum_out, f32s, t_out, p_out, sems):
     devices = stats.shape[0]
     rows = hq.shape[0] - 2
     chans = hq.shape[2]
@@ -349,7 +349,8 @@
             sigma = 0.5 + 0.5 * jnp.tanh(0.5 * shifted)
             pre = a[r].astype(F32) * sigma * (1.0 + shifted * (1.0 - sigma))
             p_out[k, r] = pre
-            copies.append(pltpu.make_async_copy(p_out.at[k, r], p_hbm.at[k, r], sems.at[len(copies)]))
+            dest = pq_hbm if is_q else pe_hbm
+            copies.append(pltpu.make_async_copy(p_out.at[k, r], dest.at[r], sems.at[len(copies)]))
             copies[-1].start()
             if 1 <= r <= rows:
                 acc_b = acc_b + pre
@@ -383,10 +384,11 @@
     send[...] = full[pl.ds(pl.multiple_of((1 - core) * n, n), n)].astype(BF)
 
 
-def down_kernel(flags, t_hbm, c_hbm, dw, out, keep, send, t, c, grad, sems):
+def down_kernel(flags, t_hbm, c_hbm, dw_hbm, out, keep, send, t, c, dw, grad, sems):
     half = out.shape[0]
     pairs, chans = out.shape[1:]
-    loads = [pltpu.make_async_copy(t_hbm, t, sems.at[0]), pltpu.make_async_copy(c_hbm, c, sems.at[1])]
+    sources = ((t_hbm, t), (c_hbm, c), (dw_hbm, dw))
+    loads = [pltpu.make_async_copy(src, dst, sems.at[i]) for i, (src, dst) in enumerate(sources)]
     for load in loads:
         load.start()
     for load in loads:
@@ -403,17 +405,13 @@
 
 
 def grad_kernel(
-    cells, flags, sums, coef, gain, h_hbm, p_hbm, x_hbm, rim_hbm, h4_hbm, keep, send, vec_out, f32s, conv_out, h_in, p_in, x, h4_out, sems
+    cells, flags, sums, coef, gain, pq, h_in, pe_hbm, x_hbm, rim_hbm, h4_hbm, keep, send, vec_out, f32s, conv_out, pe, x, h4_out, sems
 ):
-    rows = p_in.shape[1] - 2
-    chans = p_in.shape[3]
+    rows = pq.shape[0] - 2
+    chans = pq.shape[2]
     loads = []
-    for k in range(2):
-        loads.append(pltpu.make_async_copy(h_hbm.at[k], h_in.at[k], sems.at[len(loads)]))
-        loads[-1].start()
-        for r in range(rows + 2):
-            loads.append(pltpu.make_async_copy(p_hbm.at[k, r], p_in.at[k, r], sems.at[len(loads)]))
-            loads[-1].start()
+    loads.append(pltpu.make_async_copy(pe_hbm, pe, sems.at[0]))
+    loads[0].start()
     load_x = []
     for src, dst in ((x_hbm, x.at[1 : rows + 1]), (rim_hbm.at[0], x.at[0]), (rim_hbm.at[1], x.at[rows + 1])):
         load_x.append(pltpu.make_async_copy(src, dst, sems.at[len(loads) + len(load_x)]))
@@ -437,11 +435,12 @@
     bottom = jnp.where(flags[1] == 1, 0.0, 1.0)
     for k in range(2):
         is_q = k == 0
-        loads[k * (rows + 3)].wait()
+        p_in = pq if is_q else pe
+        if not is_q:
+            loads[0].wait()
         for r in range(rows + 2):
-            loads[k * (rows + 3) + 1 + r].wait()
             normed = (h_in[k, r].astype(F32) - mean) * inverse
-            value = inverse * (g * p_in[k, r] - first - normed * second)
+            value = inverse * (g * p_in[r] - first - normed * second)
             if r == 0:
                 value = value * top
             if r == rows + 1:
@@ -489,15 +488,6 @@
         out[:, :, v * 128 : v * 128 + 128] = f32s[:, v, 0:cols].astype(BF)
 
 
-def ring_total(value, axis):
-    n = lax.axis_size(axis)
-    total = value.astype(F32)
-    if n == 1:
-        return total
-    after, across, before = (lax.ppermute(value, axis, [(i, (i + k) % n) for i in range(n)]).astype(F32) for k in (1, 2, 3))
-    return (total + across) + (after + before)
-
-
 def join_kernel(conv_keep, conv_other, down_keep, down_other, out, both, sems):
     n = conv_keep.shape[0]
     step = n // 2
@@ -572,6 +562,9 @@
         lons = lax.axis_size(LON)
         pair = lax.ppermute(edges, LON, [(i, i ^ 1) for i in range(lons)])
         next_pair = lax.ppermute(edges, LON, [(i, (i + 2 * (i % 2) - 1) % lons) for i in range(lons)])
+        feat, cot, w_in = call(
+            fetch, [(features.shape, BF), (cotangent.shape, BF), (w3.shape, BF)], n_in=3, hbm=(0, 1, 2), sems=3
+        )(pinned(features), pinned(cotangent), pinned(w3))
         strip = (2 * cols + pairs + 16, chans)
         to_near, to_far = call(
             pack_lat,
@@ -579,9 +572,7 @@
             [(slab, F32), (slab, F32), ((2, 16, chans), F32)],
             n_in=5,
             smem=(0,),
-            hbm=(1, 2),
-            sems=6,
-        )(flags, pinned(features), pinned(cotangent), pair, next_pair)
+        )(flags, feat, cot, pair, next_pair)
         near = lax.ppermute(to_near, LAT, [(i, i ^ 1) for i in range(lats)])
         gaps = range(1, lats - 1, 2)
         far = lax.ppermute(to_far, LAT, [(i, i + 1) for i in gaps] + [(i + 1, i) for i in gaps])
@@ -598,47 +589,42 @@
                 ((rows, 2, cols + 56, 128), F32),
                 ((2, 2, slab[0], 128), F32),
                 ((rows, J, 5 * chans), BF),
-                ((rows, cols, chans), BF),
-                (w3.shape, BF),
             ],
             flops=2 * 960 * 2304 * 256,
             n_in=5,
             smem=(0,),
-            hbm=(1, 4),
-            sems=3,
-        )(flags, pinned(features), pair, next_pair, pinned(w3))
-        x_rim, h, hq, he, stat = call(
+            sems=1,
+        )(flags, feat, pair, next_pair, w_in)
+        x_rim, hq, he, stat = call(
             functools.partial(outer_kernel, cols),
-            [(rim_shape, BF, True), ((2,) + plane, BF, True), (plane, BF), (plane, BF), ((devices, 1, 128), F32)],
+            [(rim_shape, BF, True), (plane, BF), (plane, BF), ((devices, 1, 128), F32)],
             [
                 ((4, 2, cols + 56, 128), F32),
                 ((2, 2, 16, 128), F32),
                 ((4, J, 5 * chans), BF),
-                (w3.shape, BF),
             ],
             flops=2 * 640 * 2304 * 256,
             n_in=8,
             smem=(0,),
-            hbm=(7,),
-            sems=5,
-        )(flags, near, far, rim, hq_in, he_in, vec, pinned(w3))
+            sems=2,
+        )(flags, near, far, rim, hq_in, he_in, vec, w_in)
         stats = lax.all_to_all(stat, ALL, 0, 0, tiled=True)
     c_shape = (half + 2, J, 2 * chans)
     with jax.named_scope("back"):
-        c2, aq, ae = call(
+        c2, h, aq, ae = call(
             back_kernel,
-            [(c_shape, BF, True), (plane, BF), (plane, BF)],
+            [(c_shape, BF, True), ((2,) + plane, BF, True), (plane, BF), (plane, BF)],
             [((half + 2, pairs + 32, chans), F32), ((4,) + slab, F32), (c_shape, BF)],
             flops=2 * 400 * 2304 * 256,
-            n_in=7,
+            n_in=9,
             smem=(0,),
-            sems=1,
-        )(flags, cotangent, pair, next_pair, near, far, down_weight)
+            sems=3,
+        )(flags, cot, pair, next_pair, near, far, down_weight, hq, he)
     t_shape = (rows + 1, pairs, 3 * chans)
     with jax.named_scope("act"):
-        t, p, coef, sums = call(
+        t, pq, pe, coef, sums = call(
             functools.partial(act_kernel, cells),
-            [(t_shape, BF, True), ((2,) + plane, F32, True), ((2, chans), F32), ((few, 4, 128), F32)],
+            [(t_shape, BF, True), (plane, F32, True), (plane, F32, True), ((2, chans), F32), ((few, 4, 128), F32)],
             [((J, chans), F32), (t_shape, BF), ((2,) + plane, F32)],
             flops=1600 * 256 * 20,
             smem=(0,),
@@ -654,13 +640,13 @@
         output, down_keep, down_send = call(
             down_kernel,
             [((half, pairs, chans), BF), (half_rows, F32), (half_rows, BF)],
-            [(t_shape, BF), (c_shape, BF), ((all_rows, chans), F32)],
+            [(t_shape, BF), (c_shape, BF), (dw3.shape, BF), ((all_rows, chans), F32)],
             flops=4 * 256 * 2304 * 256,
             smem=(0,),
-            hbm=(1, 2),
+            hbm=(1, 2, 3),
             n_in=4,
-            sems=2,
-        )(flags, pinned(t), pinned(c2), dw3)
+            sems=3,
+        )(flags, pinned(t), pinned(c2), pinned(dw3))
         down_other = core_swap(down_send)
     h4_shape = (rows + 2, pairs, 4 * chans)
     with jax.named_scope("grad"):
@@ -670,17 +656,16 @@
             [
                 ((J, chans), F32),
                 ((all_rows, chans), F32),
-                ((2,) + plane, BF),
-                ((2,) + plane, F32),
+                (plane, F32),
                 ((rows + 2, pairs, 4 * chans), BF),
                 (h4_shape, BF),
             ],
             flops=2 * 1600 * 2304 * 256,
             smem=(0,),
-            hbm=(4, 5, 6, 7),
-            n_in=8,
-            sems=3 * (rows + 2) + 5,
-        )(flags, sums, coef, gain, pinned(h), pinned(p), pinned(x), pinned(x_rim))
+            hbm=(6, 7, 8),
+            n_in=9,
+            sems=3 * (rows + 2) + 3,
+        )(flags, sums, coef, gain, pq, h, pinned(pe), pinned(x), pinned(x_rim))
     with jax.named_scope("input"):
         (input_grad,) = call(
             input_kernel,
@@ -699,7 +684,10 @@
         got = lax.all_to_all(mine.reshape(chips, share, chans), NEAR, 0, 0, tiled=True)
         got, input_grad = lax.optimization_barrier((got, input_grad))
         piece = jnp.sum(got.astype(F32), axis=0).astype(BF)
-        piece = (ring_total(piece, "z_hi") * factor).astype(BF)
+        got = lax.all_to_all(
+            jnp.broadcast_to(piece[None], (lax.axis_size("z_hi"), share, chans)), "z_hi", 0, 0, tiled=True
+        )
+        piece = (jnp.sum(got.astype(F32), axis=0) * factor).astype(BF)
         whole = lax.all_to_all(jnp.broadcast_to(piece[None], (chips, share, chans)), NEAR, 0, 0, tiled=True)
         whole = whole.reshape(all_rows, chans)
         other = core_swap(whole)

time: 146 us -> 146 us (level)
  blocking collectives: 27.7 us -> 37.5 us
  waiting for transfers between devices: 40.9 us -> 35.8 us
  starting transfers between devices: 41.5 us -> 38.2 us
  Pallas kernels: 31.7 us -> 30.1 us
    all_to_all x0 -> x1, blocking collectives: none -> 9.76 us  [local(): lax.all_to_all(jnp.broadcast_to(piece[None], (lax.axis_size('z_hi'), shar...]
    ppermute x3 -> x0, waiting for transfers between devices: 5.17 us -> none  [ring_total(): lax.ppermute(value, axis, [(i, (i + k) % n) for i in range(n)]).astype(F32)]
    ppermute x3 -> x0, starting transfers between devices: 4.08 us -> none  [ring_total(): lax.ppermute(value, axis, [(i, (i + k) % n) for i in range(n)]).astype(F32)]
    pallas_call x3 -> x4, Pallas kernels: 9.7 us -> 9.92 us  [the longest x1 3.45 us: local(): call(functools.partial(act_kernel, cells), [(t_shape, BF, True), (plane,...]
  transfers between devices with their start and end apart: 13 -> 10, of which waited for: 9 -> 6; matrix products, arithmetic and copies ran while one was open for 0% -> 0% of each run, Pallas kernels for 12% -> 13%
where the time goes in v7:
time: 146 us; the launch traced here: 145 us
  starting transfers between devices  38.2 us (26%)
  blocking collectives  37.5 us (26%)
  waiting for transfers between devices  35.8 us (25%)
  Pallas kernels  30.1 us (21%)
  other arithmetic  1.55 us (1%)
    all_to_all x1, blocking collectives, local(): lax.all_to_all(jnp.broadcast_to(piece[None], (chips, share, chans)), NEAR...  20.3 us
    all_to_all x1, waiting for transfers between devices, local(): lax.all_to_all(mine.reshape(chips, share, chans), NEAR, 0, 0, tiled=True)  14.9 us
    ppermute x1, starting transfers between devices, local(): lax.ppermute(edges, LON, [(i, (i + 2 * (i % 2) - 1) % lons) for i in rang...  11.3 us
    all_to_all x1, waiting for transfers between devices, local(): stats = lax.all_to_all(stat, ALL, 0, 0, tiled=True)  10.9 us
    all_to_all x1, blocking collectives, local(): lax.all_to_all(jnp.broadcast_to(piece[None], (lax.axis_size('z_hi'), shar...  9.76 us
    ppermute x3, starting transfers between devices, core_swap(): return lax.ppermute(value, 'core', [(0, 1), (1, 0)])  7.67 us
    all_to_all x1, blocking collectives, local(): sums = lax.all_to_all(sums, FEW, 0, 0, tiled=True)  7.45 us
    all_to_all x1, starting transfers between devices, local(): stats = lax.all_to_all(stat, ALL, 0, 0, tiled=True)  6.22 us
  transfers between devices with their start and end apart: 10, of which 6 were waited for; matrix products, arithmetic and copies ran while one was open for 0% of the time, Pallas kernels for 13%

profile of v7, /device:TPU:1, one launch (start us, length us, event | category | flops | bytes accessed | tf_op | source)
XLA Modules:
  0.0 144.9 jit_solution(15996423417581872252)
XLA Ops:
  0.6 1.0 halo.4
  1.6 11.3 %collective-permute-start.1 = (bf16[2,32,256]{2,1,0:T(8,128)(2,1)S(1)}, bf16[2,32,256]{2,1,0:T(8,128)(2,1)S(1)}, u32[]{:S(2)}, u32[]{:S(2)}) collective-permute-start(bf16[2,32,256]{2,1,0:T(8,128)(2,1)S(1)} %halo.4), channel_id=1, source_target_pairs={{0,252},{4,8},{8,4},{12,16},{16,12},{20,24},{24,20},{28,32},{32,28... | collective-permute-start | bytes 98312 | tf_op jit(solution)/shard_map/halo/ppermute | solution.py:564
  12.9 0.0 collective-permute-start
  12.9 0.1 add_convert_fusion.flags
  13.0 1.5 %halo.3 = (bf16[8,128,256]{2,1,0:T(8,128)(2,1)S(1)}, bf16[4,64,256]{2,1,0:T(8,128)(2,1)S(1)}, bf16[3,768,256]{2,1,0:T(8,128)(2,1)S(1)}) custom-call(bf16[8,128,256]{2,1,0:T(8,128)(2,1)} %feat_hbm.3, bf16[4,64,256]{2,1,0:T(8,128)(2,1)} %cot_hbm.3, bf16[3,768,256]{2,1,0:T(8,128)(2,1)} %bitcast.17), custom_call_target="tpu_custom_call" | custom-call | bytes 1048576 | tf_op jit(solution)/shard_map/halo/pallas_call | solution.py:565
  14.5 0.0 collective-permute-done.1.next_pair
  14.5 2.7 %collective-permute-done.pair = bf16[2,32,256]{2,1,0:T(8,128)(2,1)S(1)} collective-permute-done((bf16[2,32,256]{2,1,0:T(8,128)(2,1)S(1)}, bf16[2,32,256]{2,1,0:T(8,128)(2,1)S(1)}, u32[]{:S(2)}, u32[]{:S(2)}) %collective-permute-start) | collective-permute-done | bytes 32800 | tf_op jit(solution)/shard_map/halo/ppermute | solution.py:563
  17.2 0.6 halo.5
  17.8 2.2 %collective-permute-start.2 = (bf16[336,256]{1,0:T(8,128)(2,1)S(1)}, bf16[336,256]{1,0:T(8,128)(2,1)S(1)}, u32[]{:S(2)}, u32[]{:S(2)}) collective-permute-start(bf16[336,256]{1,0:T(8,128)(2,1)S(1)} %get-tuple-element.46), channel_id=1, source_target_pairs={{0,1},{1,0},{2,3},{3,2},{4,5},{5,4},{6,7},{7,6},{8,9},{9,8},{10,11... | collective-permute-start | bytes 516104 | tf_op jit(solution)/shard_map/halo/ppermute | solution.py:576
  20.0 2.2 %collective-permute-start.3 = (bf16[336,256]{1,0:T(8,128)(2,1)S(1)}, bf16[336,256]{1,0:T(8,128)(2,1)S(1)}, u32[]{:S(2)}, u32[]{:S(2)}) collective-permute-start(bf16[336,256]{1,0:T(8,128)(2,1)S(1)} %get-tuple-element.47), channel_id=1, source_target_pairs={{1,2},{2,1},{5,6},{6,5},{9,10},{10,9},{13,14},{14,13},{17,18},{18,... | collective-permute-start | bytes 516104 | tf_op jit(solution)/shard_map/halo/ppermute | solution.py:578
  22.2 2.6 %conv.2 = (bf16[8,64,1024]{2,1,0:T(8,128)(2,1)}, bf16[4,80,1024]{2,1,0:T(8,128)(2,1)S(1)}, bf16[6,80,256]{2,1,0:T(8,128)(2,1)S(1)}, bf16[6,80,256]{2,1,0:T(8,128)(2,1)S(1)}, f32[2,256]{1,0:T(2,128)S(1)}) custom-call(s32[4]{0:T(128)S(1)} %add_convert_fusion.flags, bf16[8,128,256]{2,1,0:T(8,128)(2,1)S(1)} %get-tuple-element.44.feat, ...), custom_call_target="tpu_custom_call" | custom-call | flops 1132462080 | bytes 1048576 | tf_op jit(solution)/shard_map/conv/pallas_call | solution.py:585
  24.7 0.0 collective-permute-done.2.near
  24.8 1.9 %collective-permute-done.3.far = bf16[336,256]{1,0:T(8,128)(2,1)S(1)} collective-permute-done((bf16[336,256]{1,0:T(8,128)(2,1)S(1)}, bf16[336,256]{1,0:T(8,128)(2,1)S(1)}, u32[]{:S(2)}, u32[]{:S(2)}) %collective-permute-start.3) | collective-permute-done | bytes 172064 | tf_op jit(solution)/shard_map/halo/ppermute | solution.py:578
  26.7 3.1 %conv.3 = (bf16[2,64,1024]{2,1,0:T(8,128)(2,1)}, bf16[10,80,256]{2,1,0:T(8,128)(2,1)S(1)}, bf16[10,80,256]{2,1,0:T(8,128)(2,1)S(1)}, f32[256,1,128]{2,1,0:T(1,128)}) custom-call(s32[4]{0:T(128)S(1)} %add_convert_fusion.flags, bf16[336,256]{1,0:T(8,128)(2,1)S(1)} %collective-permute-done.2.near, bf16[336,256]{1,0:T(8,128)(2,1)S(1)} %collective-permute-done.3.far, ...), custom_call_target="tpu_custom_call" | custom-call | flops 754974720 | bytes 1048576 | tf_op jit(solution)/shard_map/conv/pallas_call | solution.py:598
  29.8 6.2 %all-to-all-start = ((f32[256,1,128]{2,1,0:T(1,128)}), f32[256,1,128]{2,1,0:T(1,128)S(1)}, u32[]{:S(2)}, u32[]{:S(2)}) async-start(f32[256,1,128]{2,1,0:T(1,128)} %get-tuple-element.53), calls=%async_computation | async-start | bytes 262144 | tf_op jit(solution)/shard_map/conv/all_to_all | solution.py:611
  36.0 0.0 copy-done
  36.0 0.0 copy-start.2
  36.0 0.0 copy-start.3
  36.1 1.9 %back.1 = (bf16[6,80,512]{2,1,0:T(8,128)(2,1)}, bf16[2,10,80,256]{3,2,1,0:T(8,128)(2,1)}, bf16[10,80,256]{2,1,0:T(8,128)(2,1)S(1)}, bf16[10,80,256]{2,1,0:T(8,128)(2,1)S(1)}) custom-call(s32[4]{0:T(128)S(1)} %add_convert_fusion.flags, bf16[4,64,256]{2,1,0:T(8,128)(2,1)S(1)} %get-tuple-element.45.cot, bf16[2,32,256]{2,1,0:T(8,128)(2,1)S(1)} %collective-permute-done.pair, ...), custom_call_target="tpu_custom_call" | custom-call | flops 471859200 | bytes 1048576 | tf_op jit(solution)/shard_map/back/pallas_call | solution.py:614
  37.9 10.9 %all-to-all-done.stats = f32[256,1,128]{2,1,0:T(1,128)S(1)} async-done(((f32[256,1,128]{2,1,0:T(1,128)}), f32[256,1,128]{2,1,0:T(1,128)S(1)}, u32[]{:S(2)}, u32[]{:S(2)}) %all-to-all-start) | async-done | bytes 131104 | tf_op jit(solution)/shard_map/conv/all_to_all | solution.py:611
  48.8 0.0 copy-done.2
  48.8 0.0 copy-done.3
  48.8 3.4 %act.2 = (bf16[9,64,768]{2,1,0:T(8,128)(2,1)}, f32[10,80,256]{2,1,0:T(8,128)}, f32[10,80,256]{2,1,0:T(8,128)}, f32[2,256]{1,0:T(2,128)S(1)}, f32[8,4,128]{2,1,0:T(4,128)S(1)}) custom-call(s32[4]{0:T(128)S(1)} %add_convert_fusion.flags, f32[256,1,128]{2,1,0:T(1,128)S(1)} %all-to-all-done.stats, bf16[10,80,256]{2,1,0:T(8,128)(2,1)S(1)} %get-tuple-element.54.hq, ...), custom_call_target="tpu_custom_call" | custom-call | flops 8192000 | bytes 1048576 | tf_op jit(solution)/shard_map/act/pallas_call | solution.py:625
  52.3 7.5 %all_to_all.30.rec = f32[8,4,128]{2,1,0:T(4,128)S(1)} all-to-all(f32[8,4,128]{2,1,0:T(4,128)S(1)} %get-tuple-element.59), channel_id=1, replica_groups=mesh['x'=4,'z_hi'=4,'z_lo'=2,'y_hi'=2,'y_lo'=2,'core'=2] {'x','core'}, dimensions={0} | all-to-all | bytes 32768 | tf_op jit(solution)/shard_map/act/all_to_all | solution.py:634
  59.7 0.6 act.3
  60.3 3.8 %all-to-all-start.2 = ((f32[32,4,128]{2,1,0:T(4,128)}), f32[32,4,128]{2,1,0:T(4,128)S(1)}, u32[]{:S(2)}, u32[]{:S(2)}) async-start(f32[32,4,128]{2,1,0:T(4,128)} %act.3), calls=%async_computation.2 | async-start | bytes 131072 | tf_op jit(solution)/shard_map/act/all_to_all | solution.py:637
  64.2 4.0 %down.1 = (bf16[4,64,256]{2,1,0:T(8,128)(2,1)}, f32[1152,256]{1,0:T(8,128)S(1)}, bf16[1152,256]{1,0:T(8,128)(2,1)}) custom-call(s32[4]{0:T(128)S(1)} %add_convert_fusion.flags, bf16[9,64,768]{2,1,0:T(8,128)(2,1)} %get-tuple-element.58.t_hbm, bf16[6,80,512]{2,1,0:T(8,128)(2,1)} %get-tuple-element.61.c_hbm, bf16[3,768,256]{2,1,0:T(8,128)(2,1)} %bitcast.16), custom_call_target="tpu_custom_call" | custom-call | flops 603979776 | bytes 1048576 | tf_op jit(solution)/shard_map/down/pallas_call | solution.py:640
  68.2 1.1 collective-permute-start.5
  69.3 3.8 %all-to-all-done.2.sums = f32[32,4,128]{2,1,0:T(4,128)S(1)} async-done(((f32[32,4,128]{2,1,0:T(4,128)}), f32[32,4,128]{2,1,0:T(4,128)S(1)}, u32[]{:S(2)}, u32[]{:S(2)}) %all-to-all-start.2) | async-done | bytes 65568 | tf_op jit(solution)/shard_map/act/all_to_all | solution.py:637
  73.1 0.0 copy-done.5
  73.1 4.0 %grad.1 = (bf16[10,64,1024]{2,1,0:T(8,128)(2,1)}, f32[1152,256]{1,0:T(8,128)S(1)}, bf16[1152,256]{1,0:T(8,128)(2,1)S(1)}, f32[2,256]{1,0:T(2,128)S(1)}) custom-call(s32[4]{0:T(128)S(1)} %add_convert_fusion.flags, f32[32,4,128]{2,1,0:T(4,128)S(1)} %all-to-all-done.2.sums, f32[2,256]{1,0:T(2,128)S(1)} %get-tuple-element.64.coef, f32[1,256]{1,0:T(1,128)S(1)} %bitcast.20, ...), custom_call_target="tpu_custom_call" | custom-call | flops 1887436800 | bytes 1048576 | tf_op jit(solution)/shard_map/grad/pallas_call | solution.py:653
  77.1 2.0 %collective-permute-start.4 = (bf16[1152,256]{1,0:T(8,128)(2,1)S(1)}, bf16[1152,256]{1,0:T(8,128)(2,1)S(1)}, u32[]{:S(2)}, u32[]{:S(2)}) collective-permute-start(bf16[1152,256]{1,0:T(8,128)(2,1)S(1)} %get-tuple-element.71), channel_id=1, source_target_pairs={{0,1},{1,0},{2,3},{3,2},{4,5},{5,4},{6,7},{7,6},{8,9},{9,8},{10,11... | collective-permute-start | bytes 1769480 | tf_op jit(solution)/shard_map/total/ppermute | solution.py:531
  79.1 0.0 collective-permute-done.5.down_other
  79.1 1.6 %collective-permute-done.4.conv_other = bf16[1152,256]{1,0:T(8,128)(2,1)S(1)} collective-permute-done((bf16[1152,256]{1,0:T(8,128)(2,1)S(1)}, bf16[1152,256]{1,0:T(8,128)(2,1)S(1)}, u32[]{:S(2)}, u32[]{:S(2)}) %collective-permute-start.4) | collective-permute-done | bytes 589856 | tf_op jit(solution)/shard_map/total/ppermute | solution.py:531
  80.7 1.1 total.3
  81.8 0.0 copy-start.1
  81.8 4.8 %all-to-all-start.3 = ((bf16[32,72,256]{2,1,0:T(8,128)(2,1)}), bf16[32,72,256]{2,1,0:T(8,128)(2,1)}, u32[]{:S(2)}, u32[]{:S(2)}) async-start(bf16[32,72,256]{2,1,0:T(8,128)(2,1)} %bitcast.21), calls=%async_computation.3 | async-start | bytes 2359296 | tf_op jit(solution)/shard_map/total/all_to_all | solution.py:684
  86.6 2.3 %input.1 = bf16[8,128,256]{2,1,0:T(8,128)(2,1)} custom-call(bf16[10,64,1024]{2,1,0:T(8,128)(2,1)S(1)} %copy-done.6, bf16[3,3,256,256]{3,2,1,0:T(8,128)(2,1)S(1)} %copy-done.1), custom_call_target="tpu_custom_call" | custom-call | flops 1207959552 | bytes 1048576 | tf_op jit(solution)/shard_map/input/pallas_call | solution.py:670
  88.9 14.9 %all-to-all-done.3 = bf16[32,72,256]{2,1,0:T(8,128)(2,1)} async-done(((bf16[32,72,256]{2,1,0:T(8,128)(2,1)}), bf16[32,72,256]{2,1,0:T(8,128)(2,1)}, u32[]{:S(2)}, u32[]{:S(2)}) %all-to-all-start.3) | async-done | bytes 1179680 | tf_op jit(solution)/shard_map/total/all_to_all | solution.py:684
  103.8 1.4 reduce_sum.21
  105.3 9.8 %all_to_all.31 = bf16[4,72,256]{2,1,0:T(8,128)(2,1)S(1)} all-to-all(bf16[4,72,256]{2,1,0:T(8,128)(2,1)S(1)} %broadcast_in_dim.4), channel_id=1, replica_groups=mesh['x'=4,'z_hi'=4,'z_lo'=2,'y_hi'=2,'y_lo'=2,'core'=2] {'z_hi'}, dimensions={0} | all-to-all | bytes 294912 | tf_op jit(solution)/shard_map/total/all_to_all | solution.py:687
  115.1 0.1 broadcast_in_dim.5
  115.2 20.3 %all_to_all.32 = bf16[32,72,256]{2,1,0:T(8,128)(2,1)S(1)} all-to-all(bf16[32,72,256]{2,1,0:T(8,128)(2,1)S(1)} %broadcast_in_dim.5), channel_id=1, replica_groups=mesh['x'=4,'z_hi'=4,'z_lo'=2,'y_hi'=2,'y_lo'=2,'core'=2] {'x','z_lo','y_..., dimensions={0} | all-to-all | bytes 2359296 | tf_op jit(solution)/shard_map/total/all_to_all | solution.py:691
  135.5 4.6 %collective-permute-start.6 = (bf16[2304,256]{1,0:T(8,128)(2,1)S(1)}, bf16[2304,256]{1,0:T(8,128)(2,1)S(1)}, u32[]{:S(2)}, u32[]{:S(2)}) collective-permute-start(bf16[2304,256]{1,0:T(8,128)(2,1)S(1)} %bitcast.14), channel_id=1, source_target_pairs={{0,1},{1,0},{2,3},{3,2},{4,5},{5,4},{6,7},{7,6},{8,9},{9,8},{10,11... | collective-permute-start | bytes 3538952 | tf_op jit(solution)/shard_map/total/ppermute | solution.py:531
  140.1 0.6 fusion
  140.7 2.0 %total.4 = (f32[2304,256]{1,0:T(8,128)}, f32[2304,256]{1,0:T(8,128)}) custom-call(s32[4]{0:T(128)S(1)} %add_convert_fusion.flags, bf16[2304,256]{1,0:T(8,128)(2,1)S(1)} %bitcast.15), custom_call_target="tpu_custom_call" | custom-call | bytes 1048576 | tf_op jit(solution)/shard_map/total/pallas_call | solution.py:696
  142.7 0.0 collective-permute-done.6.rows
  142.7 2.0 %total.5 = (f32[2304,256]{1,0:T(8,128)}, f32[2304,256]{1,0:T(8,128)}) custom-call(s32[4]{0:T(128)S(1)} %add_convert_fusion.flags, bf16[2304,256]{1,0:T(8,128)(2,1)S(1)} %collective-permute-done.6.rows, f32[2304,256]{1,0:T(8,128)} %get-tuple-element.77.conv_in, f32[2304,256]{1,0:T(8,128)} %get-tuple-element.78.down_in), custom_call_target="tpu_custom_call", output_to_operand_aliasing={{0}: (2, {}), {1}: (3, {})} | custom-call | bytes 1048576 | tf_op jit(solution)/shard_map/total/pallas_call | solution.py:697
  (10 shorter events, 0.1 us)
Async XLA Ops:
  1.6 12.9 %collective-permute-start.1 = (bf16[2,32,256]{2,1,0:T(8,128)(2,1)S(1)}, bf16[2,32,256]{2,1,0:T(8,128)(2,1)S(1)}, u32[]{:S(2)}, u32[]{:S(2)}) collective-permute-start(bf16[2,32,256]{2,1,0:T(8,128)(2,1)S(1)} %halo.4), channel_id=1, source_target_pairs={{0,252},{4,8},{8,4},{12,16},{16,12},{20,24},{24,20},{28,32},{32,28... | collective-permute-start | bytes 98312 | tf_op jit(solution)/shard_map/halo/ppermute | solution.py:564
  12.9 4.3 %collective-permute-start = (bf16[2,32,256]{2,1,0:T(8,128)(2,1)S(1)}, bf16[2,32,256]{2,1,0:T(8,128)(2,1)S(1)}, u32[]{:S(2)}, u32[]{:S(2)}) collective-permute-start(bf16[2,32,256]{2,1,0:T(8,128)(2,1)S(1)} %halo.4), channel_id=1, source_target_pairs={{0,4},{4,0},{8,12},{12,8},{16,20},{20,16},{24,28},{28,24},{32,36},... | collective-permute-start | bytes 98312 | tf_op jit(solution)/shard_map/halo/ppermute | solution.py:563
  17.8 7.0 %collective-permute-start.2 = (bf16[336,256]{1,0:T(8,128)(2,1)S(1)}, bf16[336,256]{1,0:T(8,128)(2,1)S(1)}, u32[]{:S(2)}, u32[]{:S(2)}) collective-permute-start(bf16[336,256]{1,0:T(8,128)(2,1)S(1)} %get-tuple-element.46), channel_id=1, source_target_pairs={{0,1},{1,0},{2,3},{3,2},{4,5},{5,4},{6,7},{7,6},{8,9},{9,8},{10,11... | collective-permute-start | bytes 516104 | tf_op jit(solution)/shard_map/halo/ppermute | solution.py:576
  20.0 6.7 %collective-permute-start.3 = (bf16[336,256]{1,0:T(8,128)(2,1)S(1)}, bf16[336,256]{1,0:T(8,128)(2,1)S(1)}, u32[]{:S(2)}, u32[]{:S(2)}) collective-permute-start(bf16[336,256]{1,0:T(8,128)(2,1)S(1)} %get-tuple-element.47), channel_id=1, source_target_pairs={{1,2},{2,1},{5,6},{6,5},{9,10},{10,9},{13,14},{14,13},{17,18},{18,... | collective-permute-start | bytes 516104 | tf_op jit(solution)/shard_map/halo/ppermute | solution.py:578
  26.7 9.4 %copy-start = (bf16[3,3,256,256]{3,2,1,0:T(8,128)(2,1)S(1)}, bf16[3,3,256,256]{3,2,1,0:T(8,128)(2,1)}, u32[]{:S(2)}) copy-start(bf16[3,3,256,256]{3,2,1,0:T(8,128)(2,1)} %dw.1) | copy-start | bytes 3538948
  29.8 19.0 %all-to-all-start = ((f32[256,1,128]{2,1,0:T(1,128)}), f32[256,1,128]{2,1,0:T(1,128)S(1)}, u32[]{:S(2)}, u32[]{:S(2)}) async-start(f32[256,1,128]{2,1,0:T(1,128)} %get-tuple-element.53), calls=%async_computation | async-start | bytes 262144 | tf_op jit(solution)/shard_map/conv/all_to_all | solution.py:611
  36.0 12.8 %copy-start.2 = (f32[256]{0:T(256)S(1)}, f32[256]{0:T(256)}, u32[]{:S(2)}) copy-start(f32[256]{0:T(256)} %param.10) | copy-start | bytes 3076
  36.0 12.8 %copy-start.3 = (f32[256]{0:T(256)S(1)}, f32[256]{0:T(256)}, u32[]{:S(2)}) copy-start(f32[256]{0:T(256)} %param.9) | copy-start | bytes 3076
  60.3 12.7 %all-to-all-start.2 = ((f32[32,4,128]{2,1,0:T(4,128)}), f32[32,4,128]{2,1,0:T(4,128)S(1)}, u32[]{:S(2)}, u32[]{:S(2)}) async-start(f32[32,4,128]{2,1,0:T(4,128)} %act.3), calls=%async_computation.2 | async-start | bytes 131072 | tf_op jit(solution)/shard_map/act/all_to_all | solution.py:637
  64.2 8.9 %copy-start.4 = (bf16[2,10,80,256]{3,2,1,0:T(8,128)(2,1)S(1)}, bf16[2,10,80,256]{3,2,1,0:T(8,128)(2,1)}, u32[]{:S(2)}) copy-start(bf16[2,10,80,256]{3,2,1,0:T(8,128)(2,1)} %get-tuple-element.66.h_in) | copy-start | bytes 2457604
  64.2 8.9 %copy-start.5 = (f32[10,80,256]{2,1,0:T(8,128)S(1)}, f32[10,80,256]{2,1,0:T(8,128)}, u32[]{:S(2)}) copy-start(f32[10,80,256]{2,1,0:T(8,128)} %get-tuple-element.65.pq) | copy-start | bytes 2457604
  68.2 10.8 %collective-permute-start.5 = (bf16[1152,256]{1,0:T(8,128)(2,1)}, bf16[1152,256]{1,0:T(8,128)(2,1)S(1)}, u32[]{:S(2)}, u32[]{:S(2)}) collective-permute-start(bf16[1152,256]{1,0:T(8,128)(2,1)} %get-tuple-element.73), channel_id=1, source_target_pairs={{0,1},{1,0},{2,3},{3,2},{4,5},{5,4},{6,7},{7,6},{8,9},{9,8},{10,11... | collective-permute-start | bytes 1769480 | tf_op jit(solution)/shard_map/down/ppermute | solution.py:531
  77.1 3.6 %collective-permute-start.4 = (bf16[1152,256]{1,0:T(8,128)(2,1)S(1)}, bf16[1152,256]{1,0:T(8,128)(2,1)S(1)}, u32[]{:S(2)}, u32[]{:S(2)}) collective-permute-start(bf16[1152,256]{1,0:T(8,128)(2,1)S(1)} %get-tuple-element.71), channel_id=1, source_target_pairs={{0,1},{1,0},{2,3},{3,2},{4,5},{5,4},{6,7},{7,6},{8,9},{9,8},{10,11... | collective-permute-start | bytes 1769480 | tf_op jit(solution)/shard_map/total/ppermute | solution.py:531
  80.7 5.9 %copy-start.6 = (bf16[10,64,1024]{2,1,0:T(8,128)(2,1)S(1)}, bf16[10,64,1024]{2,1,0:T(8,128)(2,1)}, u32[]{:S(2)}) copy-start(bf16[10,64,1024]{2,1,0:T(8,128)(2,1)} %get-tuple-element.74.h4) | copy-start | bytes 3932164
  81.8 4.8 %copy-start.1 = (bf16[3,3,256,256]{3,2,1,0:T(8,128)(2,1)S(1)}, bf16[3,3,256,256]{3,2,1,0:T(8,128)(2,1)}, u32[]{:S(2)}) copy-start(bf16[3,3,256,256]{3,2,1,0:T(8,128)(2,1)} %w.1) | copy-start | bytes 3538948
  81.8 22.0 %all-to-all-start.3 = ((bf16[32,72,256]{2,1,0:T(8,128)(2,1)}), bf16[32,72,256]{2,1,0:T(8,128)(2,1)}, u32[]{:S(2)}, u32[]{:S(2)}) async-start(bf16[32,72,256]{2,1,0:T(8,128)(2,1)} %bitcast.21), calls=%async_computation.3 | async-start | bytes 2359296 | tf_op jit(solution)/shard_map/total/all_to_all | solution.py:684
  135.5 7.3 %collective-permute-start.6 = (bf16[2304,256]{1,0:T(8,128)(2,1)S(1)}, bf16[2304,256]{1,0:T(8,128)(2,1)S(1)}, u32[]{:S(2)}, u32[]{:S(2)}) collective-permute-start(bf16[2304,256]{1,0:T(8,128)(2,1)S(1)} %bitcast.14), channel_id=1, source_target_pairs={{0,1},{1,0},{2,3},{3,2},{4,5},{5,4},{6,7},{7,6},{8,9},{9,8},{10,11... | collective-permute-start | bytes 3538952 | tf_op jit(solution)/shard_map/total/ppermute | solution.py:531

commit v8 on v7

--- a/solution.py
+++ b/solution.py
@@ -470,8 +470,13 @@
         copy.wait()
 
 
-def input_kernel(h4, w, out, f32s):
+def input_kernel(h4_hbm, w_hbm, out, f32s, h4, w, sems):
     rows, cols, chans = out.shape
+    loads = [pltpu.make_async_copy(h4_hbm, h4, sems.at[0]), pltpu.make_async_copy(w_hbm, w, sems.at[1])]
+    for load in loads:
+        load.start()
+    for load in loads:
+        load.wait()
     for k, lo in ((0, 1), (1, 0)):
         acc = None
         for a in range(3):
@@ -670,10 +675,12 @@
         (input_grad,) = call(
             input_kernel,
             [((rows, cols, chans), BF)],
-            [((rows, 2, cols + 8, 128), F32)],
+            [((rows, 2, cols + 8, 128), F32), (h4_shape, BF), (conv_weight.shape, BF)],
             flops=2 * 1024 * 2304 * 256,
             n_in=2,
-        )(h4, conv_weight)
+            hbm=(0, 1),
+            sems=2,
+        )(pinned(h4), pinned(conv_weight))
     with jax.named_scope("total"):
         whole_rows = (all_rows, chans)
         (mine,) = call(

time: 146 us -> 143 us (0.979)
  Pallas kernels: 30.1 us -> 31.8 us
  waiting for transfers between devices: 35.8 us -> 34.1 us
    pallas_call x1, Pallas kernels: 2.28 us -> 3.95 us  [local(): call(input_kernel, [((rows, cols, chans), BF)], [((rows, 2, cols + 8, 128...]
    all_to_all x1, waiting for transfers between devices: 14.9 us -> 13.2 us  [local(): lax.all_to_all(mine.reshape(chips, share, chans), NEAR, 0, 0, tiled=True)]
  transfers between devices with their start and end apart: 10 -> 10, of which waited for: 6 -> 6; matrix products, arithmetic and copies ran while one was open for 0% -> 0% of each run, Pallas kernels for 13% -> 14%
where the time goes in v8:
time: 143 us
  blocking collectives  37.7 us (26%)
  starting transfers between devices  37.2 us (26%)
  waiting for transfers between devices  34.1 us (24%)
  Pallas kernels  31.8 us (22%)
    all_to_all x1, blocking collectives, local(): lax.all_to_all(jnp.broadcast_to(piece[None], (chips, share, chans)), NEAR...  20.5 us
    all_to_all x1, waiting for transfers between devices, local(): lax.all_to_all(mine.reshape(chips, share, chans), NEAR, 0, 0, tiled=True)  13.2 us
    ppermute x1, starting transfers between devices, local(): lax.ppermute(edges, LON, [(i, (i + 2 * (i % 2) - 1) % lons) for i in rang...  11.3 us
    all_to_all x1, waiting for transfers between devices, local(): stats = lax.all_to_all(stat, ALL, 0, 0, tiled=True)  10.9 us
    all_to_all x1, blocking collectives, local(): lax.all_to_all(jnp.broadcast_to(piece[None], (lax.axis_size('z_hi'), shar...  9.76 us
    ppermute x3, starting transfers between devices, core_swap(): return lax.ppermute(value, 'core', [(0, 1), (1, 0)])  7.5 us
    all_to_all x1, blocking collectives, local(): sums = lax.all_to_all(sums, FEW, 0, 0, tiled=True)  7.45 us
    all_to_all x1, starting transfers between devices, local(): stats = lax.all_to_all(stat, ALL, 0, 0, tiled=True)  6.22 us
  transfers between devices with their start and end apart: 10, of which 6 were waited for; matrix products, arithmetic and copies ran while one was open for 0% of the time, Pallas kernels for 14%

profile of v8, /device:TPU:1, one launch (start us, length us, event | category | flops | bytes accessed | tf_op | source)
XLA Modules:
  0.0 142.8 jit_solution(8899412562306582104)
XLA Ops:
  0.6 1.0 halo.4
  1.6 11.3 %collective-permute-start.1 = (bf16[2,32,256]{2,1,0:T(8,128)(2,1)S(1)}, bf16[2,32,256]{2,1,0:T(8,128)(2,1)S(1)}, u32[]{:S(2)}, u32[]{:S(2)}) collective-permute-start(bf16[2,32,256]{2,1,0:T(8,128)(2,1)S(1)} %halo.4), channel_id=1, source_target_pairs={{0,252},{4,8},{8,4},{12,16},{16,12},{20,24},{24,20},{28,32},{32,28... | collective-permute-start | bytes 98312 | tf_op jit(solution)/shard_map/halo/ppermute | solution.py:569
  12.9 0.0 collective-permute-start
  12.9 0.1 add_convert_fusion.flags
  13.0 1.5 %halo.3 = (bf16[8,128,256]{2,1,0:T(8,128)(2,1)S(1)}, bf16[4,64,256]{2,1,0:T(8,128)(2,1)S(1)}, bf16[3,768,256]{2,1,0:T(8,128)(2,1)S(1)}) custom-call(bf16[8,128,256]{2,1,0:T(8,128)(2,1)} %feat_hbm.3, bf16[4,64,256]{2,1,0:T(8,128)(2,1)} %cot_hbm.3, bf16[3,768,256]{2,1,0:T(8,128)(2,1)} %bitcast.23), custom_call_target="tpu_custom_call" | custom-call | bytes 1048576 | tf_op jit(solution)/shard_map/halo/pallas_call | solution.py:570
  14.5 0.0 collective-permute-done.1.next_pair
  14.5 2.7 %collective-permute-done.pair = bf16[2,32,256]{2,1,0:T(8,128)(2,1)S(1)} collective-permute-done((bf16[2,32,256]{2,1,0:T(8,128)(2,1)S(1)}, bf16[2,32,256]{2,1,0:T(8,128)(2,1)S(1)}, u32[]{:S(2)}, u32[]{:S(2)}) %collective-permute-start) | collective-permute-done | bytes 32800 | tf_op jit(solution)/shard_map/halo/ppermute | solution.py:568
  17.2 0.6 halo.5
  17.8 2.2 %collective-permute-start.2 = (bf16[336,256]{1,0:T(8,128)(2,1)S(1)}, bf16[336,256]{1,0:T(8,128)(2,1)S(1)}, u32[]{:S(2)}, u32[]{:S(2)}) collective-permute-start(bf16[336,256]{1,0:T(8,128)(2,1)S(1)} %get-tuple-element.46), channel_id=1, source_target_pairs={{0,1},{1,0},{2,3},{3,2},{4,5},{5,4},{6,7},{7,6},{8,9},{9,8},{10,11... | collective-permute-start | bytes 516104 | tf_op jit(solution)/shard_map/halo/ppermute | solution.py:581
  20.0 2.2 %collective-permute-start.3 = (bf16[336,256]{1,0:T(8,128)(2,1)S(1)}, bf16[336,256]{1,0:T(8,128)(2,1)S(1)}, u32[]{:S(2)}, u32[]{:S(2)}) collective-permute-start(bf16[336,256]{1,0:T(8,128)(2,1)S(1)} %get-tuple-element.47), channel_id=1, source_target_pairs={{1,2},{2,1},{5,6},{6,5},{9,10},{10,9},{13,14},{14,13},{17,18},{18,... | collective-permute-start | bytes 516104 | tf_op jit(solution)/shard_map/halo/ppermute | solution.py:583
  22.2 2.6 %conv.2 = (bf16[8,64,1024]{2,1,0:T(8,128)(2,1)}, bf16[4,80,1024]{2,1,0:T(8,128)(2,1)S(1)}, bf16[6,80,256]{2,1,0:T(8,128)(2,1)S(1)}, bf16[6,80,256]{2,1,0:T(8,128)(2,1)S(1)}, f32[2,256]{1,0:T(2,128)S(1)}) custom-call(s32[4]{0:T(128)S(1)} %add_convert_fusion.flags, bf16[8,128,256]{2,1,0:T(8,128)(2,1)S(1)} %get-tuple-element.44.feat, ...), custom_call_target="tpu_custom_call" | custom-call | flops 1132462080 | bytes 1048576 | tf_op jit(solution)/shard_map/conv/pallas_call | solution.py:590
  24.7 0.0 collective-permute-done.2.near
  24.8 1.9 %collective-permute-done.3.far = bf16[336,256]{1,0:T(8,128)(2,1)S(1)} collective-permute-done((bf16[336,256]{1,0:T(8,128)(2,1)S(1)}, bf16[336,256]{1,0:T(8,128)(2,1)S(1)}, u32[]{:S(2)}, u32[]{:S(2)}) %collective-permute-start.3) | collective-permute-done | bytes 172064 | tf_op jit(solution)/shard_map/halo/ppermute | solution.py:583
  26.7 3.1 %conv.3 = (bf16[2,64,1024]{2,1,0:T(8,128)(2,1)}, bf16[10,80,256]{2,1,0:T(8,128)(2,1)S(1)}, bf16[10,80,256]{2,1,0:T(8,128)(2,1)S(1)}, f32[256,1,128]{2,1,0:T(1,128)}) custom-call(s32[4]{0:T(128)S(1)} %add_convert_fusion.flags, bf16[336,256]{1,0:T(8,128)(2,1)S(1)} %collective-permute-done.2.near, bf16[336,256]{1,0:T(8,128)(2,1)S(1)} %collective-permute-done.3.far, ...), custom_call_target="tpu_custom_call" | custom-call | flops 754974720 | bytes 1048576 | tf_op jit(solution)/shard_map/conv/pallas_call | solution.py:603
  29.8 6.2 %all-to-all-start = ((f32[256,1,128]{2,1,0:T(1,128)}), f32[256,1,128]{2,1,0:T(1,128)S(1)}, u32[]{:S(2)}, u32[]{:S(2)}) async-start(f32[256,1,128]{2,1,0:T(1,128)} %get-tuple-element.53), calls=%async_computation | async-start | bytes 262144 | tf_op jit(solution)/shard_map/conv/all_to_all | solution.py:616
  36.0 0.0 copy-done
  36.0 0.0 copy-start.1
  36.0 0.0 copy-start.2
  36.1 1.8 %back.1 = (bf16[6,80,512]{2,1,0:T(8,128)(2,1)}, bf16[2,10,80,256]{3,2,1,0:T(8,128)(2,1)}, bf16[10,80,256]{2,1,0:T(8,128)(2,1)S(1)}, bf16[10,80,256]{2,1,0:T(8,128)(2,1)S(1)}) custom-call(s32[4]{0:T(128)S(1)} %add_convert_fusion.flags, bf16[4,64,256]{2,1,0:T(8,128)(2,1)S(1)} %get-tuple-element.45.cot, bf16[2,32,256]{2,1,0:T(8,128)(2,1)S(1)} %collective-permute-done.pair, ...), custom_call_target="tpu_custom_call" | custom-call | flops 471859200 | bytes 1048576 | tf_op jit(solution)/shard_map/back/pallas_call | solution.py:619
  37.9 10.9 %all-to-all-done.stats = f32[256,1,128]{2,1,0:T(1,128)S(1)} async-done(((f32[256,1,128]{2,1,0:T(1,128)}), f32[256,1,128]{2,1,0:T(1,128)S(1)}, u32[]{:S(2)}, u32[]{:S(2)}) %all-to-all-start) | async-done | bytes 131104 | tf_op jit(solution)/shard_map/conv/all_to_all | solution.py:616
  48.8 0.0 copy-done.1
  48.8 3.4 %act.2 = (bf16[9,64,768]{2,1,0:T(8,128)(2,1)}, f32[10,80,256]{2,1,0:T(8,128)}, f32[10,80,256]{2,1,0:T(8,128)}, f32[2,256]{1,0:T(2,128)S(1)}, f32[8,4,128]{2,1,0:T(4,128)S(1)}) custom-call(s32[4]{0:T(128)S(1)} %add_convert_fusion.flags, f32[256,1,128]{2,1,0:T(1,128)S(1)} %all-to-all-done.stats, bf16[10,80,256]{2,1,0:T(8,128)(2,1)S(1)} %get-tuple-element.54.hq, ...), custom_call_target="tpu_custom_call" | custom-call | flops 8192000 | bytes 1048576 | tf_op jit(solution)/shard_map/act/pallas_call | solution.py:630
  52.3 7.5 %all_to_all.30.rec = f32[8,4,128]{2,1,0:T(4,128)S(1)} all-to-all(f32[8,4,128]{2,1,0:T(4,128)S(1)} %get-tuple-element.59), channel_id=1, replica_groups=mesh['x'=4,'z_hi'=4,'z_lo'=2,'y_hi'=2,'y_lo'=2,'core'=2] {'x','core'}, dimensions={0} | all-to-all | bytes 32768 | tf_op jit(solution)/shard_map/act/all_to_all | solution.py:639
  59.7 0.6 act.3
  60.3 3.8 %all-to-all-start.2 = ((f32[32,4,128]{2,1,0:T(4,128)}), f32[32,4,128]{2,1,0:T(4,128)S(1)}, u32[]{:S(2)}, u32[]{:S(2)}) async-start(f32[32,4,128]{2,1,0:T(4,128)} %act.3), calls=%async_computation.2 | async-start | bytes 131072 | tf_op jit(solution)/shard_map/act/all_to_all | solution.py:642
  64.2 0.0 copy-start.3
  64.2 0.0 copy-start.4
  64.2 4.0 %down.1 = (bf16[4,64,256]{2,1,0:T(8,128)(2,1)}, f32[1152,256]{1,0:T(8,128)S(1)}, bf16[1152,256]{1,0:T(8,128)(2,1)}) custom-call(s32[4]{0:T(128)S(1)} %add_convert_fusion.flags, bf16[9,64,768]{2,1,0:T(8,128)(2,1)} %get-tuple-element.58.t_hbm, bf16[6,80,512]{2,1,0:T(8,128)(2,1)} %get-tuple-element.61.c_hbm, bf16[3,768,256]{2,1,0:T(8,128)(2,1)} %bitcast.16), custom_call_target="tpu_custom_call" | custom-call | flops 603979776 | bytes 1048576 | tf_op jit(solution)/shard_map/down/pallas_call | solution.py:645
  68.2 1.1 collective-permute-start.5
  69.3 3.8 %all-to-all-done.2.sums = f32[32,4,128]{2,1,0:T(4,128)S(1)} async-done(((f32[32,4,128]{2,1,0:T(4,128)}), f32[32,4,128]{2,1,0:T(4,128)S(1)}, u32[]{:S(2)}, u32[]{:S(2)}) %all-to-all-start.2) | async-done | bytes 65568 | tf_op jit(solution)/shard_map/act/all_to_all | solution.py:642
  73.1 0.0 copy-done.3
  73.1 4.0 %grad.1 = (bf16[10,64,1024]{2,1,0:T(8,128)(2,1)}, f32[1152,256]{1,0:T(8,128)S(1)}, bf16[1152,256]{1,0:T(8,128)(2,1)S(1)}, f32[2,256]{1,0:T(2,128)S(1)}) custom-call(s32[4]{0:T(128)S(1)} %add_convert_fusion.flags, f32[32,4,128]{2,1,0:T(4,128)S(1)} %all-to-all-done.2.sums, f32[2,256]{1,0:T(2,128)S(1)} %get-tuple-element.64.coef, f32[1,256]{1,0:T(1,128)S(1)} %bitcast.19, ...), custom_call_target="tpu_custom_call" | custom-call | flops 1887436800 | bytes 1048576 | tf_op jit(solution)/shard_map/grad/pallas_call | solution.py:658
  77.1 2.0 %collective-permute-start.4 = (bf16[1152,256]{1,0:T(8,128)(2,1)S(1)}, bf16[1152,256]{1,0:T(8,128)(2,1)S(1)}, u32[]{:S(2)}, u32[]{:S(2)}) collective-permute-start(bf16[1152,256]{1,0:T(8,128)(2,1)S(1)} %get-tuple-element.71), channel_id=1, source_target_pairs={{0,1},{1,0},{2,3},{3,2},{4,5},{5,4},{6,7},{7,6},{8,9},{9,8},{10,11... | collective-permute-start | bytes 1769480 | tf_op jit(solution)/shard_map/total/ppermute | solution.py:536
  79.1 0.0 collective-permute-done.5.down_other
  79.1 1.6 %collective-permute-done.4.conv_other = bf16[1152,256]{1,0:T(8,128)(2,1)S(1)} collective-permute-done((bf16[1152,256]{1,0:T(8,128)(2,1)S(1)}, bf16[1152,256]{1,0:T(8,128)(2,1)S(1)}, u32[]{:S(2)}, u32[]{:S(2)}) %collective-permute-start.4) | collective-permute-done | bytes 589856 | tf_op jit(solution)/shard_map/total/ppermute | solution.py:536
  80.7 1.1 total.3
  81.8 4.0 %all-to-all-start.3 = ((bf16[32,72,256]{2,1,0:T(8,128)(2,1)}), bf16[32,72,256]{2,1,0:T(8,128)(2,1)S(1)}, u32[]{:S(2)}, u32[]{:S(2)}) async-start(bf16[32,72,256]{2,1,0:T(8,128)(2,1)} %bitcast.20), calls=%async_computation.3 | async-start | bytes 2359296 | tf_op jit(solution)/shard_map/total/all_to_all | solution.py:691
  85.8 4.0 %input.1 = bf16[8,128,256]{2,1,0:T(8,128)(2,1)} custom-call(bf16[10,64,1024]{2,1,0:T(8,128)(2,1)} %get-tuple-element.74.h4_hbm, bf16[3,3,256,256]{3,2,1,0:T(8,128)(2,1)} %w_hbm.1), custom_call_target="tpu_custom_call" | custom-call | flops 1207959552 | bytes 1048576 | tf_op jit(solution)/shard_map/input/pallas_call | solution.py:675
  89.7 13.2 %all-to-all-done.3 = bf16[32,72,256]{2,1,0:T(8,128)(2,1)S(1)} async-done(((bf16[32,72,256]{2,1,0:T(8,128)(2,1)}), bf16[32,72,256]{2,1,0:T(8,128)(2,1)S(1)}, u32[]{:S(2)}, u32[]{:S(2)}) %all-to-all-start.3) | async-done | bytes 1179680 | tf_op jit(solution)/shard_map/total/all_to_all | solution.py:691
  103.0 0.2 reduce_sum.21
  103.1 9.8 %all_to_all.31 = bf16[4,72,256]{2,1,0:T(8,128)(2,1)S(1)} all-to-all(bf16[4,72,256]{2,1,0:T(8,128)(2,1)S(1)} %broadcast_in_dim.4), channel_id=1, replica_groups=mesh['x'=4,'z_hi'=4,'z_lo'=2,'y_hi'=2,'y_lo'=2,'core'=2] {'z_hi'}, dimensions={0} | all-to-all | bytes 294912 | tf_op jit(solution)/shard_map/total/all_to_all | solution.py:694
  112.9 0.1 broadcast_in_dim.5
  113.0 20.5 %all_to_all.32 = bf16[32,72,256]{2,1,0:T(8,128)(2,1)S(1)} all-to-all(bf16[32,72,256]{2,1,0:T(8,128)(2,1)S(1)} %broadcast_in_dim.5), channel_id=1, replica_groups=mesh['x'=4,'z_hi'=4,'z_lo'=2,'y_hi'=2,'y_lo'=2,'core'=2] {'x','z_lo','y_..., dimensions={0} | all-to-all | bytes 2359296 | tf_op jit(solution)/shard_map/total/all_to_all | solution.py:698
  133.5 4.5 %collective-permute-start.6 = (bf16[2304,256]{1,0:T(8,128)(2,1)S(1)}, bf16[2304,256]{1,0:T(8,128)(2,1)S(1)}, u32[]{:S(2)}, u32[]{:S(2)}) collective-permute-start(bf16[2304,256]{1,0:T(8,128)(2,1)S(1)} %bitcast.14), channel_id=1, source_target_pairs={{0,1},{1,0},{2,3},{3,2},{4,5},{5,4},{6,7},{7,6},{8,9},{9,8},{10,11... | collective-permute-start | bytes 3538952 | tf_op jit(solution)/shard_map/total/ppermute | solution.py:536
  138.0 0.6 fusion
  138.5 2.0 %total.4 = (f32[2304,256]{1,0:T(8,128)}, f32[2304,256]{1,0:T(8,128)}) custom-call(s32[4]{0:T(128)S(1)} %add_convert_fusion.flags, bf16[2304,256]{1,0:T(8,128)(2,1)S(1)} %bitcast.15), custom_call_target="tpu_custom_call" | custom-call | bytes 1048576 | tf_op jit(solution)/shard_map/total/pallas_call | solution.py:703
  140.6 0.0 collective-permute-done.6.rows
  140.6 2.0 %total.5 = (f32[2304,256]{1,0:T(8,128)}, f32[2304,256]{1,0:T(8,128)}) custom-call(s32[4]{0:T(128)S(1)} %add_convert_fusion.flags, bf16[2304,256]{1,0:T(8,128)(2,1)S(1)} %collective-permute-done.6.rows, f32[2304,256]{1,0:T(8,128)} %get-tuple-element.77.conv_in, f32[2304,256]{1,0:T(8,128)} %get-tuple-element.78.down_in), custom_call_target="tpu_custom_call", output_to_operand_aliasing={{0}: (2, {}), {1}: (3, {})} | custom-call | bytes 1048576 | tf_op jit(solution)/shard_map/total/pallas_call | solution.py:704
  (6 shorter events, 0.0 us)
Async XLA Ops:
  1.6 12.9 %collective-permute-start.1 = (bf16[2,32,256]{2,1,0:T(8,128)(2,1)S(1)}, bf16[2,32,256]{2,1,0:T(8,128)(2,1)S(1)}, u32[]{:S(2)}, u32[]{:S(2)}) collective-permute-start(bf16[2,32,256]{2,1,0:T(8,128)(2,1)S(1)} %halo.4), channel_id=1, source_target_pairs={{0,252},{4,8},{8,4},{12,16},{16,12},{20,24},{24,20},{28,32},{32,28... | collective-permute-start | bytes 98312 | tf_op jit(solution)/shard_map/halo/ppermute | solution.py:569
  12.9 4.3 %collective-permute-start = (bf16[2,32,256]{2,1,0:T(8,128)(2,1)S(1)}, bf16[2,32,256]{2,1,0:T(8,128)(2,1)S(1)}, u32[]{:S(2)}, u32[]{:S(2)}) collective-permute-start(bf16[2,32,256]{2,1,0:T(8,128)(2,1)S(1)} %halo.4), channel_id=1, source_target_pairs={{0,4},{4,0},{8,12},{12,8},{16,20},{20,16},{24,28},{28,24},{32,36},... | collective-permute-start | bytes 98312 | tf_op jit(solution)/shard_map/halo/ppermute | solution.py:568
  17.8 7.0 %collective-permute-start.2 = (bf16[336,256]{1,0:T(8,128)(2,1)S(1)}, bf16[336,256]{1,0:T(8,128)(2,1)S(1)}, u32[]{:S(2)}, u32[]{:S(2)}) collective-permute-start(bf16[336,256]{1,0:T(8,128)(2,1)S(1)} %get-tuple-element.46), channel_id=1, source_target_pairs={{0,1},{1,0},{2,3},{3,2},{4,5},{5,4},{6,7},{7,6},{8,9},{9,8},{10,11... | collective-permute-start | bytes 516104 | tf_op jit(solution)/shard_map/halo/ppermute | solution.py:581
  20.0 6.7 %collective-permute-start.3 = (bf16[336,256]{1,0:T(8,128)(2,1)S(1)}, bf16[336,256]{1,0:T(8,128)(2,1)S(1)}, u32[]{:S(2)}, u32[]{:S(2)}) collective-permute-start(bf16[336,256]{1,0:T(8,128)(2,1)S(1)} %get-tuple-element.47), channel_id=1, source_target_pairs={{1,2},{2,1},{5,6},{6,5},{9,10},{10,9},{13,14},{14,13},{17,18},{18,... | collective-permute-start | bytes 516104 | tf_op jit(solution)/shard_map/halo/ppermute | solution.py:583
  26.7 9.3 %copy-start = (bf16[3,3,256,256]{3,2,1,0:T(8,128)(2,1)S(1)}, bf16[3,3,256,256]{3,2,1,0:T(8,128)(2,1)}, u32[]{:S(2)}) copy-start(bf16[3,3,256,256]{3,2,1,0:T(8,128)(2,1)} %dw.1) | copy-start | bytes 3538948
  29.8 19.0 %all-to-all-start = ((f32[256,1,128]{2,1,0:T(1,128)}), f32[256,1,128]{2,1,0:T(1,128)S(1)}, u32[]{:S(2)}, u32[]{:S(2)}) async-start(f32[256,1,128]{2,1,0:T(1,128)} %get-tuple-element.53), calls=%async_computation | async-start | bytes 262144 | tf_op jit(solution)/shard_map/conv/all_to_all | solution.py:616
  36.0 12.8 %copy-start.1 = (f32[256]{0:T(256)S(1)}, f32[256]{0:T(256)}, u32[]{:S(2)}) copy-start(f32[256]{0:T(256)} %param.10) | copy-start | bytes 3076
  36.0 12.8 %copy-start.2 = (f32[256]{0:T(256)S(1)}, f32[256]{0:T(256)}, u32[]{:S(2)}) copy-start(f32[256]{0:T(256)} %param.9) | copy-start | bytes 3076
  60.3 12.7 %all-to-all-start.2 = ((f32[32,4,128]{2,1,0:T(4,128)}), f32[32,4,128]{2,1,0:T(4,128)S(1)}, u32[]{:S(2)}, u32[]{:S(2)}) async-start(f32[32,4,128]{2,1,0:T(4,128)} %act.3), calls=%async_computation.2 | async-start | bytes 131072 | tf_op jit(solution)/shard_map/act/all_to_all | solution.py:642
  64.2 8.9 %copy-start.3 = (bf16[2,10,80,256]{3,2,1,0:T(8,128)(2,1)S(1)}, bf16[2,10,80,256]{3,2,1,0:T(8,128)(2,1)}, u32[]{:S(2)}) copy-start(bf16[2,10,80,256]{3,2,1,0:T(8,128)(2,1)} %get-tuple-element.66.h_in) | copy-start | bytes 2457604
  64.2 8.9 %copy-start.4 = (f32[10,80,256]{2,1,0:T(8,128)S(1)}, f32[10,80,256]{2,1,0:T(8,128)}, u32[]{:S(2)}) copy-start(f32[10,80,256]{2,1,0:T(8,128)} %get-tuple-element.65.pq) | copy-start | bytes 2457604
  68.2 10.8 %collective-permute-start.5 = (bf16[1152,256]{1,0:T(8,128)(2,1)}, bf16[1152,256]{1,0:T(8,128)(2,1)S(1)}, u32[]{:S(2)}, u32[]{:S(2)}) collective-permute-start(bf16[1152,256]{1,0:T(8,128)(2,1)} %get-tuple-element.73), channel_id=1, source_target_pairs={{0,1},{1,0},{2,3},{3,2},{4,5},{5,4},{6,7},{7,6},{8,9},{9,8},{10,11... | collective-permute-start | bytes 1769480 | tf_op jit(solution)/shard_map/down/ppermute | solution.py:536
  77.1 3.6 %collective-permute-start.4 = (bf16[1152,256]{1,0:T(8,128)(2,1)S(1)}, bf16[1152,256]{1,0:T(8,128)(2,1)S(1)}, u32[]{:S(2)}, u32[]{:S(2)}) collective-permute-start(bf16[1152,256]{1,0:T(8,128)(2,1)S(1)} %get-tuple-element.71), channel_id=1, source_target_pairs={{0,1},{1,0},{2,3},{3,2},{4,5},{5,4},{6,7},{7,6},{8,9},{9,8},{10,11... | collective-permute-start | bytes 1769480 | tf_op jit(solution)/shard_map/total/ppermute | solution.py:536
  81.8 21.2 %all-to-all-start.3 = ((bf16[32,72,256]{2,1,0:T(8,128)(2,1)}), bf16[32,72,256]{2,1,0:T(8,128)(2,1)S(1)}, u32[]{:S(2)}, u32[]{:S(2)}) async-start(bf16[32,72,256]{2,1,0:T(8,128)(2,1)} %bitcast.20), calls=%async_computation.3 | async-start | bytes 2359296 | tf_op jit(solution)/shard_map/total/all_to_all | solution.py:691
  133.5 7.1 %collective-permute-start.6 = (bf16[2304,256]{1,0:T(8,128)(2,1)S(1)}, bf16[2304,256]{1,0:T(8,128)(2,1)S(1)}, u32[]{:S(2)}, u32[]{:S(2)}) collective-permute-start(bf16[2304,256]{1,0:T(8,128)(2,1)S(1)} %bitcast.14), channel_id=1, source_target_pairs={{0,1},{1,0},{2,3},{3,2},{4,5},{5,4},{6,7},{7,6},{8,9},{9,8},{10,11... | collective-permute-start | bytes 3538952 | tf_op jit(solution)/shard_map/total/ppermute | solution.py:536

commit v9 on v8

--- a/solution.py
+++ b/solution.py
@@ -109,14 +109,11 @@
         copy.wait()
 
 
-def columns(flags, pair, next_pair, part=slice(None)):
-    low = flags[3] == 0
-    west = jnp.where(low, next_pair[0, :, part].astype(F32), pair[0, :, part].astype(F32))
-    east = jnp.where(low, pair[1, :, part].astype(F32), next_pair[1, :, part].astype(F32))
-    return west, east
-
-
-def pack_lat(flags, feat, cot, pair, next_pair, near, far, w32, e32, corner):
+def columns(from_west, from_east, part=slice(None)):
+    return from_west[0, :, part].astype(F32), from_east[1, :, part].astype(F32)
+
+
+def pack_lat(flags, feat, cot, from_west, from_east, near, far, w32, e32, corner):
     rows, cols, _ = feat.shape
     half, pairs, _ = cot.shape
     core = flags[2]
@@ -125,7 +122,7 @@
         for k in range(2):
             dest[k * cols : (k + 1) * cols] = feat[top + k]
         dest[2 * cols : 2 * cols + pairs] = cot[mid]
-    w32[...], e32[...] = columns(flags, pair, next_pair)
+    w32[...], e32[...] = columns(from_west, from_east)
     corner[...] = jnp.zeros(corner.shape, F32)
     for k, (top, mid) in enumerate(((rows - 2, half - 1), (0, 0))):
         corner[k, 0:4] = w32[2 * top : 2 * top + 4]
@@ -178,14 +175,14 @@
 
 
 def inner_kernel(
-    flags, feat, pair, next_pair, w, x_hbm, rim, hq_out, he_out, vec_out, f32s, edge, x_out, sems
+    flags, feat, from_west, from_east, w, x_hbm, rim, hq_out, he_out, vec_out, f32s, edge, x_out, sems
 ):
     rows, cols, chans = feat.shape
     pairs = cols // 2
     f32s[:, :, 16 + cols : 56 + cols] = jnp.zeros((rows, 2, 40, 128), F32)
     for v in range(2):
         part = slice(v * 128, v * 128 + 128)
-        edge[0, v], edge[1, v] = columns(flags, pair, next_pair, part)
+        edge[0, v], edge[1, v] = columns(from_west, from_east, part)
         for r in range(rows):
             f32s[r, v, 14:16] = edge[0, v, 2 * r : 2 * r + 2]
             f32s[r, v, 16 + cols : 18 + cols] = edge[1, v, 2 * r : 2 * r + 2]
@@ -266,7 +263,7 @@
     out[...] = jnp.broadcast_to(jnp.sum(rec[...], axis=0)[None], out.shape)
 
 
-def back_kernel(flags, cot, pair, next_pair, near, far, dw, hq, he, c_hbm, h_hbm, aq_out, ae_out, f32s, edge, c_out, sems):
+def back_kernel(flags, cot, from_west, from_east, near, far, dw, hq, he, c_hbm, h_hbm, aq_out, ae_out, f32s, edge, c_out, sems):
     keep_h = [pltpu.make_async_copy(h, h_hbm.at[k], sems.at[1 + k]) for k, h in enumerate((hq, he))]
     for copy in keep_h:
         copy.start()
@@ -274,7 +271,7 @@
     rows = 2 * half
     cols = 2 * pairs
     f32s[:, 16 + pairs :] = jnp.zeros((half + 2, 16, chans), F32)
-    edge[0], edge[1] = columns(flags, pair, next_pair)
+    edge[0], edge[1] = columns(from_west, from_east)
     every = slice(None)
     for k, side in enumerate(sides(flags, near, far)):
         row = k * (half + 1)
@@ -544,8 +541,7 @@
     cells = rows * cols * devices
     factor = 1.0 / math.sqrt(cells)
     lat = lax.axis_index(LAT)
-    odd = lax.axis_index(LON) % 2 == 1
-    flags = jnp.stack([lat == 0, lat == lats - 1, lax.axis_index("core") == 1, odd]).astype(jnp.int32)
+    flags = jnp.stack([lat == 0, lat == lats - 1, lax.axis_index("core") == 1]).astype(jnp.int32)
     gain = norm_gain.reshape(1, chans)
     bias = norm_bias.reshape(1, chans)
     w3 = conv_weight.reshape(3, 3 * chans, chans)
@@ -565,8 +561,8 @@
             sems=4,
         )(pinned(features), pinned(cotangent))
         lons = lax.axis_size(LON)
-        pair = lax.ppermute(edges, LON, [(i, i ^ 1) for i in range(lons)])
-        next_pair = lax.ppermute(edges, LON, [(i, (i + 2 * (i % 2) - 1) % lons) for i in range(lons)])
+        from_west = lax.ppermute(edges, LON, [(i, (i + 1) % lons) for i in range(lons)])
+        from_east = lax.ppermute(edges, LON, [(i, (i - 1) % lons) for i in range(lons)])
         feat, cot, w_in = call(
             fetch, [(features.shape, BF), (cotangent.shape, BF), (w3.shape, BF)], n_in=3, hbm=(0, 1, 2), sems=3
         )(pinned(features), pinned(cotangent), pinned(w3))
@@ -577,7 +573,7 @@
             [(slab, F32), (slab, F32), ((2, 16, chans), F32)],
             n_in=5,
             smem=(0,),
-        )(flags, feat, cot, pair, next_pair)
+        )(flags, feat, cot, from_west, from_east)
         near = lax.ppermute(to_near, LAT, [(i, i ^ 1) for i in range(lats)])
         gaps = range(1, lats - 1, 2)
         far = lax.ppermute(to_far, LAT, [(i, i + 1) for i in gaps] + [(i + 1, i) for i in gaps])
@@ -599,7 +595,7 @@
             n_in=5,
             smem=(0,),
             sems=1,
-        )(flags, feat, pair, next_pair, w_in)
+        )(flags, feat, from_west, from_east, w_in)
         x_rim, hq, he, stat = call(
             functools.partial(outer_kernel, cols),
             [(rim_shape, BF, True), (plane, BF), (plane, BF), ((devices, 1, 128), F32)],
@@ -624,7 +620,7 @@
             n_in=9,
             smem=(0,),
             sems=3,
-        )(flags, cot, pair, next_pair, near, far, down_weight, hq, he)
+        )(flags, cot, from_west, from_east, near, far, down_weight, hq, he)
     t_shape = (rows + 1, pairs, 3 * chans)
     with jax.named_scope("act"):
         t, pq, pe, coef, sums = call(

time: 143 us -> 144 us (level)
  waiting for transfers between devices: 34.1 us -> 35.8 us
    ppermute x2, waiting for transfers between devices: 2.67 us -> 6.89 us  [the longest x1 6.89 us: local(): lax.ppermute(edges, LON, [(i, (i + 1) % lons) for i in range(lons)])]
    all_to_all x1, waiting for transfers between devices: 10.9 us -> 8.32 us  [local(): stats = lax.all_to_all(stat, ALL, 0, 0, tiled=True)]
where the time goes in v9:
time: 144 us; the launch traced here: 143 us
  blocking collectives  37.7 us (26%)
  starting transfers between devices  36.2 us (25%)
  waiting for transfers between devices  35.8 us (25%)
  Pallas kernels  31.8 us (22%)
    all_to_all x1, blocking collectives, local(): lax.all_to_all(jnp.broadcast_to(piece[None], (chips, share, chans)), NEAR...  20.5 us
    all_to_all x1, waiting for transfers between devices, local(): lax.all_to_all(mine.reshape(chips, share, chans), NEAR, 0, 0, tiled=True)  13.2 us
    ppermute x1, starting transfers between devices, local(): lax.ppermute(edges, LON, [(i, (i - 1) % lons) for i in range(lons)])  11.3 us
    all_to_all x1, blocking collectives, local(): lax.all_to_all(jnp.broadcast_to(piece[None], (lax.axis_size('z_hi'), shar...  9.76 us
    all_to_all x1, waiting for transfers between devices, local(): stats = lax.all_to_all(stat, ALL, 0, 0, tiled=True)  8.32 us
    ppermute x3, starting transfers between devices, core_swap(): return lax.ppermute(value, 'core', [(0, 1), (1, 0)])  7.5 us
    all_to_all x1, blocking collectives, local(): sums = lax.all_to_all(sums, FEW, 0, 0, tiled=True)  7.45 us
    ppermute x1, waiting for transfers between devices, local(): lax.ppermute(edges, LON, [(i, (i + 1) % lons) for i in range(lons)])  6.89 us
  transfers between devices with their start and end apart: 10, of which 6 were waited for; matrix products, arithmetic and copies ran while one was open for 0% of the time, Pallas kernels for 14%

profile of v9, /device:TPU:1, one launch (start us, length us, event | category | flops | bytes accessed | tf_op | source)
XLA Modules:
  0.0 143.4 jit_solution(7785038168143491361)
XLA Ops:
  0.6 1.0 halo.4
  1.6 11.3 %collective-permute-start.1 = (bf16[2,32,256]{2,1,0:T(8,128)(2,1)S(1)}, bf16[2,32,256]{2,1,0:T(8,128)(2,1)S(1)}, u32[]{:S(2)}, u32[]{:S(2)}) collective-permute-start(bf16[2,32,256]{2,1,0:T(8,128)(2,1)S(1)} %halo.4), channel_id=1, source_target_pairs={{0,252},{4,0},{8,4},{12,8},{16,12},{20,16},{24,20},{28,24},{32,28}... | collective-permute-start | bytes 98312 | tf_op jit(solution)/shard_map/halo/ppermute | solution.py:565
  12.9 0.0 collective-permute-start
  12.9 0.1 add_convert_fusion.flags
  13.0 1.5 %halo.3 = (bf16[8,128,256]{2,1,0:T(8,128)(2,1)S(1)}, bf16[4,64,256]{2,1,0:T(8,128)(2,1)S(1)}, bf16[3,768,256]{2,1,0:T(8,128)(2,1)S(1)}) custom-call(bf16[8,128,256]{2,1,0:T(8,128)(2,1)} %feat_hbm.3, bf16[4,64,256]{2,1,0:T(8,128)(2,1)} %cot_hbm.3, bf16[3,768,256]{2,1,0:T(8,128)(2,1)} %bitcast.22), custom_call_target="tpu_custom_call" | custom-call | bytes 1048576 | tf_op jit(solution)/shard_map/halo/pallas_call | solution.py:566
  14.5 0.0 collective-permute-done.1.from_east
  14.5 6.9 %collective-permute-done.from_west = bf16[2,32,256]{2,1,0:T(8,128)(2,1)S(1)} collective-permute-done((bf16[2,32,256]{2,1,0:T(8,128)(2,1)S(1)}, bf16[2,32,256]{2,1,0:T(8,128)(2,1)S(1)}, u32[]{:S(2)}, u32[]{:S(2)}) %collective-permute-start) | collective-permute-done | bytes 32800 | tf_op jit(solution)/shard_map/halo/ppermute | solution.py:564
  21.4 0.6 halo.5
  22.0 2.2 %collective-permute-start.2 = (bf16[336,256]{1,0:T(8,128)(2,1)S(1)}, bf16[336,256]{1,0:T(8,128)(2,1)S(1)}, u32[]{:S(2)}, u32[]{:S(2)}) collective-permute-start(bf16[336,256]{1,0:T(8,128)(2,1)S(1)} %get-tuple-element.46), channel_id=1, source_target_pairs={{0,1},{1,0},{2,3},{3,2},{4,5},{5,4},{6,7},{7,6},{8,9},{9,8},{10,11... | collective-permute-start | bytes 516104 | tf_op jit(solution)/shard_map/halo/ppermute | solution.py:577
  24.2 2.2 %collective-permute-start.3 = (bf16[336,256]{1,0:T(8,128)(2,1)S(1)}, bf16[336,256]{1,0:T(8,128)(2,1)S(1)}, u32[]{:S(2)}, u32[]{:S(2)}) collective-permute-start(bf16[336,256]{1,0:T(8,128)(2,1)S(1)} %get-tuple-element.47), channel_id=1, source_target_pairs={{1,2},{2,1},{5,6},{6,5},{9,10},{10,9},{13,14},{14,13},{17,18},{18,... | collective-permute-start | bytes 516104 | tf_op jit(solution)/shard_map/halo/ppermute | solution.py:579
  26.4 2.6 %conv.2 = (bf16[8,64,1024]{2,1,0:T(8,128)(2,1)}, bf16[4,80,1024]{2,1,0:T(8,128)(2,1)S(1)}, bf16[6,80,256]{2,1,0:T(8,128)(2,1)S(1)}, bf16[6,80,256]{2,1,0:T(8,128)(2,1)S(1)}, f32[2,256]{1,0:T(2,128)S(1)}) custom-call(s32[3]{0:T(128)S(1)} %add_convert_fusion.flags, bf16[8,128,256]{2,1,0:T(8,128)(2,1)S(1)} %get-tuple-element.44.feat, ...), custom_call_target="tpu_custom_call" | custom-call | flops 1132462080 | bytes 1048576 | tf_op jit(solution)/shard_map/conv/pallas_call | solution.py:586
  29.0 0.0 collective-permute-done.2.near
  29.0 1.9 %collective-permute-done.3.far = bf16[336,256]{1,0:T(8,128)(2,1)S(1)} collective-permute-done((bf16[336,256]{1,0:T(8,128)(2,1)S(1)}, bf16[336,256]{1,0:T(8,128)(2,1)S(1)}, u32[]{:S(2)}, u32[]{:S(2)}) %collective-permute-start.3) | collective-permute-done | bytes 172064 | tf_op jit(solution)/shard_map/halo/ppermute | solution.py:579
  30.9 3.1 %conv.3 = (bf16[2,64,1024]{2,1,0:T(8,128)(2,1)}, bf16[10,80,256]{2,1,0:T(8,128)(2,1)S(1)}, bf16[10,80,256]{2,1,0:T(8,128)(2,1)S(1)}, f32[256,1,128]{2,1,0:T(1,128)}) custom-call(s32[3]{0:T(128)S(1)} %add_convert_fusion.flags, bf16[336,256]{1,0:T(8,128)(2,1)S(1)} %collective-permute-done.2.near, bf16[336,256]{1,0:T(8,128)(2,1)S(1)} %collective-permute-done.3.far, ...), custom_call_target="tpu_custom_call" | custom-call | flops 754974720 | bytes 1048576 | tf_op jit(solution)/shard_map/conv/pallas_call | solution.py:599
  34.0 5.2 %all-to-all-start = ((f32[256,1,128]{2,1,0:T(1,128)}), f32[256,1,128]{2,1,0:T(1,128)S(1)}, u32[]{:S(2)}, u32[]{:S(2)}) async-start(f32[256,1,128]{2,1,0:T(1,128)} %get-tuple-element.53), calls=%async_computation | async-start | bytes 262144 | tf_op jit(solution)/shard_map/conv/all_to_all | solution.py:612
  39.2 0.0 copy-done
  39.2 0.0 copy-start.1
  39.2 0.0 copy-start.2
  39.2 1.8 %back.1 = (bf16[6,80,512]{2,1,0:T(8,128)(2,1)}, bf16[2,10,80,256]{3,2,1,0:T(8,128)(2,1)}, bf16[10,80,256]{2,1,0:T(8,128)(2,1)S(1)}, bf16[10,80,256]{2,1,0:T(8,128)(2,1)S(1)}) custom-call(s32[3]{0:T(128)S(1)} %add_convert_fusion.flags, bf16[4,64,256]{2,1,0:T(8,128)(2,1)S(1)} %get-tuple-element.45.cot, bf16[2,32,256]{2,1,0:T(8,128)(2,1)S(1)} %collective-permute-done.from_west, ...), custom_call_target="tpu_custom_call" | custom-call | flops 471859200 | bytes 1048576 | tf_op jit(solution)/shard_map/back/pallas_call | solution.py:615
  41.1 8.3 %all-to-all-done.stats = f32[256,1,128]{2,1,0:T(1,128)S(1)} async-done(((f32[256,1,128]{2,1,0:T(1,128)}), f32[256,1,128]{2,1,0:T(1,128)S(1)}, u32[]{:S(2)}, u32[]{:S(2)}) %all-to-all-start) | async-done | bytes 131104 | tf_op jit(solution)/shard_map/conv/all_to_all | solution.py:612
  49.4 0.0 copy-done.1
  49.4 0.0 copy-done.2
  49.4 3.4 %act.2 = (bf16[9,64,768]{2,1,0:T(8,128)(2,1)}, f32[10,80,256]{2,1,0:T(8,128)}, f32[10,80,256]{2,1,0:T(8,128)}, f32[2,256]{1,0:T(2,128)S(1)}, f32[8,4,128]{2,1,0:T(4,128)S(1)}) custom-call(s32[3]{0:T(128)S(1)} %add_convert_fusion.flags, f32[256,1,128]{2,1,0:T(1,128)S(1)} %all-to-all-done.stats, bf16[10,80,256]{2,1,0:T(8,128)(2,1)S(1)} %get-tuple-element.54.hq, ...), custom_call_target="tpu_custom_call" | custom-call | flops 8192000 | bytes 1048576 | tf_op jit(solution)/shard_map/act/pallas_call | solution.py:626
  52.8 7.5 %all_to_all.30.rec = f32[8,4,128]{2,1,0:T(4,128)S(1)} all-to-all(f32[8,4,128]{2,1,0:T(4,128)S(1)} %get-tuple-element.59), channel_id=1, replica_groups=mesh['x'=4,'z_hi'=4,'z_lo'=2,'y_hi'=2,'y_lo'=2,'core'=2] {'x','core'}, dimensions={0} | all-to-all | bytes 32768 | tf_op jit(solution)/shard_map/act/all_to_all | solution.py:635
  60.3 0.6 act.3
  60.9 3.8 %all-to-all-start.2 = ((f32[32,4,128]{2,1,0:T(4,128)}), f32[32,4,128]{2,1,0:T(4,128)S(1)}, u32[]{:S(2)}, u32[]{:S(2)}) async-start(f32[32,4,128]{2,1,0:T(4,128)} %act.3), calls=%async_computation.2 | async-start | bytes 131072 | tf_op jit(solution)/shard_map/act/all_to_all | solution.py:638
  64.8 0.0 copy-start.3
  64.8 4.0 %down.1 = (bf16[4,64,256]{2,1,0:T(8,128)(2,1)}, f32[1152,256]{1,0:T(8,128)S(1)}, bf16[1152,256]{1,0:T(8,128)(2,1)}) custom-call(s32[3]{0:T(128)S(1)} %add_convert_fusion.flags, bf16[9,64,768]{2,1,0:T(8,128)(2,1)} %get-tuple-element.58.t_hbm, bf16[6,80,512]{2,1,0:T(8,128)(2,1)} %get-tuple-element.61.c_hbm, bf16[3,768,256]{2,1,0:T(8,128)(2,1)} %bitcast.15), custom_call_target="tpu_custom_call" | custom-call | flops 603979776 | bytes 1048576 | tf_op jit(solution)/shard_map/down/pallas_call | solution.py:641
  68.8 1.1 collective-permute-start.5
  69.9 3.8 %all-to-all-done.2.sums = f32[32,4,128]{2,1,0:T(4,128)S(1)} async-done(((f32[32,4,128]{2,1,0:T(4,128)}), f32[32,4,128]{2,1,0:T(4,128)S(1)}, u32[]{:S(2)}, u32[]{:S(2)}) %all-to-all-start.2) | async-done | bytes 65568 | tf_op jit(solution)/shard_map/act/all_to_all | solution.py:638
  73.6 0.0 copy-done.4
  73.6 4.0 %grad.1 = (bf16[10,64,1024]{2,1,0:T(8,128)(2,1)}, f32[1152,256]{1,0:T(8,128)S(1)}, bf16[1152,256]{1,0:T(8,128)(2,1)S(1)}, f32[2,256]{1,0:T(2,128)S(1)}) custom-call(s32[3]{0:T(128)S(1)} %add_convert_fusion.flags, f32[32,4,128]{2,1,0:T(4,128)S(1)} %all-to-all-done.2.sums, f32[2,256]{1,0:T(2,128)S(1)} %get-tuple-element.64.coef, f32[1,256]{1,0:T(1,128)S(1)} %bitcast.18, ...), custom_call_target="tpu_custom_call" | custom-call | flops 1887436800 | bytes 1048576 | tf_op jit(solution)/shard_map/grad/pallas_call | solution.py:654
  77.7 2.0 %collective-permute-start.4 = (bf16[1152,256]{1,0:T(8,128)(2,1)S(1)}, bf16[1152,256]{1,0:T(8,128)(2,1)S(1)}, u32[]{:S(2)}, u32[]{:S(2)}) collective-permute-start(bf16[1152,256]{1,0:T(8,128)(2,1)S(1)} %get-tuple-element.71), channel_id=1, source_target_pairs={{0,1},{1,0},{2,3},{3,2},{4,5},{5,4},{6,7},{7,6},{8,9},{9,8},{10,11... | collective-permute-start | bytes 1769480 | tf_op jit(solution)/shard_map/total/ppermute | solution.py:533
  79.6 0.0 collective-permute-done.5.down_other
  79.6 1.6 %collective-permute-done.4.conv_other = bf16[1152,256]{1,0:T(8,128)(2,1)S(1)} collective-permute-done((bf16[1152,256]{1,0:T(8,128)(2,1)S(1)}, bf16[1152,256]{1,0:T(8,128)(2,1)S(1)}, u32[]{:S(2)}, u32[]{:S(2)}) %collective-permute-start.4) | collective-permute-done | bytes 589856 | tf_op jit(solution)/shard_map/total/ppermute | solution.py:533
  81.3 1.1 total.3
  82.4 4.0 %all-to-all-start.3 = ((bf16[32,72,256]{2,1,0:T(8,128)(2,1)}), bf16[32,72,256]{2,1,0:T(8,128)(2,1)S(1)}, u32[]{:S(2)}, u32[]{:S(2)}) async-start(bf16[32,72,256]{2,1,0:T(8,128)(2,1)} %bitcast.19), calls=%async_computation.3 | async-start | bytes 2359296 | tf_op jit(solution)/shard_map/total/all_to_all | solution.py:687
  86.3 4.0 %input.1 = bf16[8,128,256]{2,1,0:T(8,128)(2,1)} custom-call(bf16[10,64,1024]{2,1,0:T(8,128)(2,1)} %get-tuple-element.74.h4_hbm, bf16[3,3,256,256]{3,2,1,0:T(8,128)(2,1)} %w_hbm.1), custom_call_target="tpu_custom_call" | custom-call | flops 1207959552 | bytes 1048576 | tf_op jit(solution)/shard_map/input/pallas_call | solution.py:671
  90.3 13.2 %all-to-all-done.3 = bf16[32,72,256]{2,1,0:T(8,128)(2,1)S(1)} async-done(((bf16[32,72,256]{2,1,0:T(8,128)(2,1)}), bf16[32,72,256]{2,1,0:T(8,128)(2,1)S(1)}, u32[]{:S(2)}, u32[]{:S(2)}) %all-to-all-start.3) | async-done | bytes 1179680 | tf_op jit(solution)/shard_map/total/all_to_all | solution.py:687
  103.5 0.2 reduce_sum.21
  103.7 9.8 %all_to_all.31 = bf16[4,72,256]{2,1,0:T(8,128)(2,1)S(1)} all-to-all(bf16[4,72,256]{2,1,0:T(8,128)(2,1)S(1)} %broadcast_in_dim.4), channel_id=1, replica_groups=mesh['x'=4,'z_hi'=4,'z_lo'=2,'y_hi'=2,'y_lo'=2,'core'=2] {'z_hi'}, dimensions={0} | all-to-all | bytes 294912 | tf_op jit(solution)/shard_map/total/all_to_all | solution.py:690
  113.5 0.1 broadcast_in_dim.5
  113.6 20.5 %all_to_all.32 = bf16[32,72,256]{2,1,0:T(8,128)(2,1)S(1)} all-to-all(bf16[32,72,256]{2,1,0:T(8,128)(2,1)S(1)} %broadcast_in_dim.5), channel_id=1, replica_groups=mesh['x'=4,'z_hi'=4,'z_lo'=2,'y_hi'=2,'y_lo'=2,'core'=2] {'x','z_lo','y_..., dimensions={0} | all-to-all | bytes 2359296 | tf_op jit(solution)/shard_map/total/all_to_all | solution.py:694
  134.1 4.5 %collective-permute-start.6 = (bf16[2304,256]{1,0:T(8,128)(2,1)S(1)}, bf16[2304,256]{1,0:T(8,128)(2,1)S(1)}, u32[]{:S(2)}, u32[]{:S(2)}) collective-permute-start(bf16[2304,256]{1,0:T(8,128)(2,1)S(1)} %bitcast.13), channel_id=1, source_target_pairs={{0,1},{1,0},{2,3},{3,2},{4,5},{5,4},{6,7},{7,6},{8,9},{9,8},{10,11... | collective-permute-start | bytes 3538952 | tf_op jit(solution)/shard_map/total/ppermute | solution.py:533
  138.5 0.6 fusion
  139.1 2.0 %total.4 = (f32[2304,256]{1,0:T(8,128)}, f32[2304,256]{1,0:T(8,128)}) custom-call(s32[3]{0:T(128)S(1)} %add_convert_fusion.flags, bf16[2304,256]{1,0:T(8,128)(2,1)S(1)} %bitcast.14), custom_call_target="tpu_custom_call" | custom-call | bytes 1048576 | tf_op jit(solution)/shard_map/total/pallas_call | solution.py:699
  141.2 0.0 collective-permute-done.6.rows
  141.2 2.0 %total.5 = (f32[2304,256]{1,0:T(8,128)}, f32[2304,256]{1,0:T(8,128)}) custom-call(s32[3]{0:T(128)S(1)} %add_convert_fusion.flags, bf16[2304,256]{1,0:T(8,128)(2,1)S(1)} %collective-permute-done.6.rows, f32[2304,256]{1,0:T(8,128)} %get-tuple-element.77.conv_in, f32[2304,256]{1,0:T(8,128)} %get-tuple-element.78.down_in), custom_call_target="tpu_custom_call", output_to_operand_aliasing={{0}: (2, {}), {1}: (3, {})} | custom-call | bytes 1048576 | tf_op jit(solution)/shard_map/total/pallas_call | solution.py:700
  (6 shorter events, 0.0 us)
Async XLA Ops:
  1.6 12.9 %collective-permute-start.1 = (bf16[2,32,256]{2,1,0:T(8,128)(2,1)S(1)}, bf16[2,32,256]{2,1,0:T(8,128)(2,1)S(1)}, u32[]{:S(2)}, u32[]{:S(2)}) collective-permute-start(bf16[2,32,256]{2,1,0:T(8,128)(2,1)S(1)} %halo.4), channel_id=1, source_target_pairs={{0,252},{4,0},{8,4},{12,8},{16,12},{20,16},{24,20},{28,24},{32,28}... | collective-permute-start | bytes 98312 | tf_op jit(solution)/shard_map/halo/ppermute | solution.py:565
  12.9 8.5 %collective-permute-start = (bf16[2,32,256]{2,1,0:T(8,128)(2,1)S(1)}, bf16[2,32,256]{2,1,0:T(8,128)(2,1)S(1)}, u32[]{:S(2)}, u32[]{:S(2)}) collective-permute-start(bf16[2,32,256]{2,1,0:T(8,128)(2,1)S(1)} %halo.4), channel_id=1, source_target_pairs={{0,4},{4,8},{8,12},{12,16},{16,20},{20,24},{24,28},{28,32},{32,36}... | collective-permute-start | bytes 98312 | tf_op jit(solution)/shard_map/halo/ppermute | solution.py:564
  22.0 7.0 %collective-permute-start.2 = (bf16[336,256]{1,0:T(8,128)(2,1)S(1)}, bf16[336,256]{1,0:T(8,128)(2,1)S(1)}, u32[]{:S(2)}, u32[]{:S(2)}) collective-permute-start(bf16[336,256]{1,0:T(8,128)(2,1)S(1)} %get-tuple-element.46), channel_id=1, source_target_pairs={{0,1},{1,0},{2,3},{3,2},{4,5},{5,4},{6,7},{7,6},{8,9},{9,8},{10,11... | collective-permute-start | bytes 516104 | tf_op jit(solution)/shard_map/halo/ppermute | solution.py:577
  24.2 6.7 %collective-permute-start.3 = (bf16[336,256]{1,0:T(8,128)(2,1)S(1)}, bf16[336,256]{1,0:T(8,128)(2,1)S(1)}, u32[]{:S(2)}, u32[]{:S(2)}) collective-permute-start(bf16[336,256]{1,0:T(8,128)(2,1)S(1)} %get-tuple-element.47), channel_id=1, source_target_pairs={{1,2},{2,1},{5,6},{6,5},{9,10},{10,9},{13,14},{14,13},{17,18},{18,... | collective-permute-start | bytes 516104 | tf_op jit(solution)/shard_map/halo/ppermute | solution.py:579
  30.9 8.3 %copy-start = (bf16[3,3,256,256]{3,2,1,0:T(8,128)(2,1)S(1)}, bf16[3,3,256,256]{3,2,1,0:T(8,128)(2,1)}, u32[]{:S(2)}) copy-start(bf16[3,3,256,256]{3,2,1,0:T(8,128)(2,1)} %dw.1) | copy-start | bytes 3538948
  34.0 15.4 %all-to-all-start = ((f32[256,1,128]{2,1,0:T(1,128)}), f32[256,1,128]{2,1,0:T(1,128)S(1)}, u32[]{:S(2)}, u32[]{:S(2)}) async-start(f32[256,1,128]{2,1,0:T(1,128)} %get-tuple-element.53), calls=%async_computation | async-start | bytes 262144 | tf_op jit(solution)/shard_map/conv/all_to_all | solution.py:612
  39.2 10.2 %copy-start.1 = (f32[256]{0:T(256)S(1)}, f32[256]{0:T(256)}, u32[]{:S(2)}) copy-start(f32[256]{0:T(256)} %param.10) | copy-start | bytes 3076
  39.2 10.2 %copy-start.2 = (f32[256]{0:T(256)S(1)}, f32[256]{0:T(256)}, u32[]{:S(2)}) copy-start(f32[256]{0:T(256)} %param.9) | copy-start | bytes 3076
  60.9 12.7 %all-to-all-start.2 = ((f32[32,4,128]{2,1,0:T(4,128)}), f32[32,4,128]{2,1,0:T(4,128)S(1)}, u32[]{:S(2)}, u32[]{:S(2)}) async-start(f32[32,4,128]{2,1,0:T(4,128)} %act.3), calls=%async_computation.2 | async-start | bytes 131072 | tf_op jit(solution)/shard_map/act/all_to_all | solution.py:638
  64.8 8.9 %copy-start.3 = (bf16[2,10,80,256]{3,2,1,0:T(8,128)(2,1)S(1)}, bf16[2,10,80,256]{3,2,1,0:T(8,128)(2,1)}, u32[]{:S(2)}) copy-start(bf16[2,10,80,256]{3,2,1,0:T(8,128)(2,1)} %get-tuple-element.66.h_in) | copy-start | bytes 2457604
  64.8 8.9 %copy-start.4 = (f32[10,80,256]{2,1,0:T(8,128)S(1)}, f32[10,80,256]{2,1,0:T(8,128)}, u32[]{:S(2)}) copy-start(f32[10,80,256]{2,1,0:T(8,128)} %get-tuple-element.65.pq) | copy-start | bytes 2457604
  68.8 10.8 %collective-permute-start.5 = (bf16[1152,256]{1,0:T(8,128)(2,1)}, bf16[1152,256]{1,0:T(8,128)(2,1)S(1)}, u32[]{:S(2)}, u32[]{:S(2)}) collective-permute-start(bf16[1152,256]{1,0:T(8,128)(2,1)} %get-tuple-element.73), channel_id=1, source_target_pairs={{0,1},{1,0},{2,3},{3,2},{4,5},{5,4},{6,7},{7,6},{8,9},{9,8},{10,11... | collective-permute-start | bytes 1769480 | tf_op jit(solution)/shard_map/down/ppermute | solution.py:533
  77.7 3.6 %collective-permute-start.4 = (bf16[1152,256]{1,0:T(8,128)(2,1)S(1)}, bf16[1152,256]{1,0:T(8,128)(2,1)S(1)}, u32[]{:S(2)}, u32[]{:S(2)}) collective-permute-start(bf16[1152,256]{1,0:T(8,128)(2,1)S(1)} %get-tuple-element.71), channel_id=1, source_target_pairs={{0,1},{1,0},{2,3},{3,2},{4,5},{5,4},{6,7},{7,6},{8,9},{9,8},{10,11... | collective-permute-start | bytes 1769480 | tf_op jit(solution)/shard_map/total/ppermute | solution.py:533
  82.4 21.2 %all-to-all-start.3 = ((bf16[32,72,256]{2,1,0:T(8,128)(2,1)}), bf16[32,72,256]{2,1,0:T(8,128)(2,1)S(1)}, u32[]{:S(2)}, u32[]{:S(2)}) async-start(bf16[32,72,256]{2,1,0:T(8,128)(2,1)} %bitcast.19), calls=%async_computation.3 | async-start | bytes 2359296 | tf_op jit(solution)/shard_map/total/all_to_all | solution.py:687
  134.1 7.1 %collective-permute-start.6 = (bf16[2304,256]{1,0:T(8,128)(2,1)S(1)}, bf16[2304,256]{1,0:T(8,128)(2,1)S(1)}, u32[]{:S(2)}, u32[]{:S(2)}) collective-permute-start(bf16[2304,256]{1,0:T(8,128)(2,1)S(1)} %bitcast.13), channel_id=1, source_target_pairs={{0,1},{1,0},{2,3},{3,2},{4,5},{5,4},{6,7},{7,6},{8,9},{9,8},{10,11... | collective-permute-start | bytes 3538952 | tf_op jit(solution)/shard_map/total/ppermute | solution.py:533

commit v10 on v8

--- a/solution.py
+++ b/solution.py
@@ -339,11 +339,10 @@
     bias_sum = jnp.zeros((1, chans), F32)
     gain_sum = jnp.zeros((1, chans), F32)
     copies = []
-    for k, (h, a, mask) in enumerate(((hq, aq, odd), (he, ae, even))):
-        is_q = k == 0
-        acc_b = jnp.zeros((J, chans), F32)
-        acc_g = jnp.zeros((J, chans), F32)
-        for r in range(rows + 2):
+    accs = [[jnp.zeros((J, chans), F32)] * 2 for _ in range(2)]
+    for r in range(rows + 2):
+        for k, (h, a) in enumerate(((hq, aq), (he, ae))):
+            is_q = k == 0
             normed = (h[r].astype(F32) - mean) * inverse
             shifted = g * normed + b
             sigma = 0.5 + 0.5 * jnp.tanh(0.5 * shifted)
@@ -353,8 +352,7 @@
             copies.append(pltpu.make_async_copy(p_out.at[k, r], dest.at[r], sems.at[len(copies)]))
             copies[-1].start()
             if 1 <= r <= rows:
-                acc_b = acc_b + pre
-                acc_g = acc_g + pre * normed
+                accs[k] = [accs[k][0] + pre, accs[k][1] + pre * normed]
             if r <= rows:
                 active = shifted * sigma
                 if r == 0:
@@ -367,6 +365,7 @@
                     t_out[r, :, chans : 2 * chans] = active[0:64].astype(BF)
                     copies.append(pltpu.make_async_copy(t_out.at[r], t_hbm.at[r], sems.at[len(copies)]))
                     copies[-1].start()
+    for (acc_b, acc_g), mask in zip(accs, (odd, even)):
         bias_sum = bias_sum + jnp.sum(acc_b * mask, axis=0, keepdims=True)
         gain_sum = gain_sum + jnp.sum(acc_g * mask, axis=0, keepdims=True)
     payload = jnp.concatenate(
@@ -493,19 +492,25 @@
         out[:, :, v * 128 : v * 128 + 128] = f32s[:, v, 0:cols].astype(BF)
 
 
-def join_kernel(conv_keep, conv_other, down_keep, down_other, out, both, sems):
-    n = conv_keep.shape[0]
+def join_rows(keep, other, out, both, sems, base):
+    n = keep.shape[0]
     step = n // 2
     copies = []
-    for k, (keep, other) in enumerate(((down_keep, down_other), (conv_keep, conv_other))):
-        for q in range(2):
-            part = slice(q * step, (q + 1) * step)
-            o = (1 - k) * n + q * step
-            both[o : o + step] = (keep[part] + other[part].astype(F32)).astype(BF)
-            copies.append(pltpu.make_async_copy(both.at[o : o + step], out.at[o : o + step], sems.at[2 * k + q]))
-            copies[-1].start()
+    for q in range(2):
+        part = slice(q * step, (q + 1) * step)
+        both[part] = (keep[part] + other[part].astype(F32)).astype(BF)
+        copies.append(pltpu.make_async_copy(both.at[part], out.at[base + q * step : base + (q + 1) * step], sems.at[q]))
+        copies[-1].start()
     for copy in copies:
         copy.wait()
+
+
+def join_down(keep, other, out, both, sems):
+    join_rows(keep, other, out, both, sems, keep.shape[0])
+
+
+def join_conv(keep, other, out_in, out, both, sems):
+    join_rows(keep, other, out, both, sems, 0)
 
 
 def unpack_rows(core, rows, conv, down, f32s, sems):
@@ -683,9 +688,12 @@
         )(pinned(h4), pinned(conv_weight))
     with jax.named_scope("total"):
         whole_rows = (all_rows, chans)
-        (mine,) = call(
-            join_kernel, [(whole_rows, BF, True)], [(whole_rows, BF)], n_in=4, sems=4
-        )(conv_keep, core_swap(conv_send), down_keep, down_other)
+        mine_out, room = [(whole_rows, BF, True)], [(half_rows, BF)]
+        conv_other = core_swap(conv_send)
+        (mine,) = call(join_down, mine_out, room, n_in=2, sems=2)(down_keep, down_other)
+        (mine,) = call(join_conv, mine_out, room, n_in=3, hbm=(2,), sems=2, aliases={2: 0})(
+            conv_keep, conv_other, pinned(mine)
+        )
         chips = lax.axis_size(NEAR)
         share = all_rows // chips
         got = lax.all_to_all(mine.reshape(chips, share, chans), NEAR, 0, 0, tiled=True)

time: 143 us -> 143 us (level)
  transfers between devices with their start and end apart: 10 -> 10, of which waited for: 6 -> 6; matrix products, arithmetic and copies ran while one was open for 0% -> 0% of each run, Pallas kernels for 14% -> 15%
where the time goes in v10:
time: 143 us
  blocking collectives  37.7 us (26%)
  starting transfers between devices  37.3 us (26%)
  waiting for transfers between devices  33.2 us (23%)
  Pallas kernels  32.5 us (23%)
    all_to_all x1, blocking collectives, local(): lax.all_to_all(jnp.broadcast_to(piece[None], (chips, share, chans)), NEAR...  20.4 us
    all_to_all x1, waiting for transfers between devices, local(): lax.all_to_all(mine.reshape(chips, share, chans), NEAR, 0, 0, tiled=True)  13.2 us
    ppermute x1, starting transfers between devices, local(): lax.ppermute(edges, LON, [(i, (i + 2 * (i % 2) - 1) % lons) for i in rang...  11.3 us
    all_to_all x1, waiting for transfers between devices, local(): stats = lax.all_to_all(stat, ALL, 0, 0, tiled=True)  10.9 us
    all_to_all x1, blocking collectives, local(): lax.all_to_all(jnp.broadcast_to(piece[None], (lax.axis_size('z_hi'), shar...  9.77 us
    ppermute x3, starting transfers between devices, core_swap(): return lax.ppermute(value, 'core', [(0, 1), (1, 0)])  7.53 us
    all_to_all x1, blocking collectives, local(): sums = lax.all_to_all(sums, FEW, 0, 0, tiled=True)  7.45 us
    all_to_all x1, starting transfers between devices, local(): stats = lax.all_to_all(stat, ALL, 0, 0, tiled=True)  6.22 us
  transfers between devices with their start and end apart: 10, of which 6 were waited for; matrix products, arithmetic and copies ran while one was open for 0% of the time, Pallas kernels for 15%

profile of v10, /device:TPU:1, one launch (start us, length us, event | category | flops | bytes accessed | tf_op | source)
XLA Modules:
  0.0 142.6 jit_solution(9115282584930995135)
XLA Ops:
  0.6 1.0 halo.4
  1.6 11.3 %collective-permute-start.1 = (bf16[2,32,256]{2,1,0:T(8,128)(2,1)S(1)}, bf16[2,32,256]{2,1,0:T(8,128)(2,1)S(1)}, u32[]{:S(2)}, u32[]{:S(2)}) collective-permute-start(bf16[2,32,256]{2,1,0:T(8,128)(2,1)S(1)} %halo.4), channel_id=1, source_target_pairs={{0,252},{4,8},{8,4},{12,16},{16,12},{20,24},{24,20},{28,32},{32,28... | collective-permute-start | bytes 98312 | tf_op jit(solution)/shard_map/halo/ppermute | solution.py:574
  12.9 0.0 collective-permute-start
  12.9 0.1 add_convert_fusion.flags
  13.0 1.5 %halo.3 = (bf16[8,128,256]{2,1,0:T(8,128)(2,1)S(1)}, bf16[4,64,256]{2,1,0:T(8,128)(2,1)S(1)}, bf16[3,768,256]{2,1,0:T(8,128)(2,1)S(1)}) custom-call(bf16[8,128,256]{2,1,0:T(8,128)(2,1)} %feat_hbm.3, bf16[4,64,256]{2,1,0:T(8,128)(2,1)} %cot_hbm.3, bf16[3,768,256]{2,1,0:T(8,128)(2,1)} %bitcast.23), custom_call_target="tpu_custom_call" | custom-call | bytes 1048576 | tf_op jit(solution)/shard_map/halo/pallas_call | solution.py:575
  14.5 0.0 collective-permute-done.1.next_pair
  14.5 2.7 %collective-permute-done.pair = bf16[2,32,256]{2,1,0:T(8,128)(2,1)S(1)} collective-permute-done((bf16[2,32,256]{2,1,0:T(8,128)(2,1)S(1)}, bf16[2,32,256]{2,1,0:T(8,128)(2,1)S(1)}, u32[]{:S(2)}, u32[]{:S(2)}) %collective-permute-start) | collective-permute-done | bytes 32800 | tf_op jit(solution)/shard_map/halo/ppermute | solution.py:573
  17.2 0.6 halo.5
  17.8 2.2 %collective-permute-start.2 = (bf16[336,256]{1,0:T(8,128)(2,1)S(1)}, bf16[336,256]{1,0:T(8,128)(2,1)S(1)}, u32[]{:S(2)}, u32[]{:S(2)}) collective-permute-start(bf16[336,256]{1,0:T(8,128)(2,1)S(1)} %get-tuple-element.46), channel_id=1, source_target_pairs={{0,1},{1,0},{2,3},{3,2},{4,5},{5,4},{6,7},{7,6},{8,9},{9,8},{10,11... | collective-permute-start | bytes 516104 | tf_op jit(solution)/shard_map/halo/ppermute | solution.py:586
  20.0 2.2 %collective-permute-start.3 = (bf16[336,256]{1,0:T(8,128)(2,1)S(1)}, bf16[336,256]{1,0:T(8,128)(2,1)S(1)}, u32[]{:S(2)}, u32[]{:S(2)}) collective-permute-start(bf16[336,256]{1,0:T(8,128)(2,1)S(1)} %get-tuple-element.47), channel_id=1, source_target_pairs={{1,2},{2,1},{5,6},{6,5},{9,10},{10,9},{13,14},{14,13},{17,18},{18,... | collective-permute-start | bytes 516104 | tf_op jit(solution)/shard_map/halo/ppermute | solution.py:588
  22.2 2.6 %conv.2 = (bf16[8,64,1024]{2,1,0:T(8,128)(2,1)}, bf16[4,80,1024]{2,1,0:T(8,128)(2,1)S(1)}, bf16[6,80,256]{2,1,0:T(8,128)(2,1)S(1)}, bf16[6,80,256]{2,1,0:T(8,128)(2,1)S(1)}, f32[2,256]{1,0:T(2,128)S(1)}) custom-call(s32[4]{0:T(128)S(1)} %add_convert_fusion.flags, bf16[8,128,256]{2,1,0:T(8,128)(2,1)S(1)} %get-tuple-element.44.feat, ...), custom_call_target="tpu_custom_call" | custom-call | flops 1132462080 | bytes 1048576 | tf_op jit(solution)/shard_map/conv/pallas_call | solution.py:595
  24.7 0.0 collective-permute-done.2.near
  24.8 1.9 %collective-permute-done.3.far = bf16[336,256]{1,0:T(8,128)(2,1)S(1)} collective-permute-done((bf16[336,256]{1,0:T(8,128)(2,1)S(1)}, bf16[336,256]{1,0:T(8,128)(2,1)S(1)}, u32[]{:S(2)}, u32[]{:S(2)}) %collective-permute-start.3) | collective-permute-done | bytes 172064 | tf_op jit(solution)/shard_map/halo/ppermute | solution.py:588
  26.7 3.1 %conv.3 = (bf16[2,64,1024]{2,1,0:T(8,128)(2,1)}, bf16[10,80,256]{2,1,0:T(8,128)(2,1)S(1)}, bf16[10,80,256]{2,1,0:T(8,128)(2,1)S(1)}, f32[256,1,128]{2,1,0:T(1,128)}) custom-call(s32[4]{0:T(128)S(1)} %add_convert_fusion.flags, bf16[336,256]{1,0:T(8,128)(2,1)S(1)} %collective-permute-done.2.near, bf16[336,256]{1,0:T(8,128)(2,1)S(1)} %collective-permute-done.3.far, ...), custom_call_target="tpu_custom_call" | custom-call | flops 754974720 | bytes 1048576 | tf_op jit(solution)/shard_map/conv/pallas_call | solution.py:608
  29.8 6.2 %all-to-all-start = ((f32[256,1,128]{2,1,0:T(1,128)}), f32[256,1,128]{2,1,0:T(1,128)S(1)}, u32[]{:S(2)}, u32[]{:S(2)}) async-start(f32[256,1,128]{2,1,0:T(1,128)} %get-tuple-element.53), calls=%async_computation | async-start | bytes 262144 | tf_op jit(solution)/shard_map/conv/all_to_all | solution.py:621
  36.0 0.0 copy-done
  36.0 0.0 copy-start.1
  36.0 0.0 copy-start.2
  36.1 1.8 %back.1 = (bf16[6,80,512]{2,1,0:T(8,128)(2,1)}, bf16[2,10,80,256]{3,2,1,0:T(8,128)(2,1)}, bf16[10,80,256]{2,1,0:T(8,128)(2,1)S(1)}, bf16[10,80,256]{2,1,0:T(8,128)(2,1)S(1)}) custom-call(s32[4]{0:T(128)S(1)} %add_convert_fusion.flags, bf16[4,64,256]{2,1,0:T(8,128)(2,1)S(1)} %get-tuple-element.45.cot, bf16[2,32,256]{2,1,0:T(8,128)(2,1)S(1)} %collective-permute-done.pair, ...), custom_call_target="tpu_custom_call" | custom-call | flops 471859200 | bytes 1048576 | tf_op jit(solution)/shard_map/back/pallas_call | solution.py:624
  37.9 10.9 %all-to-all-done.stats = f32[256,1,128]{2,1,0:T(1,128)S(1)} async-done(((f32[256,1,128]{2,1,0:T(1,128)}), f32[256,1,128]{2,1,0:T(1,128)S(1)}, u32[]{:S(2)}, u32[]{:S(2)}) %all-to-all-start) | async-done | bytes 131104 | tf_op jit(solution)/shard_map/conv/all_to_all | solution.py:621
  48.8 3.4 %act.2 = (bf16[9,64,768]{2,1,0:T(8,128)(2,1)}, f32[10,80,256]{2,1,0:T(8,128)}, f32[10,80,256]{2,1,0:T(8,128)}, f32[2,256]{1,0:T(2,128)S(1)}, f32[8,4,128]{2,1,0:T(4,128)S(1)}) custom-call(s32[4]{0:T(128)S(1)} %add_convert_fusion.flags, f32[256,1,128]{2,1,0:T(1,128)S(1)} %all-to-all-done.stats, bf16[10,80,256]{2,1,0:T(8,128)(2,1)S(1)} %get-tuple-element.54.hq, ...), custom_call_target="tpu_custom_call" | custom-call | flops 8192000 | bytes 1048576 | tf_op jit(solution)/shard_map/act/pallas_call | solution.py:635
  52.3 7.5 %all_to_all.30.rec = f32[8,4,128]{2,1,0:T(4,128)S(1)} all-to-all(f32[8,4,128]{2,1,0:T(4,128)S(1)} %get-tuple-element.59), channel_id=1, replica_groups=mesh['x'=4,'z_hi'=4,'z_lo'=2,'y_hi'=2,'y_lo'=2,'core'=2] {'x','core'}, dimensions={0} | all-to-all | bytes 32768 | tf_op jit(solution)/shard_map/act/all_to_all | solution.py:644
  59.7 0.6 act.3
  60.3 3.8 %all-to-all-start.2 = ((f32[32,4,128]{2,1,0:T(4,128)}), f32[32,4,128]{2,1,0:T(4,128)S(1)}, u32[]{:S(2)}, u32[]{:S(2)}) async-start(f32[32,4,128]{2,1,0:T(4,128)} %act.3), calls=%async_computation.2 | async-start | bytes 131072 | tf_op jit(solution)/shard_map/act/all_to_all | solution.py:647
  64.2 0.0 copy-start.3
  64.2 0.0 copy-start.4
  64.2 4.0 %down.1 = (bf16[4,64,256]{2,1,0:T(8,128)(2,1)}, f32[1152,256]{1,0:T(8,128)S(1)}, bf16[1152,256]{1,0:T(8,128)(2,1)}) custom-call(s32[4]{0:T(128)S(1)} %add_convert_fusion.flags, bf16[9,64,768]{2,1,0:T(8,128)(2,1)} %get-tuple-element.58.t_hbm, bf16[6,80,512]{2,1,0:T(8,128)(2,1)} %get-tuple-element.61.c_hbm, bf16[3,768,256]{2,1,0:T(8,128)(2,1)} %bitcast.16), custom_call_target="tpu_custom_call" | custom-call | flops 603979776 | bytes 1048576 | tf_op jit(solution)/shard_map/down/pallas_call | solution.py:650
  68.2 1.1 collective-permute-start.5
  69.3 3.8 %all-to-all-done.2.sums = f32[32,4,128]{2,1,0:T(4,128)S(1)} async-done(((f32[32,4,128]{2,1,0:T(4,128)}), f32[32,4,128]{2,1,0:T(4,128)S(1)}, u32[]{:S(2)}, u32[]{:S(2)}) %all-to-all-start.2) | async-done | bytes 65568 | tf_op jit(solution)/shard_map/act/all_to_all | solution.py:647
  73.1 0.0 copy-done.3
  73.1 4.0 %grad.1 = (bf16[10,64,1024]{2,1,0:T(8,128)(2,1)}, f32[1152,256]{1,0:T(8,128)S(1)}, bf16[1152,256]{1,0:T(8,128)(2,1)S(1)}, f32[2,256]{1,0:T(2,128)S(1)}) custom-call(s32[4]{0:T(128)S(1)} %add_convert_fusion.flags, f32[32,4,128]{2,1,0:T(4,128)S(1)} %all-to-all-done.2.sums, f32[2,256]{1,0:T(2,128)S(1)} %get-tuple-element.64.coef, f32[1,256]{1,0:T(1,128)S(1)} %bitcast.19, ...), custom_call_target="tpu_custom_call" | custom-call | flops 1887436800 | bytes 1048576 | tf_op jit(solution)/shard_map/grad/pallas_call | solution.py:663
  77.1 2.0 %collective-permute-start.4 = (bf16[1152,256]{1,0:T(8,128)(2,1)S(1)}, bf16[1152,256]{1,0:T(8,128)(2,1)S(1)}, u32[]{:S(2)}, u32[]{:S(2)}) collective-permute-start(bf16[1152,256]{1,0:T(8,128)(2,1)S(1)} %get-tuple-element.71), channel_id=1, source_target_pairs={{0,1},{1,0},{2,3},{3,2},{4,5},{5,4},{6,7},{7,6},{8,9},{9,8},{10,11... | collective-permute-start | bytes 1769480 | tf_op jit(solution)/shard_map/total/ppermute | solution.py:541
  79.1 0.0 collective-permute-done.5.other
  79.1 0.9 total.4.out_in
  80.0 0.7 collective-permute-done.4.other
  80.7 0.9 total.5
  81.6 4.0 %all-to-all-start.3 = ((bf16[32,72,256]{2,1,0:T(8,128)(2,1)}), bf16[32,72,256]{2,1,0:T(8,128)(2,1)S(1)}, u32[]{:S(2)}, u32[]{:S(2)}) async-start(bf16[32,72,256]{2,1,0:T(8,128)(2,1)} %bitcast.20), calls=%async_computation.3 | async-start | bytes 2359296 | tf_op jit(solution)/shard_map/total/all_to_all | solution.py:699
  85.5 4.0 %input.1 = bf16[8,128,256]{2,1,0:T(8,128)(2,1)} custom-call(bf16[10,64,1024]{2,1,0:T(8,128)(2,1)} %get-tuple-element.74.h4_hbm, bf16[3,3,256,256]{3,2,1,0:T(8,128)(2,1)} %w_hbm.1), custom_call_target="tpu_custom_call" | custom-call | flops 1207959552 | bytes 1048576 | tf_op jit(solution)/shard_map/input/pallas_call | solution.py:680
  89.5 13.2 %all-to-all-done.3 = bf16[32,72,256]{2,1,0:T(8,128)(2,1)S(1)} async-done(((bf16[32,72,256]{2,1,0:T(8,128)(2,1)}), bf16[32,72,256]{2,1,0:T(8,128)(2,1)S(1)}, u32[]{:S(2)}, u32[]{:S(2)}) %all-to-all-start.3) | async-done | bytes 1179680 | tf_op jit(solution)/shard_map/total/all_to_all | solution.py:699
  102.7 0.2 reduce_sum.21
  102.9 9.8 %all_to_all.31 = bf16[4,72,256]{2,1,0:T(8,128)(2,1)S(1)} all-to-all(bf16[4,72,256]{2,1,0:T(8,128)(2,1)S(1)} %broadcast_in_dim.4), channel_id=1, replica_groups=mesh['x'=4,'z_hi'=4,'z_lo'=2,'y_hi'=2,'y_lo'=2,'core'=2] {'z_hi'}, dimensions={0} | all-to-all | bytes 294912 | tf_op jit(solution)/shard_map/total/all_to_all | solution.py:702
  112.7 0.1 broadcast_in_dim.5
  112.8 20.4 %all_to_all.32 = bf16[32,72,256]{2,1,0:T(8,128)(2,1)S(1)} all-to-all(bf16[32,72,256]{2,1,0:T(8,128)(2,1)S(1)} %broadcast_in_dim.5), channel_id=1, replica_groups=mesh['x'=4,'z_hi'=4,'z_lo'=2,'y_hi'=2,'y_lo'=2,'core'=2] {'x','z_lo','y_..., dimensions={0} | all-to-all | bytes 2359296 | tf_op jit(solution)/shard_map/total/all_to_all | solution.py:706
  133.3 4.5 %collective-permute-start.6 = (bf16[2304,256]{1,0:T(8,128)(2,1)S(1)}, bf16[2304,256]{1,0:T(8,128)(2,1)S(1)}, u32[]{:S(2)}, u32[]{:S(2)}) collective-permute-start(bf16[2304,256]{1,0:T(8,128)(2,1)S(1)} %bitcast.14), channel_id=1, source_target_pairs={{0,1},{1,0},{2,3},{3,2},{4,5},{5,4},{6,7},{7,6},{8,9},{9,8},{10,11... | collective-permute-start | bytes 3538952 | tf_op jit(solution)/shard_map/total/ppermute | solution.py:541
  137.8 0.6 fusion
  138.3 2.0 %total.6 = (f32[2304,256]{1,0:T(8,128)}, f32[2304,256]{1,0:T(8,128)}) custom-call(s32[4]{0:T(128)S(1)} %add_convert_fusion.flags, bf16[2304,256]{1,0:T(8,128)(2,1)S(1)} %bitcast.15), custom_call_target="tpu_custom_call" | custom-call | bytes 1048576 | tf_op jit(solution)/shard_map/total/pallas_call | solution.py:711
  140.4 0.0 collective-permute-done.6.rows
  140.4 2.0 %total.7 = (f32[2304,256]{1,0:T(8,128)}, f32[2304,256]{1,0:T(8,128)}) custom-call(s32[4]{0:T(128)S(1)} %add_convert_fusion.flags, bf16[2304,256]{1,0:T(8,128)(2,1)S(1)} %collective-permute-done.6.rows, f32[2304,256]{1,0:T(8,128)} %get-tuple-element.77.conv_in, f32[2304,256]{1,0:T(8,128)} %get-tuple-element.78.down_in), custom_call_target="tpu_custom_call", output_to_operand_aliasing={{0}: (2, {}), {1}: (3, {})} | custom-call | bytes 1048576 | tf_op jit(solution)/shard_map/total/pallas_call | solution.py:712
  (7 shorter events, 0.0 us)
Async XLA Ops:
  1.6 12.9 %collective-permute-start.1 = (bf16[2,32,256]{2,1,0:T(8,128)(2,1)S(1)}, bf16[2,32,256]{2,1,0:T(8,128)(2,1)S(1)}, u32[]{:S(2)}, u32[]{:S(2)}) collective-permute-start(bf16[2,32,256]{2,1,0:T(8,128)(2,1)S(1)} %halo.4), channel_id=1, source_target_pairs={{0,252},{4,8},{8,4},{12,16},{16,12},{20,24},{24,20},{28,32},{32,28... | collective-permute-start | bytes 98312 | tf_op jit(solution)/shard_map/halo/ppermute | solution.py:574
  12.9 4.3 %collective-permute-start = (bf16[2,32,256]{2,1,0:T(8,128)(2,1)S(1)}, bf16[2,32,256]{2,1,0:T(8,128)(2,1)S(1)}, u32[]{:S(2)}, u32[]{:S(2)}) collective-permute-start(bf16[2,32,256]{2,1,0:T(8,128)(2,1)S(1)} %halo.4), channel_id=1, source_target_pairs={{0,4},{4,0},{8,12},{12,8},{16,20},{20,16},{24,28},{28,24},{32,36},... | collective-permute-start | bytes 98312 | tf_op jit(solution)/shard_map/halo/ppermute | solution.py:573
  17.8 7.0 %collective-permute-start.2 = (bf16[336,256]{1,0:T(8,128)(2,1)S(1)}, bf16[336,256]{1,0:T(8,128)(2,1)S(1)}, u32[]{:S(2)}, u32[]{:S(2)}) collective-permute-start(bf16[336,256]{1,0:T(8,128)(2,1)S(1)} %get-tuple-element.46), channel_id=1, source_target_pairs={{0,1},{1,0},{2,3},{3,2},{4,5},{5,4},{6,7},{7,6},{8,9},{9,8},{10,11... | collective-permute-start | bytes 516104 | tf_op jit(solution)/shard_map/halo/ppermute | solution.py:586
  20.0 6.7 %collective-permute-start.3 = (bf16[336,256]{1,0:T(8,128)(2,1)S(1)}, bf16[336,256]{1,0:T(8,128)(2,1)S(1)}, u32[]{:S(2)}, u32[]{:S(2)}) collective-permute-start(bf16[336,256]{1,0:T(8,128)(2,1)S(1)} %get-tuple-element.47), channel_id=1, source_target_pairs={{1,2},{2,1},{5,6},{6,5},{9,10},{10,9},{13,14},{14,13},{17,18},{18,... | collective-permute-start | bytes 516104 | tf_op jit(solution)/shard_map/halo/ppermute | solution.py:588
  26.7 9.3 %copy-start = (bf16[3,3,256,256]{3,2,1,0:T(8,128)(2,1)S(1)}, bf16[3,3,256,256]{3,2,1,0:T(8,128)(2,1)}, u32[]{:S(2)}) copy-start(bf16[3,3,256,256]{3,2,1,0:T(8,128)(2,1)} %dw.1) | copy-start | bytes 3538948
  29.8 19.0 %all-to-all-start = ((f32[256,1,128]{2,1,0:T(1,128)}), f32[256,1,128]{2,1,0:T(1,128)S(1)}, u32[]{:S(2)}, u32[]{:S(2)}) async-start(f32[256,1,128]{2,1,0:T(1,128)} %get-tuple-element.53), calls=%async_computation | async-start | bytes 262144 | tf_op jit(solution)/shard_map/conv/all_to_all | solution.py:621
  36.0 12.8 %copy-start.1 = (f32[256]{0:T(256)S(1)}, f32[256]{0:T(256)}, u32[]{:S(2)}) copy-start(f32[256]{0:T(256)} %param.10) | copy-start | bytes 3076
  36.0 12.8 %copy-start.2 = (f32[256]{0:T(256)S(1)}, f32[256]{0:T(256)}, u32[]{:S(2)}) copy-start(f32[256]{0:T(256)} %param.9) | copy-start | bytes 3076
  60.3 12.7 %all-to-all-start.2 = ((f32[32,4,128]{2,1,0:T(4,128)}), f32[32,4,128]{2,1,0:T(4,128)S(1)}, u32[]{:S(2)}, u32[]{:S(2)}) async-start(f32[32,4,128]{2,1,0:T(4,128)} %act.3), calls=%async_computation.2 | async-start | bytes 131072 | tf_op jit(solution)/shard_map/act/all_to_all | solution.py:647
  64.2 8.9 %copy-start.3 = (bf16[2,10,80,256]{3,2,1,0:T(8,128)(2,1)S(1)}, bf16[2,10,80,256]{3,2,1,0:T(8,128)(2,1)}, u32[]{:S(2)}) copy-start(bf16[2,10,80,256]{3,2,1,0:T(8,128)(2,1)} %get-tuple-element.66.h_in) | copy-start | bytes 2457604
  64.2 8.9 %copy-start.4 = (f32[10,80,256]{2,1,0:T(8,128)S(1)}, f32[10,80,256]{2,1,0:T(8,128)}, u32[]{:S(2)}) copy-start(f32[10,80,256]{2,1,0:T(8,128)} %get-tuple-element.65.pq) | copy-start | bytes 2457604
  68.2 10.8 %collective-permute-start.5 = (bf16[1152,256]{1,0:T(8,128)(2,1)}, bf16[1152,256]{1,0:T(8,128)(2,1)S(1)}, u32[]{:S(2)}, u32[]{:S(2)}) collective-permute-start(bf16[1152,256]{1,0:T(8,128)(2,1)} %get-tuple-element.73), channel_id=1, source_target_pairs={{0,1},{1,0},{2,3},{3,2},{4,5},{5,4},{6,7},{7,6},{8,9},{9,8},{10,11... | collective-permute-start | bytes 1769480 | tf_op jit(solution)/shard_map/down/ppermute | solution.py:541
  77.1 3.6 %collective-permute-start.4 = (bf16[1152,256]{1,0:T(8,128)(2,1)S(1)}, bf16[1152,256]{1,0:T(8,128)(2,1)S(1)}, u32[]{:S(2)}, u32[]{:S(2)}) collective-permute-start(bf16[1152,256]{1,0:T(8,128)(2,1)S(1)} %get-tuple-element.71), channel_id=1, source_target_pairs={{0,1},{1,0},{2,3},{3,2},{4,5},{5,4},{6,7},{7,6},{8,9},{9,8},{10,11... | collective-permute-start | bytes 1769480 | tf_op jit(solution)/shard_map/total/ppermute | solution.py:541
  81.6 21.2 %all-to-all-start.3 = ((bf16[32,72,256]{2,1,0:T(8,128)(2,1)}), bf16[32,72,256]{2,1,0:T(8,128)(2,1)S(1)}, u32[]{:S(2)}, u32[]{:S(2)}) async-start(bf16[32,72,256]{2,1,0:T(8,128)(2,1)} %bitcast.20), calls=%async_computation.3 | async-start | bytes 2359296 | tf_op jit(solution)/shard_map/total/all_to_all | solution.py:699
  133.3 7.1 %collective-permute-start.6 = (bf16[2304,256]{1,0:T(8,128)(2,1)S(1)}, bf16[2304,256]{1,0:T(8,128)(2,1)S(1)}, u32[]{:S(2)}, u32[]{:S(2)}) collective-permute-start(bf16[2304,256]{1,0:T(8,128)(2,1)S(1)} %bitcast.14), channel_id=1, source_target_pairs={{0,1},{1,0},{2,3},{3,2},{4,5},{5,4},{6,7},{7,6},{8,9},{9,8},{10,11... | collective-permute-start | bytes 3538952 | tf_op jit(solution)/shard_map/total/ppermute | solution.py:541

commit v11 on v8

--- a/solution.py
+++ b/solution.py
@@ -15,8 +15,8 @@
 LON = ("x", "z_hi", "z_lo", "y_hi")
 LAT = ("y_lo", "core")
 NEAR = ("x", "z_lo", "y_hi", "y_lo")
-FEW = ("x", "core")
-REST = ("z_hi", "z_lo", "y_hi", "y_lo")
+FEW = ("z_hi", "z_lo", "core")
+REST = ("x", "y_hi", "y_lo")
 ALL = LON + LAT
 BF = jnp.bfloat16
 F32 = jnp.float32

time: 143 us -> 144 us (level)
  blocking collectives: 37.7 us -> 41.3 us
  waiting for transfers between devices: 34.1 us -> 32 us
    all_to_all x1, blocking collectives: 7.45 us -> 10.6 us  [local(): sums = lax.all_to_all(sums, FEW, 0, 0, tiled=True)]
    all_to_all x1, waiting for transfers between devices: 3.78 us -> 1.71 us  [local(): sums = lax.all_to_all(sums, REST, 0, 0, tiled=True)]
where the time goes in v11:
time: 144 us; the launch traced here: 143 us
  blocking collectives  41.3 us (29%)
  starting transfers between devices  36.3 us (25%)
  waiting for transfers between devices  32 us (22%)
  Pallas kernels  31.7 us (22%)
    all_to_all x1, blocking collectives, local(): lax.all_to_all(jnp.broadcast_to(piece[None], (chips, share, chans)), NEAR...  20.8 us
    all_to_all x1, waiting for transfers between devices, local(): lax.all_to_all(mine.reshape(chips, share, chans), NEAR, 0, 0, tiled=True)  13.2 us
    ppermute x1, starting transfers between devices, local(): lax.ppermute(edges, LON, [(i, (i + 2 * (i % 2) - 1) % lons) for i in rang...  11.3 us
    all_to_all x1, waiting for transfers between devices, local(): stats = lax.all_to_all(stat, ALL, 0, 0, tiled=True)  10.9 us
    all_to_all x1, blocking collectives, local(): sums = lax.all_to_all(sums, FEW, 0, 0, tiled=True)  10.6 us
    all_to_all x1, blocking collectives, local(): lax.all_to_all(jnp.broadcast_to(piece[None], (lax.axis_size('z_hi'), shar...  9.82 us
    ppermute x3, starting transfers between devices, core_swap(): return lax.ppermute(value, 'core', [(0, 1), (1, 0)])  6.61 us
    all_to_all x1, starting transfers between devices, local(): stats = lax.all_to_all(stat, ALL, 0, 0, tiled=True)  6.22 us
  transfers between devices with their start and end apart: 10, of which 6 were waited for; matrix products, arithmetic and copies ran while one was open for 0% of the time, Pallas kernels for 14%

profile of v11, /device:TPU:1, one launch (start us, length us, event | category | flops | bytes accessed | tf_op | source)
XLA Modules:
  0.0 143.3 jit_solution(16126134863436288548)
XLA Ops:
  0.6 1.0 halo.4
  1.6 11.3 %collective-permute-start.1 = (bf16[2,32,256]{2,1,0:T(8,128)(2,1)S(1)}, bf16[2,32,256]{2,1,0:T(8,128)(2,1)S(1)}, u32[]{:S(2)}, u32[]{:S(2)}) collective-permute-start(bf16[2,32,256]{2,1,0:T(8,128)(2,1)S(1)} %halo.4), channel_id=1, source_target_pairs={{0,252},{4,8},{8,4},{12,16},{16,12},{20,24},{24,20},{28,32},{32,28... | collective-permute-start | bytes 98312 | tf_op jit(solution)/shard_map/halo/ppermute | solution.py:569
  12.9 0.0 collective-permute-start
  12.9 0.1 add_convert_fusion.flags
  13.0 1.5 %halo.3 = (bf16[8,128,256]{2,1,0:T(8,128)(2,1)S(1)}, bf16[4,64,256]{2,1,0:T(8,128)(2,1)S(1)}, bf16[3,768,256]{2,1,0:T(8,128)(2,1)S(1)}) custom-call(bf16[8,128,256]{2,1,0:T(8,128)(2,1)} %feat_hbm.3, bf16[4,64,256]{2,1,0:T(8,128)(2,1)} %cot_hbm.3, bf16[3,768,256]{2,1,0:T(8,128)(2,1)} %bitcast.23), custom_call_target="tpu_custom_call" | custom-call | bytes 1048576 | tf_op jit(solution)/shard_map/halo/pallas_call | solution.py:570
  14.5 0.0 collective-permute-done.1.next_pair
  14.5 2.7 %collective-permute-done.pair = bf16[2,32,256]{2,1,0:T(8,128)(2,1)S(1)} collective-permute-done((bf16[2,32,256]{2,1,0:T(8,128)(2,1)S(1)}, bf16[2,32,256]{2,1,0:T(8,128)(2,1)S(1)}, u32[]{:S(2)}, u32[]{:S(2)}) %collective-permute-start) | collective-permute-done | bytes 32800 | tf_op jit(solution)/shard_map/halo/ppermute | solution.py:568
  17.2 0.6 halo.5
  17.8 2.2 %collective-permute-start.2 = (bf16[336,256]{1,0:T(8,128)(2,1)S(1)}, bf16[336,256]{1,0:T(8,128)(2,1)S(1)}, u32[]{:S(2)}, u32[]{:S(2)}) collective-permute-start(bf16[336,256]{1,0:T(8,128)(2,1)S(1)} %get-tuple-element.46), channel_id=1, source_target_pairs={{0,1},{1,0},{2,3},{3,2},{4,5},{5,4},{6,7},{7,6},{8,9},{9,8},{10,11... | collective-permute-start | bytes 516104 | tf_op jit(solution)/shard_map/halo/ppermute | solution.py:581
  20.0 2.2 %collective-permute-start.3 = (bf16[336,256]{1,0:T(8,128)(2,1)S(1)}, bf16[336,256]{1,0:T(8,128)(2,1)S(1)}, u32[]{:S(2)}, u32[]{:S(2)}) collective-permute-start(bf16[336,256]{1,0:T(8,128)(2,1)S(1)} %get-tuple-element.47), channel_id=1, source_target_pairs={{1,2},{2,1},{5,6},{6,5},{9,10},{10,9},{13,14},{14,13},{17,18},{18,... | collective-permute-start | bytes 516104 | tf_op jit(solution)/shard_map/halo/ppermute | solution.py:583
  22.2 2.6 %conv.2 = (bf16[8,64,1024]{2,1,0:T(8,128)(2,1)}, bf16[4,80,1024]{2,1,0:T(8,128)(2,1)S(1)}, bf16[6,80,256]{2,1,0:T(8,128)(2,1)S(1)}, bf16[6,80,256]{2,1,0:T(8,128)(2,1)S(1)}, f32[2,256]{1,0:T(2,128)S(1)}) custom-call(s32[4]{0:T(128)S(1)} %add_convert_fusion.flags, bf16[8,128,256]{2,1,0:T(8,128)(2,1)S(1)} %get-tuple-element.44.feat, ...), custom_call_target="tpu_custom_call" | custom-call | flops 1132462080 | bytes 1048576 | tf_op jit(solution)/shard_map/conv/pallas_call | solution.py:590
  24.7 0.0 collective-permute-done.2.near
  24.8 1.9 %collective-permute-done.3.far = bf16[336,256]{1,0:T(8,128)(2,1)S(1)} collective-permute-done((bf16[336,256]{1,0:T(8,128)(2,1)S(1)}, bf16[336,256]{1,0:T(8,128)(2,1)S(1)}, u32[]{:S(2)}, u32[]{:S(2)}) %collective-permute-start.3) | collective-permute-done | bytes 172064 | tf_op jit(solution)/shard_map/halo/ppermute | solution.py:583
  26.7 3.1 %conv.3 = (bf16[2,64,1024]{2,1,0:T(8,128)(2,1)}, bf16[10,80,256]{2,1,0:T(8,128)(2,1)S(1)}, bf16[10,80,256]{2,1,0:T(8,128)(2,1)S(1)}, f32[256,1,128]{2,1,0:T(1,128)}) custom-call(s32[4]{0:T(128)S(1)} %add_convert_fusion.flags, bf16[336,256]{1,0:T(8,128)(2,1)S(1)} %collective-permute-done.2.near, bf16[336,256]{1,0:T(8,128)(2,1)S(1)} %collective-permute-done.3.far, ...), custom_call_target="tpu_custom_call" | custom-call | flops 754974720 | bytes 1048576 | tf_op jit(solution)/shard_map/conv/pallas_call | solution.py:603
  29.8 6.2 %all-to-all-start = ((f32[256,1,128]{2,1,0:T(1,128)}), f32[256,1,128]{2,1,0:T(1,128)S(1)}, u32[]{:S(2)}, u32[]{:S(2)}) async-start(f32[256,1,128]{2,1,0:T(1,128)} %get-tuple-element.53), calls=%async_computation | async-start | bytes 262144 | tf_op jit(solution)/shard_map/conv/all_to_all | solution.py:616
  36.0 0.0 copy-done
  36.0 0.0 copy-start.1
  36.0 0.0 copy-start.2
  36.1 1.8 %back.1 = (bf16[6,80,512]{2,1,0:T(8,128)(2,1)}, bf16[2,10,80,256]{3,2,1,0:T(8,128)(2,1)}, bf16[10,80,256]{2,1,0:T(8,128)(2,1)S(1)}, bf16[10,80,256]{2,1,0:T(8,128)(2,1)S(1)}) custom-call(s32[4]{0:T(128)S(1)} %add_convert_fusion.flags, bf16[4,64,256]{2,1,0:T(8,128)(2,1)S(1)} %get-tuple-element.45.cot, bf16[2,32,256]{2,1,0:T(8,128)(2,1)S(1)} %collective-permute-done.pair, ...), custom_call_target="tpu_custom_call" | custom-call | flops 471859200 | bytes 1048576 | tf_op jit(solution)/shard_map/back/pallas_call | solution.py:619
  37.9 10.9 %all-to-all-done.stats = f32[256,1,128]{2,1,0:T(1,128)S(1)} async-done(((f32[256,1,128]{2,1,0:T(1,128)}), f32[256,1,128]{2,1,0:T(1,128)S(1)}, u32[]{:S(2)}, u32[]{:S(2)}) %all-to-all-start) | async-done | bytes 131104 | tf_op jit(solution)/shard_map/conv/all_to_all | solution.py:616
  48.8 0.0 copy-done.1
  48.8 0.0 copy-done.2
  48.8 3.4 %act.2 = (bf16[9,64,768]{2,1,0:T(8,128)(2,1)}, f32[10,80,256]{2,1,0:T(8,128)}, f32[10,80,256]{2,1,0:T(8,128)}, f32[2,256]{1,0:T(2,128)S(1)}, f32[16,4,128]{2,1,0:T(4,128)S(1)}) custom-call(s32[4]{0:T(128)S(1)} %add_convert_fusion.flags, f32[256,1,128]{2,1,0:T(1,128)S(1)} %all-to-all-done.stats, bf16[10,80,256]{2,1,0:T(8,128)(2,1)S(1)} %get-tuple-element.54.hq, ...), custom_call_target="tpu_custom_call" | custom-call | flops 8192000 | bytes 1048576 | tf_op jit(solution)/shard_map/act/pallas_call | solution.py:630
  52.3 10.6 %all_to_all.30.rec = f32[16,4,128]{2,1,0:T(4,128)S(1)} all-to-all(f32[16,4,128]{2,1,0:T(4,128)S(1)} %get-tuple-element.59), channel_id=1, replica_groups=mesh['x'=4,'z_hi'=4,'z_lo'=2,'y_hi'=2,'y_lo'=2,'core'=2] {'z_hi','z_lo',..., dimensions={0} | all-to-all | bytes 65536 | tf_op jit(solution)/shard_map/act/all_to_all | solution.py:639
  62.9 0.6 act.3
  63.5 3.5 %all-to-all-start.2 = ((f32[16,4,128]{2,1,0:T(4,128)}), f32[16,4,128]{2,1,0:T(4,128)S(1)}, u32[]{:S(2)}, u32[]{:S(2)}) async-start(f32[16,4,128]{2,1,0:T(4,128)} %act.3), calls=%async_computation.2 | async-start | bytes 65536 | tf_op jit(solution)/shard_map/act/all_to_all | solution.py:642
  67.0 0.0 copy-start.3
  67.0 4.0 %down.1 = (bf16[4,64,256]{2,1,0:T(8,128)(2,1)}, f32[1152,256]{1,0:T(8,128)S(1)}, bf16[1152,256]{1,0:T(8,128)(2,1)}) custom-call(s32[4]{0:T(128)S(1)} %add_convert_fusion.flags, bf16[9,64,768]{2,1,0:T(8,128)(2,1)} %get-tuple-element.58.t_hbm, bf16[6,80,512]{2,1,0:T(8,128)(2,1)} %get-tuple-element.61.c_hbm, bf16[3,768,256]{2,1,0:T(8,128)(2,1)} %bitcast.16), custom_call_target="tpu_custom_call" | custom-call | flops 603979776 | bytes 1048576 | tf_op jit(solution)/shard_map/down/pallas_call | solution.py:645
  71.0 0.7 collective-permute-start.5
  71.7 1.7 %all-to-all-done.2.sums = f32[16,4,128]{2,1,0:T(4,128)S(1)} async-done(((f32[16,4,128]{2,1,0:T(4,128)}), f32[16,4,128]{2,1,0:T(4,128)S(1)}, u32[]{:S(2)}, u32[]{:S(2)}) %all-to-all-start.2) | async-done | bytes 32800 | tf_op jit(solution)/shard_map/act/all_to_all | solution.py:642
  73.4 0.0 copy-done.4
  73.4 4.0 %grad.1 = (bf16[10,64,1024]{2,1,0:T(8,128)(2,1)}, f32[1152,256]{1,0:T(8,128)S(1)}, bf16[1152,256]{1,0:T(8,128)(2,1)S(1)}, f32[2,256]{1,0:T(2,128)S(1)}) custom-call(s32[4]{0:T(128)S(1)} %add_convert_fusion.flags, f32[16,4,128]{2,1,0:T(4,128)S(1)} %all-to-all-done.2.sums, f32[2,256]{1,0:T(2,128)S(1)} %get-tuple-element.64.coef, f32[1,256]{1,0:T(1,128)S(1)} %bitcast.19, ...), custom_call_target="tpu_custom_call" | custom-call | flops 1887436800 | bytes 1048576 | tf_op jit(solution)/shard_map/grad/pallas_call | solution.py:658
  77.4 1.6 %collective-permute-start.4 = (bf16[1152,256]{1,0:T(8,128)(2,1)S(1)}, bf16[1152,256]{1,0:T(8,128)(2,1)S(1)}, u32[]{:S(2)}, u32[]{:S(2)}) collective-permute-start(bf16[1152,256]{1,0:T(8,128)(2,1)S(1)} %get-tuple-element.71), channel_id=1, source_target_pairs={{0,1},{1,0},{2,3},{3,2},{4,5},{5,4},{6,7},{7,6},{8,9},{9,8},{10,11... | collective-permute-start | bytes 1769480 | tf_op jit(solution)/shard_map/total/ppermute | solution.py:536
  79.0 0.0 collective-permute-done.5.down_other
  79.0 1.6 %collective-permute-done.4.conv_other = bf16[1152,256]{1,0:T(8,128)(2,1)S(1)} collective-permute-done((bf16[1152,256]{1,0:T(8,128)(2,1)S(1)}, bf16[1152,256]{1,0:T(8,128)(2,1)S(1)}, u32[]{:S(2)}, u32[]{:S(2)}) %collective-permute-start.4) | collective-permute-done | bytes 589856 | tf_op jit(solution)/shard_map/total/ppermute | solution.py:536
  80.7 1.1 total.3
  81.8 4.3 %all-to-all-start.3 = ((bf16[32,72,256]{2,1,0:T(8,128)(2,1)}), bf16[32,72,256]{2,1,0:T(8,128)(2,1)S(1)}, u32[]{:S(2)}, u32[]{:S(2)}) async-start(bf16[32,72,256]{2,1,0:T(8,128)(2,1)} %bitcast.20), calls=%async_computation.3 | async-start | bytes 2359296 | tf_op jit(solution)/shard_map/total/all_to_all | solution.py:691
  86.1 4.0 %input.1 = bf16[8,128,256]{2,1,0:T(8,128)(2,1)} custom-call(bf16[10,64,1024]{2,1,0:T(8,128)(2,1)} %get-tuple-element.74.h4_hbm, bf16[3,3,256,256]{3,2,1,0:T(8,128)(2,1)} %w_hbm.1), custom_call_target="tpu_custom_call" | custom-call | flops 1207959552 | bytes 1048576 | tf_op jit(solution)/shard_map/input/pallas_call | solution.py:675
  90.0 13.2 %all-to-all-done.3 = bf16[32,72,256]{2,1,0:T(8,128)(2,1)S(1)} async-done(((bf16[32,72,256]{2,1,0:T(8,128)(2,1)}), bf16[32,72,256]{2,1,0:T(8,128)(2,1)S(1)}, u32[]{:S(2)}, u32[]{:S(2)}) %all-to-all-start.3) | async-done | bytes 1179680 | tf_op jit(solution)/shard_map/total/all_to_all | solution.py:691
  103.2 0.2 reduce_sum.21
  103.4 9.8 %all_to_all.31 = bf16[4,72,256]{2,1,0:T(8,128)(2,1)S(1)} all-to-all(bf16[4,72,256]{2,1,0:T(8,128)(2,1)S(1)} %broadcast_in_dim.4), channel_id=1, replica_groups=mesh['x'=4,'z_hi'=4,'z_lo'=2,'y_hi'=2,'y_lo'=2,'core'=2] {'z_hi'}, dimensions={0} | all-to-all | bytes 294912 | tf_op jit(solution)/shard_map/total/all_to_all | solution.py:694
  113.2 0.1 broadcast_in_dim.5
  113.3 20.8 %all_to_all.32 = bf16[32,72,256]{2,1,0:T(8,128)(2,1)S(1)} all-to-all(bf16[32,72,256]{2,1,0:T(8,128)(2,1)S(1)} %broadcast_in_dim.5), channel_id=1, replica_groups=mesh['x'=4,'z_hi'=4,'z_lo'=2,'y_hi'=2,'y_lo'=2,'core'=2] {'x','z_lo','y_..., dimensions={0} | all-to-all | bytes 2359296 | tf_op jit(solution)/shard_map/total/all_to_all | solution.py:698
  134.1 4.3 %collective-permute-start.6 = (bf16[2304,256]{1,0:T(8,128)(2,1)S(1)}, bf16[2304,256]{1,0:T(8,128)(2,1)S(1)}, u32[]{:S(2)}, u32[]{:S(2)}) collective-permute-start(bf16[2304,256]{1,0:T(8,128)(2,1)S(1)} %bitcast.14), channel_id=1, source_target_pairs={{0,1},{1,0},{2,3},{3,2},{4,5},{5,4},{6,7},{7,6},{8,9},{9,8},{10,11... | collective-permute-start | bytes 3538952 | tf_op jit(solution)/shard_map/total/ppermute | solution.py:536
  138.4 0.6 fusion
  139.0 2.0 %total.4 = (f32[2304,256]{1,0:T(8,128)}, f32[2304,256]{1,0:T(8,128)}) custom-call(s32[4]{0:T(128)S(1)} %add_convert_fusion.flags, bf16[2304,256]{1,0:T(8,128)(2,1)S(1)} %bitcast.15), custom_call_target="tpu_custom_call" | custom-call | bytes 1048576 | tf_op jit(solution)/shard_map/total/pallas_call | solution.py:703
  141.1 0.0 collective-permute-done.6.rows
  141.1 2.0 %total.5 = (f32[2304,256]{1,0:T(8,128)}, f32[2304,256]{1,0:T(8,128)}) custom-call(s32[4]{0:T(128)S(1)} %add_convert_fusion.flags, bf16[2304,256]{1,0:T(8,128)(2,1)S(1)} %collective-permute-done.6.rows, f32[2304,256]{1,0:T(8,128)} %get-tuple-element.77.conv_in, f32[2304,256]{1,0:T(8,128)} %get-tuple-element.78.down_in), custom_call_target="tpu_custom_call", output_to_operand_aliasing={{0}: (2, {}), {1}: (3, {})} | custom-call | bytes 1048576 | tf_op jit(solution)/shard_map/total/pallas_call | solution.py:704
  (6 shorter events, 0.0 us)
Async XLA Ops:
  1.6 12.9 %collective-permute-start.1 = (bf16[2,32,256]{2,1,0:T(8,128)(2,1)S(1)}, bf16[2,32,256]{2,1,0:T(8,128)(2,1)S(1)}, u32[]{:S(2)}, u32[]{:S(2)}) collective-permute-start(bf16[2,32,256]{2,1,0:T(8,128)(2,1)S(1)} %halo.4), channel_id=1, source_target_pairs={{0,252},{4,8},{8,4},{12,16},{16,12},{20,24},{24,20},{28,32},{32,28... | collective-permute-start | bytes 98312 | tf_op jit(solution)/shard_map/halo/ppermute | solution.py:569
  12.9 4.3 %collective-permute-start = (bf16[2,32,256]{2,1,0:T(8,128)(2,1)S(1)}, bf16[2,32,256]{2,1,0:T(8,128)(2,1)S(1)}, u32[]{:S(2)}, u32[]{:S(2)}) collective-permute-start(bf16[2,32,256]{2,1,0:T(8,128)(2,1)S(1)} %halo.4), channel_id=1, source_target_pairs={{0,4},{4,0},{8,12},{12,8},{16,20},{20,16},{24,28},{28,24},{32,36},... | collective-permute-start | bytes 98312 | tf_op jit(solution)/shard_map/halo/ppermute | solution.py:568
  17.8 7.0 %collective-permute-start.2 = (bf16[336,256]{1,0:T(8,128)(2,1)S(1)}, bf16[336,256]{1,0:T(8,128)(2,1)S(1)}, u32[]{:S(2)}, u32[]{:S(2)}) collective-permute-start(bf16[336,256]{1,0:T(8,128)(2,1)S(1)} %get-tuple-element.46), channel_id=1, source_target_pairs={{0,1},{1,0},{2,3},{3,2},{4,5},{5,4},{6,7},{7,6},{8,9},{9,8},{10,11... | collective-permute-start | bytes 516104 | tf_op jit(solution)/shard_map/halo/ppermute | solution.py:581
  20.0 6.7 %collective-permute-start.3 = (bf16[336,256]{1,0:T(8,128)(2,1)S(1)}, bf16[336,256]{1,0:T(8,128)(2,1)S(1)}, u32[]{:S(2)}, u32[]{:S(2)}) collective-permute-start(bf16[336,256]{1,0:T(8,128)(2,1)S(1)} %get-tuple-element.47), channel_id=1, source_target_pairs={{1,2},{2,1},{5,6},{6,5},{9,10},{10,9},{13,14},{14,13},{17,18},{18,... | collective-permute-start | bytes 516104 | tf_op jit(solution)/shard_map/halo/ppermute | solution.py:583
  26.7 9.3 %copy-start = (bf16[3,3,256,256]{3,2,1,0:T(8,128)(2,1)S(1)}, bf16[3,3,256,256]{3,2,1,0:T(8,128)(2,1)}, u32[]{:S(2)}) copy-start(bf16[3,3,256,256]{3,2,1,0:T(8,128)(2,1)} %dw.1) | copy-start | bytes 3538948
  29.8 19.0 %all-to-all-start = ((f32[256,1,128]{2,1,0:T(1,128)}), f32[256,1,128]{2,1,0:T(1,128)S(1)}, u32[]{:S(2)}, u32[]{:S(2)}) async-start(f32[256,1,128]{2,1,0:T(1,128)} %get-tuple-element.53), calls=%async_computation | async-start | bytes 262144 | tf_op jit(solution)/shard_map/conv/all_to_all | solution.py:616
  36.0 12.8 %copy-start.1 = (f32[256]{0:T(256)S(1)}, f32[256]{0:T(256)}, u32[]{:S(2)}) copy-start(f32[256]{0:T(256)} %param.10) | copy-start | bytes 3076
  36.0 12.8 %copy-start.2 = (f32[256]{0:T(256)S(1)}, f32[256]{0:T(256)}, u32[]{:S(2)}) copy-start(f32[256]{0:T(256)} %param.9) | copy-start | bytes 3076
  63.5 9.9 %all-to-all-start.2 = ((f32[16,4,128]{2,1,0:T(4,128)}), f32[16,4,128]{2,1,0:T(4,128)S(1)}, u32[]{:S(2)}, u32[]{:S(2)}) async-start(f32[16,4,128]{2,1,0:T(4,128)} %act.3), calls=%async_computation.2 | async-start | bytes 65536 | tf_op jit(solution)/shard_map/act/all_to_all | solution.py:642
  67.0 6.4 %copy-start.3 = (bf16[2,10,80,256]{3,2,1,0:T(8,128)(2,1)S(1)}, bf16[2,10,80,256]{3,2,1,0:T(8,128)(2,1)}, u32[]{:S(2)}) copy-start(bf16[2,10,80,256]{3,2,1,0:T(8,128)(2,1)} %get-tuple-element.66.h_in) | copy-start | bytes 2457604
  67.0 6.4 %copy-start.4 = (f32[10,80,256]{2,1,0:T(8,128)S(1)}, f32[10,80,256]{2,1,0:T(8,128)}, u32[]{:S(2)}) copy-start(f32[10,80,256]{2,1,0:T(8,128)} %get-tuple-element.65.pq) | copy-start | bytes 2457604
  71.0 8.0 %collective-permute-start.5 = (bf16[1152,256]{1,0:T(8,128)(2,1)}, bf16[1152,256]{1,0:T(8,128)(2,1)S(1)}, u32[]{:S(2)}, u32[]{:S(2)}) collective-permute-start(bf16[1152,256]{1,0:T(8,128)(2,1)} %get-tuple-element.73), channel_id=1, source_target_pairs={{0,1},{1,0},{2,3},{3,2},{4,5},{5,4},{6,7},{7,6},{8,9},{9,8},{10,11... | collective-permute-start | bytes 1769480 | tf_op jit(solution)/shard_map/down/ppermute | solution.py:536
  77.4 3.3 %collective-permute-start.4 = (bf16[1152,256]{1,0:T(8,128)(2,1)S(1)}, bf16[1152,256]{1,0:T(8,128)(2,1)S(1)}, u32[]{:S(2)}, u32[]{:S(2)}) collective-permute-start(bf16[1152,256]{1,0:T(8,128)(2,1)S(1)} %get-tuple-element.71), channel_id=1, source_target_pairs={{0,1},{1,0},{2,3},{3,2},{4,5},{5,4},{6,7},{7,6},{8,9},{9,8},{10,11... | collective-permute-start | bytes 1769480 | tf_op jit(solution)/shard_map/total/ppermute | solution.py:536
  81.8 21.4 %all-to-all-start.3 = ((bf16[32,72,256]{2,1,0:T(8,128)(2,1)}), bf16[32,72,256]{2,1,0:T(8,128)(2,1)S(1)}, u32[]{:S(2)}, u32[]{:S(2)}) async-start(bf16[32,72,256]{2,1,0:T(8,128)(2,1)} %bitcast.20), calls=%async_computation.3 | async-start | bytes 2359296 | tf_op jit(solution)/shard_map/total/all_to_all | solution.py:691
  134.1 6.9 %collective-permute-start.6 = (bf16[2304,256]{1,0:T(8,128)(2,1)S(1)}, bf16[2304,256]{1,0:T(8,128)(2,1)S(1)}, u32[]{:S(2)}, u32[]{:S(2)}) collective-permute-start(bf16[2304,256]{1,0:T(8,128)(2,1)S(1)} %bitcast.14), channel_id=1, source_target_pairs={{0,1},{1,0},{2,3},{3,2},{4,5},{5,4},{6,7},{7,6},{8,9},{9,8},{10,11... | collective-permute-start | bytes 3538952 | tf_op jit(solution)/shard_map/total/ppermute | solution.py:536
